TPU v7x, 32 devices: a whole 2x2x4 slice. The times are simulated.
32 devices in a mesh: ctx: 4 (over y, x), fsdp: 8 (over z, core).
Axes of the slice: x: 2, y: 2, z: 4, core: 2. Of those that a mesh axis runs over, the one named last changes fastest.
Arguments:
- tokens: bfloat16 [8, 2048, 1152], P('fsdp', 'ctx'), may hold values from -6 to 6
- table: int32 [4, 2], replicated, may hold values from 0 to 7, as said below
- norm1_gain: bfloat16 [1152], P('fsdp'), may hold values from 0.5 to 1.5
- w_query: bfloat16 [1152, 1152], P('fsdp'), may hold values from -0.1875 to 0.1875
- w_key: bfloat16 [1152, 384], P('fsdp'), may hold values from -0.1875 to 0.1875
- w_value: bfloat16 [1152, 384], P('fsdp'), may hold values from -0.1875 to 0.1875
- w_out: bfloat16 [1152, 1152], P('fsdp'), may hold values from -6 to 6
- norm2_gain: bfloat16 [1152], P('fsdp'), may hold values from 0.5 to 1.5
- w_gate: bfloat16 [1152, 3072], P('fsdp'), may hold values from -0.1875 to 0.1875
- w_up: bfloat16 [1152, 3072], P('fsdp'), may hold values from -0.1875 to 0.1875
- w_down: bfloat16 [3072, 1152], P('fsdp'), may hold values from -0.109375 to 0.109375
- cotangent: bfloat16 [8, 2048, 1152], P('fsdp', 'ctx'), may hold values from -6 to 6
Outputs:
- output: bfloat16 [8, 2048, 1152], P('fsdp', 'ctx')
- grad_tokens: bfloat16 [8, 2048, 1152], P('fsdp', 'ctx')
- grad_norm1: float32 [1152], P('fsdp')
- grad_query: float32 [1152, 1152], P('fsdp')
- grad_key: float32 [1152, 384], P('fsdp')
- grad_value: float32 [1152, 384], P('fsdp')
- grad_out: float32 [1152, 1152], P('fsdp')
- grad_norm2: float32 [1152], P('fsdp')
- grad_gate: float32 [1152, 3072], P('fsdp')
- grad_up: float32 [1152, 3072], P('fsdp')
- grad_down: float32 [3072, 1152], P('fsdp')
Inputs may be any that keep to these rules, and one draw needn't show every extreme that they name: `table`: row c lists the 2 blocks of context device c; every block 0 to 7 stands once, and each row is made of consecutive pairs b, 7 - b.
All inputs are finite; a program needn't handle non-finite values.
Results may differ from a plain program's by a relative error of at most 0.022.
Values may be sent and summed in bfloat16 or wider, within the bound.
No kernel may reach another device: no remote copies, remote signals or barrier semaphores. Data moves between devices by JAX's collectives and lax.ppermute only.
A program may use at most 320 MiB of HBM per device.

v0:
```python
import jax
import jax.numpy as jnp
from jax import lax
from jax.sharding import PartitionSpec as P

H = 18
KVH = 6
HD = 64
BLK = 256


EPS = 1e-05


def dot_first(left, right):
    return lax.dot_general(
        left, right, (((0,), (0,)), ((), ())), preferred_element_type=jnp.float32
    )


def dot_last(left, right):
    return lax.dot_general(
        left, right, (((1,), (1,)), ((), ())), preferred_element_type=jnp.float32
    )


def rotate(values, places, count, sign):
    split = HD // 2
    shaped = values.reshape(values.shape[0], count, HD)
    frequency = 10000.0 ** (-(jnp.arange(split, dtype=jnp.float32) * 2.0 / HD))
    angles = places.astype(jnp.float32)[:, None] * frequency
    cosine = jnp.cos(angles)[:, None, :]
    sine = jnp.sin(angles)[:, None, :] * sign
    first_half = shaped[..., :split]
    second_half = shaped[..., split:]
    turned = jnp.concatenate(
        [first_half * cosine - second_half * sine, second_half * cosine + first_half * sine], -1
    )
    return turned.reshape(values.shape[0], count * HD)


def norm_back(values, scale_inv, gain, grad_in):
    weighted = gain.astype(jnp.float32) * grad_in
    gain_grad = jnp.sum(grad_in * values * scale_inv, 0)
    grad_out = scale_inv * weighted - values * scale_inv**3 * jnp.mean(
        weighted * values, -1, keepdims=True
    )
    return (gain_grad, grad_out)


def to_groups(values, rows):
    ratio = H // KVH
    return values.reshape(rows, KVH, ratio, HD).transpose(1, 2, 0, 3).reshape(KVH, ratio * rows, HD)


def from_groups(values, rows):
    ratio = H // KVH
    return values.reshape(KVH, ratio, rows, HD).transpose(2, 0, 1, 3).reshape(rows, H * HD)


def body(
    tokens,
    table,
    norm1_gain,
    w_query,
    w_key,
    w_value,
    w_out,
    norm2_gain,
    w_gate,
    w_up,
    w_down,
    cotangent,
):
    ratio = H // KVH
    scale = HD ** (-0.5)
    x = tokens[0].astype(jnp.float32)
    rows = x.shape[0]
    offsets = jnp.arange(BLK, dtype=jnp.int32)
    own_blocks = lax.dynamic_index_in_dim(table, lax.axis_index("ctx"), 0, keepdims=False)
    own_places = (own_blocks[:, None] * BLK + offsets[None, :]).reshape(-1)
    own_ids = jnp.tile(jnp.repeat(own_blocks, BLK), ratio)
    all_ids = jnp.repeat(table.reshape(-1), BLK)
    visible = all_ids[None, :] <= own_ids[:, None]
    forward_set = (
        lax.all_gather(norm1_gain, "fsdp", axis=0, tiled=True),
        lax.all_gather(w_query, "fsdp", axis=0, tiled=True),
        lax.all_gather(w_key, "fsdp", axis=0, tiled=True),
        lax.all_gather(w_value, "fsdp", axis=0, tiled=True),
        lax.all_gather(w_out, "fsdp", axis=0, tiled=True),
        lax.all_gather(norm2_gain, "fsdp", axis=0, tiled=True),
        lax.all_gather(w_gate, "fsdp", axis=0, tiled=True),
        lax.all_gather(w_up, "fsdp", axis=0, tiled=True),
        lax.all_gather(w_down, "fsdp", axis=0, tiled=True),
    )
    gain_one, w_q, w_k, w_v, w_o, gain_two, w_g, w_u, w_d = forward_set
    scale_one = lax.rsqrt(jnp.mean(x * x, -1, keepdims=True) + EPS)
    a = (x * scale_one * gain_one.astype(jnp.float32)).astype(jnp.bfloat16)
    q = jnp.dot(a, w_q, preferred_element_type=jnp.float32)
    k = jnp.dot(a, w_k, preferred_element_type=jnp.float32)
    v = jnp.dot(a, w_v, preferred_element_type=jnp.float32).astype(jnp.bfloat16)
    query_rot = rotate(q, own_places, H, 1.0).astype(jnp.bfloat16)
    key_rot = rotate(k, own_places, KVH, 1.0).astype(jnp.bfloat16)
    key_all, value_all = (
        lax.all_gather(key_rot, "ctx", axis=0, tiled=True),
        lax.all_gather(v, "ctx", axis=0, tiled=True),
    )
    length = key_all.shape[0]
    query_groups = to_groups(query_rot, rows)
    key_groups = key_all.reshape(length, KVH, HD).transpose(1, 0, 2)
    value_groups = value_all.reshape(length, KVH, HD).transpose(1, 0, 2)

    def group_fwd(inputs):
        query_one, key_one, value_one = inputs
        scores = dot_last(query_one, key_one) * scale
        masked = jnp.where(visible, scores, -1e30)
        top = jnp.max(masked, -1, keepdims=True)
        expo = jnp.exp(masked - top)
        total = jnp.sum(expo, -1, keepdims=True)
        probs = (expo / total).astype(jnp.bfloat16)
        mixed = jnp.dot(probs, value_one, preferred_element_type=jnp.float32)
        return (mixed.astype(jnp.bfloat16), (top + jnp.log(total))[:, 0])

    mixed_groups, log_sums = lax.map(group_fwd, (query_groups, key_groups, value_groups))
    head_out = from_groups(mixed_groups, rows)
    resid = x + jnp.dot(head_out, w_o, preferred_element_type=jnp.float32)
    scale_two = lax.rsqrt(jnp.mean(resid * resid, -1, keepdims=True) + EPS)
    b = (resid * scale_two * gain_two.astype(jnp.float32)).astype(jnp.bfloat16)
    gate_pre = jnp.dot(b, w_g, preferred_element_type=jnp.float32)
    up_pre = jnp.dot(b, w_u, preferred_element_type=jnp.float32)
    sig_gate = jax.nn.sigmoid(gate_pre)
    silu_gate = gate_pre * sig_gate
    hidden = (silu_gate * up_pre).astype(jnp.bfloat16)
    result = (resid + jnp.dot(hidden, w_d, preferred_element_type=jnp.float32)).astype(jnp.bfloat16)
    backward_set = (
        lax.all_gather(norm1_gain, "fsdp", axis=0, tiled=True),
        lax.all_gather(w_query, "fsdp", axis=0, tiled=True),
        lax.all_gather(w_key, "fsdp", axis=0, tiled=True),
        lax.all_gather(w_value, "fsdp", axis=0, tiled=True),
        lax.all_gather(w_out, "fsdp", axis=0, tiled=True),
        lax.all_gather(norm2_gain, "fsdp", axis=0, tiled=True),
        lax.all_gather(w_gate, "fsdp", axis=0, tiled=True),
        lax.all_gather(w_up, "fsdp", axis=0, tiled=True),
        lax.all_gather(w_down, "fsdp", axis=0, tiled=True),
    )
    gain_one_b, w_q_b, w_k_b, w_v_b, w_o_b, gain_two_b, w_g_b, w_u_b, w_d_b = backward_set
    dy = cotangent[0].astype(jnp.float32)
    dy_low = dy.astype(jnp.bfloat16)
    grad_d = dot_first(hidden, dy_low)
    dhidden = dot_last(dy_low, w_d_b)
    dgate = (dhidden * up_pre * sig_gate * (1.0 + gate_pre * (1.0 - sig_gate))).astype(jnp.bfloat16)
    dup_low = (dhidden * silu_gate).astype(jnp.bfloat16)
    grad_g = dot_first(b, dgate)
    grad_u = dot_first(b, dup_low)
    grad_b = dot_last(dgate, w_g_b) + dot_last(dup_low, w_u_b)
    grad_gain_two, norm_part = norm_back(resid, scale_two, gain_two_b, grad_b)
    grad_resid = dy + norm_part
    resid_low = grad_resid.astype(jnp.bfloat16)
    grad_o = dot_first(head_out, resid_low)
    dheads = dot_last(resid_low, w_o_b).astype(jnp.bfloat16)
    dhead_groups = to_groups(dheads, rows)

    def group_bwd(inputs):
        query_one, key_one, value_one, dout_one, lse_one = inputs
        scores = dot_last(query_one, key_one) * scale
        probs = jnp.exp(jnp.where(visible, scores, -1e30) - lse_one[:, None])
        probs_low = probs.astype(jnp.bfloat16)
        dprobs = dot_last(dout_one, value_one)
        inner = jnp.sum(probs * dprobs, -1, keepdims=True)
        dscores = (probs * (dprobs - inner)).astype(jnp.bfloat16)
        dquery = jnp.dot(dscores, key_one, preferred_element_type=jnp.float32) * scale
        dkey = dot_first(dscores, query_one) * scale
        dvalue = dot_first(probs_low, dout_one)
        return (dquery, dkey, dvalue)

    dquery_groups, dkey_groups, dvalue_groups = lax.map(
        group_bwd, (query_groups, key_groups, value_groups, dhead_groups, log_sums)
    )
    dquery_rot = from_groups(dquery_groups, rows)
    dkey_all = dkey_groups.transpose(1, 0, 2).reshape(length, KVH * HD)
    dvalue_all = dvalue_groups.transpose(1, 0, 2).reshape(length, KVH * HD)
    own_kv = lax.psum_scatter(
        jnp.concatenate([dkey_all, dvalue_all], 1).astype(jnp.bfloat16),
        "ctx",
        scatter_dimension=0,
        tiled=True,
    ).astype(jnp.float32)
    dq = rotate(dquery_rot, own_places, H, -1.0).astype(jnp.bfloat16)
    dk = rotate(own_kv[:, : KVH * HD], own_places, KVH, -1.0).astype(jnp.bfloat16)
    dv_low = own_kv[:, KVH * HD :].astype(jnp.bfloat16)
    grad_q = dot_first(a, dq)
    grad_k = dot_first(a, dk)
    grad_v = dot_first(a, dv_low)
    grad_a = dot_last(dq, w_q_b) + dot_last(dk, w_k_b) + dot_last(dv_low, w_v_b)
    grad_gain_one, input_part = norm_back(x, scale_one, gain_one_b, grad_a)
    grad_x = (grad_resid + input_part).astype(jnp.bfloat16)
    grad_terms = (
        grad_gain_one,
        grad_q,
        grad_k,
        grad_v,
        grad_o,
        grad_gain_two,
        grad_g,
        grad_u,
        grad_d,
    )
    shares = (
        lax.psum_scatter(
            grad_terms[0].astype(jnp.bfloat16), "fsdp", scatter_dimension=0, tiled=True
        ).astype(jnp.float32),
        lax.psum_scatter(
            grad_terms[1].astype(jnp.bfloat16), "fsdp", scatter_dimension=0, tiled=True
        ).astype(jnp.float32),
        lax.psum_scatter(
            grad_terms[2].astype(jnp.bfloat16), "fsdp", scatter_dimension=0, tiled=True
        ).astype(jnp.float32),
        lax.psum_scatter(
            grad_terms[3].astype(jnp.bfloat16), "fsdp", scatter_dimension=0, tiled=True
        ).astype(jnp.float32),
        lax.psum_scatter(
            grad_terms[4].astype(jnp.bfloat16), "fsdp", scatter_dimension=0, tiled=True
        ).astype(jnp.float32),
        lax.psum_scatter(
            grad_terms[5].astype(jnp.bfloat16), "fsdp", scatter_dimension=0, tiled=True
        ).astype(jnp.float32),
        lax.psum_scatter(
            grad_terms[6].astype(jnp.bfloat16), "fsdp", scatter_dimension=0, tiled=True
        ).astype(jnp.float32),
        lax.psum_scatter(
            grad_terms[7].astype(jnp.bfloat16), "fsdp", scatter_dimension=0, tiled=True
        ).astype(jnp.float32),
        lax.psum_scatter(
            grad_terms[8].astype(jnp.bfloat16), "fsdp", scatter_dimension=0, tiled=True
        ).astype(jnp.float32),
    )
    summed = (
        lax.psum(shares[0].astype(jnp.bfloat16), "ctx").astype(jnp.float32),
        lax.psum(shares[1].astype(jnp.bfloat16), "ctx").astype(jnp.float32),
        lax.psum(shares[2].astype(jnp.bfloat16), "ctx").astype(jnp.float32),
        lax.psum(shares[3].astype(jnp.bfloat16), "ctx").astype(jnp.float32),
        lax.psum(shares[4].astype(jnp.bfloat16), "ctx").astype(jnp.float32),
        lax.psum(shares[5].astype(jnp.bfloat16), "ctx").astype(jnp.float32),
        lax.psum(shares[6].astype(jnp.bfloat16), "ctx").astype(jnp.float32),
        lax.psum(shares[7].astype(jnp.bfloat16), "ctx").astype(jnp.float32),
        lax.psum(shares[8].astype(jnp.bfloat16), "ctx").astype(jnp.float32),
    )
    return (
        result[None],
        grad_x[None],
        summed[0],
        summed[1],
        summed[2],
        summed[3],
        summed[4],
        summed[5],
        summed[6],
        summed[7],
        summed[8],
    )


def solution(mesh):
    placed = (
        P("fsdp", "ctx", None),
        P(),
        P("fsdp"),
        P("fsdp", None),
        P("fsdp", None),
        P("fsdp", None),
        P("fsdp", None),
        P("fsdp"),
        P("fsdp", None),
        P("fsdp", None),
        P("fsdp", None),
        P("fsdp", "ctx", None),
    )
    return jax.shard_map(
        body,
        mesh=mesh,
        in_specs=placed,
        out_specs=(
            P("fsdp", "ctx", None),
            P("fsdp", "ctx", None),
            P("fsdp"),
            P("fsdp", None),
            P("fsdp", None),
            P("fsdp", None),
            P("fsdp", None),
            P("fsdp"),
            P("fsdp", None),
            P("fsdp", None),
            P("fsdp", None),
        ),
        check_vma=False,
    )
```

profile of v0, /device:TPU:0, one launch (start us, length us, event | category | flops | bytes accessed | tf_op | source)
XLA Modules:
  0.0 1124.1 jit_solution(11554610147607327843)
XLA Ops:
  11.0 18.3 %all-reduce.5 = (bf16[1152]{0:T(1024)(128)(2,1)S(1)}, bf16[1152]{0:T(1024)(128)(2,1)S(1)}) all-reduce(bf16[1152]{0:T(1024)(128)(2,1)S(1)} %dynamic-update-slice, bf16[1152]{0:T(1024)(128)(2,1)S(1)} %dynamic-update-slice.1), channel_id=1, replica_groups=mesh['ctx'=4,'fsdp'=8] {'fsdp'}, use_global_device_ids=true, to_apply=%add | all-reduce | flops 2304 | bytes 9216
  32.5 16.1 %all_gather.44 = bf16[1152,384]{1,0:T(8,128)(2,1)S(1)} all-gather(bf16[144,384]{1,0:T(8,128)(2,1)} %param.20), channel_id=1, replica_groups=mesh['ctx'=4,'fsdp'=8] {'fsdp'}, dimensions={0}, use_global_device_ids=true | all-gather | bytes 995328 | tf_op jit(solution)/shard_map/all_gather | solution.py:88
  54.0 16.4 %all_gather.46 = bf16[1152,384]{1,0:T(8,128)(2,1)S(1)} all-gather(bf16[144,384]{1,0:T(8,128)(2,1)S(1)} %copy-done.29), channel_id=1, replica_groups=mesh['ctx'=4,'fsdp'=8] {'fsdp'}, dimensions={0}, use_global_device_ids=true | all-gather | bytes 995328 | tf_op jit(solution)/shard_map/all_gather | solution.py:89
  77.4 6.2 all-gather.10.cloned.1.call-done
  83.6 4.1 copy.61
  87.7 29.3 %all-gather.12.cloned.1.call-done = bf16[2048,384]{1,0:T(8,128)(2,1)} async-done(((bf16[512,384]{1,0:T(8,128)(2,1)}), bf16[2048,384]{1,0:T(8,128)(2,1)}) %all-gather.12.cloned.1.call-update) | async-done | bytes 1572880 | tf_op jit(solution)/shard_map/all_gather | solution.py:106
  121.5 31.4 %all-gather.8.cloned.1.call-done = bf16[1152,1152]{1,0:T(8,128)(2,1)} async-done(((bf16[144,1152]{1,0:T(8,128)(2,1)}), bf16[1152,1152]{1,0:T(8,128)(2,1)}) %all-gather.8.cloned.1.call-update) | async-done | bytes 2654224 | tf_op jit(solution)/shard_map/all_gather | solution.py:87
  152.8 5.2 copy.56
  158.1 3.6 fusion.75
  163.4 68.8 %while.28 = (s32[]{:T(128)}, bf16[6,1536,64]{1,2,0:T(8,128)(2,1)}, f32[6,1536]{1,0:T(8,128)}, bf16[6,1536,64]{2,1,0:T(8,128)(2,1)S(1)}, bf16[6,2048,64]{2,1,0:T(...) while((s32[]{:T(128)}, bf16[6,1536,64]{1,2,0:T(8,128)(2,1)}, ...), condition=%wide.region_4.5_spmd.clone, body=%wide.region_1.4_spmd.clone.sunk | while | flops 833714688 | bytes 39479408 | solution.py:124
  168.4 5.0 fusion.146
  179.9 5.0 fusion.146
  191.4 5.0 fusion.146
  202.8 5.0 fusion.146
  214.3 5.0 fusion.146
  225.8 5.0 fusion.146
  232.3 4.2 reshape.317
  239.2 4.3 multiply_reduce_fusion.3
  245.1 14.2 %all-gather.16.cloned.1.call-done = bf16[1152,3072]{1,0:T(8,128)(2,1)} async-done(((bf16[144,3072]{1,0:T(8,128)(2,1)}), bf16[1152,3072]{1,0:T(8,128)(2,1)}) %all-gather.16.cloned.1.call-update) | async-done | bytes 7077904 | tf_op jit(solution)/shard_map/all_gather | solution.py:92
  259.3 9.6 fusion.91
  268.9 61.7 %all-gather.18.cloned.1.call-done = bf16[1152,3072]{1,0:T(8,128)(2,1)} async-done(((bf16[144,3072]{1,0:T(8,128)(2,1)}), bf16[1152,3072]{1,0:T(8,128)(2,1)}) %all-gather.18.cloned.1.call-update) | async-done | bytes 7077904 | tf_op jit(solution)/shard_map/all_gather | solution.py:93
  330.7 10.4 fusion.92
  341.1 61.1 %all-gather.20.cloned.1.call-done = bf16[3072,1152]{1,0:T(8,128)(2,1)} async-done(((bf16[384,1152]{1,0:T(8,128)(2,1)}), bf16[3072,1152]{1,0:T(8,128)(2,1)}) %all-gather.20.cloned.1.call-update) | async-done | bytes 7077904 | tf_op jit(solution)/shard_map/all_gather | solution.py:94
  402.2 12.1 %multiply_convert_fusion.1 = (bf16[512,3072]{1,0:T(8,128)(2,1)S(1)}, bf16[512,3072]{1,0:T(8,128)(2,1)S(1)}, bf16[512,3072]{1,0:T(8,128)(2,1)}) fusion(f32[512,3072]{1,0:T(8,128)} %fusion.91, f32[512,3072]{1,0:T(8,128)} %fusion.92, bf16[3072,1152]{1,0:T(8,128)(2,1)} %all-gather.20.cloned.1.call-done, bf16[1,512,1152]{2,1,0:T(8,128)(2,1)S(1)} %copy-done.21), kind=kOutput, calls=%fused_computation.58 | convolution fusion | flops 3647471616 | bytes 30277632 | tf_op jit(solution)/shard_map/dot_general | solution.py:22
  414.3 8.8 fusion.93
  423.2 5.2 multiply_reduce_fusion.1
  435.4 147.9 %while.29 = (s32[]{:T(128)}, f32[6,1536,64]{1,2,0:T(8,128)}, bf16[6,2048,64]{1,2,0:T(8,128)(2,1)S(1)}, bf16[6,2048,64]{1,2,0:T(8,128)(2,1)}, bf16[6,1536,64]{2,1...) while((s32[]{:T(128)}, f32[6,1536,64]{1,2,0:T(8,128)}, ...), condition=%wide.region_9.10_spmd.clone, body=%wide.region_7.9_spmd.clone.sunk | while | flops 2044951040 | bytes 136758512 | solution.py:176
  439.3 5.3 multiply_reduce_fusion.5
  444.6 4.0 multiply_convert_fusion.6
  448.5 5.8 fusion.156
  463.9 5.3 multiply_reduce_fusion.5
  469.2 4.0 multiply_convert_fusion.6
  473.2 5.8 fusion.156
  488.5 5.3 multiply_reduce_fusion.5
  493.8 4.0 multiply_convert_fusion.6
  497.8 5.8 fusion.156
  513.2 5.3 multiply_reduce_fusion.5
  518.4 4.0 multiply_convert_fusion.6
  522.4 5.8 fusion.156
  537.8 5.3 multiply_reduce_fusion.5
  543.1 4.0 multiply_convert_fusion.6
  547.0 5.8 fusion.156
  562.4 5.3 multiply_reduce_fusion.5
  567.7 4.0 multiply_convert_fusion.6
  571.6 5.8 fusion.156
  583.2 3.6 pad_maximum_fusion
  586.9 3.5 reshape.321
  598.0 4.4 convolution_convert_fusion.3
  602.5 27.0 %reduce-scatter.9.cloned.1.call-done = bf16[512,768]{0,1:T(8,128)(2,1)} async-done(((bf16[2048,768]{0,1:T(8,128)(2,1)}), bf16[512,768]{0,1:T(8,128)(2,1)}) %reduce-scatter.9.cloned.1.call-update) | async-done | bytes 786448 | tf_op jit(solution)/shard_map/reduce_scatter | solution.py:182
  637.4 9.1 convolution_convert_fusion.2
  646.6 9.0 convolution_convert_fusion.1
  655.9 9.4 convolution_convert_fusion
  665.5 4.2 reduce-scatter.11.cloned.1.call-done
  669.6 39.1 %reduce-scatter.17.cloned.1.call-done = bf16[144,1152]{1,0:T(8,128)(2,1)} async-done(((bf16[1152,1152]{1,0:T(8,128)(2,1)}), bf16[144,1152]{1,0:T(8,128)(2,1)}) %reduce-scatter.17.cloned.1.call-update) | async-done | bytes 331792 | tf_op jit(solution)/shard_map/reduce_scatter | solution.py:221
  708.8 33.6 %reduce-scatter.13.cloned.1.call-done = bf16[144,384]{1,0:T(8,128)(2,1)} async-done(((bf16[1152,384]{1,0:T(8,128)(2,1)}), bf16[144,384]{1,0:T(8,128)(2,1)}) %reduce-scatter.13.cloned.1.call-update) | async-done | bytes 110608 | tf_op jit(solution)/shard_map/reduce_scatter | solution.py:215
  742.3 33.0 %reduce-scatter.15.cloned.1.call-done = bf16[144,384]{1,0:T(8,128)(2,1)} async-done(((bf16[1152,384]{1,0:T(8,128)(2,1)}), bf16[144,384]{1,0:T(8,128)(2,1)}) %reduce-scatter.15.cloned.1.call-update) | async-done | bytes 110608 | tf_op jit(solution)/shard_map/reduce_scatter | solution.py:218
  775.4 77.9 %reduce-scatter.19.cloned.1.call-done = bf16[144,3072]{1,0:T(8,128)(2,1)} async-done(((bf16[1152,3072]{1,0:T(8,128)(2,1)}), bf16[144,3072]{1,0:T(8,128)(2,1)}) %reduce-scatter.19.cloned.1.call-update) | async-done | bytes 884752 | tf_op jit(solution)/shard_map/reduce_scatter | solution.py:227
  853.3 77.8 %reduce-scatter.21.cloned.1.call-done = bf16[144,3072]{1,0:T(8,128)(2,1)} async-done(((bf16[1152,3072]{1,0:T(8,128)(2,1)}), bf16[144,3072]{1,0:T(8,128)(2,1)}) %reduce-scatter.21.cloned.1.call-update) | async-done | bytes 884752 | tf_op jit(solution)/shard_map/reduce_scatter | solution.py:230
  931.1 77.8 %reduce-scatter.23.cloned.1.call-done = bf16[384,1152]{1,0:T(8,128)(2,1)} async-done(((bf16[3072,1152]{1,0:T(8,128)(2,1)}), bf16[384,1152]{1,0:T(8,128)(2,1)}) %reduce-scatter.23.cloned.1.call-update) | async-done | bytes 884752 | tf_op jit(solution)/shard_map/reduce_scatter | solution.py:233
  1009.5 4.1 fusion.94
  1013.7 8.7 fusion.56
  1027.1 14.6 %all-reduce.4 = (bf16[1152]{0:T(1024)(128)(2,1)}, bf16[1152]{0:T(1024)(128)(2,1)}) all-reduce(bf16[1152]{0:T(1024)(128)(2,1)S(1)} %get-tuple-element.213, bf16[1152]{0:T(1024)(128)(2,1)} %get-tuple-element.211), channel_id=3, replica_groups=mesh['ctx'=4,'fsdp'=8] {'fsdp'}, use_global_device_ids=true, to_apply=%region_13.14.clone | all-reduce | flops 2304 | bytes 9216
  1043.7 10.4 all-reduce.6
  1060.6 45.4 %all-reduce.10.cloned.1.call-done = (bf16[144,1152]{1,0:T(8,128)(2,1)}, bf16[144,384]{1,0:T(8,128)(2,1)}, bf16[144,384]{1,0:T(8,128)(2,1)}, bf16[144,1152]{1,0:T...) async-done(((bf16[144,1152]{1,0:T(8,128)(2,1)}, bf16[144,384]{1,0:T(8,128)(2,1)}, bf16[144,384]{1,0:T(8,128)(2,1)}, ...) | async-done | bytes 3538960 | tf_op jit(solution)/shard_map/psum | solution.py:239
  (276 shorter events, 172.4 us)
Async XLA Ops:
  7.2 43.8 %copy-start.3 = (bf16[1,512,1152]{2,1,0:T(8,128)(2,1)S(1)}, bf16[1,512,1152]{2,1,0:T(8,128)(2,1)}, u32[]{:S(2)}) copy-start(bf16[1,512,1152]{2,1,0:T(8,128)(2,1)} %param.16) | copy-start | bytes 3538948
  7.2 76.4 %all-gather.10.cloned.1.call-start = ((), (), s32[]{:S(2)}) async-start(), calls=%async_computation.9 | async-start | bytes 1966080 | tf_op jit(solution)/shard_map/all_gather | solution.py:105
  29.3 128.7 %copy-start.32 = (f32[1152]{0:T(1024)}, f32[1152]{0:T(1024)S(1)}, u32[]{:S(2)}) copy-start(f32[1152]{0:T(1024)S(1)} %convert_element_type.200) | copy-start | bytes 13828
  31.5 126.5 %copy-start.34 = (f32[512]{0:T(512)}, f32[512]{0:T(512)S(1)}, u32[]{:S(2)}) copy-start(f32[512]{0:T(512)S(1)} %get-tuple-element.285) | copy-start | bytes 6148
  48.6 4.4 copy-start.9
  51.0 110.7 %copy-start.14 = (f32[512,32]{0,1:T(8,128)}, f32[512,32]{0,1:T(8,128)S(1)}, u32[]{:S(2)}) copy-start(f32[512,32]{0,1:T(8,128)S(1)} %get-tuple-element.283) | copy-start | bytes 196612
  51.0 3.0 copy-start.29
  53.9 63.1 %all-gather.12.cloned.1.call-start = ((), (), s32[]{:S(2)}) async-start(), calls=%async_computation.10 | async-start | bytes 1966080 | tf_op jit(solution)/shard_map/all_gather | solution.py:106
  72.9 3.6 copy-start.39
  73.0 79.9 %all-gather.8.cloned.1.call-start = ((), (), s32[]{:S(2)}) async-start(), calls=%async_computation.8 | async-start | bytes 2985984 | tf_op jit(solution)/shard_map/all_gather | solution.py:87
  73.7 165.5 %all-gather.14.cloned.1.call-start = ((), (), s32[]{:S(2)}) async-start(), calls=%async_computation.11 | async-start | bytes 2985984 | tf_op jit(solution)/shard_map/all_gather | solution.py:90
  74.3 185.0 %all-gather.16.cloned.1.call-start = ((), (), s32[]{:S(2)}) async-start(), calls=%async_computation.12 | async-start | bytes 7962624 | tf_op jit(solution)/shard_map/all_gather | solution.py:92
  74.9 255.8 %all-gather.18.cloned.1.call-start = ((), (), s32[]{:S(2)}) async-start(), calls=%async_computation.13 | async-start | bytes 7962624 | tf_op jit(solution)/shard_map/all_gather | solution.py:93
  75.4 326.7 %all-gather.20.cloned.1.call-start = ((), (), s32[]{:S(2)}) async-start(), calls=%async_computation.14 | async-start | bytes 7962624 | tf_op jit(solution)/shard_map/all_gather | solution.py:94
  76.2 553.3 %reduce-scatter.9.cloned.1.call-start = ((), (), s32[]{:S(2)}) async-start(), calls=%async_computation.15 | async-start | bytes 3932160 | tf_op jit(solution)/shard_map/reduce_scatter | solution.py:182
  232.2 6.9 copy-start.6
  232.2 6.9 copy-start.4
  239.2 5.6 copy-start.30
  243.4 184.9 %copy-start.1 = (f32[512,1152]{1,0:T(8,128)}, f32[512,1152]{1,0:T(8,128)S(1)}, u32[]{:S(2)}) copy-start(f32[512,1152]{1,0:T(8,128)S(1)} %get-tuple-element.291) | copy-start | bytes 7077892
  245.1 14.2 %copy-start.22 = (bf16[512,1152]{1,0:T(8,128)(2,1)}, bf16[512,1152]{1,0:T(8,128)(2,1)S(1)}, u32[]{:S(2)}) copy-start(bf16[512,1152]{1,0:T(8,128)(2,1)S(1)} %multiply_convert_fusion.4) | copy-start | bytes 3538948
  268.9 133.2 %copy-start.21 = (bf16[1,512,1152]{2,1,0:T(8,128)(2,1)S(1)}, bf16[1,512,1152]{2,1,0:T(8,128)(2,1)}, u32[]{:S(2)}) copy-start(bf16[1,512,1152]{2,1,0:T(8,128)(2,1)} %param.27) | copy-start | bytes 3538948
  414.3 8.8 copy-start.43
  414.3 8.9 copy-start.41
  414.3 8.9 copy-start.31
  414.3 8.9 copy-start.37
  414.3 8.9 copy-start.40
  423.2 5.2 copy-start.38
  428.3 2.1 copy-start.13
  429.0 1.4 copy-start.7
  432.9 2.4 copy-start.18
  448.5 5.8 copy-start
  454.3 2.4 copy-start.19
  473.2 5.8 copy-start
  478.9 2.4 copy-start.19
  483.6 1.1 copy-start.20
  497.8 5.8 copy-start
  503.6 2.4 copy-start.19
  522.4 5.8 copy-start
  528.2 2.4 copy-start.19
  547.0 5.8 copy-start
  552.8 2.4 copy-start.19
  571.6 5.8 copy-start
  577.4 2.4 copy-start.19
  586.8 82.8 %reduce-scatter.11.cloned.1.call-start = ((), (), s32[]{:S(2)}) async-start(), calls=%async_computation.16 | async-start | bytes 2985984 | tf_op jit(solution)/shard_map/reduce_scatter | solution.py:212
  591.2 1.7 copy-start.5
  591.2 1.7 copy-start.33
  591.2 1.7 copy-start.35
  596.3 1.7 copy-start.8
  596.4 112.4 %reduce-scatter.17.cloned.1.call-start = ((), (), s32[]{:S(2)}) async-start(), calls=%async_computation.19 | async-start | bytes 2985984 | tf_op jit(solution)/shard_map/reduce_scatter | solution.py:221
  602.5 139.9 %reduce-scatter.13.cloned.1.call-start = ((), (), s32[]{:S(2)}) async-start(), calls=%async_computation.17 | async-start | bytes 995328 | tf_op jit(solution)/shard_map/reduce_scatter | solution.py:215
  634.4 141.0 %reduce-scatter.15.cloned.1.call-start = ((), (), s32[]{:S(2)}) async-start(), calls=%async_computation.18 | async-start | bytes 995328 | tf_op jit(solution)/shard_map/reduce_scatter | solution.py:218
  637.3 215.9 %reduce-scatter.19.cloned.1.call-start = ((), (), s32[]{:S(2)}) async-start(), calls=%async_computation.20 | async-start | bytes 7962624 | tf_op jit(solution)/shard_map/reduce_scatter | solution.py:227
  646.5 284.6 %reduce-scatter.21.cloned.1.call-start = ((), (), s32[]{:S(2)}) async-start(), calls=%async_computation.21 | async-start | bytes 7962624 | tf_op jit(solution)/shard_map/reduce_scatter | solution.py:230
  655.6 353.2 %reduce-scatter.23.cloned.1.call-start = ((), (), s32[]{:S(2)}) async-start(), calls=%async_computation.22 | async-start | bytes 7962624 | tf_op jit(solution)/shard_map/reduce_scatter | solution.py:233
  665.4 440.6 %all-reduce.10.cloned.1.call-start = ((), (), s32[]{:S(2)}) async-start(), calls=%async_computation.23 | async-start | bytes 7077888 | tf_op jit(solution)/shard_map/psum | solution.py:239
  1009.5 4.2 copy-start.2
  1009.5 4.2 copy-start.42
  1013.7 8.8 copy-start.10
  1013.7 8.8 copy-start.17
  1022.5 1.2 copy-start.12
  1022.5 1.4 copy-start.27
  1106.0 7.1 copy-start.26
  1107.9 6.5 copy-start.25
  1113.0 2.8 copy-start.24
  (11 other events, 10.8 us)
Sparse Core Ops, SparseCore 0:
  54.1 29.4 all-gather.9
  86.0 30.9 all-gather.11
  118.7 34.1 all-gather.7
  154.3 33.1 all-gather.13
  189.0 70.2 all-gather.15
  260.8 69.8 all-gather.17
  332.3 69.8 all-gather.19
  586.9 42.5 reduce-scatter.8
  631.8 37.7 reduce-scatter.10
  671.8 36.9 reduce-scatter.16
  711.6 30.6 reduce-scatter.12
  745.2 30.1 reduce-scatter.14
  777.7 75.5 reduce-scatter.18
  855.4 75.6 reduce-scatter.20
  933.2 75.5 reduce-scatter.22
  1012.5 93.3 all-reduce.9
where the time goes:
time: 1130 us; the launch traced here: 1120 us
  waiting for transfers between devices  623 us (55%)
  matrix products  277 us (25%)
  blocking collectives  75.8 us (7%)
  local copies, waits for them, and re-layouts  65.8 us (6%)
  other arithmetic  64.3 us (6%)
  between operations  16.2 us (1%)
    dot_general x25, matrix products, dot_last(): lax.dot_general(left, right, (((1,), (1,)), ((), ())), preferred_element_...  104 us
    reduce_scatter x1, waiting for transfers between devices, body(): lax.psum_scatter(grad_terms[6].astype(jnp.bfloat16), 'fsdp', scatter_dime...  77.9 us
    reduce_scatter x1, waiting for transfers between devices, body(): lax.psum_scatter(grad_terms[7].astype(jnp.bfloat16), 'fsdp', scatter_dime...  77.8 us
    reduce_scatter x1, waiting for transfers between devices, body(): lax.psum_scatter(grad_terms[8].astype(jnp.bfloat16), 'fsdp', scatter_dime...  77.8 us
    dot_general x19, matrix products, dot_first(): lax.dot_general(left, right, (((0,), (0,)), ((), ())), preferred_element_...  68 us
    all_gather x1, waiting for transfers between devices, body(): lax.all_gather(w_up, 'fsdp', axis=0, tiled=True)  61.7 us
    all_gather x1, waiting for transfers between devices, body(): lax.all_gather(w_down, 'fsdp', axis=0, tiled=True)  61.1 us
    psum x1, waiting for transfers between devices, body(): lax.psum(shares[1].astype(jnp.bfloat16), 'ctx').astype(jnp.float32)  45.4 us
  transfers between devices with their start and end apart: 16, of which 15 were waited for; matrix products, arithmetic and copies ran while one was open for 17% of the time, Pallas kernels for 0%

commit v1 on v0

--- a/solution.py
+++ b/solution.py
@@ -1,6 +1,10 @@
+import functools
+
 import jax
 import jax.numpy as jnp
 from jax import lax
+from jax.experimental import pallas as pl
+from jax.experimental.pallas import tpu as pltpu
 from jax.sharding import PartitionSpec as P
 
 H = 18
@@ -58,7 +62,7 @@
     return values.reshape(KVH, ratio, rows, HD).transpose(2, 0, 1, 3).reshape(rows, H * HD)
 
 
-def body(
+def plain_body(
     tokens,
     table,
     norm1_gain,
@@ -260,6 +264,722 @@
     )
 
 
+RATIO = H // KVH
+PAIR = 2 * RATIO * HD
+WIDE = 2 * HD
+NT = (((1,), (1,)), ((), ()))
+TN = (((0,), (0,)), ((), ()))
+NN = (((1,), (0,)), ((), ()))
+VMEM = pl.BlockSpec(memory_space=pltpu.VMEM)
+HBM = pl.BlockSpec(memory_space=pl.ANY)
+ROOM = pltpu.CompilerParams(vmem_limit_bytes=60 * 2**20)
+
+
+def mm(left, right, dims):
+    return lax.dot_general(left, right, dims, preferred_element_type=jnp.float32)
+
+
+def cost(flops, nbytes, exps=0):
+    return pl.CostEstimate(flops=int(flops), bytes_accessed=int(nbytes), transcendentals=int(exps))
+
+
+def turn(values, cosine, sine):
+    lane = lax.broadcasted_iota(jnp.int32, values.shape, 1)
+    first = lax.rem(lane, HD) < HD // 2
+    partner = jnp.where(first, pltpu.roll(values, WIDE - HD // 2, 1), pltpu.roll(values, HD // 2, 1))
+    return values * cosine + partner * sine
+
+
+def kv_kernel(x_ref, w_ref, cos_ref, sin_ref, a_ref, at_ref, kv_ref, gain_ref):
+    width = kv_ref.shape[1]
+    gains = jnp.transpose(w_ref[:, width : width + WIDE].astype(jnp.float32))[0:8]
+    gain_ref[...] = gains
+    x = x_ref[...].astype(jnp.float32)
+    inv = lax.rsqrt(jnp.mean(x * x, -1, keepdims=True) + EPS)
+    a = (x * inv * gains[0:1]).astype(jnp.bfloat16)
+    a_ref[...] = a
+    at_ref[...] = jnp.transpose(a)
+    kv = mm(a, w_ref[:, 0:width], NN)
+    for at in range(0, width, WIDE):
+        part = kv[:, at : at + WIDE]
+        if at < width // 2:
+            part = turn(part, cos_ref[...], sin_ref[...])
+        kv_ref[:, at : at + WIDE] = part.astype(jnp.bfloat16)
+
+
+def kv_project(x, w_kvg, cosine, sine):
+    rows, model = x.shape
+    width = 2 * KVH * HD
+    return pl.pallas_call(
+        kv_kernel,
+        in_specs=[VMEM] * 4,
+        out_specs=[VMEM] * 4,
+        out_shape=[
+            jax.ShapeDtypeStruct((rows, model), jnp.bfloat16),
+            jax.ShapeDtypeStruct((model, rows), jnp.bfloat16),
+            jax.ShapeDtypeStruct((rows, width), jnp.bfloat16),
+            jax.ShapeDtypeStruct((8, model), jnp.float32),
+        ],
+        compiler_params=ROOM,
+        cost_estimate=cost(2 * rows * model * width, 2 * (3 * rows * model + model * width + rows * width)),
+        name="kv_project",
+    )(x, w_kvg, cosine, sine)
+
+
+def q_kernel(a_ref, w_ref, cos_ref, sin_ref, q_ref):
+    q = mm(a_ref[...], w_ref[...], NN)
+    for at in range(0, q.shape[1], WIDE):
+        q_ref[:, at : at + WIDE] = turn(q[:, at : at + WIDE], cos_ref[...], sin_ref[...]).astype(jnp.bfloat16)
+
+
+def q_project(a, w_q, cosine, sine):
+    rows, model = a.shape
+    return pl.pallas_call(
+        q_kernel,
+        in_specs=[VMEM] * 4,
+        out_specs=VMEM,
+        out_shape=jax.ShapeDtypeStruct((rows, H * HD), jnp.bfloat16),
+        compiler_params=ROOM,
+        cost_estimate=cost(2 * rows * model * H * HD, 2 * (2 * rows * model + model * H * HD)),
+        name="q_project",
+    )(a, w_q, cosine, sine)
+
+
+def pick_heads(ref, row, group, factor):
+    own = lax.broadcasted_iota(jnp.int32, (BLK, WIDE), 1) // HD == group
+    out = []
+    for n in range(group * RATIO, (group + 1) * RATIO):
+        piece = ref[pl.ds(row, BLK), pl.ds(n // 2 * WIDE, WIDE)].astype(jnp.float32) * factor
+        if n % 2 != group:
+            piece = pltpu.roll(piece, HD, 1)
+        out.append(jnp.where(own, piece, 0.0).astype(jnp.bfloat16))
+    return jnp.concatenate(out, 0)
+
+
+def join_heads(groups):
+    lane = lax.broadcasted_iota(jnp.int32, (BLK, WIDE), 1)
+    parts = []
+    for n in range(2 * RATIO):
+        group, i = divmod(n, RATIO)
+        piece = groups[group][i * BLK : (i + 1) * BLK, :]
+        parts.append(piece if n % 2 == group else pltpu.roll(piece, HD, 1))
+    return [jnp.where(lane < HD, parts[2 * b], parts[2 * b + 1]) for b in range(RATIO)]
+
+
+def steps_of(pairs, most):
+    return max(u for u in range(1, most + 1) if pairs % u == 0)
+
+
+def attend_kernel(own_ref, slot_ref, q_ref, k_ref, v_ref, o_ref, lse_ref, s_scr, v_scr, q_scr, m_scr, a_scr):
+    rows = RATIO * BLK
+    length = v_ref.shape[0]
+    pairs = length // BLK + 1
+    lane = lax.broadcasted_iota(jnp.int32, (length, WIDE), 1)
+    first = own_ref[0] + 1
+
+    def place(t):
+        j = jnp.where(t >= first, 1, 0)
+        return j, pl.multiple_of(slot_ref[t - j * first] * BLK, BLK)
+
+    outs = [[], []]
+    for group in range(2):
+        v_scr[...] = jnp.where(lane // HD == group, v_ref[...].astype(jnp.float32), 1.0).astype(jnp.bfloat16)
+        for j in range(2):
+            q_scr[j] = pick_heads(q_ref, j * BLK, group, HD**-0.5)
+        m_scr[...] = jnp.full(m_scr.shape, -jnp.inf, jnp.float32)
+        a_scr[...] = jnp.zeros(a_scr.shape, jnp.float32)
+
+        def scores(t, carry):
+            j, at = place(t)
+            s = mm(q_scr[j], k_ref[pl.ds(at, BLK), :], NT)
+            s_scr[t] = s
+            m_scr[j] = jnp.maximum(m_scr[j], jnp.maximum(s[:, 0:WIDE], s[:, WIDE : 2 * WIDE]))
+            return carry
+
+        lax.fori_loop(0, pairs, scores, 0, unroll=steps_of(pairs, 9))
+        for j in range(2):
+            m_scr[j] = jnp.broadcast_to(jnp.max(m_scr[j], 1, keepdims=True), (rows, WIDE))
+
+        def mix(t, carry):
+            j, at = place(t)
+            top = m_scr[j]
+            p = jnp.exp(s_scr[t] - jnp.concatenate([top, top], 1)).astype(jnp.bfloat16)
+            a_scr[j] += mm(p, v_scr[pl.ds(at, BLK), :], NN)
+            return carry
+
+        lax.fori_loop(0, pairs, mix, 0, unroll=steps_of(pairs, 9))
+        own = lax.broadcasted_iota(jnp.int32, (rows, WIDE), 1) // HD == group
+        for j in range(2):
+            acc = a_scr[j]
+            total = jnp.where(own, pltpu.roll(acc, HD, 1), acc)
+            outs[j].append(acc / total)
+            lse_ref[group, j] = jnp.transpose(m_scr[j] + jnp.log(total))[0:1]
+    for j in range(2):
+        for b, part in enumerate(join_heads(outs[j])):
+            o_ref[pl.ds(j * BLK, BLK), pl.ds(b * WIDE, WIDE)] = part.astype(jnp.bfloat16)
+
+
+def attend(own, slots, q, kv):
+    rows, length = q.shape[0], kv.shape[0]
+    nblk = length // BLK
+    work = rows * length * H * (nblk + 1) // (2 * nblk)
+    wide = pl.BlockSpec((rows, PAIR), lambda p, *_: (0, p))
+    return pl.pallas_call(
+        attend_kernel,
+        grid_spec=pltpu.PrefetchScalarGridSpec(
+            num_scalar_prefetch=2,
+            grid=(KVH // 2,),
+            in_specs=[
+                wide,
+                pl.BlockSpec((length, WIDE), lambda p, *_: (0, p)),
+                pl.BlockSpec((length, WIDE), lambda p, *_: (0, p + KVH // 2)),
+            ],
+            out_specs=[wide, pl.BlockSpec((2, 2, 1, RATIO * BLK), lambda p, *_: (p, 0, 0, 0))],
+            scratch_shapes=[
+                pltpu.VMEM((nblk + 1, RATIO * BLK, BLK), jnp.float32),
+                pltpu.VMEM((length, WIDE), jnp.bfloat16),
+                pltpu.VMEM((2, RATIO * BLK, WIDE), jnp.bfloat16),
+                pltpu.VMEM((2, RATIO * BLK, WIDE), jnp.float32),
+                pltpu.VMEM((2, RATIO * BLK, WIDE), jnp.float32),
+            ],
+        ),
+        out_shape=[
+            jax.ShapeDtypeStruct((rows, H * HD), jnp.bfloat16),
+            jax.ShapeDtypeStruct((KVH, 2, 1, RATIO * BLK), jnp.float32),
+        ],
+        compiler_params=ROOM,
+        cost_estimate=cost(4 * 8 * work * HD, 4 * rows * H * HD + 2 * kv.size, work),
+        name="attend",
+    )(own, slots, q, kv, kv)
+
+
+def attend_back_kernel(
+    own_ref, slot_ref, q_ref, k_ref, v_ref, do_ref, o_ref, lse_ref, cos_ref, sin_ref,
+    dq_ref, dks_ref, dkk_ref, dvs_ref, dvk_ref, dk_scr, dv_scr, q_scr, do_scr, st_scr, a_scr,
+):
+    rows = RATIO * BLK
+    length = v_ref.shape[0]
+    pairs = length // BLK + 1
+    dk_scr[...] = jnp.zeros_like(dk_scr)
+    dv_scr[...] = jnp.zeros_like(dv_scr)
+    first = own_ref[0] + 1
+    outs = [[], []]
+    for group in range(2):
+        for j in range(2):
+            q_scr[j] = pick_heads(q_ref, j * BLK, group, HD**-0.5)
+            grads = pick_heads(do_ref, j * BLK, group, 1.0)
+            do_scr[j] = grads
+            mixed = pick_heads(o_ref, j * BLK, group, 1.0)
+            inner = jnp.sum(grads.astype(jnp.float32) * mixed.astype(jnp.float32), 1, keepdims=True)
+            st_scr[j, 0:1] = jnp.transpose(jnp.broadcast_to(inner, (rows, WIDE)))[0:1]
+            st_scr[j, 1:2] = lse_ref[group, j]
+        a_scr[...] = jnp.zeros_like(a_scr)
+
+        def step(t, carry):
+            j = jnp.where(t >= first, 1, 0)
+            at = pl.multiple_of(slot_ref[t - j * first] * BLK, BLK)
+            keys = k_ref[pl.ds(at, BLK), :]
+            qs, grads = q_scr[j], do_scr[j]
+            p = jnp.exp(mm(keys, qs, NT) - st_scr[j, 1:2])
+            dp = mm(v_ref[pl.ds(at, BLK), :], grads, NT)
+            ds = (p * (dp - st_scr[j, 0:1])).astype(jnp.bfloat16)
+            dv_scr[pl.ds(at, BLK), :] += mm(p.astype(jnp.bfloat16), grads, NN)
+            dk_scr[pl.ds(at, BLK), :] += mm(ds, qs, NN)
+            a_scr[j] += mm(ds, keys, TN)
+            return carry
+
+        lax.fori_loop(0, pairs, step, 0, unroll=steps_of(pairs, 3))
+        for j in range(2):
+            outs[j].append(a_scr[j] * HD**-0.5)
+    for j in range(2):
+        span = pl.ds(j * BLK, BLK)
+        for b, part in enumerate(join_heads(outs[j])):
+            dq_ref[span, pl.ds(b * WIDE, WIDE)] = turn(part, cos_ref[span, :], -sin_ref[span, :]).astype(jnp.bfloat16)
+    own_rows = length // 4
+    for ref, scr, order in (
+        (dks_ref, dk_scr, (1, 3)),
+        (dkk_ref, dk_scr, (0, 2)),
+        (dvs_ref, dv_scr, (2, 3)),
+        (dvk_ref, dv_scr, (0, 1)),
+    ):
+        for n, r in enumerate(order):
+            ref[n] = scr[pl.ds(r * own_rows, own_rows), :].astype(jnp.bfloat16)
+
+
+def attend_back(own, slots, q, kv, grads, mixed, lse, cosine, sine):
+    rows, length = q.shape[0], kv.shape[0]
+    nblk = length // BLK
+    work = rows * length * H * (nblk + 1) // (2 * nblk)
+    wide = pl.BlockSpec((rows, PAIR), lambda p, *_: (0, p))
+    whole = pl.BlockSpec((rows, WIDE), lambda p, *_: (0, 0))
+    half = pl.BlockSpec((2, length // 4, WIDE), lambda p, *_: (0, 0, p))
+    half_shape = jax.ShapeDtypeStruct((2, length // 4, KVH * HD), jnp.bfloat16)
+    return pl.pallas_call(
+        attend_back_kernel,
+        grid_spec=pltpu.PrefetchScalarGridSpec(
+            num_scalar_prefetch=2,
+            grid=(KVH // 2,),
+            in_specs=[
+                wide,
+                pl.BlockSpec((length, WIDE), lambda p, *_: (0, p)),
+                pl.BlockSpec((length, WIDE), lambda p, *_: (0, p + KVH // 2)),
+                wide,
+                wide,
+                pl.BlockSpec((2, 2, 1, RATIO * BLK), lambda p, *_: (p, 0, 0, 0)),
+                whole,
+                whole,
+            ],
+            out_specs=[wide, half, half, half, half],
+            scratch_shapes=[
+                pltpu.VMEM((length, WIDE), jnp.float32),
+                pltpu.VMEM((length, WIDE), jnp.float32),
+                pltpu.VMEM((2, RATIO * BLK, WIDE), jnp.bfloat16),
+                pltpu.VMEM((2, RATIO * BLK, WIDE), jnp.bfloat16),
+                pltpu.VMEM((2, 8, RATIO * BLK), jnp.float32),
+                pltpu.VMEM((2, RATIO * BLK, WIDE), jnp.float32),
+            ],
+        ),
+        out_shape=[jax.ShapeDtypeStruct((rows, H * HD), jnp.bfloat16)] + [half_shape] * 4,
+        compiler_params=ROOM,
+        cost_estimate=cost(10 * 8 * work * HD, 8 * rows * H * HD + 4 * kv.size, work),
+        name="attend_back",
+    )(own, slots, q, kv, kv, grads, mixed, lse, cosine, sine)
+
+
+def middle_kernel(
+    core_ref, ho_ref, x_ref, dy_ref, wo_ref, gain_ref, gu0_ref, gu1_ref, d0_ref, d1_ref,
+    out_ref, hot_ref, bt_ref, ht_ref, dg_ref, du_ref, dr_ref, low_ref, dh_ref, gg_ref,
+    gu_scr, d_scr, r_scr, b_scr, acc_scr, db_scr, h_scr, sem,
+):
+    r = pl.program_id(0)
+    count = pl.num_programs(0)
+    core = core_ref[0]
+    lines, cut = gu0_ref.shape[1], gu0_ref.shape[3]
+    cut_d = d0_ref.shape[2]
+
+    def copies(at, slot):
+        out = []
+        for n, (gu, d) in enumerate(((gu0_ref, d0_ref), (gu1_ref, d1_ref))):
+            other = core if n == 0 else 1 - core
+            for z in range(lines):
+                shard = 2 * z + other
+                i = 2 * (n * lines + z)
+                out.append(
+                    pltpu.make_async_copy(
+                        gu.at[at, z],
+                        gu_scr.at[slot, :, pl.ds(pl.multiple_of(shard * cut, 16), cut), :],
+                        sem.at[slot, i],
+                    )
+                )
+                out.append(
+                    pltpu.make_async_copy(
+                        d.at[at, z],
+                        d_scr.at[slot, pl.ds(pl.multiple_of(shard * cut_d, 16), cut_d), :],
+                        sem.at[slot, i + 1],
+                    )
+                )
+        return out
+
+    slot = lax.rem(r, 2)
+
+    @pl.when(r == 0)
+    def _():
+        for c in copies(0, 0):
+            c.start()
+        resid = x_ref[...].astype(jnp.float32) + mm(ho_ref[...], wo_ref[...], NN)
+        r_scr[...] = resid
+        inv = lax.rsqrt(jnp.mean(resid * resid, -1, keepdims=True) + EPS)
+        b = (resid * inv * gain_ref[1:2]).astype(jnp.bfloat16)
+        b_scr[...] = b
+        bt_ref[...] = jnp.transpose(b)
+        hot_ref[...] = jnp.transpose(ho_ref[...])
+
+    for c in copies(r, slot):
+        c.wait()
+
+    @pl.when(r + 1 < count)
+    def _():
+        for c in copies(r + 1, 1 - slot):
+            c.start()
+
+    width = dg_ref.shape[2]
+    for at in range(0, width, 256):
+        span = slice(at, at + 256)
+        gate = mm(b_scr[...], gu_scr[slot, 0, :, span], NN)
+        up = mm(b_scr[...], gu_scr[slot, 1, :, span], NN)
+        dhid = mm(dy_ref[...], d_scr[slot, span, :], NT)
+        sig = jax.nn.sigmoid(gate)
+        silu = gate * sig
+        hidden = (silu * up).astype(jnp.bfloat16)
+        h_scr[:, span] = hidden
+        ht_ref[0, span, :] = jnp.transpose(hidden)
+        dg_ref[0, :, span] = (dhid * up * sig * (1.0 + gate * (1.0 - sig))).astype(jnp.bfloat16)
+        du_ref[0, :, span] = (dhid * silu).astype(jnp.bfloat16)
+    model = acc_scr.shape[1]
+    for at in range(0, model, 384):
+        span = slice(at, at + 384)
+        acc = mm(h_scr[...], d_scr[slot, :, span], NN)
+        db = mm(dg_ref[0], gu_scr[slot, 0, span, :], NT) + mm(du_ref[0], gu_scr[slot, 1, span, :], NT)
+
+        @pl.when(r == 0)
+        def _():
+            acc_scr[:, span] = acc
+            db_scr[:, span] = db
+
+        @pl.when(r > 0)
+        def _():
+            acc_scr[:, span] += acc
+            db_scr[:, span] += db
+
+    @pl.when(r == count - 1)
+    def _():
+        resid = r_scr[...]
+        out_ref[...] = (resid + acc_scr[...]).astype(jnp.bfloat16)
+        inv = lax.rsqrt(jnp.mean(resid * resid, -1, keepdims=True) + EPS)
+        db = db_scr[...]
+        gg_ref[...] = jnp.sum(db * resid * inv, 0, keepdims=True)
+        weighted = gain_ref[1:2] * db
+        dr = (
+            dy_ref[...].astype(jnp.float32)
+            + inv * weighted
+            - resid * (inv * inv * inv) * jnp.mean(weighted * resid, -1, keepdims=True)
+        )
+        dr_ref[...] = dr
+        low = dr.astype(jnp.bfloat16)
+        low_ref[...] = low
+        dh_ref[...] = mm(low, wo_ref[...], NT).astype(jnp.bfloat16)
+
+
+def middle(core, ho, x, dy, w_o, gains, gu, d):
+    rows, model = x.shape
+    count, lines, _, cut, width = gu[0].shape
+    cut_d = d[0].shape[2]
+    once = pl.Buffered(1)
+    whole = lambda shape: pl.BlockSpec(shape, lambda r, *_: (0,) * len(shape), pipeline_mode=once)
+    act = pl.BlockSpec((1, rows, width), lambda r, *_: (r, 0, 0))
+    low = jnp.bfloat16
+    return pl.pallas_call(
+        middle_kernel,
+        grid_spec=pltpu.PrefetchScalarGridSpec(
+            num_scalar_prefetch=1,
+            grid=(count,),
+            in_specs=[
+                whole((rows, H * HD)), whole((rows, model)), whole((rows, model)), whole((H * HD, model)), whole((8, model)),
+                HBM, HBM, HBM, HBM,
+            ],
+            out_specs=[
+                whole((rows, model)), whole((H * HD, rows)), whole((model, rows)),
+                pl.BlockSpec((1, width, rows), lambda r, *_: (r, 0, 0)), act, act,
+                whole((rows, model)), whole((rows, model)), whole((rows, H * HD)), whole((1, model)),
+            ],
+            scratch_shapes=[
+                pltpu.VMEM((2, 2, 2 * lines * cut, width), low),
+                pltpu.VMEM((2, width, model), low),
+                pltpu.VMEM((rows, model), jnp.float32),
+                pltpu.VMEM((rows, model), low),
+                pltpu.VMEM((rows, model), jnp.float32),
+                pltpu.VMEM((rows, model), jnp.float32),
+                pltpu.VMEM((rows, width), low),
+                pltpu.SemaphoreType.DMA((2, 4 * lines)),
+            ],
+        ),
+        out_shape=[
+            jax.ShapeDtypeStruct((rows, model), low),
+            jax.ShapeDtypeStruct((H * HD, rows), low),
+            jax.ShapeDtypeStruct((model, rows), low),
+            jax.ShapeDtypeStruct((count, width, rows), low),
+            jax.ShapeDtypeStruct((count, rows, width), low),
+            jax.ShapeDtypeStruct((count, rows, width), low),
+            jax.ShapeDtypeStruct((rows, model), jnp.float32),
+            jax.ShapeDtypeStruct((rows, model), low),
+            jax.ShapeDtypeStruct((rows, H * HD), low),
+            jax.ShapeDtypeStruct((1, model), jnp.float32),
+        ],
+        compiler_params=ROOM,
+        cost_estimate=cost(12 * rows * model * width * count + 4 * rows * model * model, 2 * 16 * rows * model + 6 * count * width * model, rows * width * count),
+        name="middle",
+    )(core, ho, x, dy, w_o, gains, gu[0], gu[1], d[0], d[1])
+
+
+def last_kernel(x_ref, gain_ref, dr_ref, dq_ref, dk_ref, dv_ref, wq_ref, wkv_ref, cos_ref, sin_ref, gx_ref, act_ref, gg_ref):
+    half = KVH * HD
+    model = x_ref.shape[1]
+    act_ref[:, 0 : H * HD] = dq_ref[...]
+    for at in range(0, half, WIDE):
+        turned = turn(dk_ref[:, at : at + WIDE], cos_ref[...], -sin_ref[...])
+        act_ref[:, H * HD + at : H * HD + at + WIDE] = turned.astype(jnp.bfloat16)
+    act_ref[:, H * HD + half : H * HD + 2 * half] = dv_ref[...].astype(jnp.bfloat16)
+    act_ref[:, H * HD + 2 * half :] = jnp.zeros((x_ref.shape[0], act_ref.shape[1] - H * HD - 2 * half), jnp.bfloat16)
+    da = mm(dq_ref[...], wq_ref[...], NT)
+    da += mm(act_ref[:, H * HD : H * HD + 2 * half], wkv_ref[:, 0 : 2 * half], NT)
+    x = x_ref[...].astype(jnp.float32)
+    inv = lax.rsqrt(jnp.mean(x * x, -1, keepdims=True) + EPS)
+    gg_ref[...] = jnp.sum(da * x * inv, 0, keepdims=True)
+    weighted = gain_ref[0:1] * da
+    gx = dr_ref[...] + inv * weighted - x * (inv * inv * inv) * jnp.mean(weighted * x, -1, keepdims=True)
+    gx_ref[...] = gx.astype(jnp.bfloat16)
+
+
+def last(x, gains, dr, dq, dk, dv, w_q, w_kvg, cosine, sine, padded):
+    rows, model = x.shape
+    return pl.pallas_call(
+        last_kernel,
+        in_specs=[VMEM] * 10,
+        out_specs=[VMEM] * 3,
+        out_shape=[
+            jax.ShapeDtypeStruct((rows, model), jnp.bfloat16),
+            jax.ShapeDtypeStruct((rows, padded), jnp.bfloat16),
+            jax.ShapeDtypeStruct((1, model), jnp.float32),
+        ],
+        compiler_params=ROOM,
+        cost_estimate=cost(2 * rows * model * (H + 2 * KVH) * HD, 10 * rows * model + 2 * model * (H + 2 * KVH) * HD),
+        name="last",
+    )(x, gains, dr, dq, dk, dv, w_q, w_kvg, cosine, sine)
+
+
+def product_kernel(pos_ref, l0_ref, l1_ref, r0_ref, r1_ref, out_ref):
+    total = mm(l0_ref[...], r0_ref[0], NN) + mm(l1_ref[...], r1_ref[0], NN)
+    out_ref[0] = total.astype(jnp.bfloat16)
+
+
+def products(pos, left, right, blocks, width, column):
+    rows, tokens = left[0].shape
+    spec = pl.BlockSpec((rows, tokens), lambda n, *_: (0, 0))
+    act = pl.BlockSpec((1, tokens, width), lambda n, pos_ref: column(n, pos_ref))
+    return pl.pallas_call(
+        product_kernel,
+        grid_spec=pltpu.PrefetchScalarGridSpec(
+            num_scalar_prefetch=1,
+            grid=(blocks,),
+            in_specs=[spec, spec, act, act],
+            out_specs=pl.BlockSpec((1, rows, width), lambda n, *_: (n, 0, 0)),
+        ),
+        out_shape=jax.ShapeDtypeStruct((blocks, rows, width), jnp.bfloat16),
+        compiler_params=ROOM,
+        cost_estimate=cost(4 * blocks * rows * tokens * width, 4 * rows * tokens + 2 * blocks * (2 * tokens + rows) * width),
+        name="products",
+    )(pos, left[0], left[1], right[0], right[1])
+
+
+def whole_product_kernel(pos_ref, left_ref, right_ref, out_ref):
+    shards, cut = out_ref.shape[0], out_ref.shape[2]
+    total = mm(left_ref[0], right_ref[...], NN).astype(jnp.bfloat16)
+    for s in range(shards):
+        out_ref[s, 0] = total[s * cut : (s + 1) * cut]
+
+
+def down_product(pos, left, right, shards):
+    parts, rows, tokens = left.shape
+    model = right.shape[1]
+    out = pl.pallas_call(
+        whole_product_kernel,
+        grid_spec=pltpu.PrefetchScalarGridSpec(
+            num_scalar_prefetch=1,
+            grid=(parts,),
+            in_specs=[pl.BlockSpec((1, rows, tokens), lambda r, *_: (r, 0, 0)), pl.BlockSpec((tokens, model), lambda r, *_: (0, 0))],
+            out_specs=pl.BlockSpec((shards, 1, rows // shards, model), lambda r, pos_ref: (0, pos_ref[0] ^ r, 0, 0)),
+        ),
+        out_shape=jax.ShapeDtypeStruct((shards, parts, rows // shards, model), jnp.bfloat16),
+        compiler_params=ROOM,
+        cost_estimate=cost(2 * parts * rows * tokens * model, 2 * (parts * rows * tokens + tokens * model + parts * rows * model)),
+        name="down_product",
+    )(pos, left, right)
+    return out.reshape(parts * rows, model)
+
+
+ACROSS_X = [(t, t ^ 1) for t in range(4)]
+ACROSS_Y = [(t, t ^ 2) for t in range(4)]
+ACROSS_CORE = [(f, f ^ 1) for f in range(8)]
+ACROSS_PAIR = [(f, f ^ 2) for f in range(8)]
+MIDDLE = [(f, 6 - 2 * (f // 2) + f % 2) for f in (2, 3, 4, 5)]
+TO_ENDS = [(2, 0), (3, 1), (4, 6), (5, 7)]
+TO_MIDDLE = [(b, a) for a, b in TO_ENDS]
+
+
+def across_x(v):
+    return lax.ppermute(v, "ctx", ACROSS_X)
+
+
+def across_y(v):
+    return lax.ppermute(v, "ctx", ACROSS_Y)
+
+
+def other_core(v):
+    return lax.ppermute(v, "fsdp", ACROSS_CORE)
+
+
+def gather_line(v, z):
+    odd = z % 2 == 1
+    partner = lax.ppermute(v, "fsdp", ACROSS_PAIR)
+    pair = jnp.stack([jnp.where(odd, partner, v), jnp.where(odd, v, partner)])
+    far = lax.ppermute(pair, "fsdp", MIDDLE)
+    end = lax.ppermute(far, "fsdp", TO_ENDS)
+    other = far + end
+    high = z >= 2
+    return jnp.concatenate([jnp.where(high, other, pair), jnp.where(high, pair, other)])
+
+
+def gather_square(v):
+    from_x, from_y = across_x(v), across_y(v)
+    half = v.shape[0] // 2
+    far_x = across_x(from_y[:half])
+    far_y = across_y(from_x[half:])
+    return jnp.stack([v, from_x, from_y, jnp.concatenate([far_x, far_y])])
+
+
+def scatter_square(x_send, x_keep, y_send, y_keep):
+    wide = lambda v: v.astype(jnp.float32)
+    got_x, got_y = across_x(x_send), across_y(y_send)
+    pass_y = (wide(x_keep[1]) + wide(got_x[1])).astype(jnp.bfloat16)
+    pass_x = (wide(y_keep[1]) + wide(got_y[1])).astype(jnp.bfloat16)
+    last_y, last_x = across_y(pass_y), across_x(pass_x)
+    return (
+        wide(x_keep[0]) + wide(got_x[0]) + wide(last_y),
+        wide(y_keep[0]) + wide(got_y[0]) + wide(last_x),
+    )
+
+
+def scatter_line(v, z):
+    wide = lambda v: v.astype(jnp.float32)
+    side = z // 2
+    far = lax.dynamic_slice_in_dim(v, 2 * (1 - side), 2, 0)
+    near = lax.dynamic_slice_in_dim(v, 2 * side, 2, 0)
+    got = lax.ppermute(far, "fsdp", TO_MIDDLE)
+    crossed = lax.ppermute((wide(far) + wide(got)).astype(jnp.bfloat16), "fsdp", MIDDLE)
+    near = wide(near) + wide(crossed)
+    send = lax.dynamic_index_in_dim(near, 1 - z % 2, 0, keepdims=False).astype(jnp.bfloat16)
+    keep = lax.dynamic_index_in_dim(near, z % 2, 0, keepdims=False)
+    return keep + wide(lax.ppermute(send, "fsdp", ACROSS_PAIR))
+
+
+def in_order(parts, t):
+    return jnp.stack([lax.dynamic_index_in_dim(parts, t ^ q, 0, keepdims=False) for q in range(4)])
+
+
+def lanes(v, core):
+    shaped = v.reshape(4, 2, v.shape[0] // 8, v.shape[1])
+    pick = lambda c: lax.dynamic_index_in_dim(shaped, c, 1, keepdims=False).reshape(-1, v.shape[1])
+    return pick(core), pick(1 - core)
+
+
+def square_body(
+    tokens,
+    table,
+    norm1_gain,
+    w_query,
+    w_key,
+    w_value,
+    w_out,
+    norm2_gain,
+    w_gate,
+    w_up,
+    w_down,
+    cotangent,
+):
+    x, dy = tokens[0], cotangent[0]
+    rows, model = x.shape
+    t = lax.axis_index("ctx")
+    f = lax.axis_index("fsdp")
+    z, core = f // 2, f % 2
+    pos = t.reshape(1).astype(jnp.int32)
+    cut, hidden_width = w_gate.shape
+    cut_d = w_down.shape[0]
+    quarter = hidden_width // 4
+    kv_width = 2 * KVH * HD
+
+    gains_pad = jnp.pad(jnp.stack([norm1_gain, norm2_gain], 1), ((0, 0), (0, WIDE - 2)))
+    w_kvg = lax.all_gather(jnp.concatenate([w_key, w_value, gains_pad], 1), "fsdp", axis=0, tiled=True)
+    w_q = lax.all_gather(w_query, "fsdp", axis=0, tiled=True)
+    w_o = lax.all_gather(w_out, "fsdp", axis=0, tiled=True)
+
+    def own_quarter(w):
+        shaped = w.reshape(cut, 8, 4, cut_d // 4)
+        return lax.dynamic_index_in_dim(shaped, t, 2, keepdims=False).reshape(cut, quarter)
+
+    gu_own = gather_square(gather_line(jnp.stack([own_quarter(w_gate), own_quarter(w_up)]), z))
+    d_part = lax.dynamic_index_in_dim(w_down.reshape(4, cut_d // 4, model), t, 0, keepdims=False)
+    d_own = gather_square(gather_line(d_part, z))
+    gu = (gu_own, other_core(gu_own))
+    d = (d_own, other_core(d_own))
+
+    relative = jnp.arange(4) ^ t
+    offsets = jnp.arange(BLK, dtype=jnp.int32)
+    ordered = table[relative].reshape(-1)
+    own = ordered[:2].astype(jnp.int32)
+    slots = jnp.zeros((ordered.shape[0],), jnp.int32).at[ordered].set(jnp.arange(ordered.shape[0], dtype=jnp.int32))
+    places = (own[:, None] * BLK + offsets[None, :]).reshape(-1)
+    frequency = 10000.0 ** (-(jnp.arange(HD // 2, dtype=jnp.float32) * 2.0 / HD))
+    angles = places.astype(jnp.float32)[:, None] * frequency
+    cosine = jnp.tile(jnp.cos(angles), (1, 4))
+    sine = jnp.sin(angles)
+    sine = jnp.concatenate([-sine, sine, -sine, sine], 1)
+
+    a, a_t, kv_own, gains = kv_project(x, w_kvg, cosine, sine)
+    q = q_project(a, w_q, cosine, sine)
+    kv = gather_square(kv_own).reshape(4 * rows, kv_width)
+    mixed, lse = attend(own, slots, q, kv)
+    out, mixed_t, b_t, hidden_t, dgate, dup, dr, dr_low, dheads, gg2 = middle(
+        core.reshape(1).astype(jnp.int32), mixed, x, dy, w_o, gains, gu, d
+    )
+
+    grad_d = lax.psum_scatter(down_product(pos, hidden_t, dy, 8), "fsdp", scatter_dimension=0, tiled=True)
+    b_mine, b_other = lanes(b_t, core)
+    left = (b_mine, other_core(b_other))
+    gates, ups = (dgate, other_core(dgate)), (dup, other_core(dup))
+    r_gu = scatter_square(
+        products(pos, left, gates, 2, quarter, lambda n, p: (1 + 2 * n, 0, 0)),
+        products(pos, left, gates, 2, quarter, lambda n, p: (2 * n, 0, 0)),
+        products(pos, left, ups, 2, quarter, lambda n, p: (2 + n, 0, 0)),
+        products(pos, left, ups, 2, quarter, lambda n, p: (n, 0, 0)),
+    )
+    r_gu = jnp.stack([v.astype(jnp.bfloat16).reshape(4, cut, quarter) for v in r_gu], 1)
+    s_gu = scatter_line(r_gu, z).astype(jnp.bfloat16)
+    all_gu = lax.all_gather(s_gu, "ctx", axis=0, tiled=False)
+
+    def whole_columns(v):
+        return v.reshape(4, cut, 8, cut_d // 4).transpose(1, 2, 0, 3).reshape(cut, hidden_width).astype(jnp.float32)
+
+    grad_g, grad_u = whole_columns(all_gu[:, 0]), whole_columns(all_gu[:, 1])
+
+    grad_o = mm(mixed_t, dr_low, NN).astype(jnp.bfloat16)
+    grad_o = lax.psum_scatter(grad_o, "fsdp", scatter_dimension=0, tiled=True)
+    grad_o = lax.psum(grad_o, "ctx").astype(jnp.float32)
+    grad_d = lax.psum(grad_d, "ctx").astype(jnp.float32)
+    dq, dk_send, dk_keep, dv_send, dv_keep = attend_back(own, slots, q, kv, dheads, mixed, lse, cosine, sine)
+    dk, dv = scatter_square(dk_send, dk_keep, dv_send, dv_keep)
+    padded = -(-(H * HD + kv_width) // (8 * WIDE)) * 8 * WIDE
+    grad_x, act, gg1 = last(x, gains, dr, dq, dk, dv, w_q, w_kvg, cosine, sine, padded)
+    a_mine, a_other = lanes(a_t, core)
+    left = (a_mine, other_core(a_other))
+    acts = (act[None], other_core(act)[None])
+    eighth = padded // 8
+    r_qkv = scatter_square(
+        products(pos, left, acts, 2, eighth, lambda n, p: (0, 0, 2 * (p[0] ^ (1 + 2 * n)))),
+        products(pos, left, acts, 2, eighth, lambda n, p: (0, 0, 2 * (p[0] ^ (2 * n)))),
+        products(pos, left, acts, 2, eighth, lambda n, p: (0, 0, 2 * (p[0] ^ (2 + n)) + 1)),
+        products(pos, left, acts, 2, eighth, lambda n, p: (0, 0, 2 * (p[0] ^ n) + 1)),
+    )
+    r_qkv = jnp.concatenate([v.astype(jnp.bfloat16) for v in r_qkv], 1).reshape(4, cut, 2 * eighth)
+    s_qkv = scatter_line(r_qkv, z).astype(jnp.bfloat16)
+    all_qkv = in_order(gather_square(s_qkv), t)
+    grad_qkv = all_qkv.transpose(1, 0, 2).reshape(cut, padded).astype(jnp.float32)
+    gain_grads = lax.psum(jnp.concatenate([gg1, gg2]), ("ctx", "fsdp"))
+    gain_grads = lax.dynamic_slice_in_dim(gain_grads, f * cut, cut, 1)
+    return (
+        out[None],
+        grad_x[None],
+        gain_grads[0],
+        grad_qkv[:, : H * HD],
+        grad_qkv[:, H * HD : H * HD + kv_width // 2],
+        grad_qkv[:, H * HD + kv_width // 2 : H * HD + kv_width],
+        grad_o,
+        gain_grads[1],
+        grad_g,
+        grad_u,
+        grad_d,
+    )
+
+
 def solution(mesh):
     placed = (
         P("fsdp", "ctx", None),
@@ -275,8 +995,9 @@
         P("fsdp", None),
         P("fsdp", "ctx", None),
     )
+    square = mesh.shape["ctx"] == 4 and mesh.shape["fsdp"] == 8
     return jax.shard_map(
-        body,
+        square_body if square else plain_body,
         mesh=mesh,
         in_specs=placed,
         out_specs=(

time: 1130 us -> 687 us (0.61)
  waiting for transfers between devices: 623 us -> 270 us
  matrix products: 277 us -> 4.79 us
  Pallas kernels: 0 us -> 186 us
  starting transfers between devices: 1.33 us -> 70.4 us
  blocking collectives: 75.8 us -> 40.7 us
  local copies, waits for them, and re-layouts: 65.8 us -> 46.4 us
  other arithmetic: 64.3 us -> 49.6 us
    reduce_scatter x8 -> x2, waiting for transfers between devices: 370 us -> 0.01 us  [the longest x1 0.01 us: square_body(): grad_o = lax.psum_scatter(grad_o, 'fsdp', scatter_dimension=0, tiled=True)]
    dot_general x63 -> x1, matrix products: 277 us -> 4.79 us  [mm(): lax.dot_general(left, right, dims, preferred_element_type=jnp.float32)]
    ppermute x0 -> x47, waiting for transfers between devices: none -> 270 us  [the longest x14 88.1 us: across_x(): return lax.ppermute(v, 'ctx', ACROSS_X)]
    all_gather x7 -> x4, waiting for transfers between devices: 204 us -> 0.01 us  [the longest x1 0.01 us: square_body(): lax.all_gather(jnp.concatenate([w_key, w_value, gains_pad], 1), 'fsdp', a...]
    pallas_call x0 -> x15, Pallas kernels: none -> 186 us  [the longest x1 52.6 us: middle(): pl.pallas_call(middle_kernel, grid_spec=pltpu.PrefetchScalarGridSpec(num_...]
    ppermute x0 -> x47, starting transfers between devices: none -> 69.8 us  [the longest x2 24 us: scatter_line(): return keep + wide(lax.ppermute(send, 'fsdp', ACROSS_PAIR))]
    psum x1, waiting for transfers between devices: 45.4 us -> 0.01 us  [square_body(): grad_o = lax.psum(grad_o, 'ctx').astype(jnp.float32)]
    unnamed x2 -> x0, blocking collectives: 32.9 us -> none
  transfers between devices with their start and end apart: 16 -> 54, of which waited for: 15 -> 23; matrix products, arithmetic and copies ran while one was open for 17% -> 12% of each run, Pallas kernels for 0% -> 19%
where the time goes in v1:
time: 687 us; the launch traced here: 682 us
  waiting for transfers between devices  270 us (39%)
  Pallas kernels  186 us (27%)
  starting transfers between devices  70.4 us (10%)
  other arithmetic  49.6 us (7%)
  local copies, waits for them, and re-layouts  46.4 us (7%)
  blocking collectives  40.7 us (6%)
  between operations  15.1 us (2%)
    ppermute x14, waiting for transfers between devices, across_x(): return lax.ppermute(v, 'ctx', ACROSS_X)  88.1 us
    ppermute x14, waiting for transfers between devices, across_y(): return lax.ppermute(v, 'ctx', ACROSS_Y)  73.1 us
    ppermute x2, waiting for transfers between devices, gather_line(): end = lax.ppermute(far, 'fsdp', TO_ENDS)  70.4 us
    pallas_call x1, Pallas kernels, middle(): pl.pallas_call(middle_kernel, grid_spec=pltpu.PrefetchScalarGridSpec(num_...  52.6 us
    pallas_call x1, Pallas kernels, attend_back(): pl.pallas_call(attend_back_kernel, grid_spec=pltpu.PrefetchScalarGridSpec...  42.8 us
    psum x1, blocking collectives, square_body(): gain_grads = lax.psum(jnp.concatenate([gg1, gg2]), ('ctx', 'fsdp'))  40.7 us
    pallas_call x8, Pallas kernels, products(): pl.pallas_call(product_kernel, grid_spec=pltpu.PrefetchScalarGridSpec(num...  32.5 us
    pallas_call x1, Pallas kernels, attend(): pl.pallas_call(attend_kernel, grid_spec=pltpu.PrefetchScalarGridSpec(num_...  30 us
  transfers between devices with their start and end apart: 54, of which 23 were waited for; matrix products, arithmetic and copies ran while one was open for 12% of the time, Pallas kernels for 19%

profile of v1, /device:TPU:0, one launch (start us, length us, event | category | flops | bytes accessed | tf_op | source)
XLA Modules:
  0.0 682.2 jit_solution(4650830534804212180)
XLA Ops:
  7.2 2.9 reshape.237
  11.4 3.8 dynamic-slice_reduce_fusion
  15.7 3.1 collective-permute-start.4
  19.8 9.1 %collective-permute-done.4 = bf16[2,144,768]{2,1,0:T(8,128)(2,1)S(1)} collective-permute-done((bf16[2,144,768]{2,1,0:T(8,128)(2,1)S(1)}, bf16[2,144,768]{2,1,0:T(8,128)(2,1)S(1)}, u32[]{:S(2)}, u32[]{:S(2)}) %collective-permute-start.4) | collective-permute-done | bytes 442400 | tf_op jit(solution)/shard_map/ppermute | solution.py:813
  31.1 57.2 %collective-permute-done.6 = bf16[2,2,144,768]{3,2,1,0:T(8,128)(2,1)S(1)} collective-permute-done((bf16[2,2,144,768]{3,2,1,0:T(8,128)(2,1)S(1)}, bf16[2,2,144,768]{3,2,1,0:T(8,128)(2,1)S(1)}, u32[]{:S(2)}, u32[]{:S(2)}) %collective-permute-start.6) | collective-permute-done | bytes 884768 | tf_op jit(solution)/shard_map/ppermute | solution.py:816
  94.0 35.9 %collective-permute-done.7 = bf16[4,2,144,768]{3,2,1,0:T(8,128)(2,1)S(1)} collective-permute-done((bf16[4,2,144,768]{3,2,1,0:T(8,128)(2,1)}, bf16[4,2,144,768]{3,2,1,0:T(8,128)(2,1)S(1)}, u32[]{:S(2)}, u32[]{:S(2)}) %collective-permute-start.7) | collective-permute-done | bytes 1769504 | tf_op jit(solution)/shard_map/ppermute | solution.py:800
  136.0 14.0 %collective-permute-done.10 = bf16[2,2,144,768]{3,2,1,0:T(8,128)(2,1)S(1)} collective-permute-done((bf16[2,2,144,768]{3,2,1,0:T(8,128)(2,1)S(1)}, bf16[2,2,144,768]{3,2,1,0:T(8,128)(2,1)S(1)}, u32[]{:S(2)}, u32[]{:S(2)}) %collective-permute-start.10) | collective-permute-done | bytes 884768 | tf_op jit(solution)/shard_map/ppermute | solution.py:804
  150.1 2.5 collective-permute-done.9
  152.7 5.1 pad_maximum_fusion.gu0_ref
  159.1 13.2 %collective-permute-done.14 = bf16[2,96,1152]{2,1,0:T(8,128)(2,1)S(1)} collective-permute-done((bf16[2,96,1152]{2,1,0:T(8,128)(2,1)S(1)}, bf16[2,96,1152]{2,1,0:T(8,128)(2,1)S(1)}, u32[]{:S(2)}, u32[]{:S(2)}) %collective-permute-start.14) | collective-permute-done | bytes 442400 | tf_op jit(solution)/shard_map/ppermute | solution.py:816
  176.6 18.2 %collective-permute-done.16 = bf16[4,96,1152]{2,1,0:T(8,128)(2,1)S(1)} collective-permute-done((bf16[4,96,1152]{2,1,0:T(8,128)(2,1)S(1)}, bf16[4,96,1152]{2,1,0:T(8,128)(2,1)S(1)}, u32[]{:S(2)}, u32[]{:S(2)}) %collective-permute-start.16) | collective-permute-done | bytes 884768 | tf_op jit(solution)/shard_map/ppermute | solution.py:804
  201.5 5.4 collective-permute-done.17
  206.9 2.0 collective-permute-done.18
  209.9 4.4 kv_project.1
  215.9 2.2 pad_maximum_fusion.1.d0_ref
  218.3 13.5 %collective-permute-done.1 = bf16[512,768]{1,0:T(8,128)(2,1)} collective-permute-done((bf16[512,768]{1,0:T(8,128)(2,1)}, bf16[512,768]{1,0:T(8,128)(2,1)}, u32[]{:S(2)}, u32[]{:S(2)}) %collective-permute-start.1) | collective-permute-done | bytes 786464 | tf_op jit(solution)/shard_map/ppermute | solution.py:804
  231.8 1.8 slice.166
  234.2 1.8 slice.167
  238.8 5.3 q_project.1.q_ref
  245.4 3.0 pad_maximum_fusion.2
  248.4 30.0 %attend.1 = (bf16[512,1152]{1,0:T(8,128)(2,1)}, f32[6,2,1,768]{3,2,1,0:T(1,128)}) custom-call(s32[2]{0:T(128)} %slice_bitcast_fusion.own_ref, s32[8]{0:T(128)} %scatter_custom_fusion.slot_ref, bf16[512,1152]{1,0:T(8,128)(2,1)} %q_project.1.q_ref, bf16[2048,768]{1,0:T(8,128)(2,1)} %bitcast.171, bf16[2048,768]{1,0:T(8,128)(2,1)} %bitcast.172), custom_call_target="tpu_custom_call" | custom-call | flops 21743271936 | bytes 5505024 | tf_op jit(solution)/shard_map/attend/pallas_call | solution.py:427
  278.5 52.6 %middle.1 = (bf16[512,1152]{1,0:T(8,128)(2,1)}, bf16[1152,512]{1,0:T(8,128)(2,1)}, bf16[1152,512]{1,0:T(8,128)(2,1)}, bf16[4,768,512]{2,1,0:T(8,128)(2,1)}, bf16...) custom-call(s32[1]{0:T(128)} %bitcast.core_ref, ...), custom_call_target="tpu_custom_call" | custom-call | flops 24461180928 | bytes 40108032 | tf_op jit(solution)/shard_map/middle/pallas_call | solution.py:661
  331.0 4.8 convolution_convert_fusion
  336.0 8.4 %down_product.1 = bf16[8,4,96,1152]{3,2,1,0:T(8,128)(2,1)} custom-call(s32[1]{0:T(128)} %bitcast.33.pos_ref, bf16[4,768,512]{2,1,0:T(8,128)(2,1)} %get-tuple-element.58.left_ref, bf16[512,1152]{1,0:T(8,128)(2,1)} %bitcast.192), custom_call_target="tpu_custom_call" | custom-call | flops 3623878656 | bytes 11403264 | tf_op jit(solution)/shard_map/down_product/pallas_call | solution.py:774
  344.4 2.3 constant_dynamic-slice_fusion.1
  347.3 1.8 collective-permute-done.37.l1_ref
  349.1 4.9 products.15
  354.9 42.8 %attend_back.1 = (bf16[512,1152]{1,0:T(8,128)(2,1)}, bf16[2,512,384]{2,1,0:T(8,128)(2,1)}, bf16[2,512,384]{2,1,0:T(8,128)(2,1)}, bf16[2,512,384]{2,1,0:T(8,128)(2,1)}, bf16[2,512,384]{2,1,0:T(8,128)(2,1)}) custom-call(s32[2]{0:T(128)} %slice_bitcast_fusion.own_ref, s32[8]{0:T(128)} %scatter_custom_fusion.slot_ref, bf16[512,1152]{1,0:T(8,128)(2,1)} %q_project.1.q_ref, ...), custom_call_target="tpu_custom_call" | custom-call | flops 54358179840 | bytes 11010048 | tf_op jit(solution)/shard_map/attend_back/pallas_call | solution.py:517
  398.8 4.8 products.13
  405.7 11.9 %collective-permute-done.22 = bf16[2,512,384]{2,1,0:T(8,128)(2,1)} collective-permute-done((bf16[2,512,384]{2,1,0:T(8,128)(2,1)}, bf16[2,512,384]{2,1,0:T(8,128)(2,1)}, u32[]{:S(2)}, u32[]{:S(2)}) %collective-permute-start.22) | collective-permute-done | bytes 786464 | tf_op jit(solution)/shard_map/ppermute | solution.py:804
  420.1 42.1 %collective-permute-done.20 = bf16[2,512,384]{2,1,0:T(8,128)(2,1)S(1)} collective-permute-done((bf16[2,512,384]{2,1,0:T(8,128)(2,1)}, bf16[2,512,384]{2,1,0:T(8,128)(2,1)S(1)}, u32[]{:S(2)}, u32[]{:S(2)}) %collective-permute-start.20) | collective-permute-done | bytes 786464 | tf_op jit(solution)/shard_map/ppermute | solution.py:800
  462.2 2.1 fusion.11
  465.3 4.8 products.14
  470.1 5.4 products.12
  475.5 2.4 fusion.3
  481.7 2.1 bitcast_add_fusion.3.dv_ref
  483.8 2.0 bitcast_add_fusion.4.dk_ref
  485.8 9.6 %last.1 = (bf16[512,1152]{1,0:T(8,128)(2,1)}, bf16[512,2048]{1,0:T(8,128)(2,1)}, f32[1,1152]{1,0:T(1,128)}) custom-call(bf16[512,1152]{1,0:T(8,128)(2,1)} %bitcast.164, f32[8,1152]{1,0:T(8,128)} %get-tuple-element.38.gain_ref, f32[512,1152]{1,0:T(8,128)} %get-tuple-element.40.dr_ref, bf16[512,1152]{1,0:T(8,128)(2,1)} %get-tuple-element.43.dq_ref, ...), custom_call_target="tpu_custom_call" | custom-call | flops 2264924160 | bytes 10321920 | tf_op jit(solution)/shard_map/last/pallas_call | solution.py:725
  495.6 1.8 collective-permute-done.43
  497.4 2.0 fusion
  503.0 17.5 %collective-permute-done.44 = bf16[2,2,144,768]{3,2,1,0:T(8,128)(2,1)S(1)} collective-permute-done((bf16[2,2,144,768]{3,2,1,0:T(8,128)(2,1)S(1)}, bf16[2,2,144,768]{3,2,1,0:T(8,128)(2,1)S(1)}, u32[]{:S(2)}, u32[]{:S(2)}) %collective-permute-start.44) | collective-permute-done | bytes 884768 | tf_op jit(solution)/shard_map/ppermute | solution.py:847
  524.4 2.3 collective-permute-done.24.l1_ref
  528.1 3.1 products.9
  533.5 13.6 %collective-permute-start.46 = (bf16[2,144,768]{2,1,0:T(8,128)(2,1)S(1)}, bf16[2,144,768]{2,1,0:T(8,128)(2,1)S(1)}, u32[]{:S(2)}, u32[]{:S(2)}) collective-permute-start(bf16[2,144,768]{2,1,0:T(8,128)(2,1)S(1)} %fusion.10), channel_id=1, source_target_pairs={{0,2},{1,3},{2,0},{3,1},{4,6},{5,7},{6,4},{7,5},{8,10},{9,11},{10,... | collective-permute-start | bytes 1327112 | tf_op jit(solution)/shard_map/ppermute | solution.py:852
  547.1 3.1 products.11
  550.9 3.1 products.8
  557.4 3.2 products.10
  560.6 4.7 collective-permute-done.28
  566.8 6.4 collective-permute-done.27
  575.4 2.2 collective-permute-start.30
  577.6 4.2 collective-permute-done.30
  582.8 10.5 %collective-permute-start.32 = (bf16[144,512]{1,0:T(8,128)(2,1)S(1)}, bf16[144,512]{1,0:T(8,128)(2,1)S(1)}, u32[]{:S(2)}, u32[]{:S(2)}) collective-permute-start(bf16[144,512]{1,0:T(8,128)(2,1)S(1)} %fusion.17), channel_id=1, source_target_pairs={{0,2},{1,3},{2,0},{3,1},{4,6},{5,7},{6,4},{7,5},{8,10},{9,11},{10,... | collective-permute-start | bytes 442376 | tf_op jit(solution)/shard_map/ppermute | solution.py:852
  593.2 3.1 collective-permute-done.32
  599.2 40.7 %psum.21 = f32[2,1152]{1,0:T(2,128)S(1)} all-reduce(f32[2,1152]{1,0:T(2,128)S(1)} %pad_maximum_fusion.10), channel_id=1, replica_groups=mesh['ctx'=4,'fsdp'=8] {'ctx','fsdp'}, use_global_device_ids=true, to_apply=%region_1.2 | all-reduce | flops 2304 | bytes 18432 | tf_op jit(solution)/shard_map/psum | solution.py:966
  639.9 2.3 collective-permute-start.35
  644.6 2.1 collective-permute-done.36
  648.8 3.5 slice_convert_fusion
  652.3 2.3 reshape.252
  654.6 2.9 copy.100
  657.5 4.5 reshape.250
  662.0 2.3 reshape.253
  664.3 2.9 copy.101
  667.2 4.5 reshape.251
  671.7 2.5 convert_element_type.349
  (220 shorter events, 76.5 us)
Async XLA Ops:
  7.2 202.7 %all-gather.6.cloned.1.call-start = ((), (), s32[]{:S(2)}) async-start(), calls=%async_computation.2 | async-start | bytes 2322432 | tf_op jit(solution)/shard_map/all_gather | solution.py:891
  11.3 7.4 %copy-start.26 = (bf16[144]{0:T(256)(128)(2,1)S(1)}, bf16[144]{0:T(256)(128)(2,1)}, u32[]{:S(2)}) copy-start(bf16[144]{0:T(256)(128)(2,1)} %param.14) | copy-start | bytes 868
  11.4 7.6 %copy-start.21 = (bf16[144,384]{1,0:T(8,128)(2,1)S(1)}, bf16[144,384]{1,0:T(8,128)(2,1)}, u32[]{:S(2)}) copy-start(bf16[144,384]{1,0:T(8,128)(2,1)} %param.17) | copy-start | bytes 331780
  11.4 7.6 %copy-start.22 = (bf16[144,384]{1,0:T(8,128)(2,1)S(1)}, bf16[144,384]{1,0:T(8,128)(2,1)}, u32[]{:S(2)}) copy-start(bf16[144,384]{1,0:T(8,128)(2,1)} %param.16) | copy-start | bytes 331780
  15.7 13.3 %collective-permute-start.4 = (bf16[2,144,768]{2,1,0:T(8,128)(2,1)S(1)}, bf16[2,144,768]{2,1,0:T(8,128)(2,1)S(1)}, u32[]{:S(2)}, u32[]{:S(2)}) collective-permute-start(bf16[2,144,768]{2,1,0:T(8,128)(2,1)S(1)} %constant_dynamic-update-slice_fusion), channel_id=1, source_target_pairs={{0,2},{1,3},{2,0},{3,1},{4,6},{5,7},{6,4},{7,5},{8,10},{9,11},{10,... | collective-permute-start | bytes 1327112 | tf_op jit(solution)/shard_map/ppermute | solution.py:813
  19.7 219.1 %all-gather.8.cloned.1.call-start = ((), (), s32[]{:S(2)}) async-start(), calls=%async_computation.3 | async-start | bytes 2985984 | tf_op jit(solution)/shard_map/all_gather | solution.py:892
  29.1 0.7 collective-permute-start.5
  29.8 58.5 %collective-permute-start.6 = (bf16[2,2,144,768]{3,2,1,0:T(8,128)(2,1)S(1)}, bf16[2,2,144,768]{3,2,1,0:T(8,128)(2,1)S(1)}, u32[]{:S(2)}, u32[]{:S(2)}) collective-permute-start(bf16[2,2,144,768]{3,2,1,0:T(8,128)(2,1)S(1)} %collective-permute-done.5), channel_id=1, source_target_pairs={{2,0},{3,1},{4,6},{5,7},{10,8},{11,9},{12,14},{13,15},{18,16},{19,... | collective-permute-start | bytes 2654216 | tf_op jit(solution)/shard_map/ppermute | solution.py:816
  90.0 40.0 %collective-permute-start.7 = (bf16[4,2,144,768]{3,2,1,0:T(8,128)(2,1)}, bf16[4,2,144,768]{3,2,1,0:T(8,128)(2,1)S(1)}, u32[]{:S(2)}, u32[]{:S(2)}) collective-permute-start(bf16[4,2,144,768]{3,2,1,0:T(8,128)(2,1)} %get-tuple-element.66), channel_id=1, source_target_pairs={{0,8},{8,0},{16,24},{24,16},{1,9},{9,1},{17,25},{25,17},{2,10},{10... | collective-permute-start | bytes 5308424 | tf_op jit(solution)/shard_map/ppermute | solution.py:800
  91.4 40.1 %collective-permute-start.8 = (bf16[4,2,144,768]{3,2,1,0:T(8,128)(2,1)}, bf16[4,2,144,768]{3,2,1,0:T(8,128)(2,1)}, u32[]{:S(2)}, u32[]{:S(2)}) collective-permute-start(bf16[4,2,144,768]{3,2,1,0:T(8,128)(2,1)} %get-tuple-element.66), channel_id=1, source_target_pairs={{0,16},{8,24},{16,0},{24,8},{1,17},{9,25},{17,1},{25,9},{2,18},{10... | collective-permute-start | bytes 5308424 | tf_op jit(solution)/shard_map/ppermute | solution.py:804
  92.9 185.5 %all-gather.10.cloned.1.call-start = ((), (), s32[]{:S(2)}) async-start(), calls=%async_computation.4 | async-start | bytes 2985984 | tf_op jit(solution)/shard_map/all_gather | solution.py:893
  93.9 40.4 %collective-permute-start.12 = (bf16[96,1152]{1,0:T(8,128)(2,1)S(1)}, bf16[96,1152]{1,0:T(8,128)(2,1)S(1)}, u32[]{:S(2)}, u32[]{:S(2)}) collective-permute-start(bf16[96,1152]{1,0:T(8,128)(2,1)S(1)} %dynamic-slice_bitcast_fusion), channel_id=1, source_target_pairs={{0,2},{1,3},{2,0},{3,1},{4,6},{5,7},{6,4},{7,5},{8,10},{9,11},{10,... | collective-permute-start | bytes 663560 | tf_op jit(solution)/shard_map/ppermute | solution.py:813
  130.0 20.1 %collective-permute-start.10 = (bf16[2,2,144,768]{3,2,1,0:T(8,128)(2,1)S(1)}, bf16[2,2,144,768]{3,2,1,0:T(8,128)(2,1)S(1)}, u32[]{:S(2)}, u32[]{:S(2)}) collective-permute-start(bf16[2,2,144,768]{3,2,1,0:T(8,128)(2,1)S(1)} %slice.169), channel_id=1, source_target_pairs={{0,16},{8,24},{16,0},{24,8},{1,17},{9,25},{17,1},{25,9},{2,18},{10... | collective-permute-start | bytes 2654216 | tf_op jit(solution)/shard_map/ppermute | solution.py:804
  132.8 19.8 %collective-permute-start.9 = (bf16[2,2,144,768]{3,2,1,0:T(8,128)(2,1)S(1)}, bf16[2,2,144,768]{3,2,1,0:T(8,128)(2,1)S(1)}, u32[]{:S(2)}, u32[]{:S(2)}) collective-permute-start(bf16[2,2,144,768]{3,2,1,0:T(8,128)(2,1)S(1)} %slice.168), channel_id=1, source_target_pairs={{0,8},{8,0},{16,24},{24,16},{1,9},{9,1},{17,25},{25,17},{2,10},{10... | collective-permute-start | bytes 2654216 | tf_op jit(solution)/shard_map/ppermute | solution.py:800
  135.4 22.5 %collective-permute-start.13 = (bf16[2,96,1152]{2,1,0:T(8,128)(2,1)S(1)}, bf16[2,96,1152]{2,1,0:T(8,128)(2,1)S(1)}, u32[]{:S(2)}, u32[]{:S(2)}) collective-permute-start(bf16[2,96,1152]{2,1,0:T(8,128)(2,1)S(1)} %pad_maximum_fusion.8), channel_id=1, source_target_pairs={{2,4},{3,5},{4,2},{5,3},{10,12},{11,13},{12,10},{13,11},{18,20},{1... | collective-permute-start | bytes 1327112 | tf_op jit(solution)/shard_map/ppermute | solution.py:815
  157.8 120.6 %collective-permute-start.11 = (bf16[4,4,2,144,768]{4,3,2,1,0:T(8,128)(2,1)}, bf16[4,4,2,144,768]{4,3,2,1,0:T(8,128)(2,1)}, u32[]{:S(2)}, u32[]{:S(2)}) collective-permute-start(bf16[4,4,2,144,768]{4,3,2,1,0:T(8,128)(2,1)} %pad_maximum_fusion.gu0_ref), channel_id=1, source_target_pairs={{0,1},{1,0},{2,3},{3,2},{4,5},{5,4},{6,7},{7,6},{8,9},{9,8},{10,11... | collective-permute-start | bytes 21233672 | tf_op jit(solution)/shard_map/ppermute | solution.py:808
  157.9 14.5 %collective-permute-start.14 = (bf16[2,96,1152]{2,1,0:T(8,128)(2,1)S(1)}, bf16[2,96,1152]{2,1,0:T(8,128)(2,1)S(1)}, u32[]{:S(2)}, u32[]{:S(2)}) collective-permute-start(bf16[2,96,1152]{2,1,0:T(8,128)(2,1)S(1)} %collective-permute-done.13), channel_id=1, source_target_pairs={{2,0},{3,1},{4,6},{5,7},{10,8},{11,9},{12,14},{13,15},{18,16},{19,... | collective-permute-start | bytes 1327112 | tf_op jit(solution)/shard_map/ppermute | solution.py:816
  173.5 21.3 %collective-permute-start.16 = (bf16[4,96,1152]{2,1,0:T(8,128)(2,1)S(1)}, bf16[4,96,1152]{2,1,0:T(8,128)(2,1)S(1)}, u32[]{:S(2)}, u32[]{:S(2)}) collective-permute-start(bf16[4,96,1152]{2,1,0:T(8,128)(2,1)S(1)} %get-tuple-element.76), channel_id=1, source_target_pairs={{0,16},{8,24},{16,0},{24,8},{1,17},{9,25},{17,1},{25,9},{2,18},{10... | collective-permute-start | bytes 2654216 | tf_op jit(solution)/shard_map/ppermute | solution.py:804
  174.6 22.5 %collective-permute-start.15 = (bf16[4,96,1152]{2,1,0:T(8,128)(2,1)S(1)}, bf16[4,96,1152]{2,1,0:T(8,128)(2,1)S(1)}, u32[]{:S(2)}, u32[]{:S(2)}) collective-permute-start(bf16[4,96,1152]{2,1,0:T(8,128)(2,1)S(1)} %get-tuple-element.76), channel_id=1, source_target_pairs={{0,8},{8,0},{16,24},{24,16},{1,9},{9,1},{17,25},{25,17},{2,10},{10... | collective-permute-start | bytes 2654216 | tf_op jit(solution)/shard_map/ppermute | solution.py:800
  175.5 423.6 %reduce-scatter.3.cloned.1.call-start = ((), (), s32[]{:S(2)}) async-start(), calls=%async_computation.5 | async-start | bytes 2985984 | tf_op jit(solution)/shard_map/reduce_scatter | solution.py:945
  195.6 11.2 %collective-permute-start.17 = (bf16[2,96,1152]{2,1,0:T(8,128)(2,1)}, bf16[2,96,1152]{2,1,0:T(8,128)(2,1)S(1)}, u32[]{:S(2)}, u32[]{:S(2)}) collective-permute-start(bf16[2,96,1152]{2,1,0:T(8,128)(2,1)} %slice.170), channel_id=1, source_target_pairs={{0,8},{8,0},{16,24},{24,16},{1,9},{9,1},{17,25},{25,17},{2,10},{10... | collective-permute-start | bytes 1327112 | tf_op jit(solution)/shard_map/ppermute | solution.py:800
  198.0 10.9 %collective-permute-start.18 = (bf16[2,96,1152]{2,1,0:T(8,128)(2,1)}, bf16[2,96,1152]{2,1,0:T(8,128)(2,1)S(1)}, u32[]{:S(2)}, u32[]{:S(2)}) collective-permute-start(bf16[2,96,1152]{2,1,0:T(8,128)(2,1)} %slice.171), channel_id=1, source_target_pairs={{0,16},{8,24},{16,0},{24,8},{1,17},{9,25},{17,1},{25,9},{2,18},{10... | collective-permute-start | bytes 1327112 | tf_op jit(solution)/shard_map/ppermute | solution.py:804
  214.3 17.5 %collective-permute-start.1 = (bf16[512,768]{1,0:T(8,128)(2,1)}, bf16[512,768]{1,0:T(8,128)(2,1)}, u32[]{:S(2)}, u32[]{:S(2)}) collective-permute-start(bf16[512,768]{1,0:T(8,128)(2,1)} %get-tuple-element.36), channel_id=1, source_target_pairs={{0,16},{8,24},{16,0},{24,8},{1,17},{9,25},{17,1},{25,9},{2,18},{10... | collective-permute-start | bytes 2359304 | tf_op jit(solution)/shard_map/ppermute | solution.py:804
  214.9 19.4 %collective-permute-start = (bf16[512,768]{1,0:T(8,128)(2,1)}, bf16[512,768]{1,0:T(8,128)(2,1)}, u32[]{:S(2)}, u32[]{:S(2)}) collective-permute-start(bf16[512,768]{1,0:T(8,128)(2,1)} %get-tuple-element.36), channel_id=1, source_target_pairs={{0,8},{8,0},{16,24},{24,16},{1,9},{9,1},{17,25},{25,17},{2,10},{10... | collective-permute-start | bytes 2359304 | tf_op jit(solution)/shard_map/ppermute | solution.py:800
  218.2 25.9 %copy-start.6 = (bf16[4,4,96,1152]{3,2,1,0:T(8,128)(2,1)}, bf16[4,4,96,1152]{3,2,1,0:T(8,128)(2,1)S(1)}, u32[]{:S(2)}) copy-start(bf16[4,4,96,1152]{3,2,1,0:T(8,128)(2,1)S(1)} %pad_maximum_fusion.1.d0_ref) | copy-start | bytes 10616836
  218.2 60.3 %collective-permute-start.19 = (bf16[4,4,96,1152]{3,2,1,0:T(8,128)(2,1)S(1)}, bf16[4,4,96,1152]{3,2,1,0:T(8,128)(2,1)}, u32[]{:S(2)}, u32[]{:S(2)}) collective-permute-start(bf16[4,4,96,1152]{3,2,1,0:T(8,128)(2,1)S(1)} %pad_maximum_fusion.1.d0_ref), channel_id=1, source_target_pairs={{0,1},{1,0},{2,3},{3,2},{4,5},{5,4},{6,7},{7,6},{8,9},{9,8},{10,11... | collective-permute-start | bytes 10616840 | tf_op jit(solution)/shard_map/ppermute | solution.py:808
  233.6 10.5 %collective-permute-start.2 = (bf16[256,768]{1,0:T(8,128)(2,1)}, bf16[256,768]{1,0:T(8,128)(2,1)}, u32[]{:S(2)}, u32[]{:S(2)}) collective-permute-start(bf16[256,768]{1,0:T(8,128)(2,1)} %slice.166), channel_id=1, source_target_pairs={{0,8},{8,0},{16,24},{24,16},{1,9},{9,1},{17,25},{25,17},{2,10},{10... | collective-permute-start | bytes 1179656 | tf_op jit(solution)/shard_map/ppermute | solution.py:800
  236.0 8.1 %collective-permute-start.3 = (bf16[256,768]{1,0:T(8,128)(2,1)}, bf16[256,768]{1,0:T(8,128)(2,1)}, u32[]{:S(2)}, u32[]{:S(2)}) collective-permute-start(bf16[256,768]{1,0:T(8,128)(2,1)} %slice.167), channel_id=1, source_target_pairs={{0,16},{8,24},{16,0},{24,8},{1,17},{9,25},{17,1},{25,9},{2,18},{10... | collective-permute-start | bytes 1179656 | tf_op jit(solution)/shard_map/ppermute | solution.py:804
  335.8 263.3 %reduce-scatter.5.cloned.1.call-start = ((), (), s32[]{:S(2)}) async-start(), calls=%async_computation.6 | async-start | bytes 7962624 | tf_op jit(solution)/shard_map/reduce_scatter | solution.py:925
  335.9 13.2 %collective-permute-start.41 = (bf16[4,512,768]{2,1,0:T(8,128)(2,1)}, bf16[4,512,768]{2,1,0:T(8,128)(2,1)}, u32[]{:S(2)}, u32[]{:S(2)}) collective-permute-start(bf16[4,512,768]{2,1,0:T(8,128)(2,1)} %get-tuple-element.57.r0_ref), channel_id=1, source_target_pairs={{0,1},{1,0},{2,3},{3,2},{4,5},{5,4},{6,7},{7,6},{8,9},{9,8},{10,11... | collective-permute-start | bytes 9437192 | tf_op jit(solution)/shard_map/ppermute | solution.py:808
  344.4 304.4 %all-gather.12.cloned.1.call-start = ((), (), s32[]{:S(2)}) async-start(), calls=%async_computation.7 | async-start | bytes 2211840 | tf_op jit(solution)/shard_map/all_gather | solution.py:937
  346.8 2.3 collective-permute-start.37
  347.2 51.6 %collective-permute-start.38 = (bf16[4,512,768]{2,1,0:T(8,128)(2,1)S(1)}, bf16[4,512,768]{2,1,0:T(8,128)(2,1)}, u32[]{:S(2)}, u32[]{:S(2)}) collective-permute-start(bf16[4,512,768]{2,1,0:T(8,128)(2,1)S(1)} %copy-done.2), channel_id=1, source_target_pairs={{0,1},{1,0},{2,3},{3,2},{4,5},{5,4},{6,7},{7,6},{8,9},{9,8},{10,11... | collective-permute-start | bytes 9437192 | tf_op jit(solution)/shard_map/ppermute | solution.py:808
  353.9 121.6 %collective-permute-start.42 = (bf16[2,576,768]{2,1,0:T(8,128)(2,1)}, bf16[2,576,768]{2,1,0:T(8,128)(2,1)}, u32[]{:S(2)}, u32[]{:S(2)}) collective-permute-start(bf16[2,576,768]{2,1,0:T(8,128)(2,1)} %products.15), channel_id=1, source_target_pairs={{0,16},{8,24},{16,0},{24,8},{1,17},{9,25},{17,1},{25,9},{2,18},{10... | collective-permute-start | bytes 5308424 | tf_op jit(solution)/shard_map/ppermute | solution.py:804
  397.7 19.9 %collective-permute-start.22 = (bf16[2,512,384]{2,1,0:T(8,128)(2,1)}, bf16[2,512,384]{2,1,0:T(8,128)(2,1)}, u32[]{:S(2)}, u32[]{:S(2)}) collective-permute-start(bf16[2,512,384]{2,1,0:T(8,128)(2,1)} %get-tuple-element.47), channel_id=1, source_target_pairs={{0,16},{8,24},{16,0},{24,8},{1,17},{9,25},{17,1},{25,9},{2,18},{10... | collective-permute-start | bytes 2359304 | tf_op jit(solution)/shard_map/ppermute | solution.py:804
  403.6 75.6 %collective-permute-start.39 = (bf16[2,576,768]{2,1,0:T(8,128)(2,1)}, bf16[2,576,768]{2,1,0:T(8,128)(2,1)S(1)}, u32[]{:S(2)}, u32[]{:S(2)}) collective-permute-start(bf16[2,576,768]{2,1,0:T(8,128)(2,1)} %products.13), channel_id=1, source_target_pairs={{0,8},{8,0},{16,24},{24,16},{1,9},{9,1},{17,25},{25,17},{2,10},{10... | collective-permute-start | bytes 5308424 | tf_op jit(solution)/shard_map/ppermute | solution.py:800
  404.9 57.3 %collective-permute-start.20 = (bf16[2,512,384]{2,1,0:T(8,128)(2,1)}, bf16[2,512,384]{2,1,0:T(8,128)(2,1)S(1)}, u32[]{:S(2)}, u32[]{:S(2)}) collective-permute-start(bf16[2,512,384]{2,1,0:T(8,128)(2,1)} %get-tuple-element.45), channel_id=1, source_target_pairs={{0,8},{8,0},{16,24},{24,16},{1,9},{9,1},{17,25},{25,17},{2,10},{10... | collective-permute-start | bytes 2359304 | tf_op jit(solution)/shard_map/ppermute | solution.py:800
  418.8 62.9 %collective-permute-start.23 = (bf16[512,384]{1,0:T(8,128)(2,1)S(1)}, bf16[512,384]{1,0:T(8,128)(2,1)}, u32[]{:S(2)}, u32[]{:S(2)}) collective-permute-start(bf16[512,384]{1,0:T(8,128)(2,1)S(1)} %fusion.12), channel_id=1, source_target_pairs={{0,8},{8,0},{16,24},{24,16},{1,9},{9,1},{17,25},{25,17},{2,10},{10... | collective-permute-start | bytes 1179656 | tf_op jit(solution)/shard_map/ppermute | solution.py:800
  464.3 19.5 %collective-permute-start.21 = (bf16[512,384]{1,0:T(8,128)(2,1)}, bf16[512,384]{1,0:T(8,128)(2,1)}, u32[]{:S(2)}, u32[]{:S(2)}) collective-permute-start(bf16[512,384]{1,0:T(8,128)(2,1)} %fusion.11), channel_id=1, source_target_pairs={{0,16},{8,24},{16,0},{24,8},{1,17},{9,25},{17,1},{25,9},{2,18},{10... | collective-permute-start | bytes 1179656 | tf_op jit(solution)/shard_map/ppermute | solution.py:804
  478.0 19.4 %collective-permute-start.43 = (bf16[576,768]{1,0:T(8,128)(2,1)}, bf16[576,768]{1,0:T(8,128)(2,1)}, u32[]{:S(2)}, u32[]{:S(2)}) collective-permute-start(bf16[576,768]{1,0:T(8,128)(2,1)} %fusion.3), channel_id=1, source_target_pairs={{0,8},{8,0},{16,24},{24,16},{1,9},{9,1},{17,25},{25,17},{2,10},{10... | collective-permute-start | bytes 2654216 | tf_op jit(solution)/shard_map/ppermute | solution.py:800
  480.6 19.0 %collective-permute-start.40 = (bf16[576,768]{1,0:T(8,128)(2,1)}, bf16[576,768]{1,0:T(8,128)(2,1)}, u32[]{:S(2)}, u32[]{:S(2)}) collective-permute-start(bf16[576,768]{1,0:T(8,128)(2,1)} %fusion.2), channel_id=1, source_target_pairs={{0,16},{8,24},{16,0},{24,8},{1,17},{9,25},{17,1},{25,9},{2,18},{10... | collective-permute-start | bytes 2654216 | tf_op jit(solution)/shard_map/ppermute | solution.py:804
  495.5 31.2 %collective-permute-start.25 = (bf16[512,2048]{1,0:T(8,128)(2,1)}, bf16[512,2048]{1,0:T(8,128)(2,1)S(1)}, u32[]{:S(2)}, u32[]{:S(2)}) collective-permute-start(bf16[512,2048]{1,0:T(8,128)(2,1)} %get-tuple-element.52), channel_id=1, source_target_pairs={{0,1},{1,0},{2,3},{3,2},{4,5},{5,4},{6,7},{7,6},{8,9},{9,8},{10,11... | collective-permute-start | bytes 6291464 | tf_op jit(solution)/shard_map/ppermute | solution.py:808
  501.2 20.5 %copy-start.1 = (bf16[576,768]{1,0:T(8,128)(2,1)}, bf16[576,768]{1,0:T(8,128)(2,1)S(1)}, u32[]{:S(2)}) copy-start(bf16[576,768]{1,0:T(8,128)(2,1)S(1)} %fusion.1) | copy-start | bytes 2654212
  501.3 21.9 %copy-start.13 = (bf16[1152,512]{1,0:T(8,128)(2,1)S(1)}, bf16[1152,512]{1,0:T(8,128)(2,1)}, u32[]{:S(2)}) copy-start(bf16[1152,512]{1,0:T(8,128)(2,1)} %get-tuple-element.51) | copy-start | bytes 3538948
  501.3 19.2 %collective-permute-start.44 = (bf16[2,2,144,768]{3,2,1,0:T(8,128)(2,1)S(1)}, bf16[2,2,144,768]{3,2,1,0:T(8,128)(2,1)S(1)}, u32[]{:S(2)}, u32[]{:S(2)}) collective-permute-start(bf16[2,2,144,768]{3,2,1,0:T(8,128)(2,1)S(1)} %fusion.4), channel_id=1, source_target_pairs={{0,2},{1,3},{6,4},{7,5},{8,10},{9,11},{14,12},{15,13},{16,18},{17,... | collective-permute-start | bytes 2654216 | tf_op jit(solution)/shard_map/ppermute | solution.py:847
  521.7 10.3 %collective-permute-start.45 = (bf16[2,2,144,768]{3,2,1,0:T(8,128)(2,1)}, bf16[2,2,144,768]{3,2,1,0:T(8,128)(2,1)}, u32[]{:S(2)}, u32[]{:S(2)}) collective-permute-start(bf16[2,2,144,768]{3,2,1,0:T(8,128)(2,1)} %add_convert_fusion), channel_id=1, source_target_pairs={{2,4},{3,5},{4,2},{5,3},{10,12},{11,13},{12,10},{13,11},{18,20},{1... | collective-permute-start | bytes 2654216 | tf_op jit(solution)/shard_map/ppermute | solution.py:848
  524.4 2.3 collective-permute-start.24
  531.2 22.8 %collective-permute-start.26 = (bf16[2,576,256]{2,1,0:T(8,128)(2,1)}, bf16[2,576,256]{2,1,0:T(8,128)(2,1)S(1)}, u32[]{:S(2)}, u32[]{:S(2)}) collective-permute-start(bf16[2,576,256]{2,1,0:T(8,128)(2,1)} %products.9), channel_id=1, source_target_pairs={{0,8},{8,0},{16,24},{24,16},{1,9},{9,1},{17,25},{25,17},{2,10},{10... | collective-permute-start | bytes 1769480 | tf_op jit(solution)/shard_map/ppermute | solution.py:800
  533.5 22.9 %collective-permute-start.46 = (bf16[2,144,768]{2,1,0:T(8,128)(2,1)S(1)}, bf16[2,144,768]{2,1,0:T(8,128)(2,1)S(1)}, u32[]{:S(2)}, u32[]{:S(2)}) collective-permute-start(bf16[2,144,768]{2,1,0:T(8,128)(2,1)S(1)} %fusion.10), channel_id=1, source_target_pairs={{0,2},{1,3},{2,0},{3,1},{4,6},{5,7},{6,4},{7,5},{8,10},{9,11},{10,... | collective-permute-start | bytes 1327112 | tf_op jit(solution)/shard_map/ppermute | solution.py:852
  550.2 15.1 %collective-permute-start.28 = (bf16[2,576,256]{2,1,0:T(8,128)(2,1)}, bf16[2,576,256]{2,1,0:T(8,128)(2,1)}, u32[]{:S(2)}, u32[]{:S(2)}) collective-permute-start(bf16[2,576,256]{2,1,0:T(8,128)(2,1)} %products.11), channel_id=1, source_target_pairs={{0,16},{8,24},{16,0},{24,8},{1,17},{9,25},{17,1},{25,9},{2,18},{10... | collective-permute-start | bytes 1769480 | tf_op jit(solution)/shard_map/ppermute | solution.py:804
  555.1 18.1 %collective-permute-start.27 = (bf16[576,256]{1,0:T(8,128)(2,1)S(1)}, bf16[576,256]{1,0:T(8,128)(2,1)}, u32[]{:S(2)}, u32[]{:S(2)}) collective-permute-start(bf16[576,256]{1,0:T(8,128)(2,1)S(1)} %fusion.13), channel_id=1, source_target_pairs={{0,16},{8,24},{16,0},{24,8},{1,17},{9,25},{17,1},{25,9},{2,18},{10... | collective-permute-start | bytes 884744 | tf_op jit(solution)/shard_map/ppermute | solution.py:804
  557.3 15.8 %copy-start.7 = (bf16[2,576,256]{2,1,0:T(8,128)(2,1)S(1)}, bf16[2,576,256]{2,1,0:T(8,128)(2,1)}, u32[]{:S(2)}) copy-start(bf16[2,576,256]{2,1,0:T(8,128)(2,1)} %products.8) | copy-start | bytes 1769476
  557.3 114.4 %all-reduce.4.cloned.1.call-start = ((), (), s32[]{:S(2)}) async-start(), calls=%async_computation.8 | async-start | bytes 2433024 | tf_op jit(solution)/shard_map/psum | solution.py:946
  560.5 13.7 %copy-start.8 = (bf16[2,576,256]{2,1,0:T(8,128)(2,1)S(1)}, bf16[2,576,256]{2,1,0:T(8,128)(2,1)}, u32[]{:S(2)}) copy-start(bf16[2,576,256]{2,1,0:T(8,128)(2,1)} %products.10) | copy-start | bytes 1769476
  566.4 7.9 %collective-permute-start.29 = (bf16[576,256]{1,0:T(8,128)(2,1)S(1)}, bf16[576,256]{1,0:T(8,128)(2,1)S(1)}, u32[]{:S(2)}, u32[]{:S(2)}) collective-permute-start(bf16[576,256]{1,0:T(8,128)(2,1)S(1)} %fusion.14), channel_id=1, source_target_pairs={{0,8},{8,0},{16,24},{24,16},{1,9},{9,1},{17,25},{25,17},{2,10},{10... | collective-permute-start | bytes 884744 | tf_op jit(solution)/shard_map/ppermute | solution.py:800
  575.4 6.4 collective-permute-start.30
  581.9 17.3 %copy-start.23 = (f32[1,1152]{1,0:T(1,128)S(1)}, f32[1,1152]{1,0:T(1,128)}, u32[]{:S(2)}) copy-start(f32[1,1152]{1,0:T(1,128)} %get-tuple-element.50) | copy-start | bytes 13828
  581.9 17.3 %copy-start.24 = (f32[1,1152]{1,0:T(1,128)S(1)}, f32[1,1152]{1,0:T(1,128)}, u32[]{:S(2)}) copy-start(f32[1,1152]{1,0:T(1,128)} %get-tuple-element.49) | copy-start | bytes 13828
  581.9 0.7 collective-permute-start.31
  582.8 13.6 %collective-permute-start.32 = (bf16[144,512]{1,0:T(8,128)(2,1)S(1)}, bf16[144,512]{1,0:T(8,128)(2,1)S(1)}, u32[]{:S(2)}, u32[]{:S(2)}) collective-permute-start(bf16[144,512]{1,0:T(8,128)(2,1)S(1)} %fusion.17), channel_id=1, source_target_pairs={{0,2},{1,3},{2,0},{3,1},{4,6},{5,7},{6,4},{7,5},{8,10},{9,11},{10,... | collective-permute-start | bytes 442376 | tf_op jit(solution)/shard_map/ppermute | solution.py:852
  596.4 43.5 %collective-permute-start.34 = (bf16[144,512]{1,0:T(8,128)(2,1)S(1)}, bf16[144,512]{1,0:T(8,128)(2,1)S(1)}, u32[]{:S(2)}, u32[]{:S(2)}) collective-permute-start(bf16[144,512]{1,0:T(8,128)(2,1)S(1)} %fusion.15), channel_id=1, source_target_pairs={{0,16},{8,24},{16,0},{24,8},{1,17},{9,25},{17,1},{25,9},{2,18},{10... | collective-permute-start | bytes 442376 | tf_op jit(solution)/shard_map/ppermute | solution.py:804
  598.1 44.1 %collective-permute-start.33 = (bf16[144,512]{1,0:T(8,128)(2,1)S(1)}, bf16[144,512]{1,0:T(8,128)(2,1)S(1)}, u32[]{:S(2)}, u32[]{:S(2)}) collective-permute-start(bf16[144,512]{1,0:T(8,128)(2,1)S(1)} %fusion.15), channel_id=1, source_target_pairs={{0,8},{8,0},{16,24},{24,16},{1,9},{9,1},{17,25},{25,17},{2,10},{10... | collective-permute-start | bytes 442376 | tf_op jit(solution)/shard_map/ppermute | solution.py:800
  639.9 4.7 collective-permute-start.35
  642.3 4.4 collective-permute-start.36
  (18 other events, 72.8 us)
Sparse Core Ops, SparseCore 0:
  19.8 36.4 all-gather.5
  93.0 31.1 all-gather.7
  175.7 31.8 all-gather.9
  336.0 37.0 reduce-scatter.2
  375.2 75.4 reduce-scatter.4
  557.4 31.7 all-gather.11
  599.3 55.6 all-reduce.3

commit v2 on v1

--- a/solution.py
+++ b/solution.py
@@ -290,59 +290,71 @@
     return values * cosine + partner * sine
 
 
-def kv_kernel(x_ref, w_ref, cos_ref, sin_ref, a_ref, at_ref, kv_ref, gain_ref):
-    width = kv_ref.shape[1]
-    gains = jnp.transpose(w_ref[:, width : width + WIDE].astype(jnp.float32))[0:8]
-    gain_ref[...] = gains
+def far_lines(z):
+    return (z ^ 1, z ^ 2, z ^ 3)
+
+
+def qkv_kernel(
+    at_ref, x_ref, cos_ref, sin_ref, w0_ref, w1_ref, own0_ref, own1_ref, a_ref, at_out_ref, q_ref, kv_ref, gain_ref, w_ref, sem
+):
+    t, core, z = at_ref[0], at_ref[1], at_ref[2]
+    parts, lines, cut, width = w0_ref.shape
+    copies = []
+    for n, (w, own) in enumerate(((w0_ref, own0_ref), (w1_ref, own1_ref))):
+        other = core if n == 0 else 1 - core
+        row = pl.multiple_of((2 * z + other) * cut, 16)
+        copies.append((own, w_ref.at[pl.ds(row, cut), :]))
+        for k, far in enumerate(far_lines(z)):
+            row = pl.multiple_of((2 * far + other) * cut, 16)
+            for r in range(parts):
+                column = pl.multiple_of((t ^ r) * width, WIDE)
+                copies.append((w.at[r, k], w_ref.at[pl.ds(row, cut), pl.ds(column, width)]))
+    copies = [pltpu.make_async_copy(src, dst, sem.at[i]) for i, (src, dst) in enumerate(copies)]
+    for c in copies:
+        c.start()
     x = x_ref[...].astype(jnp.float32)
     inv = lax.rsqrt(jnp.mean(x * x, -1, keepdims=True) + EPS)
+    for c in copies:
+        c.wait()
+    first, half = H * HD, KVH * HD
+    gains = jnp.transpose(w_ref[:, first + 2 * half : first + 2 * half + WIDE].astype(jnp.float32))[0:8]
+    gain_ref[...] = gains
     a = (x * inv * gains[0:1]).astype(jnp.bfloat16)
     a_ref[...] = a
-    at_ref[...] = jnp.transpose(a)
-    kv = mm(a, w_ref[:, 0:width], NN)
-    for at in range(0, width, WIDE):
-        part = kv[:, at : at + WIDE]
-        if at < width // 2:
-            part = turn(part, cos_ref[...], sin_ref[...])
-        kv_ref[:, at : at + WIDE] = part.astype(jnp.bfloat16)
-
-
-def kv_project(x, w_kvg, cosine, sine):
+    at_out_ref[...] = jnp.transpose(a)
+    for at in range(0, first + 2 * half, 2 * WIDE):
+        both = mm(a_ref[...], w_ref[:, at : at + 2 * WIDE], NN)
+        for n in range(0, 2 * WIDE, WIDE):
+            part, column = both[:, n : n + WIDE], at + n
+            if column < first + half:
+                part = turn(part, cos_ref[...], sin_ref[...])
+            if column < first:
+                q_ref[:, column : column + WIDE] = part.astype(jnp.bfloat16)
+            elif column < first + 2 * half:
+                kv_ref[:, column - first : column - first + WIDE] = part.astype(jnp.bfloat16)
+
+
+def qkv_project(where, x, cosine, sine, w, own):
     rows, model = x.shape
-    width = 2 * KVH * HD
+    width = own[0].shape[1]
+    low = jnp.bfloat16
     return pl.pallas_call(
-        kv_kernel,
-        in_specs=[VMEM] * 4,
-        out_specs=[VMEM] * 4,
+        qkv_kernel,
+        in_specs=[pl.BlockSpec(memory_space=pltpu.SMEM)] + [VMEM] * 3 + [HBM] * 4,
+        out_specs=[VMEM] * 6,
         out_shape=[
-            jax.ShapeDtypeStruct((rows, model), jnp.bfloat16),
-            jax.ShapeDtypeStruct((model, rows), jnp.bfloat16),
-            jax.ShapeDtypeStruct((rows, width), jnp.bfloat16),
+            jax.ShapeDtypeStruct((rows, model), low),
+            jax.ShapeDtypeStruct((model, rows), low),
+            jax.ShapeDtypeStruct((rows, H * HD), low),
+            jax.ShapeDtypeStruct((rows, 2 * KVH * HD), low),
             jax.ShapeDtypeStruct((8, model), jnp.float32),
+            jax.ShapeDtypeStruct((model, width), low),
         ],
+        scratch_shapes=[pltpu.SemaphoreType.DMA((2 + 2 * 3 * w[0].shape[0],))],
         compiler_params=ROOM,
-        cost_estimate=cost(2 * rows * model * width, 2 * (3 * rows * model + model * width + rows * width)),
-        name="kv_project",
-    )(x, w_kvg, cosine, sine)
-
-
-def q_kernel(a_ref, w_ref, cos_ref, sin_ref, q_ref):
-    q = mm(a_ref[...], w_ref[...], NN)
-    for at in range(0, q.shape[1], WIDE):
-        q_ref[:, at : at + WIDE] = turn(q[:, at : at + WIDE], cos_ref[...], sin_ref[...]).astype(jnp.bfloat16)
-
-
-def q_project(a, w_q, cosine, sine):
-    rows, model = a.shape
-    return pl.pallas_call(
-        q_kernel,
-        in_specs=[VMEM] * 4,
-        out_specs=VMEM,
-        out_shape=jax.ShapeDtypeStruct((rows, H * HD), jnp.bfloat16),
-        compiler_params=ROOM,
-        cost_estimate=cost(2 * rows * model * H * HD, 2 * (2 * rows * model + model * H * HD)),
-        name="q_project",
-    )(a, w_q, cosine, sine)
+        cost_estimate=cost(2 * rows * model * width, 2 * (4 * rows * model + 2 * model * width)),
+        name="qkv_project",
+    )(where, x, cosine, sine, w[0], w[1], own[0], own[1])
 
 
 def pick_heads(ref, row, group, factor):
@@ -419,22 +431,24 @@
             o_ref[pl.ds(j * BLK, BLK), pl.ds(b * WIDE, WIDE)] = part.astype(jnp.bfloat16)
 
 
-def attend(own, slots, q, kv):
+def attend(own, slots, q, kv, start, count):
     rows, length = q.shape[0], kv.shape[0]
     nblk = length // BLK
-    work = rows * length * H * (nblk + 1) // (2 * nblk)
-    wide = pl.BlockSpec((rows, PAIR), lambda p, *_: (0, p))
+    work = rows * length * H * (nblk + 1) // (2 * nblk) * count // (KVH // 2)
     return pl.pallas_call(
         attend_kernel,
         grid_spec=pltpu.PrefetchScalarGridSpec(
             num_scalar_prefetch=2,
-            grid=(KVH // 2,),
+            grid=(count,),
             in_specs=[
-                wide,
-                pl.BlockSpec((length, WIDE), lambda p, *_: (0, p)),
-                pl.BlockSpec((length, WIDE), lambda p, *_: (0, p + KVH // 2)),
+                pl.BlockSpec((rows, PAIR), lambda p, *_: (0, p + start)),
+                pl.BlockSpec((length, WIDE), lambda p, *_: (0, p + start)),
+                pl.BlockSpec((length, WIDE), lambda p, *_: (0, p + start + KVH // 2)),
             ],
-            out_specs=[wide, pl.BlockSpec((2, 2, 1, RATIO * BLK), lambda p, *_: (p, 0, 0, 0))],
+            out_specs=[
+                pl.BlockSpec((rows, PAIR), lambda p, *_: (0, p)),
+                pl.BlockSpec((2, 2, 1, RATIO * BLK), lambda p, *_: (p, 0, 0, 0)),
+            ],
             scratch_shapes=[
                 pltpu.VMEM((nblk + 1, RATIO * BLK, BLK), jnp.float32),
                 pltpu.VMEM((length, WIDE), jnp.bfloat16),
@@ -444,18 +458,18 @@
             ],
         ),
         out_shape=[
-            jax.ShapeDtypeStruct((rows, H * HD), jnp.bfloat16),
-            jax.ShapeDtypeStruct((KVH, 2, 1, RATIO * BLK), jnp.float32),
+            jax.ShapeDtypeStruct((rows, PAIR * count), jnp.bfloat16),
+            jax.ShapeDtypeStruct((2 * count, 2, 1, RATIO * BLK), jnp.float32),
         ],
         compiler_params=ROOM,
-        cost_estimate=cost(4 * 8 * work * HD, 4 * rows * H * HD + 2 * kv.size, work),
+        cost_estimate=cost(4 * 8 * work * HD, 4 * rows * PAIR * count + 4 * length * WIDE * count, work),
         name="attend",
     )(own, slots, q, kv, kv)
 
 
 def attend_back_kernel(
     own_ref, slot_ref, q_ref, k_ref, v_ref, do_ref, o_ref, lse_ref, cos_ref, sin_ref,
-    dq_ref, dks_ref, dkk_ref, dvs_ref, dvk_ref, dk_scr, dv_scr, q_scr, do_scr, st_scr, a_scr,
+    dq_ref, dkv0_ref, dkv1_ref, dkv2_ref, dkv3_ref, dk_scr, dv_scr, q_scr, do_scr, st_scr, a_scr,
 ):
     rows = RATIO * BLK
     length = v_ref.shape[0]
@@ -496,40 +510,36 @@
         for b, part in enumerate(join_heads(outs[j])):
             dq_ref[span, pl.ds(b * WIDE, WIDE)] = turn(part, cos_ref[span, :], -sin_ref[span, :]).astype(jnp.bfloat16)
     own_rows = length // 4
-    for ref, scr, order in (
-        (dks_ref, dk_scr, (1, 3)),
-        (dkk_ref, dk_scr, (0, 2)),
-        (dvs_ref, dv_scr, (2, 3)),
-        (dvk_ref, dv_scr, (0, 1)),
-    ):
-        for n, r in enumerate(order):
+    for r, ref in enumerate((dkv0_ref, dkv1_ref, dkv2_ref, dkv3_ref)):
+        for n, scr in enumerate((dk_scr, dv_scr)):
             ref[n] = scr[pl.ds(r * own_rows, own_rows), :].astype(jnp.bfloat16)
 
 
-def attend_back(own, slots, q, kv, grads, mixed, lse, cosine, sine):
+def attend_back(own, slots, q, kv, grads, mixed, lse, cosine, sine, start, count):
     rows, length = q.shape[0], kv.shape[0]
     nblk = length // BLK
-    work = rows * length * H * (nblk + 1) // (2 * nblk)
+    work = rows * length * H * (nblk + 1) // (2 * nblk) * count // (KVH // 2)
     wide = pl.BlockSpec((rows, PAIR), lambda p, *_: (0, p))
+    shifted = pl.BlockSpec((rows, PAIR), lambda p, *_: (0, p + start))
     whole = pl.BlockSpec((rows, WIDE), lambda p, *_: (0, 0))
-    half = pl.BlockSpec((2, length // 4, WIDE), lambda p, *_: (0, 0, p))
-    half_shape = jax.ShapeDtypeStruct((2, length // 4, KVH * HD), jnp.bfloat16)
+    part = pl.BlockSpec((2, length // 4, WIDE), lambda p, *_: (0, 0, p))
+    part_shape = jax.ShapeDtypeStruct((2, length // 4, WIDE * count), jnp.bfloat16)
     return pl.pallas_call(
         attend_back_kernel,
         grid_spec=pltpu.PrefetchScalarGridSpec(
             num_scalar_prefetch=2,
-            grid=(KVH // 2,),
+            grid=(count,),
             in_specs=[
-                wide,
-                pl.BlockSpec((length, WIDE), lambda p, *_: (0, p)),
-                pl.BlockSpec((length, WIDE), lambda p, *_: (0, p + KVH // 2)),
-                wide,
+                shifted,
+                pl.BlockSpec((length, WIDE), lambda p, *_: (0, p + start)),
+                pl.BlockSpec((length, WIDE), lambda p, *_: (0, p + start + KVH // 2)),
+                shifted,
                 wide,
                 pl.BlockSpec((2, 2, 1, RATIO * BLK), lambda p, *_: (p, 0, 0, 0)),
                 whole,
                 whole,
             ],
-            out_specs=[wide, half, half, half, half],
+            out_specs=[wide] + [part] * 4,
             scratch_shapes=[
                 pltpu.VMEM((length, WIDE), jnp.float32),
                 pltpu.VMEM((length, WIDE), jnp.float32),
@@ -539,53 +549,92 @@
                 pltpu.VMEM((2, RATIO * BLK, WIDE), jnp.float32),
             ],
         ),
-        out_shape=[jax.ShapeDtypeStruct((rows, H * HD), jnp.bfloat16)] + [half_shape] * 4,
+        out_shape=[jax.ShapeDtypeStruct((rows, PAIR * count), jnp.bfloat16)] + [part_shape] * 4,
         compiler_params=ROOM,
-        cost_estimate=cost(10 * 8 * work * HD, 8 * rows * H * HD + 4 * kv.size, work),
+        cost_estimate=cost(10 * 8 * work * HD, 8 * rows * PAIR * count + 8 * length * WIDE * count, work),
         name="attend_back",
     )(own, slots, q, kv, kv, grads, mixed, lse, cosine, sine)
 
 
 def middle_kernel(
-    core_ref, ho_ref, x_ref, dy_ref, wo_ref, gain_ref, gu0_ref, gu1_ref, d0_ref, d1_ref,
+    at_ref, ho_ref, x_ref, dy_ref, gain_ref,
+    near0_ref, near1_ref, far0_ref, far1_ref, d0_ref, d1_ref,
+    g0_ref, g1_ref, u0_ref, u1_ref, o0_ref, o1_ref, down0_ref, down1_ref,
     out_ref, hot_ref, bt_ref, ht_ref, dg_ref, du_ref, dr_ref, low_ref, dh_ref, gg_ref,
-    gu_scr, d_scr, r_scr, b_scr, acc_scr, db_scr, h_scr, sem,
+    gu_scr, d_scr, wo_ref, r_scr, b_scr, acc_scr, db_scr, h_scr, gu_sem, o_sem, d_sem,
 ):
     r = pl.program_id(0)
     count = pl.num_programs(0)
-    core = core_ref[0]
-    lines, cut = gu0_ref.shape[1], gu0_ref.shape[3]
-    cut_d = d0_ref.shape[2]
-
-    def copies(at, slot):
+    t, core, z = at_ref[0], at_ref[1], at_ref[2]
+    lines, cut, cut_d = near0_ref.shape[1], near0_ref.shape[2], d0_ref.shape[2]
+    width = dg_ref.shape[2]
+    parts = near0_ref.shape[0] + 1
+    o_width = near0_ref.shape[3] - 2 * width
+    o_parts = wo_ref.shape[1] // o_width
+    cores = (core, 1 - core)
+    others = far_lines(z)
+
+    def piece(n, part, k):
+        near, far = ((near0_ref, far0_ref), (near1_ref, far1_ref))[n]
+        return near.at[part, k] if part < parts - 1 else far.at[k]
+
+    def gu_copies(part, slot):
         out = []
-        for n, (gu, d) in enumerate(((gu0_ref, d0_ref), (gu1_ref, d1_ref))):
-            other = core if n == 0 else 1 - core
-            for z in range(lines):
-                shard = 2 * z + other
-                i = 2 * (n * lines + z)
-                out.append(
-                    pltpu.make_async_copy(
-                        gu.at[at, z],
-                        gu_scr.at[slot, :, pl.ds(pl.multiple_of(shard * cut, 16), cut), :],
-                        sem.at[slot, i],
-                    )
-                )
-                out.append(
-                    pltpu.make_async_copy(
-                        d.at[at, z],
-                        d_scr.at[slot, pl.ds(pl.multiple_of(shard * cut_d, 16), cut_d), :],
-                        sem.at[slot, i + 1],
-                    )
-                )
-        return out
+        for n, other in enumerate(cores):
+            columns = pl.ds(pl.multiple_of((t ^ part) * width, WIDE), width)
+            rows = pl.ds(pl.multiple_of((2 * z + other) * cut, 16), cut)
+            for m, ref in enumerate(((g0_ref, u0_ref), (g1_ref, u1_ref))[n]):
+                out.append((ref.at[:, columns], gu_scr.at[slot, m, rows, :]))
+            for k in range(lines):
+                rows = pl.ds(pl.multiple_of((2 * others[k] + other) * cut, 16), cut)
+                for m in range(2):
+                    out.append((piece(n, part, k).at[:, pl.ds(m * width, width)], gu_scr.at[slot, m, rows, :]))
+        return [pltpu.make_async_copy(src, dst, gu_sem.at[slot, i]) for i, (src, dst) in enumerate(out)]
+
+    def o_copies(part):
+        out = []
+        columns = pl.ds(pl.multiple_of((t ^ part) * o_width, WIDE), o_width)
+        for n, other in enumerate(cores):
+            for k in range(lines):
+                rows = pl.ds(pl.multiple_of((2 * others[k] + other) * cut, 16), cut)
+                out.append((piece(n, part, k).at[:, pl.ds(2 * width, o_width)], wo_ref.at[rows, columns]))
+        return [pltpu.make_async_copy(src, dst, o_sem.at[part, i]) for i, (src, dst) in enumerate(out)]
+
+    def d_copies():
+        out = []
+        for n, other in enumerate(cores):
+            d, down, o = ((d0_ref, down0_ref, o0_ref), (d1_ref, down1_ref, o1_ref))[n]
+            shard = 2 * z + other
+            out.append((down, d_scr.at[pl.ds(pl.multiple_of(shard * parts * cut_d, 16), parts * cut_d), :]))
+            out.append((o, wo_ref.at[pl.ds(pl.multiple_of(shard * cut, 16), cut), :]))
+            for k in range(lines):
+                for part in range(parts):
+                    row = pl.multiple_of(((2 * others[k] + other) * parts + (t ^ part)) * cut_d, 16)
+                    out.append((d.at[part, k], d_scr.at[pl.ds(row, cut_d), :]))
+        return [pltpu.make_async_copy(src, dst, d_sem.at[i]) for i, (src, dst) in enumerate(out)]
 
     slot = lax.rem(r, 2)
 
     @pl.when(r == 0)
     def _():
-        for c in copies(0, 0):
+        for part in range(parts):
+
+            @pl.when(t ^ part < o_parts)
+            def _():
+                for c in o_copies(part):
+                    c.start()
+
+        for c in d_copies() + gu_copies(0, 0):
             c.start()
+        for part in range(parts):
+
+            @pl.when(t ^ part < o_parts)
+            def _():
+                for c in o_copies(part):
+                    c.wait()
+
+        for c in d_copies():
+            c.wait()
         resid = x_ref[...].astype(jnp.float32) + mm(ho_ref[...], wo_ref[...], NN)
         r_scr[...] = resid
         inv = lax.rsqrt(jnp.mean(resid * resid, -1, keepdims=True) + EPS)
@@ -594,20 +643,22 @@
         bt_ref[...] = jnp.transpose(b)
         hot_ref[...] = jnp.transpose(ho_ref[...])
 
-    for c in copies(r, slot):
-        c.wait()
-
-    @pl.when(r + 1 < count)
-    def _():
-        for c in copies(r + 1, 1 - slot):
-            c.start()
-
-    width = dg_ref.shape[2]
+    for part in range(parts):
+
+        @pl.when(r == part)
+        def _():
+            for c in gu_copies(part, part % 2):
+                c.wait()
+            if part + 1 < parts:
+                for c in gu_copies(part + 1, (part + 1) % 2):
+                    c.start()
+
+    down = pl.multiple_of((t ^ r) * width, 256)
     for at in range(0, width, 256):
         span = slice(at, at + 256)
         gate = mm(b_scr[...], gu_scr[slot, 0, :, span], NN)
         up = mm(b_scr[...], gu_scr[slot, 1, :, span], NN)
-        dhid = mm(dy_ref[...], d_scr[slot, span, :], NT)
+        dhid = mm(dy_ref[...], d_scr[pl.ds(down + at, 256), :], NT)
         sig = jax.nn.sigmoid(gate)
         silu = gate * sig
         hidden = (silu * up).astype(jnp.bfloat16)
@@ -618,7 +669,7 @@
     model = acc_scr.shape[1]
     for at in range(0, model, 384):
         span = slice(at, at + 384)
-        acc = mm(h_scr[...], d_scr[slot, :, span], NN)
+        acc = mm(h_scr[...], d_scr[pl.ds(down, width), span], NN)
         db = mm(dg_ref[0], gu_scr[slot, 0, span, :], NT) + mm(du_ref[0], gu_scr[slot, 1, span, :], NT)
 
         @pl.when(r == 0)
@@ -650,10 +701,11 @@
         dh_ref[...] = mm(low, wo_ref[...], NT).astype(jnp.bfloat16)
 
 
-def middle(core, ho, x, dy, w_o, gains, gu, d):
+def middle(where, ho, x, dy, gains, near, far, d, own_g, own_u, own_o, own_d):
     rows, model = x.shape
-    count, lines, _, cut, width = gu[0].shape
-    cut_d = d[0].shape[2]
+    lines, cut = near[0].shape[1:3]
+    count = near[0].shape[0] + 1
+    width = own_g[0].shape[1] // count
     once = pl.Buffered(1)
     whole = lambda shape: pl.BlockSpec(shape, lambda r, *_: (0,) * len(shape), pipeline_mode=once)
     act = pl.BlockSpec((1, rows, width), lambda r, *_: (r, 0, 0))
@@ -663,24 +715,24 @@
         grid_spec=pltpu.PrefetchScalarGridSpec(
             num_scalar_prefetch=1,
             grid=(count,),
-            in_specs=[
-                whole((rows, H * HD)), whole((rows, model)), whole((rows, model)), whole((H * HD, model)), whole((8, model)),
-                HBM, HBM, HBM, HBM,
-            ],
+            in_specs=[whole((rows, H * HD)), whole((rows, model)), whole((rows, model)), whole((8, model))] + [HBM] * 14,
             out_specs=[
                 whole((rows, model)), whole((H * HD, rows)), whole((model, rows)),
-                pl.BlockSpec((1, width, rows), lambda r, *_: (r, 0, 0)), act, act,
+                pl.BlockSpec((1, width, rows), lambda r, at_ref: (at_ref[0] ^ r, 0, 0)), act, act,
                 whole((rows, model)), whole((rows, model)), whole((rows, H * HD)), whole((1, model)),
             ],
             scratch_shapes=[
-                pltpu.VMEM((2, 2, 2 * lines * cut, width), low),
-                pltpu.VMEM((2, width, model), low),
+                pltpu.VMEM((2, 2, 2 * (lines + 1) * cut, width), low),
+                pltpu.VMEM((count * width, model), low),
+                pltpu.VMEM((H * HD, model), low),
                 pltpu.VMEM((rows, model), jnp.float32),
                 pltpu.VMEM((rows, model), low),
                 pltpu.VMEM((rows, model), jnp.float32),
                 pltpu.VMEM((rows, model), jnp.float32),
                 pltpu.VMEM((rows, width), low),
-                pltpu.SemaphoreType.DMA((2, 4 * lines)),
+                pltpu.SemaphoreType.DMA((2, 4 * (lines + 1))),
+                pltpu.SemaphoreType.DMA((count, 2 * lines)),
+                pltpu.SemaphoreType.DMA((4 + 2 * count * lines,)),
             ],
         ),
         out_shape=[
@@ -698,20 +750,26 @@
         compiler_params=ROOM,
         cost_estimate=cost(12 * rows * model * width * count + 4 * rows * model * model, 2 * 16 * rows * model + 6 * count * width * model, rows * width * count),
         name="middle",
-    )(core, ho, x, dy, w_o, gains, gu[0], gu[1], d[0], d[1])
-
-
-def last_kernel(x_ref, gain_ref, dr_ref, dq_ref, dk_ref, dv_ref, wq_ref, wkv_ref, cos_ref, sin_ref, gx_ref, act_ref, gg_ref):
+    )(where, ho, x, dy, gains, *near, *far, *d, *own_g, *own_u, *own_o, *own_d)
+
+
+def last_kernel(counts, x_ref, gain_ref, dr_ref, w_ref, cos_ref, sin_ref, *refs):
+    gx_ref, act_ref, gg_ref = refs[-3:]
     half = KVH * HD
-    model = x_ref.shape[1]
-    act_ref[:, 0 : H * HD] = dq_ref[...]
-    for at in range(0, half, WIDE):
-        turned = turn(dk_ref[:, at : at + WIDE], cos_ref[...], -sin_ref[...])
-        act_ref[:, H * HD + at : H * HD + at + WIDE] = turned.astype(jnp.bfloat16)
-    act_ref[:, H * HD + half : H * HD + 2 * half] = dv_ref[...].astype(jnp.bfloat16)
+    at = 0
+    for n, count in enumerate(counts):
+        dq_ref, shares = refs[5 * n], refs[5 * n + 1 : 5 * n + 5]
+        act_ref[:, at * PAIR : (at + count) * PAIR] = dq_ref[...]
+        for p in range(count):
+            span = slice(p * WIDE, (p + 1) * WIDE)
+            dk = sum(share[0, :, span].astype(jnp.float32) for share in shares)
+            dv = sum(share[1, :, span].astype(jnp.float32) for share in shares)
+            column = H * HD + (at + p) * WIDE
+            act_ref[:, column : column + WIDE] = turn(dk, cos_ref[...], -sin_ref[...]).astype(jnp.bfloat16)
+            act_ref[:, column + half : column + half + WIDE] = dv.astype(jnp.bfloat16)
+        at += count
     act_ref[:, H * HD + 2 * half :] = jnp.zeros((x_ref.shape[0], act_ref.shape[1] - H * HD - 2 * half), jnp.bfloat16)
-    da = mm(dq_ref[...], wq_ref[...], NT)
-    da += mm(act_ref[:, H * HD : H * HD + 2 * half], wkv_ref[:, 0 : 2 * half], NT)
+    da = mm(act_ref[:, 0 : H * HD + 2 * half], w_ref[:, 0 : H * HD + 2 * half], NT)
     x = x_ref[...].astype(jnp.float32)
     inv = lax.rsqrt(jnp.mean(x * x, -1, keepdims=True) + EPS)
     gg_ref[...] = jnp.sum(da * x * inv, 0, keepdims=True)
@@ -720,11 +778,12 @@
     gx_ref[...] = gx.astype(jnp.bfloat16)
 
 
-def last(x, gains, dr, dq, dk, dv, w_q, w_kvg, cosine, sine, padded):
+def last(x, gains, dr, w_qkv, cosine, sine, parts, counts):
     rows, model = x.shape
+    padded = w_qkv.shape[1]
     return pl.pallas_call(
-        last_kernel,
-        in_specs=[VMEM] * 10,
+        functools.partial(last_kernel, counts),
+        in_specs=[VMEM] * (6 + len(parts)),
         out_specs=[VMEM] * 3,
         out_shape=[
             jax.ShapeDtypeStruct((rows, model), jnp.bfloat16),
@@ -734,126 +793,195 @@
         compiler_params=ROOM,
         cost_estimate=cost(2 * rows * model * (H + 2 * KVH) * HD, 10 * rows * model + 2 * model * (H + 2 * KVH) * HD),
         name="last",
-    )(x, gains, dr, dq, dk, dv, w_q, w_kvg, cosine, sine)
-
-
-def product_kernel(pos_ref, l0_ref, l1_ref, r0_ref, r1_ref, out_ref):
-    total = mm(l0_ref[...], r0_ref[0], NN) + mm(l1_ref[...], r1_ref[0], NN)
-    out_ref[0] = total.astype(jnp.bfloat16)
-
-
-def products(pos, left, right, blocks, width, column):
+    )(x, gains, dr, w_qkv, cosine, sine, *parts)
+
+
+def gu_products_kernel(l0_ref, l1_ref, g0_ref, g1_ref, u0_ref, u1_ref, g_ref, u_ref):
+    @pl.when(pl.program_id(0) == 0)
+    def _():
+        g_ref[0] = (mm(l0_ref[...], g0_ref[0], NN) + mm(l1_ref[...], g1_ref[0], NN)).astype(jnp.bfloat16)
+
+    @pl.when(pl.program_id(0) == 1)
+    def _():
+        u_ref[0] = (mm(l0_ref[...], u0_ref[0], NN) + mm(l1_ref[...], u1_ref[0], NN)).astype(jnp.bfloat16)
+
+
+def gu_products(left, gates, ups, gate_parts, up_parts):
     rows, tokens = left[0].shape
-    spec = pl.BlockSpec((rows, tokens), lambda n, *_: (0, 0))
-    act = pl.BlockSpec((1, tokens, width), lambda n, pos_ref: column(n, pos_ref))
+    width = gates[0].shape[2]
+    cuts = 2
+    piece = width // cuts
+    spec = pl.BlockSpec((rows, tokens), lambda m, n, h: (0, 0))
+    first = lambda m, v, end: v * (1 - m) + end * m
+    then = lambda m, v: v * m
+
+    def gate_at(m, n, h):
+        return first(m, n, 1), first(m, h, cuts - 1)
+
+    def up_at(m, n, h):
+        return then(m, n), then(m, h)
+
+    def gate_in(m, n, h):
+        n, h = gate_at(m, n, h)
+        return gate_parts[0] + gate_parts[1] * n, 0, h
+
+    def up_in(m, n, h):
+        n, h = up_at(m, n, h)
+        return up_parts[0] + up_parts[1] * n, 0, h
+
+    def gate_out(m, n, h):
+        n, h = gate_at(m, n, h)
+        return n, 0, h
+
+    def up_out(m, n, h):
+        n, h = up_at(m, n, h)
+        return n, 0, h
+
+    act = lambda index: pl.BlockSpec((1, tokens, piece), index)
     return pl.pallas_call(
-        product_kernel,
+        gu_products_kernel,
+        grid=(2, 2, cuts),
+        in_specs=[spec, spec, act(gate_in), act(gate_in), act(up_in), act(up_in)],
+        out_specs=[pl.BlockSpec((1, rows, piece), gate_out), pl.BlockSpec((1, rows, piece), up_out)],
+        out_shape=[jax.ShapeDtypeStruct((2, rows, width), jnp.bfloat16)] * 2,
+        compiler_params=ROOM,
+        cost_estimate=cost(16 * rows * tokens * width, 4 * rows * tokens + 8 * (2 * tokens + rows) * width),
+        name="gu_products",
+    )(left[0], left[1], gates[0], gates[1], ups[0], ups[1])
+
+
+def qkv_products_kernel(where_ref, l0_ref, l1_ref, r0_ref, r1_ref, extra_ref, s0_ref, s1_ref, s2_ref, s3_ref):
+    r = pl.program_id(0)
+    total = mm(l0_ref[...], r0_ref[...], NN) + mm(l1_ref[...], r1_ref[...], NN)
+    end = where_ref[0] ^ r == pl.num_programs(0) - 1
+    wide = extra_ref.shape[1]
+    added = total[:, total.shape[1] - wide :] + jnp.where(end, 1.0, 0.0) * extra_ref[...]
+    for n, ref in enumerate((s0_ref, s1_ref, s2_ref, s3_ref)):
+
+        @pl.when(r == n)
+        def _():
+            ref[:, : total.shape[1] - wide] = total[:, : total.shape[1] - wide].astype(jnp.bfloat16)
+            ref[:, total.shape[1] - wide :] = added.astype(jnp.bfloat16)
+
+
+def qkv_products(where, left, acts, extra):
+    rows, tokens = left[0].shape
+    width = acts[0].shape[1] // 4
+    spec = pl.BlockSpec((rows, tokens), lambda r, *_: (0, 0))
+    act = pl.BlockSpec((tokens, width), lambda r, w: (0, w[0] ^ r))
+    out = pl.BlockSpec((rows, width), lambda r, *_: (0, 0))
+    return pl.pallas_call(
+        qkv_products_kernel,
         grid_spec=pltpu.PrefetchScalarGridSpec(
             num_scalar_prefetch=1,
-            grid=(blocks,),
-            in_specs=[spec, spec, act, act],
-            out_specs=pl.BlockSpec((1, rows, width), lambda n, *_: (n, 0, 0)),
+            grid=(4,),
+            in_specs=[spec, spec, act, act, pl.BlockSpec(extra.shape, lambda r, *_: (0, 0))],
+            out_specs=[out] * 4,
         ),
-        out_shape=jax.ShapeDtypeStruct((blocks, rows, width), jnp.bfloat16),
+        out_shape=[jax.ShapeDtypeStruct((rows, width), jnp.bfloat16)] * 4,
         compiler_params=ROOM,
-        cost_estimate=cost(4 * blocks * rows * tokens * width, 4 * rows * tokens + 2 * blocks * (2 * tokens + rows) * width),
-        name="products",
-    )(pos, left[0], left[1], right[0], right[1])
-
-
-def whole_product_kernel(pos_ref, left_ref, right_ref, out_ref):
-    shards, cut = out_ref.shape[0], out_ref.shape[2]
-    total = mm(left_ref[0], right_ref[...], NN).astype(jnp.bfloat16)
-    for s in range(shards):
-        out_ref[s, 0] = total[s * cut : (s + 1) * cut]
-
-
-def down_product(pos, left, right, shards):
-    parts, rows, tokens = left.shape
-    model = right.shape[1]
-    out = pl.pallas_call(
-        whole_product_kernel,
+        cost_estimate=cost(16 * rows * tokens * width, 4 * rows * tokens + 8 * (2 * tokens + rows) * width),
+        name="qkv_products",
+    )(where, left[0], left[1], acts[0], acts[1], extra)
+
+
+def place_gu_kernel(where_ref, in_ref, g_ref, u_ref):
+    g_ref[...] = in_ref[0, 0].astype(jnp.float32)
+    u_ref[...] = in_ref[0, 1].astype(jnp.float32)
+
+
+def place_gu(where, parts):
+    count, _, rows, width = parts.shape
+    out = pl.BlockSpec((rows, width), lambda n, *_: (0, n))
+    return pl.pallas_call(
+        place_gu_kernel,
         grid_spec=pltpu.PrefetchScalarGridSpec(
             num_scalar_prefetch=1,
-            grid=(parts,),
-            in_specs=[pl.BlockSpec((1, rows, tokens), lambda r, *_: (r, 0, 0)), pl.BlockSpec((tokens, model), lambda r, *_: (0, 0))],
-            out_specs=pl.BlockSpec((shards, 1, rows // shards, model), lambda r, pos_ref: (0, pos_ref[0] ^ r, 0, 0)),
+            grid=(count,),
+            in_specs=[pl.BlockSpec((1, 2, rows, width), lambda n, where_ref: (where_ref[0] ^ n, 0, 0, 0))],
+            out_specs=[out, out],
         ),
-        out_shape=jax.ShapeDtypeStruct((shards, parts, rows // shards, model), jnp.bfloat16),
-        compiler_params=ROOM,
-        cost_estimate=cost(2 * parts * rows * tokens * model, 2 * (parts * rows * tokens + tokens * model + parts * rows * model)),
-        name="down_product",
-    )(pos, left, right)
-    return out.reshape(parts * rows, model)
-
-
-ACROSS_X = [(t, t ^ 1) for t in range(4)]
-ACROSS_Y = [(t, t ^ 2) for t in range(4)]
-ACROSS_CORE = [(f, f ^ 1) for f in range(8)]
-ACROSS_PAIR = [(f, f ^ 2) for f in range(8)]
-MIDDLE = [(f, 6 - 2 * (f // 2) + f % 2) for f in (2, 3, 4, 5)]
-TO_ENDS = [(2, 0), (3, 1), (4, 6), (5, 7)]
-TO_MIDDLE = [(b, a) for a, b in TO_ENDS]
-
-
-def across_x(v):
-    return lax.ppermute(v, "ctx", ACROSS_X)
-
-
-def across_y(v):
-    return lax.ppermute(v, "ctx", ACROSS_Y)
+        out_shape=[jax.ShapeDtypeStruct((rows, count * width), jnp.float32)] * 2,
+        cost_estimate=cost(parts.size, 6 * parts.size),
+        name="place_gu",
+    )(where, parts)
+
+
+def place_qkv_kernel(where_ref, in_ref, q_ref, k_ref, v_ref, g_ref):
+    t = where_ref[0]
+    width = in_ref.shape[2]
+    spans = ((q_ref, 0, H * HD), (k_ref, H * HD, KVH * HD), (v_ref, (H + KVH) * HD, KVH * HD))
+    for n in range(in_ref.shape[0]):
+        part = in_ref[t ^ n].astype(jnp.float32)
+        for at in range(0, width, WIDE):
+            column = n * width + at
+            piece = part[:, at : at + WIDE]
+            for ref, first, size in spans:
+                if first <= column < first + size:
+                    ref[:, column - first : column - first + WIDE] = piece
+            if column == (H + 2 * KVH) * HD:
+                g_ref[...] = jnp.transpose(piece)[0:8]
+
+
+def place_qkv(where, parts):
+    rows = parts.shape[1]
+    wide = lambda columns: jax.ShapeDtypeStruct((rows, columns), jnp.float32)
+    return pl.pallas_call(
+        place_qkv_kernel,
+        in_specs=[pl.BlockSpec(memory_space=pltpu.SMEM), VMEM],
+        out_specs=[VMEM] * 4,
+        out_shape=[wide(H * HD), wide(KVH * HD), wide(KVH * HD), jax.ShapeDtypeStruct((8, rows), jnp.float32)],
+        cost_estimate=cost(parts.size, 6 * parts.size),
+        name="place_qkv",
+    )(where, parts)
+
+
+def square(v, r):
+    return lax.ppermute(v, "ctx", [(t, t ^ r) for t in range(4)])
+
+
+def line(v, k):
+    return lax.ppermute(v, "fsdp", [(f, f ^ (2 * k)) for f in range(8)])
 
 
 def other_core(v):
-    return lax.ppermute(v, "fsdp", ACROSS_CORE)
-
-
-def gather_line(v, z):
-    odd = z % 2 == 1
-    partner = lax.ppermute(v, "fsdp", ACROSS_PAIR)
-    pair = jnp.stack([jnp.where(odd, partner, v), jnp.where(odd, v, partner)])
-    far = lax.ppermute(pair, "fsdp", MIDDLE)
-    end = lax.ppermute(far, "fsdp", TO_ENDS)
-    other = far + end
-    high = z >= 2
-    return jnp.concatenate([jnp.where(high, other, pair), jnp.where(high, pair, other)])
-
-
-def gather_square(v):
-    from_x, from_y = across_x(v), across_y(v)
-    half = v.shape[0] // 2
-    far_x = across_x(from_y[:half])
-    far_y = across_y(from_x[half:])
-    return jnp.stack([v, from_x, from_y, jnp.concatenate([far_x, far_y])])
-
-
-def scatter_square(x_send, x_keep, y_send, y_keep):
-    wide = lambda v: v.astype(jnp.float32)
-    got_x, got_y = across_x(x_send), across_y(y_send)
-    pass_y = (wide(x_keep[1]) + wide(got_x[1])).astype(jnp.bfloat16)
-    pass_x = (wide(y_keep[1]) + wide(got_y[1])).astype(jnp.bfloat16)
-    last_y, last_x = across_y(pass_y), across_x(pass_x)
-    return (
-        wide(x_keep[0]) + wide(got_x[0]) + wide(last_y),
-        wide(y_keep[0]) + wide(got_y[0]) + wide(last_x),
-    )
-
-
-def scatter_line(v, z):
-    wide = lambda v: v.astype(jnp.float32)
-    side = z // 2
-    far = lax.dynamic_slice_in_dim(v, 2 * (1 - side), 2, 0)
-    near = lax.dynamic_slice_in_dim(v, 2 * side, 2, 0)
-    got = lax.ppermute(far, "fsdp", TO_MIDDLE)
-    crossed = lax.ppermute((wide(far) + wide(got)).astype(jnp.bfloat16), "fsdp", MIDDLE)
-    near = wide(near) + wide(crossed)
-    send = lax.dynamic_index_in_dim(near, 1 - z % 2, 0, keepdims=False).astype(jnp.bfloat16)
-    keep = lax.dynamic_index_in_dim(near, z % 2, 0, keepdims=False)
-    return keep + wide(lax.ppermute(send, "fsdp", ACROSS_PAIR))
-
-
-def in_order(parts, t):
-    return jnp.stack([lax.dynamic_index_in_dim(parts, t ^ q, 0, keepdims=False) for q in range(4)])
+    return lax.ppermute(v, "fsdp", [(f, f ^ 1) for f in range(8)])
+
+
+def after(v, *others):
+    return lax.optimization_barrier((v, *others))[0]
+
+
+def wide(v):
+    return v.astype(jnp.float32)
+
+
+def low(v):
+    return v.astype(jnp.bfloat16)
+
+
+def line_pieces(v):
+    return [line(v, k) for k in (1, 2, 3)]
+
+
+def hold(parts, *events):
+    return [after(v, *events) for v in parts]
+
+
+def square_near(v):
+    return [square(v, 1), square(v, 2)]
+
+
+def square_far(from_x, from_y):
+    half = from_x.shape[0] // 2
+    return [square(from_y[:half], 1), square(from_x[half:], 2)]
+
+
+def square_sum(v):
+    half = v.shape[0] // 2 // 16 * 16
+    upper, lower = v[:half], v[half:]
+    upper, lower = wide(upper) + wide(square(low(upper), 1)), wide(lower) + wide(square(low(lower), 2))
+    return jnp.concatenate([upper + wide(square(low(upper), 2)), lower + wide(square(low(lower), 1))])
 
 
 def lanes(v, core):
@@ -881,26 +1009,33 @@
     t = lax.axis_index("ctx")
     f = lax.axis_index("fsdp")
     z, core = f // 2, f % 2
-    pos = t.reshape(1).astype(jnp.int32)
+    where = jnp.stack([t, core, z]).astype(jnp.int32)
     cut, hidden_width = w_gate.shape
-    cut_d = w_down.shape[0]
-    quarter = hidden_width // 4
+    cut_d = w_down.shape[0] // 4
     kv_width = 2 * KVH * HD
 
-    gains_pad = jnp.pad(jnp.stack([norm1_gain, norm2_gain], 1), ((0, 0), (0, WIDE - 2)))
-    w_kvg = lax.all_gather(jnp.concatenate([w_key, w_value, gains_pad], 1), "fsdp", axis=0, tiled=True)
-    w_q = lax.all_gather(w_query, "fsdp", axis=0, tiled=True)
-    w_o = lax.all_gather(w_out, "fsdp", axis=0, tiled=True)
-
-    def own_quarter(w):
-        shaped = w.reshape(cut, 8, 4, cut_d // 4)
-        return lax.dynamic_index_in_dim(shaped, t, 2, keepdims=False).reshape(cut, quarter)
-
-    gu_own = gather_square(gather_line(jnp.stack([own_quarter(w_gate), own_quarter(w_up)]), z))
-    d_part = lax.dynamic_index_in_dim(w_down.reshape(4, cut_d // 4, model), t, 0, keepdims=False)
-    d_own = gather_square(gather_line(d_part, z))
-    gu = (gu_own, other_core(gu_own))
-    d = (d_own, other_core(d_own))
+    slice_of = lambda w: lax.dynamic_slice_in_dim(w, t * (w.shape[1] // 4), w.shape[1] // 4, 1)
+    filled = -(-(H * HD + kv_width + WIDE) // (8 * WIDE)) * 8 * WIDE
+    gains_own = jnp.stack([norm1_gain, norm2_gain], 1)
+    qkv_own = jnp.concatenate([w_query, w_key, w_value, gains_own], 1)
+    qkv_own = jnp.pad(qkv_own, ((0, 0), (0, filled - qkv_own.shape[1])))
+    out_width = -(-model // (4 * WIDE)) * WIDE
+    out_own = jnp.pad(w_out, ((0, 0), (0, 4 * out_width - model)))
+    guo_part = jnp.concatenate([slice_of(w_gate), slice_of(w_up), slice_of(out_own)], 1)
+    d_part = lax.dynamic_slice_in_dim(w_down, t * cut_d, cut_d, 0)
+    rows_of = lambda v: v.reshape(-1, v.shape[-1])
+    swap = lambda w: (w, other_core(w))
+    rows_of = lambda v: v.reshape(-1, v.shape[-1])
+    swap = lambda w: (w, other_core(w))
+    qkv_line = line_pieces(slice_of(qkv_own))
+    own_qkv = swap(qkv_own)
+    own_g, own_u, own_o, own_d = swap(w_gate), swap(w_up), swap(w_out), swap(w_down)
+    qkv_rows = jnp.concatenate(qkv_line)
+    d_line = line_pieces(after(d_part, *qkv_line))
+    qkv_parts = [qkv_rows] + [square(qkv_rows, r) for r in (1, 2, 3)]
+    qkv_all = after(jnp.stack(qkv_parts).reshape(4, 3, cut, -1), *d_line)
+    guo_line = line_pieces(after(guo_part, *qkv_parts, *d_line))
+    qkv_both = swap(qkv_all)
 
     relative = jnp.arange(4) ^ t
     offsets = jnp.arange(BLK, dtype=jnp.int32)
@@ -914,69 +1049,92 @@
     sine = jnp.sin(angles)
     sine = jnp.concatenate([-sine, sine, -sine, sine], 1)
 
-    a, a_t, kv_own, gains = kv_project(x, w_kvg, cosine, sine)
-    q = q_project(a, w_q, cosine, sine)
-    kv = gather_square(kv_own).reshape(4 * rows, kv_width)
-    mixed, lse = attend(own, slots, q, kv)
+    early = [w[1] for w in (own_g, own_u, own_o, own_d)]
+    a, a_t, q, kv_own, gains, w_qkv = qkv_project(where, after(x, *early), cosine, sine, qkv_both, own_qkv)
+    d_rows = after(jnp.concatenate(d_line), *qkv_parts)
+    d_near = square_near(d_rows)
+    kv_near = square_near(after(kv_own, *d_near))
+    kv_far = square_far(*kv_near)
+    d_far = square_far(*hold(d_near, *kv_far))
+    kv = jnp.concatenate([kv_own, *kv_near, *kv_far])
+    mixed_0, lse_0 = attend(own, slots, q, kv, 0, 1)
+    guo_rows = jnp.concatenate(hold(guo_line, mixed_0))
+    d_far = hold(d_far, mixed_0)
+    d = swap(jnp.stack([d_rows, *d_near, jnp.concatenate(d_far)]).reshape(4, 3, cut_d, model))
+    guo_near = square_near(guo_rows)
+    mixed_1, lse_1 = attend(own, slots, after(q, guo_rows), kv, 1, 2)
+    guo_near = hold(guo_near, mixed_1)
+    guo_far = square_far(*guo_near)
+    near = swap(jnp.stack([guo_rows, *guo_near]).reshape(3, 3, cut, -1))
+    far = swap(jnp.concatenate(guo_far).reshape(3, cut, -1))
+    mixed = jnp.concatenate([mixed_0, mixed_1], 1)
     out, mixed_t, b_t, hidden_t, dgate, dup, dr, dr_low, dheads, gg2 = middle(
-        core.reshape(1).astype(jnp.int32), mixed, x, dy, w_o, gains, gu, d
-    )
-
-    grad_d = lax.psum_scatter(down_product(pos, hidden_t, dy, 8), "fsdp", scatter_dimension=0, tiled=True)
+        where, mixed, x, dy, gains, near, far, d, own_g, own_u, own_o, own_d
+    )
+
+    gates, ups = swap(dgate), swap(dup)
     b_mine, b_other = lanes(b_t, core)
     left = (b_mine, other_core(b_other))
-    gates, ups = (dgate, other_core(dgate)), (dup, other_core(dup))
-    r_gu = scatter_square(
-        products(pos, left, gates, 2, quarter, lambda n, p: (1 + 2 * n, 0, 0)),
-        products(pos, left, gates, 2, quarter, lambda n, p: (2 * n, 0, 0)),
-        products(pos, left, ups, 2, quarter, lambda n, p: (2 + n, 0, 0)),
-        products(pos, left, ups, 2, quarter, lambda n, p: (n, 0, 0)),
-    )
-    r_gu = jnp.stack([v.astype(jnp.bfloat16).reshape(4, cut, quarter) for v in r_gu], 1)
-    s_gu = scatter_line(r_gu, z).astype(jnp.bfloat16)
-    all_gu = lax.all_gather(s_gu, "ctx", axis=0, tiled=False)
-
-    def whole_columns(v):
-        return v.reshape(4, cut, 8, cut_d // 4).transpose(1, 2, 0, 3).reshape(cut, hidden_width).astype(jnp.float32)
-
-    grad_g, grad_u = whole_columns(all_gu[:, 0]), whole_columns(all_gu[:, 1])
-
-    grad_o = mm(mixed_t, dr_low, NN).astype(jnp.bfloat16)
-    grad_o = lax.psum_scatter(grad_o, "fsdp", scatter_dimension=0, tiled=True)
-    grad_o = lax.psum(grad_o, "ctx").astype(jnp.float32)
-    grad_d = lax.psum(grad_d, "ctx").astype(jnp.float32)
-    dq, dk_send, dk_keep, dv_send, dv_keep = attend_back(own, slots, q, kv, dheads, mixed, lse, cosine, sine)
-    dk, dv = scatter_square(dk_send, dk_keep, dv_send, dv_keep)
-    padded = -(-(H * HD + kv_width) // (8 * WIDE)) * 8 * WIDE
-    grad_x, act, gg1 = last(x, gains, dr, dq, dk, dv, w_q, w_kvg, cosine, sine, padded)
+    g_send, u_send = gu_products(left, gates, ups, (1, 2), (2, 1))
+    got_x, got_y = square(g_send, 1), square(u_send, 2)
+    scatter = lambda v: lax.psum_scatter(v, "fsdp", scatter_dimension=0, tiled=True)
+    grad_d = scatter(low(mm(hidden_t.reshape(-1, rows), after(dy, g_send), NN)))
+    grad_o = scatter(low(mm(mixed_t, after(dr_low, g_send), NN)))
+    g_keep, u_keep = gu_products(left, gates, ups, (0, 2), (0, 1))
+
+    dq_1, *dkv_1 = attend_back(own, slots, after(q, g_keep), kv, dheads, mixed_1, lse_1, cosine, sine, 1, 2)
+    got_x, got_y = hold((got_x, got_y), dq_1)
+    pass_y = low(wide(g_keep[1]) + wide(got_x[1]))
+    pass_x = low(wide(u_keep[1]) + wide(got_y[1]))
+    last_y, last_x = square(pass_y, 2), square(pass_x, 1)
+    dkv_1_got = [square(v, r) for r, v in zip((1, 2, 3), dkv_1[1:])]
+    dq_0, *dkv_0 = attend_back(own, slots, after(q, pass_x, pass_y), kv, dheads, mixed_0, lse_0, cosine, sine, 0, 1)
+    last_y, last_x, *dkv_1_got = hold([last_y, last_x, *dkv_1_got], dq_0)
+    rows_at = lambda v, at: lax.dynamic_slice_in_dim(v, at * cut, cut, 0)
+
+    def gu_share(at):
+        g = sum(wide(rows_at(v, at)) for v in (g_keep[0], got_x[0], last_y))
+        u = sum(wide(rows_at(v, at)) for v in (u_keep[0], got_y[0], last_x))
+        return jnp.stack([g, u])
+
+    gu_sends = [low(gu_share(z ^ k)) for k in (1, 2, 3)]
+    gu_got = [line(v, k) for k, v in zip((1, 2, 3), gu_sends)]
+    dkv_0_got = [square(v, r) for r, v in zip((1, 2, 3), dkv_0[1:])]
+    parts = [dq_0, dkv_0[0], *dkv_0_got, dq_1, dkv_1[0], *dkv_1_got]
+    grad_x, act, gg1 = last(after(x, *gu_sends), gains, dr, w_qkv, cosine, sine, parts, (1, 2))
+
     a_mine, a_other = lanes(a_t, core)
     left = (a_mine, other_core(a_other))
-    acts = (act[None], other_core(act)[None])
-    eighth = padded // 8
-    r_qkv = scatter_square(
-        products(pos, left, acts, 2, eighth, lambda n, p: (0, 0, 2 * (p[0] ^ (1 + 2 * n)))),
-        products(pos, left, acts, 2, eighth, lambda n, p: (0, 0, 2 * (p[0] ^ (2 * n)))),
-        products(pos, left, acts, 2, eighth, lambda n, p: (0, 0, 2 * (p[0] ^ (2 + n)) + 1)),
-        products(pos, left, acts, 2, eighth, lambda n, p: (0, 0, 2 * (p[0] ^ n) + 1)),
-    )
-    r_qkv = jnp.concatenate([v.astype(jnp.bfloat16) for v in r_qkv], 1).reshape(4, cut, 2 * eighth)
-    s_qkv = scatter_line(r_qkv, z).astype(jnp.bfloat16)
-    all_qkv = in_order(gather_square(s_qkv), t)
-    grad_qkv = all_qkv.transpose(1, 0, 2).reshape(cut, padded).astype(jnp.float32)
-    gain_grads = lax.psum(jnp.concatenate([gg1, gg2]), ("ctx", "fsdp"))
-    gain_grads = lax.dynamic_slice_in_dim(gain_grads, f * cut, cut, 1)
+    gain_rows = jnp.concatenate([gg1, gg2])
+    gain_rows = (gain_rows + other_core(gain_rows)).reshape(2, 4, 2, cut)
+    gain_rows = lax.dynamic_index_in_dim(gain_rows, core, 2, keepdims=False).reshape(2, 4 * cut)
+    extra = jnp.pad(gain_rows.T, ((0, 0), (0, WIDE - 2)))
+    qkv_keep, *qkv_sends = qkv_products(where, left, swap(act), extra)
+    shares = [qkv_keep] + [square(v, r) for r, v in zip((1, 2, 3), qkv_sends)]
+    gu_got = hold(gu_got, qkv_keep)
+    s_gu = low(gu_share(z) + sum(wide(v) for v in gu_got))
+    all_gu = jnp.stack([s_gu] + [square(s_gu, r) for r in (1, 2, 3)])
+    grad_g, grad_u = place_gu(where, all_gu)
+    shares = hold(shares, s_gu)
+    qkv_share = lambda at: sum(wide(rows_at(v, at)) for v in shares)
+    qkv_sends = [low(qkv_share(z ^ k)) for k in (1, 2, 3)]
+    qkv_got = [line(v, k) for k, v in zip((1, 2, 3), qkv_sends)]
+    grad_do = square_sum(jnp.concatenate([after(grad_d, *qkv_sends), after(grad_o, *qkv_sends)]))
+    s_qkv = low(qkv_share(z) + sum(wide(v) for v in qkv_got))
+    all_qkv = jnp.stack([s_qkv] + [square(s_qkv, r) for r in (1, 2, 3)])
+    grad_q, grad_k, grad_v, grad_gains = place_qkv(where, all_qkv)
     return (
         out[None],
         grad_x[None],
-        gain_grads[0],
-        grad_qkv[:, : H * HD],
-        grad_qkv[:, H * HD : H * HD + kv_width // 2],
-        grad_qkv[:, H * HD + kv_width // 2 : H * HD + kv_width],
-        grad_o,
-        gain_grads[1],
+        grad_gains[0],
+        grad_q,
+        grad_k,
+        grad_v,
+        grad_do[4 * cut_d :],
+        grad_gains[1],
         grad_g,
         grad_u,
-        grad_d,
+        grad_do[: 4 * cut_d],
     )
 
 

time: 687 us -> 549 us (0.80)
  waiting for transfers between devices: 270 us -> 191 us
  blocking collectives: 40.7 us -> 0 us
  other arithmetic: 49.6 us -> 28.6 us
  matrix products: 4.79 us -> 14 us
  local copies, waits for them, and re-layouts: 46.4 us -> 39.3 us
    ppermute x47 -> x68, waiting for transfers between devices: 270 us -> 191 us  [the longest x38 140 us: square(): return lax.ppermute(v, 'ctx', [(t, t ^ r) for t in range(4)])]
    psum x1 -> x0, blocking collectives: 40.7 us -> none  [square_body(): gain_grads = lax.psum(jnp.concatenate([gg1, gg2]), ('ctx', 'fsdp'))]
    convert_element_type x9 -> x0, local copies, waits for them, and re-layouts: 19.6 us -> none  [the longest x6 19.4 us: whole_columns(): v.reshape(4, cut, 8, cut_d // 4).transpose(1, 2, 0, 3)]
    convert_element_type x17 -> x7, other arithmetic: 24.1 us -> 7.39 us  [low(): return v.astype(jnp.bfloat16)]
    unnamed x59 -> x91, local copies, waits for them, and re-layouts: 1.72 us -> 14.3 us
    dot_general x1 -> x2, matrix products: 4.79 us -> 14 us  [mm(): lax.dot_general(left, right, dims, preferred_element_type=jnp.float32)]
    pallas_call x12 -> x7, Pallas kernels: 60.2 us -> 54.2 us  [the longest x2 21.4 us: gu_products(): pl.pallas_call(gu_products_kernel, grid=(2, 2, cuts), in_specs=[spec, spe...]
    another operation x16 -> x11, other arithmetic: 16.6 us -> 11.3 us  [the longest x5 3.42 us: gu_share(): return jnp.stack([g, u])]
  transfers between devices with their start and end apart: 54 -> 70, of which waited for: 23 -> 32; matrix products, arithmetic and copies ran while one was open for 12% -> 10% of each run, Pallas kernels for 19% -> 23%
where the time goes in v2:
time: 549 us; the launch traced here: 544 us
  waiting for transfers between devices  191 us (35%)
  Pallas kernels  183 us (33%)
  starting transfers between devices  73.7 us (13%)
  local copies, waits for them, and re-layouts  39.3 us (7%)
  other arithmetic  28.6 us (5%)
  between operations  15 us (3%)
  matrix products  14 us (3%)
    ppermute x38, waiting for transfers between devices, square(): return lax.ppermute(v, 'ctx', [(t, t ^ r) for t in range(4)])  140 us
    pallas_call x1, Pallas kernels, middle(): pl.pallas_call(middle_kernel, grid_spec=pltpu.PrefetchScalarGridSpec(num_...  49.3 us
    pallas_call x2, Pallas kernels, attend_back(): pl.pallas_call(attend_back_kernel, grid_spec=pltpu.PrefetchScalarGridSpec...  46.3 us
    ppermute x38, starting transfers between devices, square(): return lax.ppermute(v, 'ctx', [(t, t ^ r) for t in range(4)])  42.4 us
    ppermute x15, waiting for transfers between devices, line(): return lax.ppermute(v, 'fsdp', [(f, f ^ 2 * k) for f in range(8)])  41.2 us
    pallas_call x2, Pallas kernels, attend(): pl.pallas_call(attend_kernel, grid_spec=pltpu.PrefetchScalarGridSpec(num_...  33.1 us
    ppermute x15, starting transfers between devices, line(): return lax.ppermute(v, 'fsdp', [(f, f ^ 2 * k) for f in range(8)])  28.6 us
    pallas_call x2, Pallas kernels, gu_products(): pl.pallas_call(gu_products_kernel, grid=(2, 2, cuts), in_specs=[spec, spe...  21.4 us
  transfers between devices with their start and end apart: 70, of which 32 were waited for; matrix products, arithmetic and copies ran while one was open for 10% of the time, Pallas kernels for 23%

profile of v2, /device:TPU:0, one launch (start us, length us, event | category | flops | bytes accessed | tf_op | source)
XLA Modules:
  0.0 544.1 jit_solution(12680453390660572336)
XLA Ops:
  10.0 3.1 collective-permute-start.4
  13.1 2.6 collective-permute-start.5
  15.6 3.3 collective-permute-done.4
  18.9 8.1 %collective-permute-done.5 = bf16[144,512]{1,0:T(8,128)(2,1)S(1)} collective-permute-done((bf16[144,512]{1,0:T(8,128)(2,1)S(1)}, bf16[144,512]{1,0:T(8,128)(2,1)S(1)}, u32[]{:S(2)}, u32[]{:S(2)}) %collective-permute-start.5) | collective-permute-done | bytes 147488 | tf_op jit(solution)/shard_map/ppermute | solution.py:944
  27.1 1.6 collective-permute-start.7
  31.6 2.3 collective-permute-start.10
  35.0 5.2 collective-permute-done.7
  40.3 2.3 collective-permute-start.12
  42.5 4.7 collective-permute-done.8
  53.4 1.8 fusion.19
  64.2 2.2 pad_maximum_fusion.15.sin_ref
  67.2 8.3 %qkv_project.1 = (bf16[512,1152]{1,0:T(8,128)(2,1)}, bf16[1152,512]{1,0:T(8,128)(2,1)}, bf16[512,1152]{1,0:T(8,128)(2,1)}, bf16[512,768]{1,0:T(8,128)(2,1)}, f32...) custom-call(s32[3]{0:T(128)} %pad_add_fusion.at_ref.where_ref, bf16[512,1152]{1,0:T(8,128)(2,1)} %bitcast.136, ...), custom_call_target="tpu_custom_call" | custom-call | flops 2415919104 | bytes 14155776 | tf_op jit(solution)/shard_map/qkv_project/pallas_call | solution.py:341
  83.3 2.8 collective-permute-start.23
  86.1 2.5 collective-permute-start.22
  88.7 8.1 %collective-permute-done.18 = bf16[512,768]{1,0:T(8,128)(2,1)S(1)} collective-permute-done((bf16[512,768]{1,0:T(8,128)(2,1)}, bf16[512,768]{1,0:T(8,128)(2,1)S(1)}, u32[]{:S(2)}, u32[]{:S(2)}) %collective-permute-start.18) | collective-permute-done | bytes 786464 | tf_op jit(solution)/shard_map/ppermute | solution.py:940
  99.2 7.2 %collective-permute-done.19 = bf16[256,768]{1,0:T(8,128)(2,1)S(1)} collective-permute-done((bf16[256,768]{1,0:T(8,128)(2,1)S(1)}, bf16[256,768]{1,0:T(8,128)(2,1)S(1)}, u32[]{:S(2)}, u32[]{:S(2)}) %collective-permute-start.19) | collective-permute-done | bytes 393248 | tf_op jit(solution)/shard_map/ppermute | solution.py:940
  107.3 1.7 copy-done.28
  108.9 12.2 %attend.2 = (bf16[512,384]{1,0:T(8,128)(2,1)}, f32[2,2,1,768]{3,2,1,0:T(1,128)}) custom-call(s32[2]{0:T(128)} %slice_bitcast_fusion.own_ref, s32[8]{0:T(128)} %scatter_custom_fusion.slot_ref, bf16[512,1152]{1,0:T(8,128)(2,1)} %get-tuple-element.129.q_ref, bf16[2048,768]{1,0:T(8,128)(2,1)} %copy-done.28, bf16[2048,768]{1,0:T(8,128)(2,1)} %copy-done.28), custom_call_target="tpu_custom_call" | custom-call | flops 7247757312 | bytes 1835008 | tf_op jit(solution)/shard_map/attend/pallas_call | solution.py:438
  121.1 12.8 %collective-permute-done.22 = bf16[144,1920]{1,0:T(8,128)(2,1)S(1)} collective-permute-done((bf16[144,1920]{1,0:T(8,128)(2,1)S(1)}, bf16[144,1920]{1,0:T(8,128)(2,1)S(1)}, u32[]{:S(2)}, u32[]{:S(2)}) %collective-permute-start.22) | collective-permute-done | bytes 552992 | tf_op jit(solution)/shard_map/ppermute | solution.py:944
  138.0 20.9 %attend.3 = (bf16[512,768]{1,0:T(8,128)(2,1)}, f32[4,2,1,768]{3,2,1,0:T(1,128)}) custom-call(s32[2]{0:T(128)} %slice_bitcast_fusion.own_ref, s32[8]{0:T(128)} %scatter_custom_fusion.slot_ref, bf16[512,1152]{1,0:T(8,128)(2,1)} %get-tuple-element.129.q_ref, bf16[2048,768]{1,0:T(8,128)(2,1)} %copy-done.28, bf16[2048,768]{1,0:T(8,128)(2,1)} %copy-done.28), custom_call_target="tpu_custom_call" | custom-call | flops 14495514624 | bytes 3670016 | tf_op jit(solution)/shard_map/attend/pallas_call | solution.py:438
  158.8 16.1 %collective-permute-done.24 = bf16[432,1920]{1,0:T(8,128)(2,1)S(1)} collective-permute-done((bf16[432,1920]{1,0:T(8,128)(2,1)}, bf16[432,1920]{1,0:T(8,128)(2,1)S(1)}, u32[]{:S(2)}, u32[]{:S(2)}) %collective-permute-start.24) | collective-permute-done | bytes 1658912 | tf_op jit(solution)/shard_map/ppermute | solution.py:940
  176.0 1.8 pad_maximum_fusion.near0_ref
  181.4 7.8 %collective-permute-done.30 = bf16[144,1152]{1,0:T(8,128)(2,1)S(1)} collective-permute-done((bf16[144,1152]{1,0:T(8,128)(2,1)S(1)}, bf16[144,1152]{1,0:T(8,128)(2,1)S(1)}, u32[]{:S(2)}, u32[]{:S(2)}) %collective-permute-start.30) | collective-permute-done | bytes 331808 | tf_op jit(solution)/shard_map/ppermute | solution.py:940
  192.8 1.7 pad_maximum_fusion.1.d0_ref
  194.6 15.7 %collective-permute-done.28 = bf16[216,1920]{1,0:T(8,128)(2,1)S(1)} collective-permute-done((bf16[216,1920]{1,0:T(8,128)(2,1)S(1)}, bf16[216,1920]{1,0:T(8,128)(2,1)S(1)}, u32[]{:S(2)}, u32[]{:S(2)}) %collective-permute-start.28) | collective-permute-done | bytes 829472 | tf_op jit(solution)/shard_map/ppermute | solution.py:940
  212.1 2.2 collective-permute-done.29.far1_ref
  215.5 1.6 copy-done.31
  217.1 49.3 %middle.1 = (bf16[512,1152]{1,0:T(8,128)(2,1)}, bf16[1152,512]{1,0:T(8,128)(2,1)}, bf16[1152,512]{1,0:T(8,128)(2,1)}, bf16[4,768,512]{2,1,0:T(8,128)(2,1)}, bf16...) custom-call(s32[3]{0:T(128)} %pad_add_fusion.at_ref.where_ref, ...), custom_call_target="tpu_custom_call" | custom-call | flops 24461180928 | bytes 40108032 | tf_op jit(solution)/shard_map/middle/pallas_call | solution.py:713
  266.9 2.8 constant_dynamic-slice_fusion.2
  269.9 7.0 %collective-permute-done.33.l1_ref = bf16[576,512]{1,0:T(8,128)(2,1)S(1)} collective-permute-done((bf16[576,512]{1,0:T(8,128)(2,1)S(1)}, bf16[576,512]{1,0:T(8,128)(2,1)S(1)}, u32[]{:S(2)}, u32[]{:S(2)}) %collective-permute-start.33) | collective-permute-done | bytes 589856 | tf_op jit(solution)/shard_map/ppermute | solution.py:948
  277.8 1.6 copy-done
  279.5 10.7 %gu_products.3 = (bf16[2,576,768]{2,1,0:T(8,128)(2,1)}, bf16[2,576,768]{2,1,0:T(8,128)(2,1)}) custom-call(bf16[576,512]{1,0:T(8,128)(2,1)} %bitcast.127, bf16[576,512]{1,0:T(8,128)(2,1)} %copy-done.5, bf16[4,512,768]{2,1,0:T(8,128)(2,1)} %get-tuple-element.117.g0_ref, bf16[4,512,768]{2,1,0:T(8,128)(2,1)} %copy-done, ...), custom_call_target="tpu_custom_call" | custom-call | flops 3623878656 | bytes 11010048 | tf_op jit(solution)/shard_map/gu_products/pallas_call | solution.py:841
  290.1 4.8 convolution_convert_fusion.1
  296.2 9.2 %convolution_convert_fusion = bf16[3072,1152]{1,0:T(8,128)(2,1)} fusion(bf16[3072,512]{1,0:T(8,128)(2,1)} %bitcast.163, bf16[512,1152]{1,0:T(8,128)(2,1)S(1)} %bitcast.161), kind=kOutput, calls=%fused_computation.2 | convolution fusion | flops 3627417600 | bytes 11403264 | tf_op jit(solution)/shard_map/dot_general | solution.py:279
  305.4 1.8 collective-permute-start.36
  307.2 10.8 %gu_products.2 = (bf16[2,576,768]{2,1,0:T(8,128)(2,1)}, bf16[2,576,768]{2,1,0:T(8,128)(2,1)}) custom-call(bf16[576,512]{1,0:T(8,128)(2,1)} %bitcast.128, bf16[576,512]{1,0:T(8,128)(2,1)} %copy-done.5, bf16[4,512,768]{2,1,0:T(8,128)(2,1)} %get-tuple-element.117.g0_ref, bf16[4,512,768]{2,1,0:T(8,128)(2,1)} %copy-done, ...), custom_call_target="tpu_custom_call" | custom-call | flops 3623878656 | bytes 11010048 | tf_op jit(solution)/shard_map/gu_products/pallas_call | solution.py:841
  320.5 29.8 %attend_back.2 = (bf16[512,768]{1,0:T(8,128)(2,1)}, bf16[2,512,256]{2,1,0:T(8,128)(2,1)}, bf16[2,512,256]{2,1,0:T(8,128)(2,1)}, bf16[2,512,256]{2,1,0:T(8,128)(2,1)}, bf16[2,512,256]{2,1,0:T(8,128)(2,1)}) custom-call(s32[2]{0:T(128)} %slice_bitcast_fusion.own_ref, s32[8]{0:T(128)} %scatter_custom_fusion.slot_ref, ...), custom_call_target="tpu_custom_call" | custom-call | flops 36238786560 | bytes 7340032 | tf_op jit(solution)/shard_map/attend_back/pallas_call | solution.py:527
  355.1 17.2 %collective-permute-done.38 = bf16[2,576,768]{2,1,0:T(8,128)(2,1)S(1)} collective-permute-done((bf16[2,576,768]{2,1,0:T(8,128)(2,1)}, bf16[2,576,768]{2,1,0:T(8,128)(2,1)S(1)}, u32[]{:S(2)}, u32[]{:S(2)}) %collective-permute-start.38) | collective-permute-done | bytes 1769504 | tf_op jit(solution)/shard_map/ppermute | solution.py:940
  372.2 3.0 fusion.2
  378.1 16.5 %attend_back.3 = (bf16[512,384]{1,0:T(8,128)(2,1)}, bf16[2,512,128]{2,1,0:T(8,128)(2,1)}, bf16[2,512,128]{2,1,0:T(8,128)(2,1)}, bf16[2,512,128]{2,1,0:T(8,128)(2,1)}, bf16[2,512,128]{2,1,0:T(8,128)(2,1)}) custom-call(s32[2]{0:T(128)} %slice_bitcast_fusion.own_ref, s32[8]{0:T(128)} %scatter_custom_fusion.slot_ref, ...), custom_call_target="tpu_custom_call" | custom-call | flops 18119393280 | bytes 3670016 | tf_op jit(solution)/shard_map/attend_back/pallas_call | solution.py:527
  399.6 5.0 collective-permute-done.37
  404.6 1.6 fusion.6
  406.3 1.7 fusion.5
  408.1 4.4 collective-permute-done.41.refs_3_
  413.3 10.1 %last.1 = (bf16[512,1152]{1,0:T(8,128)(2,1)}, bf16[512,2048]{1,0:T(8,128)(2,1)}, f32[1,1152]{1,0:T(1,128)}) custom-call(bf16[512,1152]{1,0:T(8,128)(2,1)} %bitcast.138, f32[8,1152]{1,0:T(8,128)} %get-tuple-element.108.gain_ref, f32[512,1152]{1,0:T(8,128)} %get-tuple-element.135.dr_ref, bf16[1152,2048]{1,0:T(8,128)(2,1)} %get-tuple-element.136.w_ref, ...), custom_call_target="tpu_custom_call" | custom-call | flops 2264924160 | bytes 10321920 | tf_op jit(solution)/shard_map/last/pallas_call | solution.py:784
  424.8 3.2 collective-permute-start.50
  428.0 1.9 collective-permute-start.51
  431.7 7.6 %qkv_products.1 = (bf16[576,512]{1,0:T(8,128)(2,1)}, bf16[576,512]{1,0:T(8,128)(2,1)}, bf16[576,512]{1,0:T(8,128)(2,1)}, bf16[576,512]{1,0:T(8,128)(2,1)}) custom-call(s32[3]{0:T(128)} %pad_add_fusion.at_ref.where_ref, bf16[576,512]{1,0:T(8,128)(2,1)} %bitcast.144, bf16[576,512]{1,0:T(8,128)(2,1)} %collective-permute-done.46.l1_ref, ...), custom_call_target="tpu_custom_call" | custom-call | flops 2415919104 | bytes 7733248 | tf_op jit(solution)/shard_map/qkv_products/pallas_call | solution.py:873
  441.1 5.4 collective-permute-done.49
  447.7 10.3 %collective-permute-done.50 = bf16[2,144,768]{2,1,0:T(8,128)(2,1)} collective-permute-done((bf16[2,144,768]{2,1,0:T(8,128)(2,1)S(1)}, bf16[2,144,768]{2,1,0:T(8,128)(2,1)}, u32[]{:S(2)}, u32[]{:S(2)}) %collective-permute-start.50) | collective-permute-done | bytes 442400 | tf_op jit(solution)/shard_map/ppermute | solution.py:944
  461.4 1.7 collective-permute-start.65
  463.1 6.0 %collective-permute-done.54 = bf16[576,512]{1,0:T(8,128)(2,1)S(1)} collective-permute-done((bf16[576,512]{1,0:T(8,128)(2,1)}, bf16[576,512]{1,0:T(8,128)(2,1)S(1)}, u32[]{:S(2)}, u32[]{:S(2)}) %collective-permute-start.54) | collective-permute-done | bytes 589856 | tf_op jit(solution)/shard_map/ppermute | solution.py:940
  469.3 3.7 collective-permute-start.55
  474.0 3.9 collective-permute-done.63
  477.9 2.0 collective-permute-start.57
  479.9 7.3 %collective-permute-done.65 = bf16[2,144,768]{2,1,0:T(8,128)(2,1)S(1)} collective-permute-done((bf16[2,144,768]{2,1,0:T(8,128)(2,1)S(1)}, bf16[2,144,768]{2,1,0:T(8,128)(2,1)S(1)}, u32[]{:S(2)}, u32[]{:S(2)}) %collective-permute-start.65) | collective-permute-done | bytes 442400 | tf_op jit(solution)/shard_map/ppermute | solution.py:940
  494.1 1.7 collective-permute-start.60
  497.1 12.0 %collective-permute-done.58 = bf16[144,512]{1,0:T(8,128)(2,1)S(1)} collective-permute-done((bf16[144,512]{1,0:T(8,128)(2,1)S(1)}, bf16[144,512]{1,0:T(8,128)(2,1)S(1)}, u32[]{:S(2)}, u32[]{:S(2)}) %collective-permute-start.58) | collective-permute-done | bytes 147488 | tf_op jit(solution)/shard_map/ppermute | solution.py:940
  509.1 1.9 collective-permute-done.60
  511.9 4.6 place_gu.1
  516.5 2.1 place_qkv.1
  520.3 1.6 collective-permute-start.62
  523.2 8.7 %collective-permute-done.67 = bf16[256,1152]{1,0:T(8,128)(2,1)S(1)} collective-permute-done((bf16[256,1152]{1,0:T(8,128)(2,1)S(1)}, bf16[256,1152]{1,0:T(8,128)(2,1)S(1)}, u32[]{:S(2)}, u32[]{:S(2)}) %collective-permute-start.67) | collective-permute-done | bytes 589856 | tf_op jit(solution)/shard_map/ppermute | solution.py:940
  532.1 2.6 collective-permute-done.62
  (258 shorter events, 93.3 us)
Async XLA Ops:
  7.2 481.4 %reduce-scatter.5.cloned.1.call-start = ((), (), s32[]{:S(2)}) async-start(), calls=%async_computation.3 | async-start | bytes 2985984 | tf_op jit(solution)/shard_map/reduce_scatter | solution.py:1080
  10.0 8.9 %collective-permute-start.4 = (bf16[144,512]{1,0:T(8,128)(2,1)S(1)}, bf16[144,512]{1,0:T(8,128)(2,1)S(1)}, u32[]{:S(2)}, u32[]{:S(2)}) collective-permute-start(bf16[144,512]{1,0:T(8,128)(2,1)S(1)} %constant_dynamic-slice_fusion.8), channel_id=1, source_target_pairs={{0,2},{1,3},{2,0},{3,1},{4,6},{5,7},{6,4},{7,5},{8,10},{9,11},{10,... | collective-permute-start | bytes 442376 | tf_op jit(solution)/shard_map/ppermute | solution.py:944
  13.1 14.0 %collective-permute-start.5 = (bf16[144,512]{1,0:T(8,128)(2,1)S(1)}, bf16[144,512]{1,0:T(8,128)(2,1)S(1)}, u32[]{:S(2)}, u32[]{:S(2)}) collective-permute-start(bf16[144,512]{1,0:T(8,128)(2,1)S(1)} %constant_dynamic-slice_fusion.8), channel_id=1, source_target_pairs={{0,4},{1,5},{2,6},{3,7},{4,0},{5,1},{6,2},{7,3},{8,12},{9,13},{10,... | collective-permute-start | bytes 442376 | tf_op jit(solution)/shard_map/ppermute | solution.py:944
  15.6 11.4 %collective-permute-start.6 = (bf16[144,512]{1,0:T(8,128)(2,1)S(1)}, bf16[144,512]{1,0:T(8,128)(2,1)S(1)}, u32[]{:S(2)}, u32[]{:S(2)}) collective-permute-start(bf16[144,512]{1,0:T(8,128)(2,1)S(1)} %constant_dynamic-slice_fusion.8), channel_id=1, source_target_pairs={{0,6},{1,7},{2,4},{3,5},{4,2},{5,3},{6,0},{7,1},{8,14},{9,15},{10,... | collective-permute-start | bytes 442376 | tf_op jit(solution)/shard_map/ppermute | solution.py:944
  27.1 13.2 %collective-permute-start.7 = (bf16[432,512]{1,0:T(8,128)(2,1)S(1)}, bf16[432,512]{1,0:T(8,128)(2,1)S(1)}, u32[]{:S(2)}, u32[]{:S(2)}) collective-permute-start(bf16[432,512]{1,0:T(8,128)(2,1)S(1)} %constant_dynamic-update-slice_fusion), channel_id=1, source_target_pairs={{0,8},{8,0},{16,24},{24,16},{1,9},{9,1},{17,25},{25,17},{2,10},{10... | collective-permute-start | bytes 1327112 | tf_op jit(solution)/shard_map/ppermute | solution.py:940
  28.7 18.6 %collective-permute-start.8 = (bf16[432,512]{1,0:T(8,128)(2,1)S(1)}, bf16[432,512]{1,0:T(8,128)(2,1)S(1)}, u32[]{:S(2)}, u32[]{:S(2)}) collective-permute-start(bf16[432,512]{1,0:T(8,128)(2,1)S(1)} %constant_dynamic-update-slice_fusion), channel_id=1, source_target_pairs={{0,16},{8,24},{16,0},{24,8},{1,17},{9,25},{17,1},{25,9},{2,18},{10... | collective-permute-start | bytes 1327112 | tf_op jit(solution)/shard_map/ppermute | solution.py:940
  30.2 17.1 %collective-permute-start.9 = (bf16[432,512]{1,0:T(8,128)(2,1)S(1)}, bf16[432,512]{1,0:T(8,128)(2,1)S(1)}, u32[]{:S(2)}, u32[]{:S(2)}) collective-permute-start(bf16[432,512]{1,0:T(8,128)(2,1)S(1)} %constant_dynamic-update-slice_fusion), channel_id=1, source_target_pairs={{0,24},{8,16},{16,8},{24,0},{1,25},{9,17},{17,9},{25,1},{2,26},{10... | collective-permute-start | bytes 1327112 | tf_op jit(solution)/shard_map/ppermute | solution.py:940
  31.6 18.0 %collective-permute-start.10 = (bf16[96,1152]{1,0:T(8,128)(2,1)S(1)}, bf16[96,1152]{1,0:T(8,128)(2,1)S(1)}, u32[]{:S(2)}, u32[]{:S(2)}) collective-permute-start(bf16[96,1152]{1,0:T(8,128)(2,1)S(1)} %constant_dynamic-slice_fusion.7), channel_id=1, source_target_pairs={{0,2},{1,3},{2,0},{3,1},{4,6},{5,7},{6,4},{7,5},{8,10},{9,11},{10,... | collective-permute-start | bytes 663560 | tf_op jit(solution)/shard_map/ppermute | solution.py:944
  33.9 16.9 %collective-permute-start.11 = (bf16[96,1152]{1,0:T(8,128)(2,1)S(1)}, bf16[96,1152]{1,0:T(8,128)(2,1)S(1)}, u32[]{:S(2)}, u32[]{:S(2)}) collective-permute-start(bf16[96,1152]{1,0:T(8,128)(2,1)S(1)} %constant_dynamic-slice_fusion.7), channel_id=1, source_target_pairs={{0,4},{1,5},{2,6},{3,7},{4,0},{5,1},{6,2},{7,3},{8,12},{9,13},{10,... | collective-permute-start | bytes 663560 | tf_op jit(solution)/shard_map/ppermute | solution.py:944
  40.3 10.6 %collective-permute-start.12 = (bf16[96,1152]{1,0:T(8,128)(2,1)S(1)}, bf16[96,1152]{1,0:T(8,128)(2,1)S(1)}, u32[]{:S(2)}, u32[]{:S(2)}) collective-permute-start(bf16[96,1152]{1,0:T(8,128)(2,1)S(1)} %constant_dynamic-slice_fusion.7), channel_id=1, source_target_pairs={{0,6},{1,7},{2,4},{3,5},{4,2},{5,3},{6,0},{7,1},{8,14},{9,15},{10,... | collective-permute-start | bytes 663560 | tf_op jit(solution)/shard_map/ppermute | solution.py:944
  50.9 15.6 %collective-permute-start.13 = (bf16[4,3,144,512]{3,2,1,0:T(8,128)(2,1)S(1)}, bf16[4,3,144,512]{3,2,1,0:T(8,128)(2,1)}, u32[]{:S(2)}, u32[]{:S(2)}) collective-permute-start(bf16[4,3,144,512]{3,2,1,0:T(8,128)(2,1)S(1)} %pad_maximum_fusion.3.w0_ref), channel_id=1, source_target_pairs={{0,1},{1,0},{2,3},{3,2},{4,5},{5,4},{6,7},{7,6},{8,9},{9,8},{10,11... | collective-permute-start | bytes 5308424 | tf_op jit(solution)/shard_map/ppermute | solution.py:948
  51.5 14.9 %collective-permute-start.3 = (bf16[384,1152]{1,0:T(8,128)(2,1)}, bf16[384,1152]{1,0:T(8,128)(2,1)}, u32[]{:S(2)}, u32[]{:S(2)}) collective-permute-start(bf16[384,1152]{1,0:T(8,128)(2,1)} %down0_ref.1), channel_id=1, source_target_pairs={{0,1},{1,0},{2,3},{3,2},{4,5},{5,4},{6,7},{7,6},{8,9},{9,8},{10,11... | collective-permute-start | bytes 2654216 | tf_op jit(solution)/shard_map/ppermute | solution.py:948
  52.0 8.6 %collective-permute-start.1 = (bf16[144,3072]{1,0:T(8,128)(2,1)}, bf16[144,3072]{1,0:T(8,128)(2,1)}, u32[]{:S(2)}, u32[]{:S(2)}) collective-permute-start(bf16[144,3072]{1,0:T(8,128)(2,1)} %u0_ref.1), channel_id=1, source_target_pairs={{0,1},{1,0},{2,3},{3,2},{4,5},{5,4},{6,7},{7,6},{8,9},{9,8},{10,11... | collective-permute-start | bytes 2654216 | tf_op jit(solution)/shard_map/ppermute | solution.py:948
  57.8 8.6 %collective-permute-start.14 = (bf16[144,2048]{1,0:T(8,128)(2,1)}, bf16[144,2048]{1,0:T(8,128)(2,1)S(1)}, u32[]{:S(2)}, u32[]{:S(2)}) collective-permute-start(bf16[144,2048]{1,0:T(8,128)(2,1)} %pad.12.own0_ref), channel_id=1, source_target_pairs={{0,1},{1,0},{2,3},{3,2},{4,5},{5,4},{6,7},{7,6},{8,9},{9,8},{10,11... | collective-permute-start | bytes 1769480 | tf_op jit(solution)/shard_map/ppermute | solution.py:948
  59.1 17.4 %collective-permute-start.15 = (bf16[288,1152]{1,0:T(8,128)(2,1)S(1)}, bf16[288,1152]{1,0:T(8,128)(2,1)}, u32[]{:S(2)}, u32[]{:S(2)}) collective-permute-start(bf16[288,1152]{1,0:T(8,128)(2,1)S(1)} %pad_maximum_fusion.7), channel_id=1, source_target_pairs={{0,8},{8,0},{16,24},{24,16},{1,9},{9,1},{17,25},{25,17},{2,10},{10... | collective-permute-start | bytes 1990664 | tf_op jit(solution)/shard_map/ppermute | solution.py:940
  60.7 17.1 %collective-permute-start.16 = (bf16[288,1152]{1,0:T(8,128)(2,1)S(1)}, bf16[288,1152]{1,0:T(8,128)(2,1)}, u32[]{:S(2)}, u32[]{:S(2)}) collective-permute-start(bf16[288,1152]{1,0:T(8,128)(2,1)S(1)} %pad_maximum_fusion.7), channel_id=1, source_target_pairs={{0,16},{8,24},{16,0},{24,8},{1,17},{9,25},{17,1},{25,9},{2,18},{10... | collective-permute-start | bytes 1990664 | tf_op jit(solution)/shard_map/ppermute | solution.py:940
  77.8 19.0 %collective-permute-start.18 = (bf16[512,768]{1,0:T(8,128)(2,1)}, bf16[512,768]{1,0:T(8,128)(2,1)S(1)}, u32[]{:S(2)}, u32[]{:S(2)}) collective-permute-start(bf16[512,768]{1,0:T(8,128)(2,1)} %get-tuple-element.100), channel_id=1, source_target_pairs={{0,16},{8,24},{16,0},{24,8},{1,17},{9,25},{17,1},{25,9},{2,18},{10... | collective-permute-start | bytes 2359304 | tf_op jit(solution)/shard_map/ppermute | solution.py:940
  79.3 18.8 %collective-permute-start.17 = (bf16[512,768]{1,0:T(8,128)(2,1)}, bf16[512,768]{1,0:T(8,128)(2,1)S(1)}, u32[]{:S(2)}, u32[]{:S(2)}) collective-permute-start(bf16[512,768]{1,0:T(8,128)(2,1)} %get-tuple-element.100), channel_id=1, source_target_pairs={{0,8},{8,0},{16,24},{24,16},{1,9},{9,1},{17,25},{25,17},{2,10},{10... | collective-permute-start | bytes 2359304 | tf_op jit(solution)/shard_map/ppermute | solution.py:940
  83.3 37.8 %collective-permute-start.23 = (bf16[144,1920]{1,0:T(8,128)(2,1)S(1)}, bf16[144,1920]{1,0:T(8,128)(2,1)S(1)}, u32[]{:S(2)}, u32[]{:S(2)}) collective-permute-start(bf16[144,1920]{1,0:T(8,128)(2,1)S(1)} %pad_maximum_fusion.11), channel_id=1, source_target_pairs={{0,6},{1,7},{2,4},{3,5},{4,2},{5,3},{6,0},{7,1},{8,14},{9,15},{10,... | collective-permute-start | bytes 1658888 | tf_op jit(solution)/shard_map/ppermute | solution.py:944
  86.1 47.9 %collective-permute-start.22 = (bf16[144,1920]{1,0:T(8,128)(2,1)S(1)}, bf16[144,1920]{1,0:T(8,128)(2,1)S(1)}, u32[]{:S(2)}, u32[]{:S(2)}) collective-permute-start(bf16[144,1920]{1,0:T(8,128)(2,1)S(1)} %pad_maximum_fusion.11), channel_id=1, source_target_pairs={{0,4},{1,5},{2,6},{3,7},{4,0},{5,1},{6,2},{7,3},{8,12},{9,13},{10,... | collective-permute-start | bytes 1658888 | tf_op jit(solution)/shard_map/ppermute | solution.py:944
  88.6 45.4 %collective-permute-start.21 = (bf16[144,1920]{1,0:T(8,128)(2,1)S(1)}, bf16[144,1920]{1,0:T(8,128)(2,1)S(1)}, u32[]{:S(2)}, u32[]{:S(2)}) collective-permute-start(bf16[144,1920]{1,0:T(8,128)(2,1)S(1)} %pad_maximum_fusion.11), channel_id=1, source_target_pairs={{0,2},{1,3},{2,0},{3,1},{4,6},{5,7},{6,4},{7,5},{8,10},{9,11},{10,... | collective-permute-start | bytes 1658888 | tf_op jit(solution)/shard_map/ppermute | solution.py:944
  96.8 9.6 %collective-permute-start.19 = (bf16[256,768]{1,0:T(8,128)(2,1)S(1)}, bf16[256,768]{1,0:T(8,128)(2,1)S(1)}, u32[]{:S(2)}, u32[]{:S(2)}) collective-permute-start(bf16[256,768]{1,0:T(8,128)(2,1)S(1)} %slice.102), channel_id=1, source_target_pairs={{0,8},{8,0},{16,24},{24,16},{1,9},{9,1},{17,25},{25,17},{2,10},{10... | collective-permute-start | bytes 1179656 | tf_op jit(solution)/shard_map/ppermute | solution.py:940
  98.1 9.1 %collective-permute-start.20 = (bf16[256,768]{1,0:T(8,128)(2,1)S(1)}, bf16[256,768]{1,0:T(8,128)(2,1)S(1)}, u32[]{:S(2)}, u32[]{:S(2)}) collective-permute-start(bf16[256,768]{1,0:T(8,128)(2,1)S(1)} %slice.103), channel_id=1, source_target_pairs={{0,16},{8,24},{16,0},{24,8},{1,17},{9,25},{17,1},{25,9},{2,18},{10... | collective-permute-start | bytes 1179656 | tf_op jit(solution)/shard_map/ppermute | solution.py:940
  136.5 38.4 %collective-permute-start.24 = (bf16[432,1920]{1,0:T(8,128)(2,1)}, bf16[432,1920]{1,0:T(8,128)(2,1)S(1)}, u32[]{:S(2)}, u32[]{:S(2)}) collective-permute-start(bf16[432,1920]{1,0:T(8,128)(2,1)} %constant_dynamic-update-slice_fusion.8), channel_id=1, source_target_pairs={{0,8},{8,0},{16,24},{24,16},{1,9},{9,1},{17,25},{25,17},{2,10},{10... | collective-permute-start | bytes 4976648 | tf_op jit(solution)/shard_map/ppermute | solution.py:940
  137.9 38.1 %collective-permute-start.25 = (bf16[432,1920]{1,0:T(8,128)(2,1)}, bf16[432,1920]{1,0:T(8,128)(2,1)S(1)}, u32[]{:S(2)}, u32[]{:S(2)}) collective-permute-start(bf16[432,1920]{1,0:T(8,128)(2,1)} %constant_dynamic-update-slice_fusion.8), channel_id=1, source_target_pairs={{0,16},{8,24},{16,0},{24,8},{1,17},{9,25},{17,1},{25,9},{2,18},{10... | collective-permute-start | bytes 4976648 | tf_op jit(solution)/shard_map/ppermute | solution.py:940
  177.8 36.5 %collective-permute-start.26 = (bf16[3,3,144,1920]{3,2,1,0:T(8,128)(2,1)S(1)}, bf16[3,3,144,1920]{3,2,1,0:T(8,128)(2,1)S(1)}, u32[]{:S(2)}, u32[]{:S(2)}) collective-permute-start(bf16[3,3,144,1920]{3,2,1,0:T(8,128)(2,1)S(1)} %pad_maximum_fusion.near0_ref), channel_id=1, source_target_pairs={{0,1},{1,0},{2,3},{3,2},{4,5},{5,4},{6,7},{7,6},{8,9},{9,8},{10,11... | collective-permute-start | bytes 14929928 | tf_op jit(solution)/shard_map/ppermute | solution.py:948
  179.2 10.0 %collective-permute-start.30 = (bf16[144,1152]{1,0:T(8,128)(2,1)S(1)}, bf16[144,1152]{1,0:T(8,128)(2,1)S(1)}, u32[]{:S(2)}, u32[]{:S(2)}) collective-permute-start(bf16[144,1152]{1,0:T(8,128)(2,1)S(1)} %slice.84), channel_id=1, source_target_pairs={{0,8},{8,0},{16,24},{24,16},{1,9},{9,1},{17,25},{25,17},{2,10},{10... | collective-permute-start | bytes 995336 | tf_op jit(solution)/shard_map/ppermute | solution.py:940
  180.8 9.7 %collective-permute-start.31 = (bf16[144,1152]{1,0:T(8,128)(2,1)S(1)}, bf16[144,1152]{1,0:T(8,128)(2,1)S(1)}, u32[]{:S(2)}, u32[]{:S(2)}) collective-permute-start(bf16[144,1152]{1,0:T(8,128)(2,1)S(1)} %slice.85), channel_id=1, source_target_pairs={{0,16},{8,24},{16,0},{24,8},{1,17},{9,25},{17,1},{25,9},{2,18},{10... | collective-permute-start | bytes 995336 | tf_op jit(solution)/shard_map/ppermute | solution.py:940
  190.8 19.5 %collective-permute-start.28 = (bf16[216,1920]{1,0:T(8,128)(2,1)S(1)}, bf16[216,1920]{1,0:T(8,128)(2,1)S(1)}, u32[]{:S(2)}, u32[]{:S(2)}) collective-permute-start(bf16[216,1920]{1,0:T(8,128)(2,1)S(1)} %slice.83), channel_id=1, source_target_pairs={{0,16},{8,24},{16,0},{24,8},{1,17},{9,25},{17,1},{25,9},{2,18},{10... | collective-permute-start | bytes 2488328 | tf_op jit(solution)/shard_map/ppermute | solution.py:940
  191.3 19.2 %collective-permute-start.27 = (bf16[216,1920]{1,0:T(8,128)(2,1)S(1)}, bf16[216,1920]{1,0:T(8,128)(2,1)S(1)}, u32[]{:S(2)}, u32[]{:S(2)}) collective-permute-start(bf16[216,1920]{1,0:T(8,128)(2,1)S(1)} %slice.82), channel_id=1, source_target_pairs={{0,8},{8,0},{16,24},{24,16},{1,9},{9,1},{17,25},{25,17},{2,10},{10... | collective-permute-start | bytes 2488328 | tf_op jit(solution)/shard_map/ppermute | solution.py:940
  194.6 17.5 %collective-permute-start.32 = (bf16[4,3,96,1152]{3,2,1,0:T(8,128)(2,1)S(1)}, bf16[4,3,96,1152]{3,2,1,0:T(8,128)(2,1)S(1)}, u32[]{:S(2)}, u32[]{:S(2)}) collective-permute-start(bf16[4,3,96,1152]{3,2,1,0:T(8,128)(2,1)S(1)} %pad_maximum_fusion.1.d0_ref), channel_id=1, source_target_pairs={{0,1},{1,0},{2,3},{3,2},{4,5},{5,4},{6,7},{7,6},{8,9},{9,8},{10,11... | collective-permute-start | bytes 7962632 | tf_op jit(solution)/shard_map/ppermute | solution.py:948
  266.4 10.6 %collective-permute-start.34 = (bf16[4,512,768]{2,1,0:T(8,128)(2,1)}, bf16[4,512,768]{2,1,0:T(8,128)(2,1)S(1)}, u32[]{:S(2)}, u32[]{:S(2)}) collective-permute-start(bf16[4,512,768]{2,1,0:T(8,128)(2,1)} %get-tuple-element.117.g0_ref), channel_id=1, source_target_pairs={{0,1},{1,0},{2,3},{3,2},{4,5},{5,4},{6,7},{7,6},{8,9},{9,8},{10,11... | collective-permute-start | bytes 9437192 | tf_op jit(solution)/shard_map/ppermute | solution.py:948
  266.6 11.2 %collective-permute-start.35 = (bf16[4,512,768]{2,1,0:T(8,128)(2,1)}, bf16[4,512,768]{2,1,0:T(8,128)(2,1)}, u32[]{:S(2)}, u32[]{:S(2)}) collective-permute-start(bf16[4,512,768]{2,1,0:T(8,128)(2,1)} %get-tuple-element.118.u0_ref), channel_id=1, source_target_pairs={{0,1},{1,0},{2,3},{3,2},{4,5},{5,4},{6,7},{7,6},{8,9},{9,8},{10,11... | collective-permute-start | bytes 9437192 | tf_op jit(solution)/shard_map/ppermute | solution.py:948
  295.0 193.7 %reduce-scatter.3.cloned.1.call-start = ((), (), s32[]{:S(2)}) async-start(), calls=%async_computation.2 | async-start | bytes 7962624 | tf_op jit(solution)/shard_map/reduce_scatter | solution.py:1080
  305.4 49.6 %collective-permute-start.36 = (bf16[2,576,768]{2,1,0:T(8,128)(2,1)}, bf16[2,576,768]{2,1,0:T(8,128)(2,1)}, u32[]{:S(2)}, u32[]{:S(2)}) collective-permute-start(bf16[2,576,768]{2,1,0:T(8,128)(2,1)} %get-tuple-element.120), channel_id=1, source_target_pairs={{0,8},{8,0},{16,24},{24,16},{1,9},{9,1},{17,25},{25,17},{2,10},{10... | collective-permute-start | bytes 5308424 | tf_op jit(solution)/shard_map/ppermute | solution.py:940
  319.2 53.0 %collective-permute-start.38 = (bf16[2,576,768]{2,1,0:T(8,128)(2,1)}, bf16[2,576,768]{2,1,0:T(8,128)(2,1)S(1)}, u32[]{:S(2)}, u32[]{:S(2)}) collective-permute-start(bf16[2,576,768]{2,1,0:T(8,128)(2,1)} %get-tuple-element.127), channel_id=1, source_target_pairs={{0,16},{8,24},{16,0},{24,8},{1,17},{9,25},{17,1},{25,9},{2,18},{10... | collective-permute-start | bytes 5308424 | tf_op jit(solution)/shard_map/ppermute | solution.py:940
  350.3 45.7 %collective-permute-start.45 = (bf16[2,512,256]{2,1,0:T(8,128)(2,1)}, bf16[2,512,256]{2,1,0:T(8,128)(2,1)S(1)}, u32[]{:S(2)}, u32[]{:S(2)}) collective-permute-start(bf16[2,512,256]{2,1,0:T(8,128)(2,1)} %get-tuple-element.146), channel_id=1, source_target_pairs={{0,24},{8,16},{16,8},{24,0},{1,25},{9,17},{17,9},{25,1},{2,26},{10... | collective-permute-start | bytes 1572872 | tf_op jit(solution)/shard_map/ppermute | solution.py:940
  350.9 45.1 %collective-permute-start.44 = (bf16[2,512,256]{2,1,0:T(8,128)(2,1)}, bf16[2,512,256]{2,1,0:T(8,128)(2,1)}, u32[]{:S(2)}, u32[]{:S(2)}) collective-permute-start(bf16[2,512,256]{2,1,0:T(8,128)(2,1)} %get-tuple-element.144), channel_id=1, source_target_pairs={{0,16},{8,24},{16,0},{24,8},{1,17},{9,25},{17,1},{25,9},{2,18},{10... | collective-permute-start | bytes 1572872 | tf_op jit(solution)/shard_map/ppermute | solution.py:940
  352.4 43.6 %collective-permute-start.43 = (bf16[2,512,256]{2,1,0:T(8,128)(2,1)}, bf16[2,512,256]{2,1,0:T(8,128)(2,1)}, u32[]{:S(2)}, u32[]{:S(2)}) collective-permute-start(bf16[2,512,256]{2,1,0:T(8,128)(2,1)} %get-tuple-element.142), channel_id=1, source_target_pairs={{0,8},{8,0},{16,24},{24,16},{1,9},{9,1},{17,25},{25,17},{2,10},{10... | collective-permute-start | bytes 1572872 | tf_op jit(solution)/shard_map/ppermute | solution.py:940
  375.2 29.4 %collective-permute-start.37 = (bf16[576,768]{1,0:T(8,128)(2,1)}, bf16[576,768]{1,0:T(8,128)(2,1)}, u32[]{:S(2)}, u32[]{:S(2)}) collective-permute-start(bf16[576,768]{1,0:T(8,128)(2,1)} %fusion.2), channel_id=1, source_target_pairs={{0,16},{8,24},{16,0},{24,8},{1,17},{9,25},{17,1},{25,9},{2,18},{10... | collective-permute-start | bytes 2654216 | tf_op jit(solution)/shard_map/ppermute | solution.py:940
  377.5 27.1 %collective-permute-start.39 = (bf16[576,768]{1,0:T(8,128)(2,1)}, bf16[576,768]{1,0:T(8,128)(2,1)}, u32[]{:S(2)}, u32[]{:S(2)}) collective-permute-start(bf16[576,768]{1,0:T(8,128)(2,1)} %fusion.3), channel_id=1, source_target_pairs={{0,8},{8,0},{16,24},{24,16},{1,9},{9,1},{17,25},{25,17},{2,10},{10... | collective-permute-start | bytes 2654216 | tf_op jit(solution)/shard_map/ppermute | solution.py:940
  396.0 12.0 %collective-permute-start.40 = (bf16[2,512,128]{2,1,0:T(8,128)(2,1)S(1)}, bf16[2,512,128]{2,1,0:T(8,128)(2,1)S(1)}, u32[]{:S(2)}, u32[]{:S(2)}) collective-permute-start(bf16[2,512,128]{2,1,0:T(8,128)(2,1)S(1)} %copy-done.39), channel_id=1, source_target_pairs={{0,8},{8,0},{16,24},{24,16},{1,9},{9,1},{17,25},{25,17},{2,10},{10... | collective-permute-start | bytes 786440 | tf_op jit(solution)/shard_map/ppermute | solution.py:940
  397.6 15.0 %collective-permute-start.41 = (bf16[2,512,128]{2,1,0:T(8,128)(2,1)S(1)}, bf16[2,512,128]{2,1,0:T(8,128)(2,1)S(1)}, u32[]{:S(2)}, u32[]{:S(2)}) collective-permute-start(bf16[2,512,128]{2,1,0:T(8,128)(2,1)S(1)} %copy-done.38), channel_id=1, source_target_pairs={{0,16},{8,24},{16,0},{24,8},{1,17},{9,25},{17,1},{25,9},{2,18},{10... | collective-permute-start | bytes 786440 | tf_op jit(solution)/shard_map/ppermute | solution.py:940
  398.4 14.1 %collective-permute-start.42 = (bf16[2,512,128]{2,1,0:T(8,128)(2,1)S(1)}, bf16[2,512,128]{2,1,0:T(8,128)(2,1)S(1)}, u32[]{:S(2)}, u32[]{:S(2)}) collective-permute-start(bf16[2,512,128]{2,1,0:T(8,128)(2,1)S(1)} %copy-done.37), channel_id=1, source_target_pairs={{0,24},{8,16},{16,8},{24,0},{1,25},{9,17},{17,9},{25,1},{2,26},{10... | collective-permute-start | bytes 786440 | tf_op jit(solution)/shard_map/ppermute | solution.py:940
  423.4 8.2 %collective-permute-start.47 = (bf16[512,2048]{1,0:T(8,128)(2,1)}, bf16[512,2048]{1,0:T(8,128)(2,1)}, u32[]{:S(2)}, u32[]{:S(2)}) collective-permute-start(bf16[512,2048]{1,0:T(8,128)(2,1)} %get-tuple-element.150.r0_ref), channel_id=1, source_target_pairs={{0,1},{1,0},{2,3},{3,2},{4,5},{5,4},{6,7},{7,6},{8,9},{9,8},{10,11... | collective-permute-start | bytes 6291464 | tf_op jit(solution)/shard_map/ppermute | solution.py:948
  424.8 21.7 %collective-permute-start.49 = (bf16[2,144,768]{2,1,0:T(8,128)(2,1)S(1)}, bf16[2,144,768]{2,1,0:T(8,128)(2,1)}, u32[]{:S(2)}, u32[]{:S(2)}) collective-permute-start(bf16[2,144,768]{2,1,0:T(8,128)(2,1)S(1)} %pad_maximum_fusion.12), channel_id=1, source_target_pairs={{0,2},{1,3},{2,0},{3,1},{4,6},{5,7},{6,4},{7,5},{8,10},{9,11},{10,... | collective-permute-start | bytes 1327112 | tf_op jit(solution)/shard_map/ppermute | solution.py:944
  424.8 33.3 %collective-permute-start.50 = (bf16[2,144,768]{2,1,0:T(8,128)(2,1)S(1)}, bf16[2,144,768]{2,1,0:T(8,128)(2,1)}, u32[]{:S(2)}, u32[]{:S(2)}) collective-permute-start(bf16[2,144,768]{2,1,0:T(8,128)(2,1)S(1)} %pad_maximum_fusion.13), channel_id=1, source_target_pairs={{0,4},{1,5},{2,6},{3,7},{4,0},{5,1},{6,2},{7,3},{8,12},{9,13},{10,... | collective-permute-start | bytes 1327112 | tf_op jit(solution)/shard_map/ppermute | solution.py:944
  428.0 30.1 %collective-permute-start.51 = (bf16[2,144,768]{2,1,0:T(8,128)(2,1)S(1)}, bf16[2,144,768]{2,1,0:T(8,128)(2,1)}, u32[]{:S(2)}, u32[]{:S(2)}) collective-permute-start(bf16[2,144,768]{2,1,0:T(8,128)(2,1)S(1)} %pad_maximum_fusion.14), channel_id=1, source_target_pairs={{0,6},{1,7},{2,4},{3,5},{4,2},{5,3},{6,0},{7,1},{8,14},{9,15},{10,... | collective-permute-start | bytes 1327112 | tf_op jit(solution)/shard_map/ppermute | solution.py:944
  439.3 22.1 %collective-permute-start.52 = (bf16[576,512]{1,0:T(8,128)(2,1)}, bf16[576,512]{1,0:T(8,128)(2,1)S(1)}, u32[]{:S(2)}, u32[]{:S(2)}) collective-permute-start(bf16[576,512]{1,0:T(8,128)(2,1)} %get-tuple-element.158), channel_id=1, source_target_pairs={{0,8},{8,0},{16,24},{24,16},{1,9},{9,1},{17,25},{25,17},{2,10},{10... | collective-permute-start | bytes 1769480 | tf_op jit(solution)/shard_map/ppermute | solution.py:940
  439.7 23.5 %collective-permute-start.53 = (bf16[576,512]{1,0:T(8,128)(2,1)}, bf16[576,512]{1,0:T(8,128)(2,1)S(1)}, u32[]{:S(2)}, u32[]{:S(2)}) collective-permute-start(bf16[576,512]{1,0:T(8,128)(2,1)} %get-tuple-element.160), channel_id=1, source_target_pairs={{0,16},{8,24},{16,0},{24,8},{1,17},{9,25},{17,1},{25,9},{2,18},{10... | collective-permute-start | bytes 1769480 | tf_op jit(solution)/shard_map/ppermute | solution.py:940
  446.5 22.5 %collective-permute-start.54 = (bf16[576,512]{1,0:T(8,128)(2,1)}, bf16[576,512]{1,0:T(8,128)(2,1)S(1)}, u32[]{:S(2)}, u32[]{:S(2)}) collective-permute-start(bf16[576,512]{1,0:T(8,128)(2,1)} %get-tuple-element.162), channel_id=1, source_target_pairs={{0,24},{8,16},{16,8},{24,0},{1,25},{9,17},{17,9},{25,1},{2,26},{10... | collective-permute-start | bytes 1769480 | tf_op jit(solution)/shard_map/ppermute | solution.py:940
  459.5 18.3 %collective-permute-start.63 = (bf16[2,144,768]{2,1,0:T(8,128)(2,1)S(1)}, bf16[2,144,768]{2,1,0:T(8,128)(2,1)S(1)}, u32[]{:S(2)}, u32[]{:S(2)}) collective-permute-start(bf16[2,144,768]{2,1,0:T(8,128)(2,1)S(1)} %fusion.4), channel_id=1, source_target_pairs={{0,8},{8,0},{16,24},{24,16},{1,9},{9,1},{17,25},{25,17},{2,10},{10... | collective-permute-start | bytes 1327112 | tf_op jit(solution)/shard_map/ppermute | solution.py:940
  460.0 19.9 %collective-permute-start.64 = (bf16[2,144,768]{2,1,0:T(8,128)(2,1)S(1)}, bf16[2,144,768]{2,1,0:T(8,128)(2,1)S(1)}, u32[]{:S(2)}, u32[]{:S(2)}) collective-permute-start(bf16[2,144,768]{2,1,0:T(8,128)(2,1)S(1)} %fusion.4), channel_id=1, source_target_pairs={{0,16},{8,24},{16,0},{24,8},{1,17},{9,25},{17,1},{25,9},{2,18},{10... | collective-permute-start | bytes 1327112 | tf_op jit(solution)/shard_map/ppermute | solution.py:940
  461.4 25.7 %collective-permute-start.65 = (bf16[2,144,768]{2,1,0:T(8,128)(2,1)S(1)}, bf16[2,144,768]{2,1,0:T(8,128)(2,1)S(1)}, u32[]{:S(2)}, u32[]{:S(2)}) collective-permute-start(bf16[2,144,768]{2,1,0:T(8,128)(2,1)S(1)} %fusion.4), channel_id=1, source_target_pairs={{0,24},{8,16},{16,8},{24,0},{1,25},{9,17},{17,9},{25,1},{2,26},{10... | collective-permute-start | bytes 1327112 | tf_op jit(solution)/shard_map/ppermute | solution.py:940
  469.3 21.6 %collective-permute-start.55 = (bf16[144,512]{1,0:T(8,128)(2,1)S(1)}, bf16[144,512]{1,0:T(8,128)(2,1)S(1)}, u32[]{:S(2)}, u32[]{:S(2)}) collective-permute-start(bf16[144,512]{1,0:T(8,128)(2,1)S(1)} %get-tuple-element.185), channel_id=1, source_target_pairs={{0,2},{1,3},{2,0},{3,1},{4,6},{5,7},{6,4},{7,5},{8,10},{9,11},{10,... | collective-permute-start | bytes 442376 | tf_op jit(solution)/shard_map/ppermute | solution.py:944
  473.0 17.9 %collective-permute-start.56 = (bf16[144,512]{1,0:T(8,128)(2,1)S(1)}, bf16[144,512]{1,0:T(8,128)(2,1)S(1)}, u32[]{:S(2)}, u32[]{:S(2)}) collective-permute-start(bf16[144,512]{1,0:T(8,128)(2,1)S(1)} %get-tuple-element.187), channel_id=1, source_target_pairs={{0,4},{1,5},{2,6},{3,7},{4,0},{5,1},{6,2},{7,3},{8,12},{9,13},{10,... | collective-permute-start | bytes 442376 | tf_op jit(solution)/shard_map/ppermute | solution.py:944
  477.9 13.1 %collective-permute-start.57 = (bf16[144,512]{1,0:T(8,128)(2,1)S(1)}, bf16[144,512]{1,0:T(8,128)(2,1)S(1)}, u32[]{:S(2)}, u32[]{:S(2)}) collective-permute-start(bf16[144,512]{1,0:T(8,128)(2,1)S(1)} %get-tuple-element.186), channel_id=1, source_target_pairs={{0,6},{1,7},{2,4},{3,5},{4,2},{5,3},{6,0},{7,1},{8,14},{9,15},{10,... | collective-permute-start | bytes 442376 | tf_op jit(solution)/shard_map/ppermute | solution.py:944
  489.8 28.8 %collective-permute-start.66 = (bf16[256,1152]{1,0:T(8,128)(2,1)S(1)}, bf16[256,1152]{1,0:T(8,128)(2,1)S(1)}, u32[]{:S(2)}, u32[]{:S(2)}) collective-permute-start(bf16[256,1152]{1,0:T(8,128)(2,1)S(1)} %slice.98), channel_id=1, source_target_pairs={{0,8},{8,0},{16,24},{24,16},{1,9},{9,1},{17,25},{25,17},{2,10},{10... | collective-permute-start | bytes 1769480 | tf_op jit(solution)/shard_map/ppermute | solution.py:940
  492.2 16.9 %collective-permute-start.58 = (bf16[144,512]{1,0:T(8,128)(2,1)S(1)}, bf16[144,512]{1,0:T(8,128)(2,1)S(1)}, u32[]{:S(2)}, u32[]{:S(2)}) collective-permute-start(bf16[144,512]{1,0:T(8,128)(2,1)S(1)} %add_convert_fusion.2), channel_id=1, source_target_pairs={{0,8},{8,0},{16,24},{24,16},{1,9},{9,1},{17,25},{25,17},{2,10},{10... | collective-permute-start | bytes 442376 | tf_op jit(solution)/shard_map/ppermute | solution.py:940
  493.3 15.8 %collective-permute-start.59 = (bf16[144,512]{1,0:T(8,128)(2,1)S(1)}, bf16[144,512]{1,0:T(8,128)(2,1)S(1)}, u32[]{:S(2)}, u32[]{:S(2)}) collective-permute-start(bf16[144,512]{1,0:T(8,128)(2,1)S(1)} %add_convert_fusion.2), channel_id=1, source_target_pairs={{0,16},{8,24},{16,0},{24,8},{1,17},{9,25},{17,1},{25,9},{2,18},{10... | collective-permute-start | bytes 442376 | tf_op jit(solution)/shard_map/ppermute | solution.py:940
  494.1 16.9 %collective-permute-start.60 = (bf16[144,512]{1,0:T(8,128)(2,1)S(1)}, bf16[144,512]{1,0:T(8,128)(2,1)S(1)}, u32[]{:S(2)}, u32[]{:S(2)}) collective-permute-start(bf16[144,512]{1,0:T(8,128)(2,1)S(1)} %add_convert_fusion.2), channel_id=1, source_target_pairs={{0,24},{8,16},{16,8},{24,0},{1,25},{9,17},{17,9},{25,1},{2,26},{10... | collective-permute-start | bytes 442376 | tf_op jit(solution)/shard_map/ppermute | solution.py:940
  495.8 24.3 %collective-permute-start.61 = (bf16[272,1152]{1,0:T(8,128)(2,1)S(1)}, bf16[272,1152]{1,0:T(8,128)(2,1)S(1)}, u32[]{:S(2)}, u32[]{:S(2)}) collective-permute-start(bf16[272,1152]{1,0:T(8,128)(2,1)S(1)} %pad_maximum_fusion.9), channel_id=1, source_target_pairs={{0,16},{8,24},{16,0},{24,8},{1,17},{9,25},{17,1},{25,9},{2,18},{10... | collective-permute-start | bytes 1880072 | tf_op jit(solution)/shard_map/ppermute | solution.py:940
  518.7 13.2 %collective-permute-start.67 = (bf16[256,1152]{1,0:T(8,128)(2,1)S(1)}, bf16[256,1152]{1,0:T(8,128)(2,1)S(1)}, u32[]{:S(2)}, u32[]{:S(2)}) collective-permute-start(bf16[256,1152]{1,0:T(8,128)(2,1)S(1)} %fusion.1), channel_id=1, source_target_pairs={{0,16},{8,24},{16,0},{24,8},{1,17},{9,25},{17,1},{25,9},{2,18},{10... | collective-permute-start | bytes 1769480 | tf_op jit(solution)/shard_map/ppermute | solution.py:940
  520.3 14.4 %collective-permute-start.62 = (bf16[272,1152]{1,0:T(8,128)(2,1)S(1)}, bf16[272,1152]{1,0:T(8,128)(2,1)S(1)}, u32[]{:S(2)}, u32[]{:S(2)}) collective-permute-start(bf16[272,1152]{1,0:T(8,128)(2,1)S(1)} %fusion), channel_id=1, source_target_pairs={{0,8},{8,0},{16,24},{24,16},{1,9},{9,1},{17,25},{25,17},{2,10},{10... | collective-permute-start | bytes 1880072 | tf_op jit(solution)/shard_map/ppermute | solution.py:940
  (47 other events, 386.8 us)
Sparse Core Ops, SparseCore 0:
  295.1 38.0 reduce-scatter.4
  335.5 76.2 reduce-scatter.2

commit v3 on v2

--- a/solution.py
+++ b/solution.py
@@ -303,7 +303,7 @@
     for n, (w, own) in enumerate(((w0_ref, own0_ref), (w1_ref, own1_ref))):
         other = core if n == 0 else 1 - core
         row = pl.multiple_of((2 * z + other) * cut, 16)
-        copies.append((own, w_ref.at[pl.ds(row, cut), :]))
+        copies.append((own.at[:, pl.ds(0, parts * width)], w_ref.at[pl.ds(row, cut), :]))
         for k, far in enumerate(far_lines(z)):
             row = pl.multiple_of((2 * far + other) * cut, 16)
             for r in range(parts):
@@ -336,7 +336,7 @@
 
 def qkv_project(where, x, cosine, sine, w, own):
     rows, model = x.shape
-    width = own[0].shape[1]
+    width = 4 * w[0].shape[3]
     low = jnp.bfloat16
     return pl.pallas_call(
         qkv_kernel,
@@ -468,9 +468,9 @@
 
 
 def attend_back_kernel(
-    own_ref, slot_ref, q_ref, k_ref, v_ref, do_ref, o_ref, lse_ref, cos_ref, sin_ref,
-    dq_ref, dkv0_ref, dkv1_ref, dkv2_ref, dkv3_ref, dk_scr, dv_scr, q_scr, do_scr, st_scr, a_scr,
+    own_ref, slot_ref, where_ref, q_ref, k_ref, v_ref, do_ref, o_ref, lse_ref, cos_ref, sin_ref, *refs
 ):
+    dq_ref, dkv_ref, dk_scr, dv_scr, q_scr, do_scr, st_scr, a_scr = refs[-8:]
     rows = RATIO * BLK
     length = v_ref.shape[0]
     pairs = length // BLK + 1
@@ -510,24 +510,25 @@
         for b, part in enumerate(join_heads(outs[j])):
             dq_ref[span, pl.ds(b * WIDE, WIDE)] = turn(part, cos_ref[span, :], -sin_ref[span, :]).astype(jnp.bfloat16)
     own_rows = length // 4
-    for r, ref in enumerate((dkv0_ref, dkv1_ref, dkv2_ref, dkv3_ref)):
-        for n, scr in enumerate((dk_scr, dv_scr)):
-            ref[n] = scr[pl.ds(r * own_rows, own_rows), :].astype(jnp.bfloat16)
-
-
-def attend_back(own, slots, q, kv, grads, mixed, lse, cosine, sine, start, count):
+    for n, (scr, order) in enumerate(((dk_scr, (1, 3, 0, 2)), (dv_scr, (2, 3, 0, 1)))):
+        for i, r in enumerate(order):
+            dkv_ref[n, i] = scr[pl.ds(r * own_rows, own_rows), :].astype(jnp.bfloat16)
+
+
+def attend_back(own, slots, where, q, kv, grads, mixed, lse, cosine, sine, start, count, into=None):
     rows, length = q.shape[0], kv.shape[0]
     nblk = length // BLK
     work = rows * length * H * (nblk + 1) // (2 * nblk) * count // (KVH // 2)
     wide = pl.BlockSpec((rows, PAIR), lambda p, *_: (0, p))
     shifted = pl.BlockSpec((rows, PAIR), lambda p, *_: (0, p + start))
     whole = pl.BlockSpec((rows, WIDE), lambda p, *_: (0, 0))
-    part = pl.BlockSpec((2, length // 4, WIDE), lambda p, *_: (0, 0, p))
-    part_shape = jax.ShapeDtypeStruct((2, length // 4, WIDE * count), jnp.bfloat16)
+    part = pl.BlockSpec((2, 4, length // 4, WIDE), lambda p, *_: (0, 0, 0, p + start))
+    part_shape = jax.ShapeDtypeStruct((2, 4, length // 4, KVH * HD), jnp.bfloat16)
+    more = [] if into is None else [into]
     return pl.pallas_call(
         attend_back_kernel,
         grid_spec=pltpu.PrefetchScalarGridSpec(
-            num_scalar_prefetch=2,
+            num_scalar_prefetch=3,
             grid=(count,),
             in_specs=[
                 shifted,
@@ -538,8 +539,9 @@
                 pl.BlockSpec((2, 2, 1, RATIO * BLK), lambda p, *_: (p, 0, 0, 0)),
                 whole,
                 whole,
-            ],
-            out_specs=[wide] + [part] * 4,
+            ]
+            + [HBM] * len(more),
+            out_specs=[wide, part],
             scratch_shapes=[
                 pltpu.VMEM((length, WIDE), jnp.float32),
                 pltpu.VMEM((length, WIDE), jnp.float32),
@@ -549,28 +551,30 @@
                 pltpu.VMEM((2, RATIO * BLK, WIDE), jnp.float32),
             ],
         ),
-        out_shape=[jax.ShapeDtypeStruct((rows, PAIR * count), jnp.bfloat16)] + [part_shape] * 4,
+        out_shape=[jax.ShapeDtypeStruct((rows, PAIR * count), jnp.bfloat16), part_shape],
+        input_output_aliases={} if into is None else {11: 1},
         compiler_params=ROOM,
-        cost_estimate=cost(10 * 8 * work * HD, 8 * rows * PAIR * count + 8 * length * WIDE * count, work),
+        cost_estimate=cost(1000, 1000) if into is None else cost(80 * work * HD, 8 * rows * PAIR * count + 8 * length * WIDE * count, work),
         name="attend_back",
-    )(own, slots, q, kv, kv, grads, mixed, lse, cosine, sine)
+    )(own, slots, where, q, kv, kv, grads, mixed, lse, cosine, sine, *more)
 
 
 def middle_kernel(
     at_ref, ho_ref, x_ref, dy_ref, gain_ref,
-    near0_ref, near1_ref, far0_ref, far1_ref, d0_ref, d1_ref,
-    g0_ref, g1_ref, u0_ref, u1_ref, o0_ref, o1_ref, down0_ref, down1_ref,
-    out_ref, hot_ref, bt_ref, ht_ref, dg_ref, du_ref, dr_ref, low_ref, dh_ref, gg_ref,
-    gu_scr, d_scr, wo_ref, r_scr, b_scr, acc_scr, db_scr, h_scr, gu_sem, o_sem, d_sem,
+    near0_ref, near1_ref, far0_ref, far1_ref, p0_ref, p1_ref, o0_ref, o1_ref, all0_ref, all1_ref, down0_ref, down1_ref,
+    out_ref, go_ref, bt_ref, gd_ref, gs_ref, gk_ref, us_ref, uk_ref, dr_ref, dh_ref, gg_ref,
+    gu_scr, d_scr, wo_ref, r_scr, b_scr, acc_scr, db_scr, h_scr, dg_ref, du_ref, gu_sem, o_sem, d_sem,
 ):
     r = pl.program_id(0)
     count = pl.num_programs(0)
     t, core, z = at_ref[0], at_ref[1], at_ref[2]
-    lines, cut, cut_d = near0_ref.shape[1], near0_ref.shape[2], d0_ref.shape[2]
-    width = dg_ref.shape[2]
-    parts = near0_ref.shape[0] + 1
-    o_width = near0_ref.shape[3] - 2 * width
-    o_parts = wo_ref.shape[1] // o_width
+    parts, lines, cut = p0_ref.shape[:3]
+    width = dg_ref.shape[1]
+    model = wo_ref.shape[1]
+    third = width // 2
+    cut_d = down0_ref.shape[0] // parts
+    first_g = all0_ref.shape[1] - model - 2 * parts * width
+    alls, ps = (all0_ref, all1_ref), (p0_ref, p1_ref)
     cores = (core, 1 - core)
     others = far_lines(z)
 
@@ -581,67 +585,59 @@
     def gu_copies(part, slot):
         out = []
         for n, other in enumerate(cores):
-            columns = pl.ds(pl.multiple_of((t ^ part) * width, WIDE), width)
             rows = pl.ds(pl.multiple_of((2 * z + other) * cut, 16), cut)
-            for m, ref in enumerate(((g0_ref, u0_ref), (g1_ref, u1_ref))[n]):
-                out.append((ref.at[:, columns], gu_scr.at[slot, m, rows, :]))
+            for m in range(2):
+                column = pl.multiple_of(first_g + (m * parts + (t ^ part)) * width, WIDE)
+                out.append((alls[n].at[:, pl.ds(column, width)], gu_scr.at[slot, m, rows, :]))
             for k in range(lines):
                 rows = pl.ds(pl.multiple_of((2 * others[k] + other) * cut, 16), cut)
                 for m in range(2):
                     out.append((piece(n, part, k).at[:, pl.ds(m * width, width)], gu_scr.at[slot, m, rows, :]))
         return [pltpu.make_async_copy(src, dst, gu_sem.at[slot, i]) for i, (src, dst) in enumerate(out)]
 
-    def o_copies(part):
+    def o_copies():
         out = []
-        columns = pl.ds(pl.multiple_of((t ^ part) * o_width, WIDE), o_width)
         for n, other in enumerate(cores):
-            for k in range(lines):
-                rows = pl.ds(pl.multiple_of((2 * others[k] + other) * cut, 16), cut)
-                out.append((piece(n, part, k).at[:, pl.ds(2 * width, o_width)], wo_ref.at[rows, columns]))
-        return [pltpu.make_async_copy(src, dst, o_sem.at[part, i]) for i, (src, dst) in enumerate(out)]
+            for line in range(lines + 1):
+                rows = pl.ds(pl.multiple_of((2 * line + other) * cut, 16), cut)
+                out.append(((o0_ref, o1_ref)[n].at[line], wo_ref.at[rows, :]))
+        return [pltpu.make_async_copy(src, dst, o_sem.at[i]) for i, (src, dst) in enumerate(out)]
 
     def d_copies():
         out = []
         for n, other in enumerate(cores):
-            d, down, o = ((d0_ref, down0_ref, o0_ref), (d1_ref, down1_ref, o1_ref))[n]
-            shard = 2 * z + other
-            out.append((down, d_scr.at[pl.ds(pl.multiple_of(shard * parts * cut_d, 16), parts * cut_d), :]))
-            out.append((o, wo_ref.at[pl.ds(pl.multiple_of(shard * cut, 16), cut), :]))
+            row = pl.multiple_of((2 * z + other) * parts * cut_d, 16)
+            out.append(((down0_ref, down1_ref)[n], d_scr.at[pl.ds(row, parts * cut_d), :]))
             for k in range(lines):
                 for part in range(parts):
                     row = pl.multiple_of(((2 * others[k] + other) * parts + (t ^ part)) * cut_d, 16)
-                    out.append((d.at[part, k], d_scr.at[pl.ds(row, cut_d), :]))
+                    p = ps[n].at[part, k]
+                    out.append((p.at[pl.ds(0, cut_d), :], d_scr.at[pl.ds(row, cut_d), pl.ds(0, width)]))
+                    for m in range(2):
+                        src = p.at[pl.ds(cut_d, cut_d // 2), pl.ds(m * third, third)]
+                        row_m = pl.multiple_of(row + m * (cut_d // 2), 16)
+                        out.append((src, d_scr.at[pl.ds(row_m, cut_d // 2), pl.ds(width, third)]))
         return [pltpu.make_async_copy(src, dst, d_sem.at[i]) for i, (src, dst) in enumerate(out)]
 
     slot = lax.rem(r, 2)
 
     @pl.when(r == 0)
     def _():
-        for part in range(parts):
-
-            @pl.when(t ^ part < o_parts)
-            def _():
-                for c in o_copies(part):
-                    c.start()
-
-        for c in d_copies() + gu_copies(0, 0):
+        for c in o_copies():
             c.start()
-        for part in range(parts):
-
-            @pl.when(t ^ part < o_parts)
-            def _():
-                for c in o_copies(part):
-                    c.wait()
-
-        for c in d_copies():
+        for c in gu_copies(0, 0) + d_copies():
+            c.start()
+        for c in o_copies():
             c.wait()
         resid = x_ref[...].astype(jnp.float32) + mm(ho_ref[...], wo_ref[...], NN)
         r_scr[...] = resid
         inv = lax.rsqrt(jnp.mean(resid * resid, -1, keepdims=True) + EPS)
         b = (resid * inv * gain_ref[1:2]).astype(jnp.bfloat16)
         b_scr[...] = b
-        bt_ref[...] = jnp.transpose(b)
-        hot_ref[...] = jnp.transpose(ho_ref[...])
+        turned = jnp.transpose(b)
+        for shard in range(2 * (lines + 1)):
+            rows = slice(shard * cut, (shard + 1) * cut)
+            bt_ref[lax.rem(shard + core, 2), shard // 2 * cut : (shard // 2 + 1) * cut] = turned[rows]
 
     for part in range(parts):
 
@@ -649,6 +645,9 @@
         def _():
             for c in gu_copies(part, part % 2):
                 c.wait()
+            if part == 0:
+                for c in d_copies():
+                    c.wait()
             if part + 1 < parts:
                 for c in gu_copies(part + 1, (part + 1) % 2):
                     c.start()
@@ -663,14 +662,20 @@
         silu = gate * sig
         hidden = (silu * up).astype(jnp.bfloat16)
         h_scr[:, span] = hidden
-        ht_ref[0, span, :] = jnp.transpose(hidden)
-        dg_ref[0, :, span] = (dhid * up * sig * (1.0 + gate * (1.0 - sig))).astype(jnp.bfloat16)
-        du_ref[0, :, span] = (dhid * silu).astype(jnp.bfloat16)
-    model = acc_scr.shape[1]
-    for at in range(0, model, 384):
-        span = slice(at, at + 384)
+        dg_ref[:, span] = (dhid * up * sig * (1.0 + gate * (1.0 - sig))).astype(jnp.bfloat16)
+        du_ref[:, span] = (dhid * silu).astype(jnp.bfloat16)
+    for n, (g_ref, u_ref) in enumerate(((gk_ref, uk_ref), (gs_ref, uk_ref), (gk_ref, us_ref), (gs_ref, us_ref))):
+
+        @pl.when(r == n)
+        def _():
+            g_ref[0] = dg_ref[...]
+            u_ref[0] = du_ref[...]
+
+    gd_ref[0] = mm(h_scr[...], dy_ref[...], TN).astype(jnp.bfloat16)
+    for at in range(0, model, 1152):
+        span = slice(at, at + 1152)
         acc = mm(h_scr[...], d_scr[pl.ds(down, width), span], NN)
-        db = mm(dg_ref[0], gu_scr[slot, 0, span, :], NT) + mm(du_ref[0], gu_scr[slot, 1, span, :], NT)
+        db = mm(dg_ref[...], gu_scr[slot, 0, span, :], NT) + mm(du_ref[...], gu_scr[slot, 1, span, :], NT)
 
         @pl.when(r == 0)
         def _():
@@ -697,29 +702,30 @@
         )
         dr_ref[...] = dr
         low = dr.astype(jnp.bfloat16)
-        low_ref[...] = low
+        go_ref[...] = mm(ho_ref[...], low, TN).astype(jnp.bfloat16)
         dh_ref[...] = mm(low, wo_ref[...], NT).astype(jnp.bfloat16)
 
 
-def middle(where, ho, x, dy, gains, near, far, d, own_g, own_u, own_o, own_d):
+def middle(where, ho, x, dy, gains, near, far, p, o, own_all, own_d):
     rows, model = x.shape
     lines, cut = near[0].shape[1:3]
     count = near[0].shape[0] + 1
-    width = own_g[0].shape[1] // count
+    width = near[0].shape[3] // 2
     once = pl.Buffered(1)
     whole = lambda shape: pl.BlockSpec(shape, lambda r, *_: (0,) * len(shape), pipeline_mode=once)
-    act = pl.BlockSpec((1, rows, width), lambda r, *_: (r, 0, 0))
+    act = lambda at: pl.BlockSpec((1, rows, width), lambda r, *_: (at(r), 0, 0))
     low = jnp.bfloat16
     return pl.pallas_call(
         middle_kernel,
         grid_spec=pltpu.PrefetchScalarGridSpec(
             num_scalar_prefetch=1,
             grid=(count,),
-            in_specs=[whole((rows, H * HD)), whole((rows, model)), whole((rows, model)), whole((8, model))] + [HBM] * 14,
+            in_specs=[whole((rows, H * HD)), whole((rows, model)), whole((rows, model)), whole((8, model))] + [HBM] * 12,
             out_specs=[
-                whole((rows, model)), whole((H * HD, rows)), whole((model, rows)),
-                pl.BlockSpec((1, width, rows), lambda r, at_ref: (at_ref[0] ^ r, 0, 0)), act, act,
-                whole((rows, model)), whole((rows, model)), whole((rows, H * HD)), whole((1, model)),
+                whole((rows, model)), whole((H * HD, model)), whole((2, model // 2, rows)),
+                pl.BlockSpec((1, width, model), lambda r, at_ref: (at_ref[0] ^ r, 0, 0)),
+                act(lambda r: r // 3), act(lambda r: r // 2), act(lambda r: r // 3), act(lambda r: (r + 2) // 3),
+                whole((rows, model)), whole((rows, H * HD)), whole((1, model)),
             ],
             scratch_shapes=[
                 pltpu.VMEM((2, 2, 2 * (lines + 1) * cut, width), low),
@@ -730,46 +736,62 @@
                 pltpu.VMEM((rows, model), jnp.float32),
                 pltpu.VMEM((rows, model), jnp.float32),
                 pltpu.VMEM((rows, width), low),
+                pltpu.VMEM((rows, width), low),
+                pltpu.VMEM((rows, width), low),
                 pltpu.SemaphoreType.DMA((2, 4 * (lines + 1))),
-                pltpu.SemaphoreType.DMA((count, 2 * lines)),
-                pltpu.SemaphoreType.DMA((4 + 2 * count * lines,)),
+                pltpu.SemaphoreType.DMA((2 * (lines + 1),)),
+                pltpu.SemaphoreType.DMA((2 + 6 * count * lines,)),
             ],
         ),
         out_shape=[
             jax.ShapeDtypeStruct((rows, model), low),
-            jax.ShapeDtypeStruct((H * HD, rows), low),
-            jax.ShapeDtypeStruct((model, rows), low),
-            jax.ShapeDtypeStruct((count, width, rows), low),
-            jax.ShapeDtypeStruct((count, rows, width), low),
-            jax.ShapeDtypeStruct((count, rows, width), low),
+            jax.ShapeDtypeStruct((H * HD, model), low),
+            jax.ShapeDtypeStruct((2, model // 2, rows), low),
+            jax.ShapeDtypeStruct((count, width, model), low),
+            *[jax.ShapeDtypeStruct((2, rows, width), low)] * 4,
             jax.ShapeDtypeStruct((rows, model), jnp.float32),
-            jax.ShapeDtypeStruct((rows, model), low),
             jax.ShapeDtypeStruct((rows, H * HD), low),
             jax.ShapeDtypeStruct((1, model), jnp.float32),
         ],
         compiler_params=ROOM,
         cost_estimate=cost(12 * rows * model * width * count + 4 * rows * model * model, 2 * 16 * rows * model + 6 * count * width * model, rows * width * count),
         name="middle",
-    )(where, ho, x, dy, gains, *near, *far, *d, *own_g, *own_u, *own_o, *own_d)
-
-
-def last_kernel(counts, x_ref, gain_ref, dr_ref, w_ref, cos_ref, sin_ref, *refs):
-    gx_ref, act_ref, gg_ref = refs[-3:]
+    )(where, ho, x, dy, gains, *near, *far, *p, *o, *own_all, *own_d)
+
+
+def act_kernel(counts, cos_ref, sin_ref, dkv_ref, gx_ref, lasty_ref, gy_ref, lastx_ref, *refs):
+    act_ref = refs[-1]
     half = KVH * HD
     at = 0
-    for n, count in enumerate(counts):
-        dq_ref, shares = refs[5 * n], refs[5 * n + 1 : 5 * n + 5]
+    for dq_ref, count in zip(refs, counts):
         act_ref[:, at * PAIR : (at + count) * PAIR] = dq_ref[...]
-        for p in range(count):
-            span = slice(p * WIDE, (p + 1) * WIDE)
-            dk = sum(share[0, :, span].astype(jnp.float32) for share in shares)
-            dv = sum(share[1, :, span].astype(jnp.float32) for share in shares)
-            column = H * HD + (at + p) * WIDE
-            act_ref[:, column : column + WIDE] = turn(dk, cos_ref[...], -sin_ref[...]).astype(jnp.bfloat16)
-            act_ref[:, column + half : column + half + WIDE] = dv.astype(jnp.bfloat16)
         at += count
-    act_ref[:, H * HD + 2 * half :] = jnp.zeros((x_ref.shape[0], act_ref.shape[1] - H * HD - 2 * half), jnp.bfloat16)
-    da = mm(act_ref[:, 0 : H * HD + 2 * half], w_ref[:, 0 : H * HD + 2 * half], NT)
+    for p in range(at):
+        span = slice(p * WIDE, (p + 1) * WIDE)
+        dk = sum(v.astype(jnp.float32) for v in (dkv_ref[0, 2, :, span], gx_ref[0, :, span], lasty_ref[:, span]))
+        dv = sum(v.astype(jnp.float32) for v in (dkv_ref[1, 2, :, span], gy_ref[0, :, span], lastx_ref[:, span]))
+        column = H * HD + p * WIDE
+        act_ref[:, column : column + WIDE] = turn(dk, cos_ref[...], -sin_ref[...]).astype(jnp.bfloat16)
+        act_ref[:, column + half : column + half + WIDE] = dv.astype(jnp.bfloat16)
+    act_ref[:, H * HD + 2 * half :] = jnp.zeros((act_ref.shape[0], act_ref.shape[1] - H * HD - 2 * half), jnp.bfloat16)
+
+
+def make_act(cosine, sine, shares, parts, counts, width):
+    rows = cosine.shape[0]
+    return pl.pallas_call(
+        functools.partial(act_kernel, counts),
+        in_specs=[VMEM] * (7 + len(parts)),
+        out_specs=VMEM,
+        out_shape=jax.ShapeDtypeStruct((rows, width), jnp.bfloat16),
+        compiler_params=ROOM,
+        cost_estimate=cost(10 * rows * width, 6 * rows * width),
+        name="make_act",
+    )(cosine, sine, *shares, *parts)
+
+
+def last_kernel(x_ref, gain_ref, dr_ref, w_ref, act_ref, gx_ref, gg_ref):
+    used = (H + 2 * KVH) * HD
+    da = mm(act_ref[:, 0:used], w_ref[:, 0:used], NT)
     x = x_ref[...].astype(jnp.float32)
     inv = lax.rsqrt(jnp.mean(x * x, -1, keepdims=True) + EPS)
     gg_ref[...] = jnp.sum(da * x * inv, 0, keepdims=True)
@@ -778,22 +800,17 @@
     gx_ref[...] = gx.astype(jnp.bfloat16)
 
 
-def last(x, gains, dr, w_qkv, cosine, sine, parts, counts):
+def last(x, gains, dr, w_qkv, act):
     rows, model = x.shape
-    padded = w_qkv.shape[1]
     return pl.pallas_call(
-        functools.partial(last_kernel, counts),
-        in_specs=[VMEM] * (6 + len(parts)),
-        out_specs=[VMEM] * 3,
-        out_shape=[
-            jax.ShapeDtypeStruct((rows, model), jnp.bfloat16),
-            jax.ShapeDtypeStruct((rows, padded), jnp.bfloat16),
-            jax.ShapeDtypeStruct((1, model), jnp.float32),
-        ],
+        last_kernel,
+        in_specs=[VMEM] * 5,
+        out_specs=[VMEM] * 2,
+        out_shape=[jax.ShapeDtypeStruct((rows, model), jnp.bfloat16), jax.ShapeDtypeStruct((1, model), jnp.float32)],
         compiler_params=ROOM,
         cost_estimate=cost(2 * rows * model * (H + 2 * KVH) * HD, 10 * rows * model + 2 * model * (H + 2 * KVH) * HD),
         name="last",
-    )(x, gains, dr, w_qkv, cosine, sine, *parts)
+    )(x, gains, dr, w_qkv, act)
 
 
 def gu_products_kernel(l0_ref, l1_ref, g0_ref, g1_ref, u0_ref, u1_ref, g_ref, u_ref):
@@ -806,10 +823,10 @@
         u_ref[0] = (mm(l0_ref[...], u0_ref[0], NN) + mm(l1_ref[...], u1_ref[0], NN)).astype(jnp.bfloat16)
 
 
-def gu_products(left, gates, ups, gate_parts, up_parts):
+def gu_products(left, gates, ups):
     rows, tokens = left[0].shape
     width = gates[0].shape[2]
-    cuts = 2
+    cuts = 1
     piece = width // cuts
     spec = pl.BlockSpec((rows, tokens), lambda m, n, h: (0, 0))
     first = lambda m, v, end: v * (1 - m) + end * m
@@ -823,11 +840,11 @@
 
     def gate_in(m, n, h):
         n, h = gate_at(m, n, h)
-        return gate_parts[0] + gate_parts[1] * n, 0, h
+        return n, 0, h
 
     def up_in(m, n, h):
         n, h = up_at(m, n, h)
-        return up_parts[0] + up_parts[1] * n, 0, h
+        return n, 0, h
 
     def gate_out(m, n, h):
         n, h = gate_at(m, n, h)
@@ -850,21 +867,16 @@
     )(left[0], left[1], gates[0], gates[1], ups[0], ups[1])
 
 
-def qkv_products_kernel(where_ref, l0_ref, l1_ref, r0_ref, r1_ref, extra_ref, s0_ref, s1_ref, s2_ref, s3_ref):
-    r = pl.program_id(0)
+def qkv_products_kernel(where_ref, l0_ref, l1_ref, r0_ref, r1_ref, s0_ref, s1_ref, s2_ref, s3_ref):
     total = mm(l0_ref[...], r0_ref[...], NN) + mm(l1_ref[...], r1_ref[...], NN)
-    end = where_ref[0] ^ r == pl.num_programs(0) - 1
-    wide = extra_ref.shape[1]
-    added = total[:, total.shape[1] - wide :] + jnp.where(end, 1.0, 0.0) * extra_ref[...]
     for n, ref in enumerate((s0_ref, s1_ref, s2_ref, s3_ref)):
 
-        @pl.when(r == n)
+        @pl.when(pl.program_id(0) == n)
         def _():
-            ref[:, : total.shape[1] - wide] = total[:, : total.shape[1] - wide].astype(jnp.bfloat16)
-            ref[:, total.shape[1] - wide :] = added.astype(jnp.bfloat16)
-
-
-def qkv_products(where, left, acts, extra):
+            ref[...] = total.astype(jnp.bfloat16)
+
+
+def qkv_products(where, left, acts):
     rows, tokens = left[0].shape
     width = acts[0].shape[1] // 4
     spec = pl.BlockSpec((rows, tokens), lambda r, *_: (0, 0))
@@ -875,14 +887,14 @@
         grid_spec=pltpu.PrefetchScalarGridSpec(
             num_scalar_prefetch=1,
             grid=(4,),
-            in_specs=[spec, spec, act, act, pl.BlockSpec(extra.shape, lambda r, *_: (0, 0))],
+            in_specs=[spec, spec, act, act],
             out_specs=[out] * 4,
         ),
         out_shape=[jax.ShapeDtypeStruct((rows, width), jnp.bfloat16)] * 4,
         compiler_params=ROOM,
         cost_estimate=cost(16 * rows * tokens * width, 4 * rows * tokens + 8 * (2 * tokens + rows) * width),
         name="qkv_products",
-    )(where, left[0], left[1], acts[0], acts[1], extra)
+    )(where, left[0], left[1], acts[0], acts[1])
 
 
 def place_gu_kernel(where_ref, in_ref, g_ref, u_ref):
@@ -907,7 +919,7 @@
     )(where, parts)
 
 
-def place_qkv_kernel(where_ref, in_ref, q_ref, k_ref, v_ref, g_ref):
+def place_qkv_kernel(where_ref, in_ref, q_ref, k_ref, v_ref):
     t = where_ref[0]
     width = in_ref.shape[2]
     spans = ((q_ref, 0, H * HD), (k_ref, H * HD, KVH * HD), (v_ref, (H + KVH) * HD, KVH * HD))
@@ -919,8 +931,6 @@
             for ref, first, size in spans:
                 if first <= column < first + size:
                     ref[:, column - first : column - first + WIDE] = piece
-            if column == (H + 2 * KVH) * HD:
-                g_ref[...] = jnp.transpose(piece)[0:8]
 
 
 def place_qkv(where, parts):
@@ -929,8 +939,8 @@
     return pl.pallas_call(
         place_qkv_kernel,
         in_specs=[pl.BlockSpec(memory_space=pltpu.SMEM), VMEM],
-        out_specs=[VMEM] * 4,
-        out_shape=[wide(H * HD), wide(KVH * HD), wide(KVH * HD), jax.ShapeDtypeStruct((8, rows), jnp.float32)],
+        out_specs=[VMEM] * 3,
+        out_shape=[wide(H * HD), wide(KVH * HD), wide(KVH * HD)],
         cost_estimate=cost(parts.size, 6 * parts.size),
         name="place_qkv",
     )(where, parts)
@@ -960,8 +970,19 @@
     return v.astype(jnp.bfloat16)
 
 
-def line_pieces(v):
-    return [line(v, k) for k in (1, 2, 3)]
+LINES = [[0, 2, 4, 6], [1, 3, 5, 7]]
+
+
+def line_all(v):
+    return lax.all_to_all(v, "fsdp", 0, 0, axis_index_groups=LINES, tiled=True)
+
+
+def line_spread(v):
+    return line_all(jnp.broadcast_to(v[None], (4, *v.shape)))
+
+
+def far_pieces(got, z):
+    return [lax.dynamic_index_in_dim(got, z ^ k, 0, keepdims=False) for k in (1, 2, 3)]
 
 
 def hold(parts, *events):
@@ -975,13 +996,6 @@
 def square_far(from_x, from_y):
     half = from_x.shape[0] // 2
     return [square(from_y[:half], 1), square(from_x[half:], 2)]
-
-
-def square_sum(v):
-    half = v.shape[0] // 2 // 16 * 16
-    upper, lower = v[:half], v[half:]
-    upper, lower = wide(upper) + wide(square(low(upper), 1)), wide(lower) + wide(square(low(lower), 2))
-    return jnp.concatenate([upper + wide(square(low(upper), 2)), lower + wide(square(low(lower), 1))])
 
 
 def lanes(v, core):
@@ -1014,29 +1028,6 @@
     cut_d = w_down.shape[0] // 4
     kv_width = 2 * KVH * HD
 
-    slice_of = lambda w: lax.dynamic_slice_in_dim(w, t * (w.shape[1] // 4), w.shape[1] // 4, 1)
-    filled = -(-(H * HD + kv_width + WIDE) // (8 * WIDE)) * 8 * WIDE
-    gains_own = jnp.stack([norm1_gain, norm2_gain], 1)
-    qkv_own = jnp.concatenate([w_query, w_key, w_value, gains_own], 1)
-    qkv_own = jnp.pad(qkv_own, ((0, 0), (0, filled - qkv_own.shape[1])))
-    out_width = -(-model // (4 * WIDE)) * WIDE
-    out_own = jnp.pad(w_out, ((0, 0), (0, 4 * out_width - model)))
-    guo_part = jnp.concatenate([slice_of(w_gate), slice_of(w_up), slice_of(out_own)], 1)
-    d_part = lax.dynamic_slice_in_dim(w_down, t * cut_d, cut_d, 0)
-    rows_of = lambda v: v.reshape(-1, v.shape[-1])
-    swap = lambda w: (w, other_core(w))
-    rows_of = lambda v: v.reshape(-1, v.shape[-1])
-    swap = lambda w: (w, other_core(w))
-    qkv_line = line_pieces(slice_of(qkv_own))
-    own_qkv = swap(qkv_own)
-    own_g, own_u, own_o, own_d = swap(w_gate), swap(w_up), swap(w_out), swap(w_down)
-    qkv_rows = jnp.concatenate(qkv_line)
-    d_line = line_pieces(after(d_part, *qkv_line))
-    qkv_parts = [qkv_rows] + [square(qkv_rows, r) for r in (1, 2, 3)]
-    qkv_all = after(jnp.stack(qkv_parts).reshape(4, 3, cut, -1), *d_line)
-    guo_line = line_pieces(after(guo_part, *qkv_parts, *d_line))
-    qkv_both = swap(qkv_all)
-
     relative = jnp.arange(4) ^ t
     offsets = jnp.arange(BLK, dtype=jnp.int32)
     ordered = table[relative].reshape(-1)
@@ -1049,89 +1040,130 @@
     sine = jnp.sin(angles)
     sine = jnp.concatenate([-sine, sine, -sine, sine], 1)
 
-    early = [w[1] for w in (own_g, own_u, own_o, own_d)]
-    a, a_t, q, kv_own, gains, w_qkv = qkv_project(where, after(x, *early), cosine, sine, qkv_both, own_qkv)
-    d_rows = after(jnp.concatenate(d_line), *qkv_parts)
-    d_near = square_near(d_rows)
-    kv_near = square_near(after(kv_own, *d_near))
+    slice_of = lambda w: lax.dynamic_slice_in_dim(w, t * (w.shape[1] // 4), w.shape[1] // 4, 1)
+    filled = -(-(H * HD + kv_width + WIDE) // (8 * WIDE)) * 8 * WIDE
+    gains_own = jnp.stack([norm1_gain, norm2_gain], 1)
+    qkv_own = jnp.concatenate([w_query, w_key, w_value, gains_own], 1)
+    qkv_own = jnp.pad(qkv_own, ((0, 0), (0, filled - qkv_own.shape[1])))
+    gu_part = jnp.concatenate([slice_of(w_gate), slice_of(w_up)], 1)
+    width = hidden_width // 4
+    d_part = lax.dynamic_slice_in_dim(w_down, t * cut_d, cut_d, 0)
+    d_below = jnp.concatenate([d_part[: cut_d // 2, width:], d_part[cut_d // 2 :, width:]], 1)
+    d_part = jnp.concatenate([d_part[:, :width], d_below])
+    swap = lambda w: (w, other_core(w))
+    qkv_line = line_spread(slice_of(qkv_own))
+    own_all = swap(jnp.concatenate([qkv_own, w_gate, w_up, w_out], 1))
+    own_d = swap(w_down)
+    qkv_line = after(qkv_line, cosine, sine, slots, gu_part, d_part)
+    qkv_rows = jnp.concatenate(far_pieces(qkv_line, z))
+    d_line = line_spread(after(d_part, qkv_line))
+    qkv_parts = [qkv_rows] + [square(qkv_rows, r) for r in (1, 2, 3)]
+    qkv_all = after(jnp.stack(qkv_parts).reshape(4, 3, cut, -1), own_all[1], own_d[1], d_line)
+    qkv_both = swap(qkv_all)
+
+    a, a_t, q, kv_own, gains, w_qkv = qkv_project(where, x, cosine, sine, qkv_both, own_all)
+    kv_near = square_near(kv_own)
+    gu_line = line_spread(after(gu_part, d_line))
     kv_far = square_far(*kv_near)
-    d_far = square_far(*hold(d_near, *kv_far))
+    d_rows = jnp.concatenate(far_pieces(d_line, z))
+    d_rest = [square(after(d_rows, *kv_far), r) for r in (1, 2, 3)]
     kv = jnp.concatenate([kv_own, *kv_near, *kv_far])
     mixed_0, lse_0 = attend(own, slots, q, kv, 0, 1)
-    guo_rows = jnp.concatenate(hold(guo_line, mixed_0))
-    d_far = hold(d_far, mixed_0)
-    d = swap(jnp.stack([d_rows, *d_near, jnp.concatenate(d_far)]).reshape(4, 3, cut_d, model))
-    guo_near = square_near(guo_rows)
-    mixed_1, lse_1 = attend(own, slots, after(q, guo_rows), kv, 1, 2)
-    guo_near = hold(guo_near, mixed_1)
-    guo_far = square_far(*guo_near)
-    near = swap(jnp.stack([guo_rows, *guo_near]).reshape(3, 3, cut, -1))
-    far = swap(jnp.concatenate(guo_far).reshape(3, cut, -1))
+    gu_line = after(gu_line, mixed_0)
+    gu_rows = jnp.concatenate(far_pieces(gu_line, z))
+    gu_near = square_near(gu_rows)
+    o_line = line_spread(after(w_out, gu_line))
+    d_rest = hold(d_rest, mixed_0)
+    mixed_1, lse_1 = attend(own, slots, after(q, gu_rows, *d_rest), kv, 1, 2)
+    o_line = after(o_line, mixed_1)
+    gu_near = hold(gu_near, o_line)
+    gu_far = square_far(*gu_near)
+    o = swap(o_line)
+    near = swap(jnp.stack([gu_rows, *gu_near]).reshape(3, 3, cut, -1))
+    d = swap(jnp.stack([d_rows, *d_rest]).reshape(4, 3, cut, -1))
+    far = swap(jnp.concatenate(gu_far).reshape(3, cut, -1))
     mixed = jnp.concatenate([mixed_0, mixed_1], 1)
-    out, mixed_t, b_t, hidden_t, dgate, dup, dr, dr_low, dheads, gg2 = middle(
-        where, mixed, x, dy, gains, near, far, d, own_g, own_u, own_o, own_d
-    )
-
-    gates, ups = swap(dgate), swap(dup)
-    b_mine, b_other = lanes(b_t, core)
-    left = (b_mine, other_core(b_other))
-    g_send, u_send = gu_products(left, gates, ups, (1, 2), (2, 1))
+    out, grad_o, b_t, grad_d, g_s, g_k, u_s, u_k, dr, dheads, gg2 = middle(
+        where, mixed, x, dy, gains, near, far, d, o, own_all, own_d
+    )
+
+    left = (b_t[0], other_core(b_t[1]))
+    g_send, u_send = gu_products(left, swap(g_s), swap(u_s))
     got_x, got_y = square(g_send, 1), square(u_send, 2)
     scatter = lambda v: lax.psum_scatter(v, "fsdp", scatter_dimension=0, tiled=True)
-    grad_d = scatter(low(mm(hidden_t.reshape(-1, rows), after(dy, g_send), NN)))
-    grad_o = scatter(low(mm(mixed_t, after(dr_low, g_send), NN)))
-    g_keep, u_keep = gu_products(left, gates, ups, (0, 2), (0, 1))
-
-    dq_1, *dkv_1 = attend_back(own, slots, after(q, g_keep), kv, dheads, mixed_1, lse_1, cosine, sine, 1, 2)
+    grad_d, grad_o = scatter(grad_d.reshape(-1, model)), scatter(grad_o)
+    kept = [(after(v[0], g_send), v[1]) for v in (swap(g_k), swap(u_k))]
+    g_keep, u_keep = gu_products(left, *kept)
+
+    dq_1, dkv = attend_back(own, slots, where, after(q, g_keep), kv, dheads, mixed_1, lse_1, cosine, sine, 1, 2)
     got_x, got_y = hold((got_x, got_y), dq_1)
     pass_y = low(wide(g_keep[1]) + wide(got_x[1]))
     pass_x = low(wide(u_keep[1]) + wide(got_y[1]))
     last_y, last_x = square(pass_y, 2), square(pass_x, 1)
-    dkv_1_got = [square(v, r) for r, v in zip((1, 2, 3), dkv_1[1:])]
-    dq_0, *dkv_0 = attend_back(own, slots, after(q, pass_x, pass_y), kv, dheads, mixed_0, lse_0, cosine, sine, 0, 1)
-    last_y, last_x, *dkv_1_got = hold([last_y, last_x, *dkv_1_got], dq_0)
-    rows_at = lambda v, at: lax.dynamic_slice_in_dim(v, at * cut, cut, 0)
+    dq_0, dkv = attend_back(
+        own, slots, where, after(q, pass_x, pass_y), kv, dheads, mixed_0, lse_0, cosine, sine, 0, 1, dkv
+    )
+    last_y, last_x = hold([last_y, last_x], dq_0)
+    dkv = after(dkv, last_y, last_x)
+    kv_x, kv_y = square(dkv[0, :2], 1), square(dkv[1, :2], 2)
+    rows_at = lambda v, at: v[at * cut : (at + 1) * cut]
 
     def gu_share(at):
         g = sum(wide(rows_at(v, at)) for v in (g_keep[0], got_x[0], last_y))
         u = sum(wide(rows_at(v, at)) for v in (u_keep[0], got_y[0], last_x))
         return jnp.stack([g, u])
 
-    gu_sends = [low(gu_share(z ^ k)) for k in (1, 2, 3)]
-    gu_got = [line(v, k) for k, v in zip((1, 2, 3), gu_sends)]
-    dkv_0_got = [square(v, r) for r, v in zip((1, 2, 3), dkv_0[1:])]
-    parts = [dq_0, dkv_0[0], *dkv_0_got, dq_1, dkv_1[0], *dkv_1_got]
-    grad_x, act, gg1 = last(after(x, *gu_sends), gains, dr, w_qkv, cosine, sine, parts, (1, 2))
+    gu_sends = jnp.stack([low(gu_share(at)) for at in range(4)])
+    gu_got = line_all(gu_sends)
+    kv_x, kv_y = hold([kv_x, kv_y], gu_sends)
+    kv_last_y = square(low(wide(dkv[0, 3]) + wide(kv_x[1])), 2)
+    kv_last_x = square(low(wide(dkv[1, 3]) + wide(kv_y[1])), 1)
+    act = make_act(cosine, sine, [dkv, kv_x, kv_last_y, kv_y, kv_last_x], [dq_0, dq_1], (1, 2), filled)
+    grad_do = jnp.concatenate([grad_d, grad_o])
+    half = grad_do.shape[0] // 32 * 16
+    do_upper, do_lower = hold([grad_do[:half], grad_do[half:]], kv_last_x, kv_last_y)
+    do_got = [square(do_upper, 1), square(do_lower, 2)]
+    acts = swap(act)
 
     a_mine, a_other = lanes(a_t, core)
     left = (a_mine, other_core(a_other))
-    gain_rows = jnp.concatenate([gg1, gg2])
-    gain_rows = (gain_rows + other_core(gain_rows)).reshape(2, 4, 2, cut)
-    gain_rows = lax.dynamic_index_in_dim(gain_rows, core, 2, keepdims=False).reshape(2, 4 * cut)
-    extra = jnp.pad(gain_rows.T, ((0, 0), (0, WIDE - 2)))
-    qkv_keep, *qkv_sends = qkv_products(where, left, swap(act), extra)
+    qkv_keep, *qkv_sends = qkv_products(where, left, acts)
     shares = [qkv_keep] + [square(v, r) for r, v in zip((1, 2, 3), qkv_sends)]
-    gu_got = hold(gu_got, qkv_keep)
-    s_gu = low(gu_share(z) + sum(wide(v) for v in gu_got))
-    all_gu = jnp.stack([s_gu] + [square(s_gu, r) for r in (1, 2, 3)])
-    grad_g, grad_u = place_gu(where, all_gu)
-    shares = hold(shares, s_gu)
+    do_got = hold(do_got, qkv_keep)
+    do_upper, do_lower = low(wide(do_upper) + wide(do_got[0])), low(wide(do_lower) + wide(do_got[1]))
+    do_got = [square(do_upper, 2), square(do_lower, 1)]
+    grad_x, gg1 = last(after(x, do_upper, do_lower), gains, dr, w_qkv, act)
+    do_got = hold(do_got, gg1)
+    shares = hold(shares, gg1, *do_got)
     qkv_share = lambda at: sum(wide(rows_at(v, at)) for v in shares)
-    qkv_sends = [low(qkv_share(z ^ k)) for k in (1, 2, 3)]
-    qkv_got = [line(v, k) for k, v in zip((1, 2, 3), qkv_sends)]
-    grad_do = square_sum(jnp.concatenate([after(grad_d, *qkv_sends), after(grad_o, *qkv_sends)]))
-    s_qkv = low(qkv_share(z) + sum(wide(v) for v in qkv_got))
-    all_qkv = jnp.stack([s_qkv] + [square(s_qkv, r) for r in (1, 2, 3)])
-    grad_q, grad_k, grad_v, grad_gains = place_qkv(where, all_qkv)
+    qkv_sends = jnp.stack([low(qkv_share(at)) for at in range(4)])
+    gu_got = after(gu_got, gg1)
+    qkv_got = line_all(after(qkv_sends, gu_got))
+    s_gu = low(sum(wide(gu_got[n]) for n in range(4)))
+    all_gu = [s_gu] + [square(after(s_gu, qkv_sends), r) for r in (1, 2, 3)]
+    gain_rows = after(jnp.concatenate([gg1, gg2]), qkv_sends)
+    gain_rows += other_core(gain_rows)
+    gain_rows += square(gain_rows, 1)
+    gain_rows += square(gain_rows, 2)
+    gain_rows += line(gain_rows, 1)
+    gain_rows += line(gain_rows, 2)
+    gain_rows = lax.dynamic_slice_in_dim(gain_rows, f * cut, cut, 1)
+    all_gu = hold(all_gu, gain_rows)
+    qkv_got = after(qkv_got, gain_rows, *all_gu)
+    s_qkv = low(sum(wide(qkv_got[n]) for n in range(4)))
+    all_qkv = [s_qkv] + [square(s_qkv, r) for r in (1, 2, 3)]
+    grad_do = jnp.concatenate([wide(do_upper) + wide(do_got[0]), wide(do_lower) + wide(do_got[1])])
+    grad_g, grad_u = place_gu(where, jnp.stack(hold(all_gu, s_qkv)))
+    grad_q, grad_k, grad_v = place_qkv(where, jnp.stack(all_qkv))
     return (
         out[None],
         grad_x[None],
-        grad_gains[0],
+        gain_rows[0],
         grad_q,
         grad_k,
         grad_v,
         grad_do[4 * cut_d :],
-        grad_gains[1],
+        gain_rows[1],
         grad_g,
         grad_u,
         grad_do[: 4 * cut_d],

time: 549 us -> 511 us (0.931)
  waiting for transfers between devices: 191 us -> 147 us
  matrix products: 14 us -> 0 us
  other arithmetic: 28.6 us -> 39.5 us
    ppermute x15 -> x2, waiting for transfers between devices: 41.2 us -> 4.64 us  [line(): return lax.ppermute(v, 'fsdp', [(f, f ^ 2 * k) for f in range(8)])]
    all_to_all x0 -> x6, starting transfers between devices: none -> 28.1 us  [line_all(): return lax.all_to_all(v, 'fsdp', 0, 0, axis_index_groups=LINES, tiled=True)]
    ppermute x15 -> x2, starting transfers between devices: 28.6 us -> 6.83 us  [line(): return lax.ppermute(v, 'fsdp', [(f, f ^ 2 * k) for f in range(8)])]
    dot_general x2 -> x0, matrix products: 14 us -> none  [mm(): lax.dot_general(left, right, dims, preferred_element_type=jnp.float32)]
    ppermute x38 -> x37, waiting for transfers between devices: 140 us -> 131 us  [square(): return lax.ppermute(v, 'ctx', [(t, t ^ r) for t in range(4)])]
    another operation x5 -> x8, other arithmetic: 7.16 us -> 13.9 us  [the longest x1 3.18 us: square_body(): d = swap(jnp.stack([d_rows, *d_rest]).reshape(4, 3, cut, -1))]
    pallas_call x1, Pallas kernels: 49.3 us -> 55.7 us  [middle(): pl.pallas_call(middle_kernel, grid_spec=pltpu.PrefetchScalarGridSpec(num_...]
    broadcast_in_dim x0 -> x4, local copies, waits for them, and re-layouts: none -> 6.24 us  [line_spread(): return line_all(jnp.broadcast_to(v[None], (4, *v.shape)))]
  transfers between devices with their start and end apart: 70 -> 62, of which waited for: 32 -> 31; matrix products, arithmetic and copies ran while one was open for 10% -> 12% of each run, Pallas kernels for 23% -> 25%
where the time goes in v3:
time: 511 us; the launch traced here: 506 us
  Pallas kernels  188 us (37%)
  waiting for transfers between devices  147 us (29%)
  starting transfers between devices  77.5 us (15%)
  other arithmetic  39.5 us (8%)
  local copies, waits for them, and re-layouts  39 us (8%)
  between operations  14.9 us (3%)
    ppermute x37, waiting for transfers between devices, square(): return lax.ppermute(v, 'ctx', [(t, t ^ r) for t in range(4)])  131 us
    pallas_call x1, Pallas kernels, middle(): pl.pallas_call(middle_kernel, grid_spec=pltpu.PrefetchScalarGridSpec(num_...  55.7 us
    pallas_call x2, Pallas kernels, attend_back(): pl.pallas_call(attend_back_kernel, grid_spec=pltpu.PrefetchScalarGridSpec...  46.6 us
    ppermute x37, starting transfers between devices, square(): return lax.ppermute(v, 'ctx', [(t, t ^ r) for t in range(4)])  40.4 us
    pallas_call x2, Pallas kernels, attend(): pl.pallas_call(attend_kernel, grid_spec=pltpu.PrefetchScalarGridSpec(num_...  33.2 us
    all_to_all x6, starting transfers between devices, line_all(): return lax.all_to_all(v, 'fsdp', 0, 0, axis_index_groups=LINES, tiled=True)  28.1 us
    pallas_call x2, Pallas kernels, gu_products(): pl.pallas_call(gu_products_kernel, grid=(2, 2, cuts), in_specs=[spec, spe...  17.1 us
    unnamed x74, local copies, waits for them, and re-layouts  10.7 us
  transfers between devices with their start and end apart: 62, of which 31 were waited for; matrix products, arithmetic and copies ran while one was open for 12% of the time, Pallas kernels for 25%

profile of v3, /device:TPU:0, one launch (start us, length us, event | category | flops | bytes accessed | tf_op | source)
XLA Modules:
  0.0 506.4 jit_solution(12595895660664712394)
XLA Ops:
  10.8 6.3 %all-to-all-start = ((bf16[4,144,512]{2,1,0:T(8,128)(2,1)}), bf16[4,144,512]{2,1,0:T(8,128)(2,1)S(1)}, u32[]{:S(2)}, u32[]{:S(2)}) async-start(bf16[4,144,512]{2,1,0:T(8,128)(2,1)} %broadcast_in_dim.12), calls=%async_computation | async-start | bytes 1179648 | tf_op jit(solution)/shard_map/all_to_all | solution.py:977
  17.2 1.7 pad_maximum_fusion.1.own0_ref.all0_ref
  19.8 1.8 fusion.25
  21.6 1.7 copy.39
  26.9 2.0 pad_maximum_fusion.15.sin_ref
  30.8 2.2 all-to-all-done
  33.9 1.9 broadcast_in_dim.13
  35.8 4.2 all-to-all-start.1
  40.2 2.5 collective-permute-start.2
  43.7 10.4 %collective-permute-done.2 = bf16[432,512]{1,0:T(8,128)(2,1)S(1)} collective-permute-done((bf16[432,512]{1,0:T(8,128)(2,1)S(1)}, bf16[432,512]{1,0:T(8,128)(2,1)S(1)}, u32[]{:S(2)}, u32[]{:S(2)}) %collective-permute-start.2) | collective-permute-done | bytes 442400 | tf_op jit(solution)/shard_map/ppermute | solution.py:950
  54.2 9.0 %collective-permute-done.1 = bf16[432,512]{1,0:T(8,128)(2,1)S(1)} collective-permute-done((bf16[432,512]{1,0:T(8,128)(2,1)S(1)}, bf16[432,512]{1,0:T(8,128)(2,1)S(1)}, u32[]{:S(2)}, u32[]{:S(2)}) %collective-permute-start.1) | collective-permute-done | bytes 442400 | tf_op jit(solution)/shard_map/ppermute | solution.py:950
  63.3 1.4 pad_maximum_fusion.4.w0_ref
  66.1 5.1 %all-to-all-start.2 = ((bf16[4,144,1536]{2,1,0:T(8,128)(2,1)}), bf16[4,144,1536]{2,1,0:T(8,128)(2,1)}, u32[]{:S(2)}, u32[]{:S(2)}) async-start(bf16[4,144,1536]{2,1,0:T(8,128)(2,1)} %broadcast_in_dim.14), calls=%async_computation.2 | async-start | bytes 3538944 | tf_op jit(solution)/shard_map/all_to_all | solution.py:977
  73.9 7.9 %qkv_project.1 = (bf16[512,1152]{1,0:T(8,128)(2,1)}, bf16[1152,512]{1,0:T(8,128)(2,1)}, bf16[512,1152]{1,0:T(8,128)(2,1)}, bf16[512,768]{1,0:T(8,128)(2,1)}, f32...) custom-call(s32[3]{0:T(128)} %pad_add_fusion.at_ref.where_ref, bf16[512,1152]{1,0:T(8,128)(2,1)} %bitcast.169, ...), custom_call_target="tpu_custom_call" | custom-call | flops 2415919104 | bytes 14155776 | tf_op jit(solution)/shard_map/qkv_project/pallas_call | solution.py:341
  81.9 1.5 collective-permute-start.7
  85.9 15.9 %collective-permute-done.7 = bf16[512,768]{1,0:T(8,128)(2,1)S(1)} collective-permute-done((bf16[512,768]{1,0:T(8,128)(2,1)}, bf16[512,768]{1,0:T(8,128)(2,1)S(1)}, u32[]{:S(2)}, u32[]{:S(2)}) %collective-permute-start.7) | collective-permute-done | bytes 786464 | tf_op jit(solution)/shard_map/ppermute | solution.py:950
  101.8 1.6 collective-permute-start.8
  104.4 8.0 %collective-permute-done.8 = bf16[256,768]{1,0:T(8,128)(2,1)S(1)} collective-permute-done((bf16[256,768]{1,0:T(8,128)(2,1)S(1)}, bf16[256,768]{1,0:T(8,128)(2,1)S(1)}, u32[]{:S(2)}, u32[]{:S(2)}) %collective-permute-start.8) | collective-permute-done | bytes 393248 | tf_op jit(solution)/shard_map/ppermute | solution.py:950
  115.7 1.5 collective-permute-start.10
  117.3 1.6 copy-done
  118.9 12.3 %attend.2 = (bf16[512,384]{1,0:T(8,128)(2,1)}, f32[2,2,1,768]{3,2,1,0:T(1,128)}) custom-call(s32[2]{0:T(128)} %slice_bitcast_fusion.4.own_ref, s32[8]{0:T(128)} %scatter_custom_fusion.slot_ref, bf16[512,1152]{1,0:T(8,128)(2,1)} %get-tuple-element.137.q_ref, bf16[2048,768]{1,0:T(8,128)(2,1)} %copy-done, bf16[2048,768]{1,0:T(8,128)(2,1)} %copy-done), custom_call_target="tpu_custom_call" | custom-call | flops 7247757312 | bytes 1835008 | tf_op jit(solution)/shard_map/attend/pallas_call | solution.py:438
  131.2 2.1 broadcast_in_dim.15
  133.3 4.4 all-to-all-start.3
  141.2 3.1 collective-permute-done.11
  144.3 1.8 collective-permute-done.10
  146.0 20.9 %attend.3 = (bf16[512,768]{1,0:T(8,128)(2,1)}, f32[4,2,1,768]{3,2,1,0:T(1,128)}) custom-call(s32[2]{0:T(128)} %slice_bitcast_fusion.4.own_ref, s32[8]{0:T(128)} %scatter_custom_fusion.slot_ref, bf16[512,1152]{1,0:T(8,128)(2,1)} %get-tuple-element.137.q_ref, bf16[2048,768]{1,0:T(8,128)(2,1)} %copy-done, bf16[2048,768]{1,0:T(8,128)(2,1)} %copy-done), custom_call_target="tpu_custom_call" | custom-call | flops 14495514624 | bytes 3670016 | tf_op jit(solution)/shard_map/attend/pallas_call | solution.py:438
  167.4 5.1 %collective-permute-done.14 = bf16[432,1536]{1,0:T(8,128)(2,1)S(1)} collective-permute-done((bf16[432,1536]{1,0:T(8,128)(2,1)S(1)}, bf16[432,1536]{1,0:T(8,128)(2,1)S(1)}, u32[]{:S(2)}, u32[]{:S(2)}) %collective-permute-start.14) | collective-permute-done | bytes 1327136 | tf_op jit(solution)/shard_map/ppermute | solution.py:950
  172.5 1.6 pad_maximum_fusion.near0_ref
  174.2 3.2 pad_maximum_fusion.2.p0_ref
  177.5 1.7 slice.281
  181.2 15.1 %collective-permute-done.16 = bf16[216,1536]{1,0:T(8,128)(2,1)S(1)} collective-permute-done((bf16[216,1536]{1,0:T(8,128)(2,1)S(1)}, bf16[216,1536]{1,0:T(8,128)(2,1)S(1)}, u32[]{:S(2)}, u32[]{:S(2)}) %collective-permute-start.16) | collective-permute-done | bytes 663584 | tf_op jit(solution)/shard_map/ppermute | solution.py:950
  198.2 1.7 collective-permute-done.18.far1_ref
  199.9 1.9 copy-done.25
  202.2 55.7 %middle.1 = (bf16[512,1152]{1,0:T(8,128)(2,1)}, bf16[1152,1152]{1,0:T(8,128)(2,1)}, bf16[2,576,512]{2,1,0:T(8,128)(2,1)}, bf16[4,768,1152]{2,1,0:T(8,128)(2,1)},...) custom-call(s32[3]{0:T(128)} %pad_add_fusion.at_ref.where_ref, ...), custom_call_target="tpu_custom_call" | custom-call | flops 24461180928 | bytes 40108032 | tf_op jit(solution)/shard_map/middle/pallas_call | solution.py:718
  261.4 5.1 %collective-permute-done.21.l1_ref = bf16[576,512]{1,0:T(8,128)(2,1)S(1)} collective-permute-done((bf16[576,512]{1,0:T(8,128)(2,1)S(1)}, bf16[576,512]{1,0:T(8,128)(2,1)S(1)}, u32[]{:S(2)}, u32[]{:S(2)}) %collective-permute-start.21) | collective-permute-done | bytes 589856 | tf_op jit(solution)/shard_map/ppermute | solution.py:958
  269.4 8.5 %gu_products.2 = (bf16[2,576,768]{2,1,0:T(8,128)(2,1)}, bf16[2,576,768]{2,1,0:T(8,128)(2,1)}) custom-call(bf16[576,512]{1,0:T(8,128)(2,1)} %get-tuple-element.209.l0_ref, bf16[576,512]{1,0:T(8,128)(2,1)} %copy-done.33, bf16[2,512,768]{2,1,0:T(8,128)(2,1)} %get-tuple-element.122.g0_ref, bf16[2,512,768]{2,1,0:T(8,128)(2,1)} %copy-done.29, ...), custom_call_target="tpu_custom_call" | custom-call | flops 3623878656 | bytes 11010048 | tf_op jit(solution)/shard_map/gu_products/pallas_call | solution.py:858
  281.2 8.5 %gu_products.3 = (bf16[2,576,768]{2,1,0:T(8,128)(2,1)}, bf16[2,576,768]{2,1,0:T(8,128)(2,1)}) custom-call(bf16[576,512]{1,0:T(8,128)(2,1)} %get-tuple-element.209.l0_ref, bf16[576,512]{1,0:T(8,128)(2,1)} %copy-done.33, bf16[2,512,768]{2,1,0:T(8,128)(2,1)} %get-tuple-element.125.g0_ref, bf16[2,512,768]{2,1,0:T(8,128)(2,1)} %copy-done.28, ...), custom_call_target="tpu_custom_call" | custom-call | flops 3623878656 | bytes 11010048 | tf_op jit(solution)/shard_map/gu_products/pallas_call | solution.py:858
  289.7 29.9 %attend_back.2 = (bf16[512,768]{1,0:T(8,128)(2,1)}, bf16[2,4,512,384]{3,2,1,0:T(8,128)(2,1)}) custom-call(s32[2]{0:T(128)} %slice_bitcast_fusion.4.own_ref, s32[8]{0:T(128)} %scatter_custom_fusion.slot_ref, s32[3]{0:T(128)} %pad_add_fusion.at_ref.where_ref, bf16[512,1152]{1,0:T(8,128)(2,1)} %get-tuple-element.137.q_ref, bf16[2048,768]{1,0:T(8,128)(2,1)} %copy-done, ...), custom_call_target="tpu_custom_call" | custom-call | flops 1000 | bytes 1000 | tf_op jit(solution)/shard_map/attend_back/pallas_call | solution.py:528
  320.1 2.6 fusion.1
  325.8 16.7 %attend_back.3 = (bf16[512,384]{1,0:T(8,128)(2,1)}, bf16[2,4,512,384]{3,2,1,0:T(8,128)(2,1)}) custom-call(s32[2]{0:T(128)} %slice_bitcast_fusion.4.own_ref, s32[8]{0:T(128)} %scatter_custom_fusion.slot_ref, s32[3]{0:T(128)} %pad_add_fusion.at_ref.where_ref, bf16[512,1152]{1,0:T(8,128)(2,1)} %get-tuple-element.137.q_ref, ...), custom_call_target="tpu_custom_call", output_to_operand_aliasing={{1}: (11, {})} | custom-call | flops 18119393280 | bytes 3670016 | tf_op jit(solution)/shard_map/attend_back/pallas_call | solution.py:528
  342.5 1.6 collective-permute-done.28
  344.1 2.0 collective-permute-done.29
  346.1 1.8 slice_bitcast_fusion
  349.8 1.9 fusion.13
  353.5 12.7 %collective-permute-done.32.gx_ref = bf16[2,512,384]{2,1,0:T(8,128)(2,1)S(1)} collective-permute-done((bf16[2,512,384]{2,1,0:T(8,128)(2,1)S(1)}, bf16[2,512,384]{2,1,0:T(8,128)(2,1)S(1)}, u32[]{:S(2)}, u32[]{:S(2)}) %collective-permute-start.32) | collective-permute-done | bytes 786464 | tf_op jit(solution)/shard_map/ppermute | solution.py:950
  366.3 1.8 fusion.2
  370.0 7.1 %collective-permute-done.33.lasty_ref = bf16[512,384]{1,0:T(8,128)(2,1)S(1)} collective-permute-done((bf16[512,384]{1,0:T(8,128)(2,1)S(1)}, bf16[512,384]{1,0:T(8,128)(2,1)S(1)}, u32[]{:S(2)}, u32[]{:S(2)}) %collective-permute-start.33) | collective-permute-done | bytes 393248 | tf_op jit(solution)/shard_map/ppermute | solution.py:950
  378.6 5.2 %make_act.1.r0_ref.act_ref = bf16[512,2048]{1,0:T(8,128)(2,1)} custom-call(f32[512,128]{1,0:T(8,128)} %copy.42.cos_ref, f32[512,128]{1,0:T(8,128)} %pad_maximum_fusion.15.sin_ref, bf16[2,4,512,384]{3,2,1,0:T(8,128)(2,1)} %get-tuple-element.144.dkv_ref, bf16[2,512,384]{2,1,0:T(8,128)(2,1)} %copy-done.7, bf16[512,384]{1,0:T(8,128)(2,1)} %copy-done.20, ...), custom_call_target="tpu_custom_call" | custom-call | flops 10485760 | bytes 6291456 | tf_op jit(solution)/shard_map/make_act/pallas_call | solution.py:781
  387.6 3.6 all-to-all-start.4
  393.5 7.5 %qkv_products.1 = (bf16[576,512]{1,0:T(8,128)(2,1)}, bf16[576,512]{1,0:T(8,128)(2,1)}, bf16[576,512]{1,0:T(8,128)(2,1)}, bf16[576,512]{1,0:T(8,128)(2,1)}) custom-call(s32[3]{0:T(128)} %pad_add_fusion.at_ref.where_ref, bf16[576,512]{1,0:T(8,128)(2,1)} %bitcast.180, bf16[576,512]{1,0:T(8,128)(2,1)} %collective-permute-done.35.l1_ref, ...), custom_call_target="tpu_custom_call" | custom-call | flops 2415919104 | bytes 7733248 | tf_op jit(solution)/shard_map/qkv_products/pallas_call | solution.py:885
  401.1 6.3 %collective-permute-done.34 = bf16[256,1152]{1,0:T(8,128)(2,1)} collective-permute-done((bf16[256,1152]{1,0:T(8,128)(2,1)S(1)}, bf16[256,1152]{1,0:T(8,128)(2,1)}, u32[]{:S(2)}, u32[]{:S(2)}) %collective-permute-start.34) | collective-permute-done | bytes 589856 | tf_op jit(solution)/shard_map/ppermute | solution.py:950
  415.7 8.4 %last.1 = (bf16[512,1152]{1,0:T(8,128)(2,1)}, f32[1,1152]{1,0:T(1,128)}) custom-call(bf16[512,1152]{1,0:T(8,128)(2,1)} %bitcast.171, f32[8,1152]{1,0:T(8,128)} %get-tuple-element.113.gain_ref, f32[512,1152]{1,0:T(8,128)} %get-tuple-element.155.dr_ref, bf16[1152,2048]{1,0:T(8,128)(2,1)} %get-tuple-element.156.w_ref, bf16[512,2048]{1,0:T(8,128)(2,1)} %make_act.1.r0_ref.act_ref), custom_call_target="tpu_custom_call" | custom-call | flops 2264924160 | bytes 10321920 | tf_op jit(solution)/shard_map/last/pallas_call | solution.py:805
  424.9 15.4 %collective-permute-done.38 = bf16[256,1152]{1,0:T(8,128)(2,1)} collective-permute-done((bf16[256,1152]{1,0:T(8,128)(2,1)S(1)}, bf16[256,1152]{1,0:T(8,128)(2,1)}, u32[]{:S(2)}, u32[]{:S(2)}) %collective-permute-start.38) | collective-permute-done | bytes 589856 | tf_op jit(solution)/shard_map/ppermute | solution.py:950
  440.2 10.2 %collective-permute-done.41 = bf16[576,512]{1,0:T(8,128)(2,1)} collective-permute-done((bf16[576,512]{1,0:T(8,128)(2,1)}, bf16[576,512]{1,0:T(8,128)(2,1)}, u32[]{:S(2)}, u32[]{:S(2)}) %collective-permute-start.41) | collective-permute-done | bytes 589856 | tf_op jit(solution)/shard_map/ppermute | solution.py:950
  450.4 2.0 fusion.21
  455.5 2.6 collective-permute-done.44
  463.9 4.5 all-to-all-start.5
  468.4 2.1 collective-permute-start.46
  471.7 4.6 collective-permute-done.46
  476.3 4.7 collective-permute-start.47
  487.7 2.6 pad_maximum_fusion.5.in_ref
  490.3 1.5 collective-permute-done.52
  492.7 4.6 place_gu.1
  497.3 2.1 place_qkv.1
  (228 shorter events, 84.3 us)
Async XLA Ops:
  10.8 22.2 %all-to-all-start = ((bf16[4,144,512]{2,1,0:T(8,128)(2,1)}), bf16[4,144,512]{2,1,0:T(8,128)(2,1)S(1)}, u32[]{:S(2)}, u32[]{:S(2)}) async-start(bf16[4,144,512]{2,1,0:T(8,128)(2,1)} %broadcast_in_dim.12), calls=%async_computation | async-start | bytes 1179648 | tf_op jit(solution)/shard_map/all_to_all | solution.py:977
  18.9 45.8 %collective-permute-start.3 = (bf16[144,9344]{1,0:T(8,128)(2,1)S(1)}, bf16[144,9344]{1,0:T(8,128)(2,1)}, u32[]{:S(2)}, u32[]{:S(2)}) collective-permute-start(bf16[144,9344]{1,0:T(8,128)(2,1)S(1)} %pad_maximum_fusion.1.own0_ref.all0_ref), channel_id=1, source_target_pairs={{0,1},{1,0},{2,3},{3,2},{4,5},{5,4},{6,7},{7,6},{8,9},{9,8},{10,11... | collective-permute-start | bytes 8073224 | tf_op jit(solution)/shard_map/ppermute | solution.py:958
  35.8 28.9 %all-to-all-start.1 = ((bf16[4,144,768]{2,1,0:T(8,128)(2,1)}), bf16[4,144,768]{2,1,0:T(8,128)(2,1)}, u32[]{:S(2)}, u32[]{:S(2)}) async-start(bf16[4,144,768]{2,1,0:T(8,128)(2,1)} %broadcast_in_dim.13), calls=%async_computation.1 | async-start | bytes 1769472 | tf_op jit(solution)/shard_map/all_to_all | solution.py:977
  40.0 24.7 %collective-permute-start.4 = (bf16[384,1152]{1,0:T(8,128)(2,1)}, bf16[384,1152]{1,0:T(8,128)(2,1)}, u32[]{:S(2)}, u32[]{:S(2)}) collective-permute-start(bf16[384,1152]{1,0:T(8,128)(2,1)} %down0_ref.1), channel_id=1, source_target_pairs={{0,1},{1,0},{2,3},{3,2},{4,5},{5,4},{6,7},{7,6},{8,9},{9,8},{10,11... | collective-permute-start | bytes 2654216 | tf_op jit(solution)/shard_map/ppermute | solution.py:958
  40.2 14.0 %collective-permute-start.2 = (bf16[432,512]{1,0:T(8,128)(2,1)S(1)}, bf16[432,512]{1,0:T(8,128)(2,1)S(1)}, u32[]{:S(2)}, u32[]{:S(2)}) collective-permute-start(bf16[432,512]{1,0:T(8,128)(2,1)S(1)} %pad_maximum_fusion.14), channel_id=1, source_target_pairs={{0,24},{8,16},{16,8},{24,0},{1,25},{9,17},{17,9},{25,1},{2,26},{10... | collective-permute-start | bytes 1327112 | tf_op jit(solution)/shard_map/ppermute | solution.py:950
  42.7 20.5 %collective-permute-start.1 = (bf16[432,512]{1,0:T(8,128)(2,1)S(1)}, bf16[432,512]{1,0:T(8,128)(2,1)S(1)}, u32[]{:S(2)}, u32[]{:S(2)}) collective-permute-start(bf16[432,512]{1,0:T(8,128)(2,1)S(1)} %pad_maximum_fusion.14), channel_id=1, source_target_pairs={{0,16},{8,24},{16,0},{24,8},{1,17},{9,25},{17,1},{25,9},{2,18},{10... | collective-permute-start | bytes 1327112 | tf_op jit(solution)/shard_map/ppermute | solution.py:950
  43.2 20.0 %collective-permute-start = (bf16[432,512]{1,0:T(8,128)(2,1)S(1)}, bf16[432,512]{1,0:T(8,128)(2,1)S(1)}, u32[]{:S(2)}, u32[]{:S(2)}) collective-permute-start(bf16[432,512]{1,0:T(8,128)(2,1)S(1)} %pad_maximum_fusion.14), channel_id=1, source_target_pairs={{0,8},{8,0},{16,24},{24,16},{1,9},{9,1},{17,25},{25,17},{2,10},{10... | collective-permute-start | bytes 1327112 | tf_op jit(solution)/shard_map/ppermute | solution.py:950
  64.7 8.0 %collective-permute-start.5 = (bf16[4,3,144,512]{3,2,1,0:T(8,128)(2,1)}, bf16[4,3,144,512]{3,2,1,0:T(8,128)(2,1)S(1)}, u32[]{:S(2)}, u32[]{:S(2)}) collective-permute-start(bf16[4,3,144,512]{3,2,1,0:T(8,128)(2,1)} %pad_maximum_fusion.4.w0_ref), channel_id=1, source_target_pairs={{0,1},{1,0},{2,3},{3,2},{4,5},{5,4},{6,7},{7,6},{8,9},{9,8},{10,11... | collective-permute-start | bytes 5308424 | tf_op jit(solution)/shard_map/ppermute | solution.py:958
  66.1 65.1 %all-to-all-start.2 = ((bf16[4,144,1536]{2,1,0:T(8,128)(2,1)}), bf16[4,144,1536]{2,1,0:T(8,128)(2,1)}, u32[]{:S(2)}, u32[]{:S(2)}) async-start(bf16[4,144,1536]{2,1,0:T(8,128)(2,1)} %broadcast_in_dim.14), calls=%async_computation.2 | async-start | bytes 3538944 | tf_op jit(solution)/shard_map/all_to_all | solution.py:977
  81.9 19.9 %collective-permute-start.7 = (bf16[512,768]{1,0:T(8,128)(2,1)}, bf16[512,768]{1,0:T(8,128)(2,1)S(1)}, u32[]{:S(2)}, u32[]{:S(2)}) collective-permute-start(bf16[512,768]{1,0:T(8,128)(2,1)} %get-tuple-element.103), channel_id=1, source_target_pairs={{0,16},{8,24},{16,0},{24,8},{1,17},{9,25},{17,1},{25,9},{2,18},{10... | collective-permute-start | bytes 2359304 | tf_op jit(solution)/shard_map/ppermute | solution.py:950
  83.4 20.0 %collective-permute-start.6 = (bf16[512,768]{1,0:T(8,128)(2,1)}, bf16[512,768]{1,0:T(8,128)(2,1)S(1)}, u32[]{:S(2)}, u32[]{:S(2)}) collective-permute-start(bf16[512,768]{1,0:T(8,128)(2,1)} %get-tuple-element.103), channel_id=1, source_target_pairs={{0,8},{8,0},{16,24},{24,16},{1,9},{9,1},{17,25},{25,17},{2,10},{10... | collective-permute-start | bytes 2359304 | tf_op jit(solution)/shard_map/ppermute | solution.py:950
  101.8 10.6 %collective-permute-start.8 = (bf16[256,768]{1,0:T(8,128)(2,1)S(1)}, bf16[256,768]{1,0:T(8,128)(2,1)S(1)}, u32[]{:S(2)}, u32[]{:S(2)}) collective-permute-start(bf16[256,768]{1,0:T(8,128)(2,1)S(1)} %slice.350), channel_id=1, source_target_pairs={{0,8},{8,0},{16,24},{24,16},{1,9},{9,1},{17,25},{25,17},{2,10},{10... | collective-permute-start | bytes 1179656 | tf_op jit(solution)/shard_map/ppermute | solution.py:950
  103.4 10.3 %collective-permute-start.9 = (bf16[256,768]{1,0:T(8,128)(2,1)S(1)}, bf16[256,768]{1,0:T(8,128)(2,1)S(1)}, u32[]{:S(2)}, u32[]{:S(2)}) collective-permute-start(bf16[256,768]{1,0:T(8,128)(2,1)S(1)} %slice.351), channel_id=1, source_target_pairs={{0,16},{8,24},{16,0},{24,8},{1,17},{9,25},{17,1},{25,9},{2,18},{10... | collective-permute-start | bytes 1179656 | tf_op jit(solution)/shard_map/ppermute | solution.py:950
  113.7 27.5 %collective-permute-start.12 = (bf16[432,768]{1,0:T(8,128)(2,1)S(1)}, bf16[432,768]{1,0:T(8,128)(2,1)}, u32[]{:S(2)}, u32[]{:S(2)}) collective-permute-start(bf16[432,768]{1,0:T(8,128)(2,1)S(1)} %pad_maximum_fusion.9), channel_id=1, source_target_pairs={{0,24},{8,16},{16,8},{24,0},{1,25},{9,17},{17,9},{25,1},{2,26},{10... | collective-permute-start | bytes 1990664 | tf_op jit(solution)/shard_map/ppermute | solution.py:950
  115.1 29.2 %collective-permute-start.11 = (bf16[432,768]{1,0:T(8,128)(2,1)S(1)}, bf16[432,768]{1,0:T(8,128)(2,1)}, u32[]{:S(2)}, u32[]{:S(2)}) collective-permute-start(bf16[432,768]{1,0:T(8,128)(2,1)S(1)} %pad_maximum_fusion.9), channel_id=1, source_target_pairs={{0,16},{8,24},{16,0},{24,8},{1,17},{9,25},{17,1},{25,9},{2,18},{10... | collective-permute-start | bytes 1990664 | tf_op jit(solution)/shard_map/ppermute | solution.py:950
  115.7 30.3 %collective-permute-start.10 = (bf16[432,768]{1,0:T(8,128)(2,1)S(1)}, bf16[432,768]{1,0:T(8,128)(2,1)}, u32[]{:S(2)}, u32[]{:S(2)}) collective-permute-start(bf16[432,768]{1,0:T(8,128)(2,1)S(1)} %pad_maximum_fusion.9), channel_id=1, source_target_pairs={{0,8},{8,0},{16,24},{24,16},{1,9},{9,1},{17,25},{25,17},{2,10},{10... | collective-permute-start | bytes 1990664 | tf_op jit(solution)/shard_map/ppermute | solution.py:950
  133.3 34.1 %all-to-all-start.3 = ((bf16[4,144,1152]{2,1,0:T(8,128)(2,1)}), bf16[4,144,1152]{2,1,0:T(8,128)(2,1)}, u32[]{:S(2)}, u32[]{:S(2)}) async-start(bf16[4,144,1152]{2,1,0:T(8,128)(2,1)} %broadcast_in_dim.15), calls=%async_computation.3 | async-start | bytes 2654208 | tf_op jit(solution)/shard_map/all_to_all | solution.py:977
  137.7 247.7 %reduce-scatter.5.cloned.1.call-start = ((), (), s32[]{:S(2)}) async-start(), calls=%async_computation.9 | async-start | bytes 2985984 | tf_op jit(solution)/shard_map/reduce_scatter | solution.py:1093
  139.2 33.3 %collective-permute-start.14 = (bf16[432,1536]{1,0:T(8,128)(2,1)S(1)}, bf16[432,1536]{1,0:T(8,128)(2,1)S(1)}, u32[]{:S(2)}, u32[]{:S(2)}) collective-permute-start(bf16[432,1536]{1,0:T(8,128)(2,1)S(1)} %pad_maximum_fusion.6), channel_id=1, source_target_pairs={{0,16},{8,24},{16,0},{24,8},{1,17},{9,25},{17,1},{25,9},{2,18},{10... | collective-permute-start | bytes 3981320 | tf_op jit(solution)/shard_map/ppermute | solution.py:950
  140.0 32.5 %collective-permute-start.13 = (bf16[432,1536]{1,0:T(8,128)(2,1)S(1)}, bf16[432,1536]{1,0:T(8,128)(2,1)}, u32[]{:S(2)}, u32[]{:S(2)}) collective-permute-start(bf16[432,1536]{1,0:T(8,128)(2,1)S(1)} %pad_maximum_fusion.6), channel_id=1, source_target_pairs={{0,8},{8,0},{16,24},{24,16},{1,9},{9,1},{17,25},{25,17},{2,10},{10... | collective-permute-start | bytes 3981320 | tf_op jit(solution)/shard_map/ppermute | solution.py:950
  174.1 25.8 %collective-permute-start.15 = (bf16[3,3,144,1536]{3,2,1,0:T(8,128)(2,1)S(1)}, bf16[3,3,144,1536]{3,2,1,0:T(8,128)(2,1)S(1)}, u32[]{:S(2)}, u32[]{:S(2)}) collective-permute-start(bf16[3,3,144,1536]{3,2,1,0:T(8,128)(2,1)S(1)} %pad_maximum_fusion.near0_ref), channel_id=1, source_target_pairs={{0,1},{1,0},{2,3},{3,2},{4,5},{5,4},{6,7},{7,6},{8,9},{9,8},{10,11... | collective-permute-start | bytes 11943944 | tf_op jit(solution)/shard_map/ppermute | solution.py:958
  177.4 19.4 %copy-start.4 = (bf16[4,3,144,768]{3,2,1,0:T(8,128)(2,1)}, bf16[4,3,144,768]{3,2,1,0:T(8,128)(2,1)S(1)}, u32[]{:S(2)}) copy-start(bf16[4,3,144,768]{3,2,1,0:T(8,128)(2,1)S(1)} %pad_maximum_fusion.2.p0_ref) | copy-start | bytes 7962628
  177.4 20.8 %collective-permute-start.19 = (bf16[4,3,144,768]{3,2,1,0:T(8,128)(2,1)S(1)}, bf16[4,3,144,768]{3,2,1,0:T(8,128)(2,1)S(1)}, u32[]{:S(2)}, u32[]{:S(2)}) collective-permute-start(bf16[4,3,144,768]{3,2,1,0:T(8,128)(2,1)S(1)} %pad_maximum_fusion.2.p0_ref), channel_id=1, source_target_pairs={{0,1},{1,0},{2,3},{3,2},{4,5},{5,4},{6,7},{7,6},{8,9},{9,8},{10,11... | collective-permute-start | bytes 7962632 | tf_op jit(solution)/shard_map/ppermute | solution.py:958
  177.5 19.4 %copy-start.3 = (bf16[512,768]{1,0:T(8,128)(2,1)S(1)}, bf16[512,768]{1,0:T(8,128)(2,1)}, u32[]{:S(2)}) copy-start(bf16[512,768]{1,0:T(8,128)(2,1)} %get-tuple-element.112.o_ref) | copy-start | bytes 2359300
  179.3 17.0 %collective-permute-start.16 = (bf16[216,1536]{1,0:T(8,128)(2,1)S(1)}, bf16[216,1536]{1,0:T(8,128)(2,1)S(1)}, u32[]{:S(2)}, u32[]{:S(2)}) collective-permute-start(bf16[216,1536]{1,0:T(8,128)(2,1)S(1)} %slice.280), channel_id=1, source_target_pairs={{0,8},{8,0},{16,24},{24,16},{1,9},{9,1},{17,25},{25,17},{2,10},{10... | collective-permute-start | bytes 1990664 | tf_op jit(solution)/shard_map/ppermute | solution.py:950
  179.9 16.7 %collective-permute-start.17 = (bf16[216,1536]{1,0:T(8,128)(2,1)S(1)}, bf16[216,1536]{1,0:T(8,128)(2,1)S(1)}, u32[]{:S(2)}, u32[]{:S(2)}) collective-permute-start(bf16[216,1536]{1,0:T(8,128)(2,1)S(1)} %slice.281), channel_id=1, source_target_pairs={{0,16},{8,24},{16,0},{24,8},{1,17},{9,25},{17,1},{25,9},{2,18},{10... | collective-permute-start | bytes 1990664 | tf_op jit(solution)/shard_map/ppermute | solution.py:950
  181.2 17.0 %collective-permute-start.20 = (bf16[4,144,1152]{2,1,0:T(8,128)(2,1)}, bf16[4,144,1152]{2,1,0:T(8,128)(2,1)S(1)}, u32[]{:S(2)}, u32[]{:S(2)}) collective-permute-start(bf16[4,144,1152]{2,1,0:T(8,128)(2,1)} %all-to-all-done.3.o0_ref), channel_id=1, source_target_pairs={{0,1},{1,0},{2,3},{3,2},{4,5},{5,4},{6,7},{7,6},{8,9},{9,8},{10,11... | collective-permute-start | bytes 3981320 | tf_op jit(solution)/shard_map/ppermute | solution.py:958
  196.8 3.1 collective-permute-start.18
  257.9 127.5 %reduce-scatter.3.cloned.1.call-start = ((), (), s32[]{:S(2)}) async-start(), calls=%async_computation.8 | async-start | bytes 7962624 | tf_op jit(solution)/shard_map/reduce_scatter | solution.py:1093
  259.4 7.1 %collective-permute-start.22 = (bf16[2,512,768]{2,1,0:T(8,128)(2,1)S(1)}, bf16[2,512,768]{2,1,0:T(8,128)(2,1)S(1)}, u32[]{:S(2)}, u32[]{:S(2)}) collective-permute-start(bf16[2,512,768]{2,1,0:T(8,128)(2,1)S(1)} %copy-done.27), channel_id=1, source_target_pairs={{0,1},{1,0},{2,3},{3,2},{4,5},{5,4},{6,7},{7,6},{8,9},{9,8},{10,11... | collective-permute-start | bytes 4718600 | tf_op jit(solution)/shard_map/ppermute | solution.py:958
  259.5 8.8 %collective-permute-start.23 = (bf16[2,512,768]{2,1,0:T(8,128)(2,1)}, bf16[2,512,768]{2,1,0:T(8,128)(2,1)S(1)}, u32[]{:S(2)}, u32[]{:S(2)}) collective-permute-start(bf16[2,512,768]{2,1,0:T(8,128)(2,1)} %get-tuple-element.123.u0_ref), channel_id=1, source_target_pairs={{0,1},{1,0},{2,3},{3,2},{4,5},{5,4},{6,7},{7,6},{8,9},{9,8},{10,11... | collective-permute-start | bytes 4718600 | tf_op jit(solution)/shard_map/ppermute | solution.py:958
  260.8 5.7 %collective-permute-start.21 = (bf16[576,512]{1,0:T(8,128)(2,1)S(1)}, bf16[576,512]{1,0:T(8,128)(2,1)S(1)}, u32[]{:S(2)}, u32[]{:S(2)}) collective-permute-start(bf16[576,512]{1,0:T(8,128)(2,1)S(1)} %get-tuple-element.208), channel_id=1, source_target_pairs={{0,1},{1,0},{2,3},{3,2},{4,5},{5,4},{6,7},{7,6},{8,9},{9,8},{10,11... | collective-permute-start | bytes 1769480 | tf_op jit(solution)/shard_map/ppermute | solution.py:958
  260.9 19.2 %collective-permute-start.24 = (bf16[2,512,768]{2,1,0:T(8,128)(2,1)}, bf16[2,512,768]{2,1,0:T(8,128)(2,1)S(1)}, u32[]{:S(2)}, u32[]{:S(2)}) collective-permute-start(bf16[2,512,768]{2,1,0:T(8,128)(2,1)} %get-tuple-element.125.g0_ref), channel_id=1, source_target_pairs={{0,1},{1,0},{2,3},{3,2},{4,5},{5,4},{6,7},{7,6},{8,9},{9,8},{10,11... | collective-permute-start | bytes 4718600 | tf_op jit(solution)/shard_map/ppermute | solution.py:958
  261.3 18.8 %collective-permute-start.25 = (bf16[2,512,768]{2,1,0:T(8,128)(2,1)}, bf16[2,512,768]{2,1,0:T(8,128)(2,1)}, u32[]{:S(2)}, u32[]{:S(2)}) collective-permute-start(bf16[2,512,768]{2,1,0:T(8,128)(2,1)} %get-tuple-element.127.u0_ref), channel_id=1, source_target_pairs={{0,1},{1,0},{2,3},{3,2},{4,5},{5,4},{6,7},{7,6},{8,9},{9,8},{10,11... | collective-permute-start | bytes 4718600 | tf_op jit(solution)/shard_map/ppermute | solution.py:958
  278.0 41.7 %collective-permute-start.27 = (bf16[2,576,768]{2,1,0:T(8,128)(2,1)}, bf16[2,576,768]{2,1,0:T(8,128)(2,1)}, u32[]{:S(2)}, u32[]{:S(2)}) collective-permute-start(bf16[2,576,768]{2,1,0:T(8,128)(2,1)} %get-tuple-element.124), channel_id=1, source_target_pairs={{0,8},{8,0},{16,24},{24,16},{1,9},{9,1},{17,25},{25,17},{2,10},{10... | collective-permute-start | bytes 5308424 | tf_op jit(solution)/shard_map/ppermute | solution.py:950
  279.3 40.8 %collective-permute-start.26 = (bf16[2,576,768]{2,1,0:T(8,128)(2,1)}, bf16[2,576,768]{2,1,0:T(8,128)(2,1)S(1)}, u32[]{:S(2)}, u32[]{:S(2)}) collective-permute-start(bf16[2,576,768]{2,1,0:T(8,128)(2,1)} %get-tuple-element.129), channel_id=1, source_target_pairs={{0,16},{8,24},{16,0},{24,8},{1,17},{9,25},{17,1},{25,9},{2,18},{10... | collective-permute-start | bytes 5308424 | tf_op jit(solution)/shard_map/ppermute | solution.py:950
  322.7 21.3 %collective-permute-start.28 = (bf16[576,768]{1,0:T(8,128)(2,1)}, bf16[576,768]{1,0:T(8,128)(2,1)}, u32[]{:S(2)}, u32[]{:S(2)}) collective-permute-start(bf16[576,768]{1,0:T(8,128)(2,1)} %fusion.1), channel_id=1, source_target_pairs={{0,16},{8,24},{16,0},{24,8},{1,17},{9,25},{17,1},{25,9},{2,18},{10... | collective-permute-start | bytes 2654216 | tf_op jit(solution)/shard_map/ppermute | solution.py:950
  324.8 21.3 %collective-permute-start.29 = (bf16[576,768]{1,0:T(8,128)(2,1)}, bf16[576,768]{1,0:T(8,128)(2,1)S(1)}, u32[]{:S(2)}, u32[]{:S(2)}) collective-permute-start(bf16[576,768]{1,0:T(8,128)(2,1)} %fusion), channel_id=1, source_target_pairs={{0,8},{8,0},{16,24},{24,16},{1,9},{9,1},{17,25},{25,17},{2,10},{10... | collective-permute-start | bytes 2654216 | tf_op jit(solution)/shard_map/ppermute | solution.py:950
  347.9 18.2 %collective-permute-start.32 = (bf16[2,512,384]{2,1,0:T(8,128)(2,1)S(1)}, bf16[2,512,384]{2,1,0:T(8,128)(2,1)S(1)}, u32[]{:S(2)}, u32[]{:S(2)}) collective-permute-start(bf16[2,512,384]{2,1,0:T(8,128)(2,1)S(1)} %get-tuple-element.197), channel_id=1, source_target_pairs={{0,8},{8,0},{16,24},{24,16},{1,9},{9,1},{17,25},{25,17},{2,10},{10... | collective-permute-start | bytes 2359304 | tf_op jit(solution)/shard_map/ppermute | solution.py:950
  348.7 17.6 %collective-permute-start.30 = (bf16[2,512,384]{2,1,0:T(8,128)(2,1)S(1)}, bf16[2,512,384]{2,1,0:T(8,128)(2,1)S(1)}, u32[]{:S(2)}, u32[]{:S(2)}) collective-permute-start(bf16[2,512,384]{2,1,0:T(8,128)(2,1)S(1)} %get-tuple-element.198), channel_id=1, source_target_pairs={{0,16},{8,24},{16,0},{24,8},{1,17},{9,25},{17,1},{25,9},{2,18},{10... | collective-permute-start | bytes 2359304 | tf_op jit(solution)/shard_map/ppermute | solution.py:950
  368.1 9.0 %collective-permute-start.33 = (bf16[512,384]{1,0:T(8,128)(2,1)S(1)}, bf16[512,384]{1,0:T(8,128)(2,1)S(1)}, u32[]{:S(2)}, u32[]{:S(2)}) collective-permute-start(bf16[512,384]{1,0:T(8,128)(2,1)S(1)} %get-tuple-element.195), channel_id=1, source_target_pairs={{0,16},{8,24},{16,0},{24,8},{1,17},{9,25},{17,1},{25,9},{2,18},{10... | collective-permute-start | bytes 1179656 | tf_op jit(solution)/shard_map/ppermute | solution.py:950
  369.3 8.2 %collective-permute-start.31 = (bf16[512,384]{1,0:T(8,128)(2,1)S(1)}, bf16[512,384]{1,0:T(8,128)(2,1)S(1)}, u32[]{:S(2)}, u32[]{:S(2)}) collective-permute-start(bf16[512,384]{1,0:T(8,128)(2,1)S(1)} %get-tuple-element.196), channel_id=1, source_target_pairs={{0,8},{8,0},{16,24},{24,16},{1,9},{9,1},{17,25},{25,17},{2,10},{10... | collective-permute-start | bytes 1179656 | tf_op jit(solution)/shard_map/ppermute | solution.py:950
  383.7 9.8 %collective-permute-start.36 = (bf16[512,2048]{1,0:T(8,128)(2,1)}, bf16[512,2048]{1,0:T(8,128)(2,1)}, u32[]{:S(2)}, u32[]{:S(2)}) collective-permute-start(bf16[512,2048]{1,0:T(8,128)(2,1)} %make_act.1.r0_ref.act_ref), channel_id=1, source_target_pairs={{0,1},{1,0},{2,3},{3,2},{4,5},{5,4},{6,7},{7,6},{8,9},{9,8},{10,11... | collective-permute-start | bytes 6291464 | tf_op jit(solution)/shard_map/ppermute | solution.py:958
  384.9 8.7 %collective-permute-start.35 = (bf16[576,512]{1,0:T(8,128)(2,1)}, bf16[576,512]{1,0:T(8,128)(2,1)}, u32[]{:S(2)}, u32[]{:S(2)}) collective-permute-start(bf16[576,512]{1,0:T(8,128)(2,1)} %bitcast.60), channel_id=1, source_target_pairs={{0,1},{1,0},{2,3},{3,2},{4,5},{5,4},{6,7},{7,6},{8,9},{9,8},{10,11... | collective-permute-start | bytes 1769480 | tf_op jit(solution)/shard_map/ppermute | solution.py:958
  386.5 20.9 %collective-permute-start.37 = (bf16[272,1152]{1,0:T(8,128)(2,1)S(1)}, bf16[272,1152]{1,0:T(8,128)(2,1)}, u32[]{:S(2)}, u32[]{:S(2)}) collective-permute-start(bf16[272,1152]{1,0:T(8,128)(2,1)S(1)} %pad_maximum_fusion.10), channel_id=1, source_target_pairs={{0,16},{8,24},{16,0},{24,8},{1,17},{9,25},{17,1},{25,9},{2,18},{10... | collective-permute-start | bytes 1880072 | tf_op jit(solution)/shard_map/ppermute | solution.py:950
  387.6 65.8 %all-to-all-start.4 = ((bf16[4,2,144,768]{3,2,1,0:T(8,128)(2,1)}), bf16[4,2,144,768]{3,2,1,0:T(8,128)(2,1)S(1)}, u32[]{:S(2)}, u32[]{:S(2)}) async-start(bf16[4,2,144,768]{3,2,1,0:T(8,128)(2,1)} %maximum_maximum_fusion), calls=%async_computation.6 | async-start | bytes 3538944 | tf_op jit(solution)/shard_map/all_to_all | solution.py:977
  392.3 15.1 %collective-permute-start.34 = (bf16[256,1152]{1,0:T(8,128)(2,1)S(1)}, bf16[256,1152]{1,0:T(8,128)(2,1)}, u32[]{:S(2)}, u32[]{:S(2)}) collective-permute-start(bf16[256,1152]{1,0:T(8,128)(2,1)S(1)} %slice.352), channel_id=1, source_target_pairs={{0,8},{8,0},{16,24},{24,16},{1,9},{9,1},{17,25},{25,17},{2,10},{10... | collective-permute-start | bytes 1769480 | tf_op jit(solution)/shard_map/ppermute | solution.py:950
  408.7 31.5 %collective-permute-start.39 = (bf16[272,1152]{1,0:T(8,128)(2,1)S(1)}, bf16[272,1152]{1,0:T(8,128)(2,1)}, u32[]{:S(2)}, u32[]{:S(2)}) collective-permute-start(bf16[272,1152]{1,0:T(8,128)(2,1)S(1)} %add_convert_fusion.2), channel_id=1, source_target_pairs={{0,8},{8,0},{16,24},{24,16},{1,9},{9,1},{17,25},{25,17},{2,10},{10... | collective-permute-start | bytes 1880072 | tf_op jit(solution)/shard_map/ppermute | solution.py:950
  411.2 29.1 %collective-permute-start.38 = (bf16[256,1152]{1,0:T(8,128)(2,1)S(1)}, bf16[256,1152]{1,0:T(8,128)(2,1)}, u32[]{:S(2)}, u32[]{:S(2)}) collective-permute-start(bf16[256,1152]{1,0:T(8,128)(2,1)S(1)} %add_convert_fusion.3), channel_id=1, source_target_pairs={{0,16},{8,24},{16,0},{24,8},{1,17},{9,25},{17,1},{25,9},{2,18},{10... | collective-permute-start | bytes 1769480 | tf_op jit(solution)/shard_map/ppermute | solution.py:950
  412.2 28.0 %collective-permute-start.42 = (bf16[576,512]{1,0:T(8,128)(2,1)}, bf16[576,512]{1,0:T(8,128)(2,1)}, u32[]{:S(2)}, u32[]{:S(2)}) collective-permute-start(bf16[576,512]{1,0:T(8,128)(2,1)} %get-tuple-element.167), channel_id=1, source_target_pairs={{0,24},{8,16},{16,8},{24,0},{1,25},{9,17},{17,9},{25,1},{2,26},{10... | collective-permute-start | bytes 1769480 | tf_op jit(solution)/shard_map/ppermute | solution.py:950
  413.5 36.9 %collective-permute-start.41 = (bf16[576,512]{1,0:T(8,128)(2,1)}, bf16[576,512]{1,0:T(8,128)(2,1)}, u32[]{:S(2)}, u32[]{:S(2)}) collective-permute-start(bf16[576,512]{1,0:T(8,128)(2,1)} %get-tuple-element.165), channel_id=1, source_target_pairs={{0,16},{8,24},{16,0},{24,8},{1,17},{9,25},{17,1},{25,9},{2,18},{10... | collective-permute-start | bytes 1769480 | tf_op jit(solution)/shard_map/ppermute | solution.py:950
  414.5 35.9 %collective-permute-start.40 = (bf16[576,512]{1,0:T(8,128)(2,1)}, bf16[576,512]{1,0:T(8,128)(2,1)}, u32[]{:S(2)}, u32[]{:S(2)}) collective-permute-start(bf16[576,512]{1,0:T(8,128)(2,1)} %get-tuple-element.163), channel_id=1, source_target_pairs={{0,8},{8,0},{16,24},{24,16},{1,9},{9,1},{17,25},{25,17},{2,10},{10... | collective-permute-start | bytes 1769480 | tf_op jit(solution)/shard_map/ppermute | solution.py:950
  453.3 1.2 collective-permute-start.43
  454.5 3.7 collective-permute-start.44
  458.2 10.2 %collective-permute-start.45 = (f32[2,1152]{1,0:T(2,128)S(1)}, f32[2,1152]{1,0:T(2,128)S(1)}, u32[]{:S(2)}, u32[]{:S(2)}) collective-permute-start(f32[2,1152]{1,0:T(2,128)S(1)} %add.326), channel_id=1, source_target_pairs={{0,16},{8,24},{16,0},{24,8},{1,17},{9,25},{17,1},{25,9},{2,18},{10... | collective-permute-start | bytes 27656 | tf_op jit(solution)/shard_map/ppermute | solution.py:950
  460.4 23.6 %collective-permute-start.50 = (bf16[2,144,768]{2,1,0:T(8,128)(2,1)S(1)}, bf16[2,144,768]{2,1,0:T(8,128)(2,1)S(1)}, u32[]{:S(2)}, u32[]{:S(2)}) collective-permute-start(bf16[2,144,768]{2,1,0:T(8,128)(2,1)S(1)} %fusion.4), channel_id=1, source_target_pairs={{0,24},{8,16},{16,8},{24,0},{1,25},{9,17},{17,9},{25,1},{2,26},{10... | collective-permute-start | bytes 1327112 | tf_op jit(solution)/shard_map/ppermute | solution.py:950
  461.7 22.3 %collective-permute-start.49 = (bf16[2,144,768]{2,1,0:T(8,128)(2,1)S(1)}, bf16[2,144,768]{2,1,0:T(8,128)(2,1)}, u32[]{:S(2)}, u32[]{:S(2)}) collective-permute-start(bf16[2,144,768]{2,1,0:T(8,128)(2,1)S(1)} %fusion.4), channel_id=1, source_target_pairs={{0,16},{8,24},{16,0},{24,8},{1,17},{9,25},{17,1},{25,9},{2,18},{10... | collective-permute-start | bytes 1327112 | tf_op jit(solution)/shard_map/ppermute | solution.py:950
  462.7 21.3 %collective-permute-start.48 = (bf16[2,144,768]{2,1,0:T(8,128)(2,1)S(1)}, bf16[2,144,768]{2,1,0:T(8,128)(2,1)}, u32[]{:S(2)}, u32[]{:S(2)}) collective-permute-start(bf16[2,144,768]{2,1,0:T(8,128)(2,1)S(1)} %fusion.4), channel_id=1, source_target_pairs={{0,8},{8,0},{16,24},{24,16},{1,9},{9,1},{17,25},{25,17},{2,10},{10... | collective-permute-start | bytes 1327112 | tf_op jit(solution)/shard_map/ppermute | solution.py:950
  463.9 20.0 %all-to-all-start.5 = ((bf16[4,144,512]{2,1,0:T(8,128)(2,1)}), bf16[4,144,512]{2,1,0:T(8,128)(2,1)S(1)}, u32[]{:S(2)}, u32[]{:S(2)}) async-start(bf16[4,144,512]{2,1,0:T(8,128)(2,1)} %pad_maximum_fusion.11), calls=%async_computation.7 | async-start | bytes 1179648 | tf_op jit(solution)/shard_map/all_to_all | solution.py:977
  468.4 7.9 %collective-permute-start.46 = (f32[2,1152]{1,0:T(2,128)S(1)}, f32[2,1152]{1,0:T(2,128)S(1)}, u32[]{:S(2)}, u32[]{:S(2)}) collective-permute-start(f32[2,1152]{1,0:T(2,128)S(1)} %add.327), channel_id=1, source_target_pairs={{0,2},{1,3},{2,0},{3,1},{4,6},{5,7},{6,4},{7,5},{8,10},{9,11},{10,... | collective-permute-start | bytes 27656 | tf_op jit(solution)/shard_map/ppermute | solution.py:954
  476.3 7.0 %collective-permute-start.47 = (f32[2,1152]{1,0:T(2,128)S(1)}, f32[2,1152]{1,0:T(2,128)S(1)}, u32[]{:S(2)}, u32[]{:S(2)}) collective-permute-start(f32[2,1152]{1,0:T(2,128)S(1)} %add.328), channel_id=1, source_target_pairs={{0,4},{1,5},{2,6},{3,7},{4,0},{5,1},{6,2},{7,3},{8,12},{9,13},{10,... | collective-permute-start | bytes 27656 | tf_op jit(solution)/shard_map/ppermute | solution.py:954
  484.1 6.2 %collective-permute-start.53 = (bf16[144,512]{1,0:T(8,128)(2,1)S(1)}, bf16[144,512]{1,0:T(8,128)(2,1)S(1)}, u32[]{:S(2)}, u32[]{:S(2)}) collective-permute-start(bf16[144,512]{1,0:T(8,128)(2,1)S(1)} %fusion.33), channel_id=1, source_target_pairs={{0,24},{8,16},{16,8},{24,0},{1,25},{9,17},{17,9},{25,1},{2,26},{10... | collective-permute-start | bytes 442376 | tf_op jit(solution)/shard_map/ppermute | solution.py:950
  485.4 6.4 %collective-permute-start.52 = (bf16[144,512]{1,0:T(8,128)(2,1)S(1)}, bf16[144,512]{1,0:T(8,128)(2,1)S(1)}, u32[]{:S(2)}, u32[]{:S(2)}) collective-permute-start(bf16[144,512]{1,0:T(8,128)(2,1)S(1)} %fusion.33), channel_id=1, source_target_pairs={{0,16},{8,24},{16,0},{24,8},{1,17},{9,25},{17,1},{25,9},{2,18},{10... | collective-permute-start | bytes 442376 | tf_op jit(solution)/shard_map/ppermute | solution.py:950
  486.4 5.4 %collective-permute-start.51 = (bf16[144,512]{1,0:T(8,128)(2,1)S(1)}, bf16[144,512]{1,0:T(8,128)(2,1)S(1)}, u32[]{:S(2)}, u32[]{:S(2)}) collective-permute-start(bf16[144,512]{1,0:T(8,128)(2,1)S(1)} %fusion.33), channel_id=1, source_target_pairs={{0,8},{8,0},{16,24},{24,16},{1,9},{9,1},{17,25},{25,17},{2,10},{10... | collective-permute-start | bytes 442376 | tf_op jit(solution)/shard_map/ppermute | solution.py:950
  (32 other events, 162.5 us)
Sparse Core Ops, SparseCore 0:
  258.0 36.8 reduce-scatter.4
  297.2 77.1 reduce-scatter.2

commit v4 on v3

--- a/solution.py
+++ b/solution.py
@@ -535,8 +535,8 @@
                 pl.BlockSpec((length, WIDE), lambda p, *_: (0, p + start)),
                 pl.BlockSpec((length, WIDE), lambda p, *_: (0, p + start + KVH // 2)),
                 shifted,
-                wide,
-                pl.BlockSpec((2, 2, 1, RATIO * BLK), lambda p, *_: (p, 0, 0, 0)),
+                shifted,
+                pl.BlockSpec((2, 2, 1, RATIO * BLK), lambda p, *_: (p + start, 0, 0, 0)),
                 whole,
                 whole,
             ]
@@ -561,26 +561,27 @@
 
 def middle_kernel(
     at_ref, ho_ref, x_ref, dy_ref, gain_ref,
-    near0_ref, near1_ref, far0_ref, far1_ref, p0_ref, p1_ref, o0_ref, o1_ref, all0_ref, all1_ref, down0_ref, down1_ref,
-    out_ref, go_ref, bt_ref, gd_ref, gs_ref, gk_ref, us_ref, uk_ref, dr_ref, dh_ref, gg_ref,
-    gu_scr, d_scr, wo_ref, r_scr, b_scr, acc_scr, db_scr, h_scr, dg_ref, du_ref, gu_sem, o_sem, d_sem,
+    *refs,
 ):
     r = pl.program_id(0)
     count = pl.num_programs(0)
     t, core, z = at_ref[0], at_ref[1], at_ref[2]
-    parts, lines, cut = p0_ref.shape[:3]
+    parts = 4
+    sent, (d0_ref, d1_ref, all0_ref, all1_ref) = refs[: 2 * parts], refs[2 * parts : 2 * parts + 4]
+    out_ref, low_ref, bt_ref, gd_ref, gs_ref, gk_ref, us_ref, uk_ref, dr_ref, dh_ref, gg_ref = refs[-24:-13]
+    gu_scr, d_scr, wo_ref, r_scr, b_scr, acc_scr, db_scr, h_scr, dg_ref, du_ref, gu_sem, o_sem, d_sem = refs[-13:]
+    lines, cut, columns_sent = sent[0].shape
     width = dg_ref.shape[1]
     model = wo_ref.shape[1]
-    third = width // 2
-    cut_d = down0_ref.shape[0] // parts
+    o_width = columns_sent - 2 * width
+    o_parts = model // o_width
     first_g = all0_ref.shape[1] - model - 2 * parts * width
-    alls, ps = (all0_ref, all1_ref), (p0_ref, p1_ref)
+    alls = (all0_ref, all1_ref)
     cores = (core, 1 - core)
     others = far_lines(z)
 
     def piece(n, part, k):
-        near, far = ((near0_ref, far0_ref), (near1_ref, far1_ref))[n]
-        return near.at[part, k] if part < parts - 1 else far.at[k]
+        return sent[2 * part + n].at[k]
 
     def gu_copies(part, slot):
         out = []
@@ -595,39 +596,54 @@
                     out.append((piece(n, part, k).at[:, pl.ds(m * width, width)], gu_scr.at[slot, m, rows, :]))
         return [pltpu.make_async_copy(src, dst, gu_sem.at[slot, i]) for i, (src, dst) in enumerate(out)]
 
-    def o_copies():
+    def o_copies(part):
+        out = []
+        columns = pl.ds(pl.multiple_of((t ^ part) * o_width, WIDE), o_width)
+        for n, other in enumerate(cores):
+            for k in range(lines):
+                rows = pl.ds(pl.multiple_of((2 * others[k] + other) * cut, 16), cut)
+                out.append((piece(n, part, k).at[:, pl.ds(2 * width, o_width)], wo_ref.at[rows, columns]))
+        return [pltpu.make_async_copy(src, dst, o_sem.at[part, i]) for i, (src, dst) in enumerate(out)]
+
+    def own_copies():
         out = []
         for n, other in enumerate(cores):
-            for line in range(lines + 1):
-                rows = pl.ds(pl.multiple_of((2 * line + other) * cut, 16), cut)
-                out.append(((o0_ref, o1_ref)[n].at[line], wo_ref.at[rows, :]))
-        return [pltpu.make_async_copy(src, dst, o_sem.at[i]) for i, (src, dst) in enumerate(out)]
+            rows = pl.ds(pl.multiple_of((2 * z + other) * cut, 16), cut)
+            out.append((alls[n].at[:, pl.ds(first_g + 2 * parts * width, model)], wo_ref.at[rows, :]))
+        return [pltpu.make_async_copy(src, dst, o_sem.at[parts, i]) for i, (src, dst) in enumerate(out)]
 
     def d_copies():
         out = []
+        cut_d = d0_ref.shape[1]
         for n, other in enumerate(cores):
-            row = pl.multiple_of((2 * z + other) * parts * cut_d, 16)
-            out.append(((down0_ref, down1_ref)[n], d_scr.at[pl.ds(row, parts * cut_d), :]))
-            for k in range(lines):
-                for part in range(parts):
-                    row = pl.multiple_of(((2 * others[k] + other) * parts + (t ^ part)) * cut_d, 16)
-                    p = ps[n].at[part, k]
-                    out.append((p.at[pl.ds(0, cut_d), :], d_scr.at[pl.ds(row, cut_d), pl.ds(0, width)]))
-                    for m in range(2):
-                        src = p.at[pl.ds(cut_d, cut_d // 2), pl.ds(m * third, third)]
-                        row_m = pl.multiple_of(row + m * (cut_d // 2), 16)
-                        out.append((src, d_scr.at[pl.ds(row_m, cut_d // 2), pl.ds(width, third)]))
+            for line in range(lines + 1):
+                row = pl.multiple_of((2 * line + other) * cut_d, 16)
+                out.append(((d0_ref, d1_ref)[n].at[line], d_scr.at[pl.ds(row, cut_d), :]))
         return [pltpu.make_async_copy(src, dst, d_sem.at[i]) for i, (src, dst) in enumerate(out)]
 
     slot = lax.rem(r, 2)
 
     @pl.when(r == 0)
     def _():
-        for c in o_copies():
+        for part in range(parts):
+
+            @pl.when((t ^ part) < o_parts)
+            def _():
+                for c in o_copies(part):
+                    c.start()
+
+        for c in own_copies():
             c.start()
         for c in gu_copies(0, 0) + d_copies():
             c.start()
-        for c in o_copies():
+        for part in range(parts):
+
+            @pl.when((t ^ part) < o_parts)
+            def _():
+                for c in o_copies(part):
+                    c.wait()
+
+        for c in own_copies():
             c.wait()
         resid = x_ref[...].astype(jnp.float32) + mm(ho_ref[...], wo_ref[...], NN)
         r_scr[...] = resid
@@ -702,15 +718,15 @@
         )
         dr_ref[...] = dr
         low = dr.astype(jnp.bfloat16)
-        go_ref[...] = mm(ho_ref[...], low, TN).astype(jnp.bfloat16)
+        low_ref[...] = low
         dh_ref[...] = mm(low, wo_ref[...], NT).astype(jnp.bfloat16)
 
 
-def middle(where, ho, x, dy, gains, near, far, p, o, own_all, own_d):
+def middle(where, ho, x, dy, gains, sent, d, own_all):
     rows, model = x.shape
-    lines, cut = near[0].shape[1:3]
-    count = near[0].shape[0] + 1
-    width = near[0].shape[3] // 2
+    lines, cut = sent[0][0].shape[:2]
+    count = len(sent)
+    width = d[0].shape[0] * d[0].shape[1] * 2 // count
     once = pl.Buffered(1)
     whole = lambda shape: pl.BlockSpec(shape, lambda r, *_: (0,) * len(shape), pipeline_mode=once)
     act = lambda at: pl.BlockSpec((1, rows, width), lambda r, *_: (at(r), 0, 0))
@@ -722,7 +738,7 @@
             grid=(count,),
             in_specs=[whole((rows, H * HD)), whole((rows, model)), whole((rows, model)), whole((8, model))] + [HBM] * 12,
             out_specs=[
-                whole((rows, model)), whole((H * HD, model)), whole((2, model // 2, rows)),
+                whole((rows, model)), whole((rows, model)), whole((2, model // 2, rows)),
                 pl.BlockSpec((1, width, model), lambda r, at_ref: (at_ref[0] ^ r, 0, 0)),
                 act(lambda r: r // 3), act(lambda r: r // 2), act(lambda r: r // 3), act(lambda r: (r + 2) // 3),
                 whole((rows, model)), whole((rows, H * HD)), whole((1, model)),
@@ -739,13 +755,13 @@
                 pltpu.VMEM((rows, width), low),
                 pltpu.VMEM((rows, width), low),
                 pltpu.SemaphoreType.DMA((2, 4 * (lines + 1))),
+                pltpu.SemaphoreType.DMA((count + 1, 2 * lines)),
                 pltpu.SemaphoreType.DMA((2 * (lines + 1),)),
-                pltpu.SemaphoreType.DMA((2 + 6 * count * lines,)),
             ],
         ),
         out_shape=[
             jax.ShapeDtypeStruct((rows, model), low),
-            jax.ShapeDtypeStruct((H * HD, model), low),
+            jax.ShapeDtypeStruct((rows, model), low),
             jax.ShapeDtypeStruct((2, model // 2, rows), low),
             jax.ShapeDtypeStruct((count, width, model), low),
             *[jax.ShapeDtypeStruct((2, rows, width), low)] * 4,
@@ -756,7 +772,7 @@
         compiler_params=ROOM,
         cost_estimate=cost(12 * rows * model * width * count + 4 * rows * model * model, 2 * 16 * rows * model + 6 * count * width * model, rows * width * count),
         name="middle",
-    )(where, ho, x, dy, gains, *near, *far, *p, *o, *own_all, *own_d)
+    )(where, ho, x, dy, gains, *[v for pair in sent for v in pair], *d, *own_all)
 
 
 def act_kernel(counts, cos_ref, sin_ref, dkv_ref, gx_ref, lasty_ref, gy_ref, lastx_ref, *refs):
@@ -897,53 +913,59 @@
     )(where, left[0], left[1], acts[0], acts[1])
 
 
-def place_gu_kernel(where_ref, in_ref, g_ref, u_ref):
-    g_ref[...] = in_ref[0, 0].astype(jnp.float32)
-    u_ref[...] = in_ref[0, 1].astype(jnp.float32)
+def place_gu_kernel(where_ref, p0_ref, p1_ref, p2_ref, p3_ref, g_ref, u_ref):
+    for r, ref in enumerate((p0_ref, p1_ref, p2_ref, p3_ref)):
+
+        @pl.when(pl.program_id(0) == r)
+        def _():
+            g_ref[...] = ref[0].astype(jnp.float32)
+            u_ref[...] = ref[1].astype(jnp.float32)
 
 
 def place_gu(where, parts):
-    count, _, rows, width = parts.shape
-    out = pl.BlockSpec((rows, width), lambda n, *_: (0, n))
+    _, rows, width = parts[0].shape
+    out = pl.BlockSpec((rows, width), lambda r, w: (0, w[0] ^ r))
     return pl.pallas_call(
         place_gu_kernel,
         grid_spec=pltpu.PrefetchScalarGridSpec(
             num_scalar_prefetch=1,
-            grid=(count,),
-            in_specs=[pl.BlockSpec((1, 2, rows, width), lambda n, where_ref: (where_ref[0] ^ n, 0, 0, 0))],
+            grid=(4,),
+            in_specs=[pl.BlockSpec((2, rows, width), lambda r, *_: (0, 0, 0))] * 4,
             out_specs=[out, out],
         ),
-        out_shape=[jax.ShapeDtypeStruct((rows, count * width), jnp.float32)] * 2,
-        cost_estimate=cost(parts.size, 6 * parts.size),
+        out_shape=[jax.ShapeDtypeStruct((rows, 4 * width), jnp.float32)] * 2,
+        compiler_params=ROOM,
+        cost_estimate=cost(1000, 1000),
         name="place_gu",
-    )(where, parts)
-
-
-def place_qkv_kernel(where_ref, in_ref, q_ref, k_ref, v_ref):
-    t = where_ref[0]
-    width = in_ref.shape[2]
+    )(where, *parts)
+
+
+def place_qkv_kernel(in_ref, q_ref, k_ref, v_ref, g_ref):
+    width = in_ref.shape[2] - WIDE
     spans = ((q_ref, 0, H * HD), (k_ref, H * HD, KVH * HD), (v_ref, (H + KVH) * HD, KVH * HD))
+    gains = 0.0
     for n in range(in_ref.shape[0]):
-        part = in_ref[t ^ n].astype(jnp.float32)
+        part = in_ref[n].astype(jnp.float32)
+        gains += part[:, width:]
         for at in range(0, width, WIDE):
             column = n * width + at
-            piece = part[:, at : at + WIDE]
             for ref, first, size in spans:
                 if first <= column < first + size:
-                    ref[:, column - first : column - first + WIDE] = piece
-
-
-def place_qkv(where, parts):
+                    ref[:, column - first : column - first + WIDE] = part[:, at : at + WIDE]
+    g_ref[...] = jnp.transpose(gains)[0:8]
+
+
+def place_qkv(parts):
     rows = parts.shape[1]
-    wide = lambda columns: jax.ShapeDtypeStruct((rows, columns), jnp.float32)
+    shape = lambda columns: jax.ShapeDtypeStruct((rows, columns), jnp.float32)
     return pl.pallas_call(
         place_qkv_kernel,
-        in_specs=[pl.BlockSpec(memory_space=pltpu.SMEM), VMEM],
-        out_specs=[VMEM] * 3,
-        out_shape=[wide(H * HD), wide(KVH * HD), wide(KVH * HD)],
+        in_specs=[VMEM],
+        out_specs=[VMEM] * 4,
+        out_shape=[shape(H * HD), shape(KVH * HD), shape(KVH * HD), jax.ShapeDtypeStruct((8, rows), jnp.float32)],
         cost_estimate=cost(parts.size, 6 * parts.size),
         name="place_qkv",
-    )(where, parts)
+    )(parts)
 
 
 def square(v, r):
@@ -1045,63 +1067,56 @@
     gains_own = jnp.stack([norm1_gain, norm2_gain], 1)
     qkv_own = jnp.concatenate([w_query, w_key, w_value, gains_own], 1)
     qkv_own = jnp.pad(qkv_own, ((0, 0), (0, filled - qkv_own.shape[1])))
-    gu_part = jnp.concatenate([slice_of(w_gate), slice_of(w_up)], 1)
-    width = hidden_width // 4
-    d_part = lax.dynamic_slice_in_dim(w_down, t * cut_d, cut_d, 0)
-    d_below = jnp.concatenate([d_part[: cut_d // 2, width:], d_part[cut_d // 2 :, width:]], 1)
-    d_part = jnp.concatenate([d_part[:, :width], d_below])
+    o_whole = jnp.pad(w_out, ((0, 0), (0, 2 * (hidden_width // 4) - model)))
+    guo_part = jnp.concatenate([slice_of(w_gate), slice_of(w_up), slice_of(o_whole)], 1)
     swap = lambda w: (w, other_core(w))
-    qkv_line = line_spread(slice_of(qkv_own))
+    qkv_slice = slice_of(qkv_own)
+    qkv_line = [line(qkv_slice, k) for k in (1, 2, 3)]
     own_all = swap(jnp.concatenate([qkv_own, w_gate, w_up, w_out], 1))
-    own_d = swap(w_down)
-    qkv_line = after(qkv_line, cosine, sine, slots, gu_part, d_part)
-    qkv_rows = jnp.concatenate(far_pieces(qkv_line, z))
-    d_line = line_spread(after(d_part, qkv_line))
+    qkv_rows = jnp.concatenate(hold(qkv_line, cosine, sine, slots, guo_part))
+    guo_line = line_spread(after(guo_part, *qkv_line))
     qkv_parts = [qkv_rows] + [square(qkv_rows, r) for r in (1, 2, 3)]
-    qkv_all = after(jnp.stack(qkv_parts).reshape(4, 3, cut, -1), own_all[1], own_d[1], d_line)
+    qkv_all = after(jnp.stack(qkv_parts).reshape(4, 3, cut, -1), own_all[1])
     qkv_both = swap(qkv_all)
 
     a, a_t, q, kv_own, gains, w_qkv = qkv_project(where, x, cosine, sine, qkv_both, own_all)
     kv_near = square_near(kv_own)
-    gu_line = line_spread(after(gu_part, d_line))
+    guo_line = after(guo_line, kv_own)
+    d_line = line_all(after(jnp.broadcast_to(w_down[None], (4, *w_down.shape)), guo_line))
     kv_far = square_far(*kv_near)
-    d_rows = jnp.concatenate(far_pieces(d_line, z))
-    d_rest = [square(after(d_rows, *kv_far), r) for r in (1, 2, 3)]
+    guo_rows = after(jnp.concatenate(far_pieces(after(guo_line, *kv_near), z)), *kv_far)
+    guo_near = square_near(guo_rows)
+    guo_own = other_core(guo_rows.reshape(3, cut, -1))
     kv = jnp.concatenate([kv_own, *kv_near, *kv_far])
-    mixed_0, lse_0 = attend(own, slots, q, kv, 0, 1)
-    gu_line = after(gu_line, mixed_0)
-    gu_rows = jnp.concatenate(far_pieces(gu_line, z))
-    gu_near = square_near(gu_rows)
-    o_line = line_spread(after(w_out, gu_line))
-    d_rest = hold(d_rest, mixed_0)
-    mixed_1, lse_1 = attend(own, slots, after(q, gu_rows, *d_rest), kv, 1, 2)
-    o_line = after(o_line, mixed_1)
-    gu_near = hold(gu_near, o_line)
-    gu_far = square_far(*gu_near)
-    o = swap(o_line)
-    near = swap(jnp.stack([gu_rows, *gu_near]).reshape(3, 3, cut, -1))
-    d = swap(jnp.stack([d_rows, *d_rest]).reshape(4, 3, cut, -1))
-    far = swap(jnp.concatenate(gu_far).reshape(3, cut, -1))
-    mixed = jnp.concatenate([mixed_0, mixed_1], 1)
-    out, grad_o, b_t, grad_d, g_s, g_k, u_s, u_k, dr, dheads, gg2 = middle(
-        where, mixed, x, dy, gains, near, far, d, o, own_all, own_d
+    mixed, lse = attend(own, slots, after(q, guo_rows), kv, 0, KVH // 2)
+    guo_near = hold(guo_near, mixed)
+    half = guo_rows.shape[0] // 2
+    guo_far = [square(guo_near[1][:half], 1), square(guo_near[0][half:], 2)]
+    d = swap(after(d_line, *guo_far))
+    shaped = lambda v: v.reshape(3, cut, -1)
+    guo = [(shaped(guo_rows), after(guo_own, mixed))] + [swap(shaped(v)) for v in guo_near]
+    guo.append(swap(shaped(after(jnp.concatenate(guo_far), *[v[1] for v in guo]))))
+    out, dr_low, b_t, grad_d, g_s, g_k, u_s, u_k, dr, dheads, gg2 = middle(
+        where, mixed, x, dy, gains, guo, d, own_all
     )
 
     left = (b_t[0], other_core(b_t[1]))
-    g_send, u_send = gu_products(left, swap(g_s), swap(u_s))
+    g_s, u_s = swap(g_s), swap(u_s)
+    grad_o = low(mm(mixed, dr_low, TN))
+    g_send, u_send = gu_products(left, (after(g_s[0], grad_o), g_s[1]), u_s)
     got_x, got_y = square(g_send, 1), square(u_send, 2)
     scatter = lambda v: lax.psum_scatter(v, "fsdp", scatter_dimension=0, tiled=True)
     grad_d, grad_o = scatter(grad_d.reshape(-1, model)), scatter(grad_o)
     kept = [(after(v[0], g_send), v[1]) for v in (swap(g_k), swap(u_k))]
     g_keep, u_keep = gu_products(left, *kept)
 
-    dq_1, dkv = attend_back(own, slots, where, after(q, g_keep), kv, dheads, mixed_1, lse_1, cosine, sine, 1, 2)
+    dq_1, dkv = attend_back(own, slots, where, after(q, g_keep), kv, dheads, mixed, lse, cosine, sine, 1, 2)
     got_x, got_y = hold((got_x, got_y), dq_1)
     pass_y = low(wide(g_keep[1]) + wide(got_x[1]))
     pass_x = low(wide(u_keep[1]) + wide(got_y[1]))
     last_y, last_x = square(pass_y, 2), square(pass_x, 1)
     dq_0, dkv = attend_back(
-        own, slots, where, after(q, pass_x, pass_y), kv, dheads, mixed_0, lse_0, cosine, sine, 0, 1, dkv
+        own, slots, where, after(q, pass_x, pass_y), kv, dheads, mixed, lse, cosine, sine, 0, 1, dkv
     )
     last_y, last_x = hold([last_y, last_x], dq_0)
     dkv = after(dkv, last_y, last_x)
@@ -1118,43 +1133,40 @@
     kv_x, kv_y = hold([kv_x, kv_y], gu_sends)
     kv_last_y = square(low(wide(dkv[0, 3]) + wide(kv_x[1])), 2)
     kv_last_x = square(low(wide(dkv[1, 3]) + wide(kv_y[1])), 1)
-    act = make_act(cosine, sine, [dkv, kv_x, kv_last_y, kv_y, kv_last_x], [dq_0, dq_1], (1, 2), filled)
     grad_do = jnp.concatenate([grad_d, grad_o])
     half = grad_do.shape[0] // 32 * 16
-    do_upper, do_lower = hold([grad_do[:half], grad_do[half:]], kv_last_x, kv_last_y)
+    do_upper, do_lower = hold([grad_do[:half], grad_do[half:]], kv_x, kv_y)
     do_got = [square(do_upper, 1), square(do_lower, 2)]
+    act = make_act(after(cosine, do_upper, do_lower), sine, [dkv, kv_x, kv_last_y, kv_y, kv_last_x], [dq_0, dq_1], (1, 2), filled)
     acts = swap(act)
 
     a_mine, a_other = lanes(a_t, core)
     left = (a_mine, other_core(a_other))
     qkv_keep, *qkv_sends = qkv_products(where, left, acts)
     shares = [qkv_keep] + [square(v, r) for r, v in zip((1, 2, 3), qkv_sends)]
-    do_got = hold(do_got, qkv_keep)
-    do_upper, do_lower = low(wide(do_upper) + wide(do_got[0])), low(wide(do_lower) + wide(do_got[1]))
-    do_got = [square(do_upper, 2), square(do_lower, 1)]
-    grad_x, gg1 = last(after(x, do_upper, do_lower), gains, dr, w_qkv, act)
-    do_got = hold(do_got, gg1)
-    shares = hold(shares, gg1, *do_got)
+    grad_x, gg1 = last(after(x, qkv_keep), gains, dr, w_qkv, act)
+    shares = hold(shares, gg1)
+    gain_rows = jnp.concatenate([gg1, gg2])
+    gain_rows += other_core(gain_rows)
+    gain_rows = lax.dynamic_index_in_dim(gain_rows.reshape(2, 4, 2, cut), core, 2, keepdims=False)
+    gain_columns = jnp.pad(low(gain_rows.transpose(1, 2, 0)), ((0, 0), (0, 0), (0, WIDE - 2)))
     qkv_share = lambda at: sum(wide(rows_at(v, at)) for v in shares)
     qkv_sends = jnp.stack([low(qkv_share(at)) for at in range(4)])
+    qkv_sends = jnp.concatenate([qkv_sends, gain_columns], 2)
     gu_got = after(gu_got, gg1)
     qkv_got = line_all(after(qkv_sends, gu_got))
+    do_got = hold(do_got, gg1)
+    do_upper, do_lower = low(wide(do_upper) + wide(do_got[0])), low(wide(do_lower) + wide(do_got[1]))
+    do_got = [square(after(do_upper, qkv_sends), 2), square(after(do_lower, qkv_sends), 1)]
     s_gu = low(sum(wide(gu_got[n]) for n in range(4)))
     all_gu = [s_gu] + [square(after(s_gu, qkv_sends), r) for r in (1, 2, 3)]
-    gain_rows = after(jnp.concatenate([gg1, gg2]), qkv_sends)
-    gain_rows += other_core(gain_rows)
-    gain_rows += square(gain_rows, 1)
-    gain_rows += square(gain_rows, 2)
-    gain_rows += line(gain_rows, 1)
-    gain_rows += line(gain_rows, 2)
-    gain_rows = lax.dynamic_slice_in_dim(gain_rows, f * cut, cut, 1)
-    all_gu = hold(all_gu, gain_rows)
-    qkv_got = after(qkv_got, gain_rows, *all_gu)
     s_qkv = low(sum(wide(qkv_got[n]) for n in range(4)))
-    all_qkv = [s_qkv] + [square(s_qkv, r) for r in (1, 2, 3)]
-    grad_do = jnp.concatenate([wide(do_upper) + wide(do_got[0]), wide(do_lower) + wide(do_got[1])])
-    grad_g, grad_u = place_gu(where, jnp.stack(hold(all_gu, s_qkv)))
-    grad_q, grad_k, grad_v = place_qkv(where, jnp.stack(all_qkv))
+    all_qkv = lax.all_to_all(jnp.broadcast_to(s_qkv[None], (4, *s_qkv.shape)), "ctx", 0, 0, tiled=True)
+    do_got, all_gu = hold(do_got, s_qkv), hold(all_gu, s_qkv)
+    do_upper, do_lower = wide(do_upper) + wide(do_got[0]), wide(do_lower) + wide(do_got[1])
+    below = 4 * cut_d - half
+    grad_g, grad_u = place_gu(where, all_gu)
+    grad_q, grad_k, grad_v, gain_rows = place_qkv(all_qkv)
     return (
         out[None],
         grad_x[None],
@@ -1162,11 +1174,11 @@
         grad_q,
         grad_k,
         grad_v,
-        grad_do[4 * cut_d :],
+        do_lower[below:],
         gain_rows[1],
         grad_g,
         grad_u,
-        grad_do[: 4 * cut_d],
+        jnp.concatenate([do_upper, do_lower[:below]]),
     )
 
 

time: 511 us -> 504 us (0.986)
  starting transfers between devices: 77.5 us -> 62.9 us
  other arithmetic: 39.5 us -> 31.5 us
  waiting for transfers between devices: 147 us -> 155 us
  local copies, waits for them, and re-layouts: 39 us -> 45.9 us
    ppermute x37 -> x29, waiting for transfers between devices: 131 us -> 89.8 us  [square(): return lax.ppermute(v, 'ctx', [(t, t ^ r) for t in range(4)])]
    all_to_all x6 -> x4, waiting for transfers between devices: 2.62 us -> 30 us  [line_all(): return lax.all_to_all(v, 'fsdp', 0, 0, axis_index_groups=LINES, tiled=True)]
    ppermute x15, waiting for transfers between devices: 8.63 us -> 20.7 us  [other_core(): return lax.ppermute(v, 'fsdp', [(f, f ^ 1) for f in range(8)])]
    all_to_all x6 -> x4, starting transfers between devices: 28.1 us -> 17.8 us  [line_all(): return lax.all_to_all(v, 'fsdp', 0, 0, axis_index_groups=LINES, tiled=True)]
    another operation x5 -> x1, other arithmetic: 9.63 us -> 1.43 us  [square_body(): qkv_all = after(jnp.stack(qkv_parts).reshape(4, 3, cut, -1), own_all[1])]
    unnamed x74 -> x81, local copies, waits for them, and re-layouts: 10.7 us -> 18.7 us
    ppermute x37 -> x29, starting transfers between devices: 40.4 us -> 33 us  [square(): return lax.ppermute(v, 'ctx', [(t, t ^ r) for t in range(4)])]
    pallas_call x2 -> x1, Pallas kernels: 33.2 us -> 30 us  [attend(): pl.pallas_call(attend_kernel, grid_spec=pltpu.PrefetchScalarGridSpec(num_...]
  transfers between devices with their start and end apart: 62 -> 54, of which waited for: 31 -> 31; matrix products, arithmetic and copies ran while one was open for 12% -> 12% of each run, Pallas kernels for 25% -> 25%
where the time goes in v4:
time: 504 us; the launch traced here: 497 us
  Pallas kernels  183 us (36%)
  waiting for transfers between devices  155 us (31%)
  starting transfers between devices  62.9 us (12%)
  local copies, waits for them, and re-layouts  45.9 us (9%)
  other arithmetic  31.5 us (6%)
  between operations  14.8 us (3%)
    ppermute x29, waiting for transfers between devices, square(): return lax.ppermute(v, 'ctx', [(t, t ^ r) for t in range(4)])  89.8 us
    pallas_call x1, Pallas kernels, middle(): pl.pallas_call(middle_kernel, grid_spec=pltpu.PrefetchScalarGridSpec(num_...  53.1 us
    pallas_call x2, Pallas kernels, attend_back(): pl.pallas_call(attend_back_kernel, grid_spec=pltpu.PrefetchScalarGridSpec...  46.7 us
    ppermute x29, starting transfers between devices, square(): return lax.ppermute(v, 'ctx', [(t, t ^ r) for t in range(4)])  33 us
    all_to_all x4, waiting for transfers between devices, line_all(): return lax.all_to_all(v, 'fsdp', 0, 0, axis_index_groups=LINES, tiled=True)  30 us
    pallas_call x1, Pallas kernels, attend(): pl.pallas_call(attend_kernel, grid_spec=pltpu.PrefetchScalarGridSpec(num_...  30 us
    ppermute x15, waiting for transfers between devices, other_core(): return lax.ppermute(v, 'fsdp', [(f, f ^ 1) for f in range(8)])  20.7 us
    unnamed x81, local copies, waits for them, and re-layouts  18.7 us
  transfers between devices with their start and end apart: 54, of which 31 were waited for; matrix products, arithmetic and copies ran while one was open for 12% of the time, Pallas kernels for 25%

profile of v4, /device:TPU:0, one launch (start us, length us, event | category | flops | bytes accessed | tf_op | source)
XLA Modules:
  0.0 497.1 jit_solution(12560204979438922928)
XLA Ops:
  10.0 5.1 %collective-permute-start.2 = (bf16[144,512]{1,0:T(8,128)(2,1)S(1)}, bf16[144,512]{1,0:T(8,128)(2,1)}, u32[]{:S(2)}, u32[]{:S(2)}) collective-permute-start(bf16[144,512]{1,0:T(8,128)(2,1)S(1)} %constant_dynamic-slice_fusion.5), channel_id=1, source_target_pairs={{0,6},{1,7},{2,4},{3,5},{4,2},{5,3},{6,0},{7,1},{8,14},{9,15},{10,... | collective-permute-start | bytes 442376 | tf_op jit(solution)/shard_map/ppermute | solution.py:976
  18.5 1.5 collective-permute-done.2
  20.0 7.7 %collective-permute-done.1 = bf16[144,512]{1,0:T(8,128)(2,1)} collective-permute-done((bf16[144,512]{1,0:T(8,128)(2,1)S(1)}, bf16[144,512]{1,0:T(8,128)(2,1)}, u32[]{:S(2)}, u32[]{:S(2)}) %collective-permute-start.1) | collective-permute-done | bytes 147488 | tf_op jit(solution)/shard_map/ppermute | solution.py:976
  27.7 1.5 broadcast_in_dim.12
  29.2 4.5 all-to-all-start
  39.8 2.5 collective-permute-start.5
  43.4 10.6 %collective-permute-done.5 = bf16[432,512]{1,0:T(8,128)(2,1)S(1)} collective-permute-done((bf16[432,512]{1,0:T(8,128)(2,1)S(1)}, bf16[432,512]{1,0:T(8,128)(2,1)S(1)}, u32[]{:S(2)}, u32[]{:S(2)}) %collective-permute-start.5) | collective-permute-done | bytes 442400 | tf_op jit(solution)/shard_map/ppermute | solution.py:972
  53.9 7.6 %collective-permute-done.4 = bf16[432,512]{1,0:T(8,128)(2,1)S(1)} collective-permute-done((bf16[432,512]{1,0:T(8,128)(2,1)S(1)}, bf16[432,512]{1,0:T(8,128)(2,1)S(1)}, u32[]{:S(2)}, u32[]{:S(2)}) %collective-permute-start.4) | collective-permute-done | bytes 442400 | tf_op jit(solution)/shard_map/ppermute | solution.py:972
  64.5 2.4 collective-permute-done.7.w1_ref
  68.1 8.0 %qkv_project.1 = (bf16[512,1152]{1,0:T(8,128)(2,1)}, bf16[1152,512]{1,0:T(8,128)(2,1)}, bf16[512,1152]{1,0:T(8,128)(2,1)}, bf16[512,768]{1,0:T(8,128)(2,1)}, f32...) custom-call(s32[3]{0:T(128)} %pad_add_fusion.at_ref.where_ref, bf16[512,1152]{1,0:T(8,128)(2,1)} %bitcast.152, ...), custom_call_target="tpu_custom_call" | custom-call | flops 2415919104 | bytes 14155776 | tf_op jit(solution)/shard_map/qkv_project/pallas_call | solution.py:341
  76.2 7.9 %all-to-all-done = bf16[4,144,1920]{2,1,0:T(8,128)(2,1)} async-done(((bf16[4,144,1920]{2,1,0:T(8,128)(2,1)}), bf16[4,144,1920]{2,1,0:T(8,128)(2,1)}, u32[]{:S(2)}, u32[]{:S(2)}) %all-to-all-start) | async-done | bytes 2211872 | tf_op jit(solution)/shard_map/all_to_all | solution.py:999
  84.0 2.0 broadcast_in_dim.13
  86.1 4.7 all-to-all-start.1
  91.0 1.6 collective-permute-start.9
  92.6 1.5 collective-permute-start.8
  95.8 14.1 %collective-permute-done.9 = bf16[512,768]{1,0:T(8,128)(2,1)} collective-permute-done((bf16[512,768]{1,0:T(8,128)(2,1)}, bf16[512,768]{1,0:T(8,128)(2,1)}, u32[]{:S(2)}, u32[]{:S(2)}) %collective-permute-start.9) | collective-permute-done | bytes 786464 | tf_op jit(solution)/shard_map/ppermute | solution.py:972
  110.9 1.6 collective-permute-start.10
  113.5 1.6 collective-permute-start.11
  116.3 1.5 dynamic-slice_bitcast_fusion.2
  120.3 2.3 collective-permute-done.11
  122.5 1.5 collective-permute-start.15
  124.7 1.7 copy-done
  126.3 30.0 %attend.1 = (bf16[512,1152]{1,0:T(8,128)(2,1)}, f32[6,2,1,768]{3,2,1,0:T(1,128)}) custom-call(s32[2]{0:T(128)} %slice_bitcast_fusion.4.own_ref, s32[8]{0:T(128)} %scatter_custom_fusion.slot_ref, bf16[512,1152]{1,0:T(8,128)(2,1)} %get-tuple-element.138.q_ref, bf16[2048,768]{1,0:T(8,128)(2,1)} %copy-done, bf16[2048,768]{1,0:T(8,128)(2,1)} %copy-done), custom_call_target="tpu_custom_call" | custom-call | flops 21743271936 | bytes 5505024 | tf_op jit(solution)/shard_map/attend/pallas_call | solution.py:438
  156.3 1.8 collective-permute-done.15
  162.7 15.0 %collective-permute-done.17 = bf16[216,1920]{1,0:T(8,128)(2,1)S(1)} collective-permute-done((bf16[216,1920]{1,0:T(8,128)(2,1)S(1)}, bf16[216,1920]{1,0:T(8,128)(2,1)S(1)}, u32[]{:S(2)}, u32[]{:S(2)}) %collective-permute-start.17) | collective-permute-done | bytes 829472 | tf_op jit(solution)/shard_map/ppermute | solution.py:972
  180.2 6.6 %collective-permute-done.14.refs_3_ = bf16[3,144,1920]{2,1,0:T(8,128)(2,1)S(1)} collective-permute-done((bf16[3,144,1920]{2,1,0:T(8,128)(2,1)}, bf16[3,144,1920]{2,1,0:T(8,128)(2,1)S(1)}, u32[]{:S(2)}, u32[]{:S(2)}) %collective-permute-start.14) | collective-permute-done | bytes 1658912 | tf_op jit(solution)/shard_map/ppermute | solution.py:980
  186.8 2.4 collective-permute-done.16.refs_5_
  189.3 3.4 collective-permute-done.19.refs_7_
  195.0 53.1 %middle.1 = (bf16[512,1152]{1,0:T(8,128)(2,1)}, bf16[512,1152]{1,0:T(8,128)(2,1)}, bf16[2,576,512]{2,1,0:T(8,128)(2,1)}, bf16[4,768,1152]{2,1,0:T(8,128)(2,1)}, ...) custom-call(s32[3]{0:T(128)} %pad_add_fusion.at_ref.where_ref, ...), custom_call_target="tpu_custom_call" | custom-call | flops 24461180928 | bytes 40108032 | tf_op jit(solution)/shard_map/middle/pallas_call | solution.py:734
  248.1 4.5 convolution_convert_fusion
  256.1 4.8 collective-permute-done.22.l1_ref
  264.2 8.5 %gu_products.2 = (bf16[2,576,768]{2,1,0:T(8,128)(2,1)}, bf16[2,576,768]{2,1,0:T(8,128)(2,1)}) custom-call(bf16[576,512]{1,0:T(8,128)(2,1)} %get-tuple-element.203.l0_ref, bf16[576,512]{1,0:T(8,128)(2,1)} %copy-done.34, bf16[2,512,768]{2,1,0:T(8,128)(2,1)} %get-tuple-element.123.g0_ref, bf16[2,512,768]{2,1,0:T(8,128)(2,1)} %copy-done.32, ...), custom_call_target="tpu_custom_call" | custom-call | flops 3623878656 | bytes 11010048 | tf_op jit(solution)/shard_map/gu_products/pallas_call | solution.py:874
  272.7 1.5 collective-permute-start.28
  275.1 8.6 %gu_products.3 = (bf16[2,576,768]{2,1,0:T(8,128)(2,1)}, bf16[2,576,768]{2,1,0:T(8,128)(2,1)}) custom-call(bf16[576,512]{1,0:T(8,128)(2,1)} %get-tuple-element.203.l0_ref, bf16[576,512]{1,0:T(8,128)(2,1)} %copy-done.34, bf16[2,512,768]{2,1,0:T(8,128)(2,1)} %get-tuple-element.126.g0_ref, bf16[2,512,768]{2,1,0:T(8,128)(2,1)} %collective-permute-done.25.g1_ref, ...), custom_call_target="tpu_custom_call" | custom-call | flops 3623878656 | bytes 11010048 | tf_op jit(solution)/shard_map/gu_products/pallas_call | solution.py:874
  283.8 29.9 %attend_back.2 = (bf16[512,768]{1,0:T(8,128)(2,1)}, bf16[2,4,512,384]{3,2,1,0:T(8,128)(2,1)}) custom-call(s32[2]{0:T(128)} %slice_bitcast_fusion.4.own_ref, s32[8]{0:T(128)} %scatter_custom_fusion.slot_ref, s32[3]{0:T(128)} %pad_add_fusion.at_ref.where_ref, bf16[512,1152]{1,0:T(8,128)(2,1)} %get-tuple-element.138.q_ref, bf16[2048,768]{1,0:T(8,128)(2,1)} %copy-done, ...), custom_call_target="tpu_custom_call" | custom-call | flops 1000 | bytes 1000 | tf_op jit(solution)/shard_map/attend_back/pallas_call | solution.py:528
  315.0 3.2 fusion.2
  320.8 16.8 %attend_back.3 = (bf16[512,384]{1,0:T(8,128)(2,1)}, bf16[2,4,512,384]{3,2,1,0:T(8,128)(2,1)}) custom-call(s32[2]{0:T(128)} %slice_bitcast_fusion.4.own_ref, s32[8]{0:T(128)} %scatter_custom_fusion.slot_ref, s32[3]{0:T(128)} %pad_add_fusion.at_ref.where_ref, bf16[512,1152]{1,0:T(8,128)(2,1)} %get-tuple-element.138.q_ref, ...), custom_call_target="tpu_custom_call", output_to_operand_aliasing={{1}: (11, {})} | custom-call | flops 18119393280 | bytes 3670016 | tf_op jit(solution)/shard_map/attend_back/pallas_call | solution.py:528
  337.6 1.8 collective-permute-done.29
  339.4 1.7 collective-permute-done.30
  341.1 1.5 slice_bitcast_fusion
  344.4 2.2 fusion.15
  348.2 12.2 %collective-permute-done.32.gy_ref = bf16[2,512,384]{2,1,0:T(8,128)(2,1)S(1)} collective-permute-done((bf16[2,512,384]{2,1,0:T(8,128)(2,1)S(1)}, bf16[2,512,384]{2,1,0:T(8,128)(2,1)S(1)}, u32[]{:S(2)}, u32[]{:S(2)}) %collective-permute-start.32) | collective-permute-done | bytes 786464 | tf_op jit(solution)/shard_map/ppermute | solution.py:972
  361.2 2.5 fusion.3
  365.3 4.2 reduce-scatter.3.cloned.1.call-done
  374.1 5.2 %make_act.1.r0_ref.act_ref = bf16[512,2048]{1,0:T(8,128)(2,1)} custom-call(f32[512,128]{1,0:T(8,128)} %copy.49.cos_ref, f32[512,128]{1,0:T(8,128)} %pad_maximum_fusion.7.sin_ref, bf16[2,4,512,384]{3,2,1,0:T(8,128)(2,1)} %get-tuple-element.144.dkv_ref, bf16[2,512,384]{2,1,0:T(8,128)(2,1)} %copy-done.6, bf16[512,384]{1,0:T(8,128)(2,1)} %copy-done.24, ...), custom_call_target="tpu_custom_call" | custom-call | flops 10485760 | bytes 6291456 | tf_op jit(solution)/shard_map/make_act/pallas_call | solution.py:797
  379.3 3.6 all-to-all-start.2
  382.9 2.2 constant_dynamic-slice_fusion.1
  385.6 1.5 collective-permute-start.40
  388.0 7.5 %qkv_products.1 = (bf16[576,512]{1,0:T(8,128)(2,1)}, bf16[576,512]{1,0:T(8,128)(2,1)}, bf16[576,512]{1,0:T(8,128)(2,1)}, bf16[576,512]{1,0:T(8,128)(2,1)}) custom-call(s32[3]{0:T(128)} %pad_add_fusion.at_ref.where_ref, bf16[576,512]{1,0:T(8,128)(2,1)} %bitcast.162, bf16[576,512]{1,0:T(8,128)(2,1)} %copy-done.35, bf16[512,2048]{1,0:T(8,128)(2,1)} %make_act.1.r0_ref.act_ref, ...), custom_call_target="tpu_custom_call" | custom-call | flops 2415919104 | bytes 7733248 | tf_op jit(solution)/shard_map/qkv_products/pallas_call | solution.py:901
  395.6 1.5 collective-permute-start.36
  397.0 1.5 collective-permute-start.37
  399.1 8.5 %last.1 = (bf16[512,1152]{1,0:T(8,128)(2,1)}, f32[1,1152]{1,0:T(1,128)}) custom-call(bf16[512,1152]{1,0:T(8,128)(2,1)} %bitcast.154, f32[8,1152]{1,0:T(8,128)} %get-tuple-element.109.gain_ref, f32[512,1152]{1,0:T(8,128)} %get-tuple-element.152.dr_ref, bf16[1152,2048]{1,0:T(8,128)(2,1)} %get-tuple-element.153.w_ref, bf16[512,2048]{1,0:T(8,128)(2,1)} %make_act.1.r0_ref.act_ref), custom_call_target="tpu_custom_call" | custom-call | flops 2264924160 | bytes 10321920 | tf_op jit(solution)/shard_map/last/pallas_call | solution.py:821
  410.6 14.4 %all-to-all-done.2 = bf16[4,2,144,768]{3,2,1,0:T(8,128)(2,1)S(1)} async-done(((bf16[4,2,144,768]{3,2,1,0:T(8,128)(2,1)}), bf16[4,2,144,768]{3,2,1,0:T(8,128)(2,1)S(1)}, u32[]{:S(2)}, u32[]{:S(2)}) %all-to-all-start.2) | async-done | bytes 1769504 | tf_op jit(solution)/shard_map/all_to_all | solution.py:999
  427.0 1.8 fusion.24
  429.8 5.0 %all-to-all-start.3 = ((bf16[4,144,640]{2,1,0:T(8,128)(2,1)}), bf16[4,144,640]{2,1,0:T(8,128)(2,1)S(1)}, u32[]{:S(2)}, u32[]{:S(2)}) async-start(bf16[4,144,640]{2,1,0:T(8,128)(2,1)} %fusion.5), calls=%async_computation.5 | async-start | bytes 1474560 | tf_op jit(solution)/shard_map/all_to_all | solution.py:999
  434.8 2.0 add_convert_fusion.2
  439.7 1.5 collective-permute-start.46
  442.8 1.5 collective-permute-start.43
  445.7 7.8 %all-to-all-done.3 = bf16[4,144,640]{2,1,0:T(8,128)(2,1)S(1)} async-done(((bf16[4,144,640]{2,1,0:T(8,128)(2,1)}), bf16[4,144,640]{2,1,0:T(8,128)(2,1)S(1)}, u32[]{:S(2)}, u32[]{:S(2)}) %all-to-all-start.3) | async-done | bytes 737312 | tf_op jit(solution)/shard_map/all_to_all | solution.py:999
  453.6 12.0 %collective-permute-done.46 = bf16[256,1152]{1,0:T(8,128)(2,1)} collective-permute-done((bf16[256,1152]{1,0:T(8,128)(2,1)S(1)}, bf16[256,1152]{1,0:T(8,128)(2,1)}, u32[]{:S(2)}, u32[]{:S(2)}) %collective-permute-start.46) | collective-permute-done | bytes 589856 | tf_op jit(solution)/shard_map/ppermute | solution.py:972
  468.0 3.5 all-to-all-start.4
  472.8 6.2 %collective-permute-done.43.p2_ref = bf16[2,144,768]{2,1,0:T(8,128)(2,1)} collective-permute-done((bf16[2,144,768]{2,1,0:T(8,128)(2,1)}, bf16[2,144,768]{2,1,0:T(8,128)(2,1)}, u32[]{:S(2)}, u32[]{:S(2)}) %collective-permute-start.43) | collective-permute-done | bytes 442400 | tf_op jit(solution)/shard_map/ppermute | solution.py:972
  479.1 4.4 place_gu.1
  486.5 2.1 place_qkv.1
  (207 shorter events, 79.0 us)
Async XLA Ops:
  7.2 8.6 %copy-start.16 = (bf16[144,1152]{1,0:T(8,128)(2,1)S(1)}, bf16[144,1152]{1,0:T(8,128)(2,1)}, u32[]{:S(2)}) copy-start(bf16[144,1152]{1,0:T(8,128)(2,1)} %param.18) | copy-start | bytes 995332
  10.0 10.0 %collective-permute-start.2 = (bf16[144,512]{1,0:T(8,128)(2,1)S(1)}, bf16[144,512]{1,0:T(8,128)(2,1)}, u32[]{:S(2)}, u32[]{:S(2)}) collective-permute-start(bf16[144,512]{1,0:T(8,128)(2,1)S(1)} %constant_dynamic-slice_fusion.5), channel_id=1, source_target_pairs={{0,6},{1,7},{2,4},{3,5},{4,2},{5,3},{6,0},{7,1},{8,14},{9,15},{10,... | collective-permute-start | bytes 442376 | tf_op jit(solution)/shard_map/ppermute | solution.py:976
  15.1 12.6 %collective-permute-start.1 = (bf16[144,512]{1,0:T(8,128)(2,1)S(1)}, bf16[144,512]{1,0:T(8,128)(2,1)}, u32[]{:S(2)}, u32[]{:S(2)}) collective-permute-start(bf16[144,512]{1,0:T(8,128)(2,1)S(1)} %constant_dynamic-slice_fusion.5), channel_id=1, source_target_pairs={{0,4},{1,5},{2,6},{3,7},{4,0},{5,1},{6,2},{7,3},{8,12},{9,13},{10,... | collective-permute-start | bytes 442376 | tf_op jit(solution)/shard_map/ppermute | solution.py:976
  15.1 12.6 %collective-permute-start = (bf16[144,512]{1,0:T(8,128)(2,1)S(1)}, bf16[144,512]{1,0:T(8,128)(2,1)}, u32[]{:S(2)}, u32[]{:S(2)}) collective-permute-start(bf16[144,512]{1,0:T(8,128)(2,1)S(1)} %constant_dynamic-slice_fusion.5), channel_id=1, source_target_pairs={{0,2},{1,3},{2,0},{3,1},{4,6},{5,7},{6,4},{7,5},{8,10},{9,11},{10,... | collective-permute-start | bytes 442376 | tf_op jit(solution)/shard_map/ppermute | solution.py:976
  16.1 13.1 %copy-start.1 = (bf16[144,9344]{1,0:T(8,128)(2,1)}, bf16[144,9344]{1,0:T(8,128)(2,1)S(1)}, u32[]{:S(2)}) copy-start(bf16[144,9344]{1,0:T(8,128)(2,1)S(1)} %pad_maximum_fusion.own0_ref.refs_10_) | copy-start | bytes 8073220
  16.1 46.9 %collective-permute-start.6 = (bf16[144,9344]{1,0:T(8,128)(2,1)S(1)}, bf16[144,9344]{1,0:T(8,128)(2,1)}, u32[]{:S(2)}, u32[]{:S(2)}) collective-permute-start(bf16[144,9344]{1,0:T(8,128)(2,1)S(1)} %pad_maximum_fusion.own0_ref.refs_10_), channel_id=1, source_target_pairs={{0,1},{1,0},{2,3},{3,2},{4,5},{5,4},{6,7},{7,6},{8,9},{9,8},{10,11... | collective-permute-start | bytes 8073224 | tf_op jit(solution)/shard_map/ppermute | solution.py:980
  29.2 54.8 %all-to-all-start = ((bf16[4,144,1920]{2,1,0:T(8,128)(2,1)}), bf16[4,144,1920]{2,1,0:T(8,128)(2,1)}, u32[]{:S(2)}, u32[]{:S(2)}) async-start(bf16[4,144,1920]{2,1,0:T(8,128)(2,1)} %broadcast_in_dim.12), calls=%async_computation | async-start | bytes 4423680 | tf_op jit(solution)/shard_map/all_to_all | solution.py:999
  39.8 14.1 %collective-permute-start.5 = (bf16[432,512]{1,0:T(8,128)(2,1)S(1)}, bf16[432,512]{1,0:T(8,128)(2,1)S(1)}, u32[]{:S(2)}, u32[]{:S(2)}) collective-permute-start(bf16[432,512]{1,0:T(8,128)(2,1)S(1)} %constant_dynamic-update-slice_fusion), channel_id=1, source_target_pairs={{0,24},{8,16},{16,8},{24,0},{1,25},{9,17},{17,9},{25,1},{2,26},{10... | collective-permute-start | bytes 1327112 | tf_op jit(solution)/shard_map/ppermute | solution.py:972
  42.3 19.2 %collective-permute-start.4 = (bf16[432,512]{1,0:T(8,128)(2,1)S(1)}, bf16[432,512]{1,0:T(8,128)(2,1)S(1)}, u32[]{:S(2)}, u32[]{:S(2)}) collective-permute-start(bf16[432,512]{1,0:T(8,128)(2,1)S(1)} %constant_dynamic-update-slice_fusion), channel_id=1, source_target_pairs={{0,16},{8,24},{16,0},{24,8},{1,17},{9,25},{17,1},{25,9},{2,18},{10... | collective-permute-start | bytes 1327112 | tf_op jit(solution)/shard_map/ppermute | solution.py:972
  42.8 18.7 %collective-permute-start.3 = (bf16[432,512]{1,0:T(8,128)(2,1)S(1)}, bf16[432,512]{1,0:T(8,128)(2,1)S(1)}, u32[]{:S(2)}, u32[]{:S(2)}) collective-permute-start(bf16[432,512]{1,0:T(8,128)(2,1)S(1)} %constant_dynamic-update-slice_fusion), channel_id=1, source_target_pairs={{0,8},{8,0},{16,24},{24,16},{1,9},{9,1},{17,25},{25,17},{2,10},{10... | collective-permute-start | bytes 1327112 | tf_op jit(solution)/shard_map/ppermute | solution.py:972
  63.0 3.9 collective-permute-start.7
  68.1 15.9 %copy-start.19 = (bf16[384,1152]{1,0:T(8,128)(2,1)S(1)}, bf16[384,1152]{1,0:T(8,128)(2,1)}, u32[]{:S(2)}) copy-start(bf16[384,1152]{1,0:T(8,128)(2,1)} %param.22) | copy-start | bytes 2654212
  86.1 91.9 %all-to-all-start.1 = ((bf16[4,384,1152]{2,1,0:T(8,128)(2,1)}), bf16[4,384,1152]{2,1,0:T(8,128)(2,1)}, u32[]{:S(2)}, u32[]{:S(2)}) async-start(bf16[4,384,1152]{2,1,0:T(8,128)(2,1)} %broadcast_in_dim.13), calls=%async_computation.1 | async-start | bytes 7077888 | tf_op jit(solution)/shard_map/all_to_all | solution.py:999
  90.8 274.5 %reduce-scatter.5.cloned.1.call-start = ((), (), s32[]{:S(2)}) async-start(), calls=%async_computation.8 | async-start | bytes 2985984 | tf_op jit(solution)/shard_map/reduce_scatter | solution.py:1108
  91.0 18.9 %collective-permute-start.9 = (bf16[512,768]{1,0:T(8,128)(2,1)}, bf16[512,768]{1,0:T(8,128)(2,1)}, u32[]{:S(2)}, u32[]{:S(2)}) collective-permute-start(bf16[512,768]{1,0:T(8,128)(2,1)} %get-tuple-element.103), channel_id=1, source_target_pairs={{0,16},{8,24},{16,0},{24,8},{1,17},{9,25},{17,1},{25,9},{2,18},{10... | collective-permute-start | bytes 2359304 | tf_op jit(solution)/shard_map/ppermute | solution.py:972
  92.6 19.9 %collective-permute-start.8 = (bf16[512,768]{1,0:T(8,128)(2,1)}, bf16[512,768]{1,0:T(8,128)(2,1)}, u32[]{:S(2)}, u32[]{:S(2)}) collective-permute-start(bf16[512,768]{1,0:T(8,128)(2,1)} %get-tuple-element.103), channel_id=1, source_target_pairs={{0,8},{8,0},{16,24},{24,16},{1,9},{9,1},{17,25},{25,17},{2,10},{10... | collective-permute-start | bytes 2359304 | tf_op jit(solution)/shard_map/ppermute | solution.py:972
  110.9 9.4 %collective-permute-start.10 = (bf16[256,768]{1,0:T(8,128)(2,1)S(1)}, bf16[256,768]{1,0:T(8,128)(2,1)S(1)}, u32[]{:S(2)}, u32[]{:S(2)}) collective-permute-start(bf16[256,768]{1,0:T(8,128)(2,1)S(1)} %slice.338), channel_id=1, source_target_pairs={{0,8},{8,0},{16,24},{24,16},{1,9},{9,1},{17,25},{25,17},{2,10},{10... | collective-permute-start | bytes 1179656 | tf_op jit(solution)/shard_map/ppermute | solution.py:972
  113.5 9.0 %collective-permute-start.11 = (bf16[256,768]{1,0:T(8,128)(2,1)S(1)}, bf16[256,768]{1,0:T(8,128)(2,1)S(1)}, u32[]{:S(2)}, u32[]{:S(2)}) collective-permute-start(bf16[256,768]{1,0:T(8,128)(2,1)S(1)} %slice.339), channel_id=1, source_target_pairs={{0,16},{8,24},{16,0},{24,8},{1,17},{9,25},{17,1},{25,9},{2,18},{10... | collective-permute-start | bytes 1179656 | tf_op jit(solution)/shard_map/ppermute | solution.py:972
  122.5 35.6 %collective-permute-start.15 = (bf16[432,1920]{1,0:T(8,128)(2,1)}, bf16[432,1920]{1,0:T(8,128)(2,1)}, u32[]{:S(2)}, u32[]{:S(2)}) collective-permute-start(bf16[432,1920]{1,0:T(8,128)(2,1)} %pad_maximum_fusion.3), channel_id=1, source_target_pairs={{0,16},{8,24},{16,0},{24,8},{1,17},{9,25},{17,1},{25,9},{2,18},{10... | collective-permute-start | bytes 4976648 | tf_op jit(solution)/shard_map/ppermute | solution.py:972
  124.0 35.1 %collective-permute-start.13 = (bf16[432,1920]{1,0:T(8,128)(2,1)}, bf16[432,1920]{1,0:T(8,128)(2,1)}, u32[]{:S(2)}, u32[]{:S(2)}) collective-permute-start(bf16[432,1920]{1,0:T(8,128)(2,1)} %pad_maximum_fusion.3), channel_id=1, source_target_pairs={{0,8},{8,0},{16,24},{24,16},{1,9},{9,1},{17,25},{25,17},{2,10},{10... | collective-permute-start | bytes 4976648 | tf_op jit(solution)/shard_map/ppermute | solution.py:972
  161.6 16.2 %collective-permute-start.17 = (bf16[216,1920]{1,0:T(8,128)(2,1)S(1)}, bf16[216,1920]{1,0:T(8,128)(2,1)S(1)}, u32[]{:S(2)}, u32[]{:S(2)}) collective-permute-start(bf16[216,1920]{1,0:T(8,128)(2,1)S(1)} %slice.268), channel_id=1, source_target_pairs={{0,8},{8,0},{16,24},{24,16},{1,9},{9,1},{17,25},{25,17},{2,10},{10... | collective-permute-start | bytes 2488328 | tf_op jit(solution)/shard_map/ppermute | solution.py:972
  162.2 15.8 %collective-permute-start.18 = (bf16[216,1920]{1,0:T(8,128)(2,1)S(1)}, bf16[216,1920]{1,0:T(8,128)(2,1)S(1)}, u32[]{:S(2)}, u32[]{:S(2)}) collective-permute-start(bf16[216,1920]{1,0:T(8,128)(2,1)S(1)} %slice.269), channel_id=1, source_target_pairs={{0,16},{8,24},{16,0},{24,8},{1,17},{9,25},{17,1},{25,9},{2,18},{10... | collective-permute-start | bytes 2488328 | tf_op jit(solution)/shard_map/ppermute | solution.py:972
  162.7 16.2 %collective-permute-start.12 = (bf16[3,144,1920]{2,1,0:T(8,128)(2,1)}, bf16[3,144,1920]{2,1,0:T(8,128)(2,1)}, u32[]{:S(2)}, u32[]{:S(2)}) collective-permute-start(bf16[3,144,1920]{2,1,0:T(8,128)(2,1)} %bitcast.16.refs_0_), channel_id=1, source_target_pairs={{0,1},{1,0},{2,3},{3,2},{4,5},{5,4},{6,7},{7,6},{8,9},{9,8},{10,11... | collective-permute-start | bytes 4976648 | tf_op jit(solution)/shard_map/ppermute | solution.py:980
  178.0 14.7 %collective-permute-start.20 = (bf16[4,384,1152]{2,1,0:T(8,128)(2,1)}, bf16[4,384,1152]{2,1,0:T(8,128)(2,1)S(1)}, u32[]{:S(2)}, u32[]{:S(2)}) collective-permute-start(bf16[4,384,1152]{2,1,0:T(8,128)(2,1)} %all-to-all-done.1.refs_8_), channel_id=1, source_target_pairs={{0,1},{1,0},{2,3},{3,2},{4,5},{5,4},{6,7},{7,6},{8,9},{9,8},{10,11... | collective-permute-start | bytes 10616840 | tf_op jit(solution)/shard_map/ppermute | solution.py:980
  178.0 8.8 %collective-permute-start.14 = (bf16[3,144,1920]{2,1,0:T(8,128)(2,1)}, bf16[3,144,1920]{2,1,0:T(8,128)(2,1)S(1)}, u32[]{:S(2)}, u32[]{:S(2)}) collective-permute-start(bf16[3,144,1920]{2,1,0:T(8,128)(2,1)} %bitcast.17.refs_2_), channel_id=1, source_target_pairs={{0,1},{1,0},{2,3},{3,2},{4,5},{5,4},{6,7},{7,6},{8,9},{9,8},{10,11... | collective-permute-start | bytes 4976648 | tf_op jit(solution)/shard_map/ppermute | solution.py:980
  178.5 10.7 %collective-permute-start.16 = (bf16[3,144,1920]{2,1,0:T(8,128)(2,1)}, bf16[3,144,1920]{2,1,0:T(8,128)(2,1)S(1)}, u32[]{:S(2)}, u32[]{:S(2)}) collective-permute-start(bf16[3,144,1920]{2,1,0:T(8,128)(2,1)} %bitcast.18.refs_4_), channel_id=1, source_target_pairs={{0,1},{1,0},{2,3},{3,2},{4,5},{5,4},{6,7},{7,6},{8,9},{9,8},{10,11... | collective-permute-start | bytes 4976648 | tf_op jit(solution)/shard_map/ppermute | solution.py:980
  180.2 14.8 %copy-start.13 = (bf16[432,1920]{1,0:T(8,128)(2,1)}, bf16[432,1920]{1,0:T(8,128)(2,1)S(1)}, u32[]{:S(2)}) copy-start(bf16[432,1920]{1,0:T(8,128)(2,1)S(1)} %pad_maximum_fusion.4) | copy-start | bytes 4976644
  189.2 3.5 collective-permute-start.19
  195.0 53.1 %copy-start.17 = (bf16[512,1152]{1,0:T(8,128)(2,1)S(1)}, bf16[512,1152]{1,0:T(8,128)(2,1)}, u32[]{:S(2)}) copy-start(bf16[512,1152]{1,0:T(8,128)(2,1)} %get-tuple-element.108.ho_ref.o_ref) | copy-start | bytes 3538948
  252.6 116.9 %reduce-scatter.3.cloned.1.call-start = ((), (), s32[]{:S(2)}) async-start(), calls=%async_computation.7 | async-start | bytes 7962624 | tf_op jit(solution)/shard_map/reduce_scatter | solution.py:1108
  254.1 6.8 %collective-permute-start.23 = (bf16[2,512,768]{2,1,0:T(8,128)(2,1)S(1)}, bf16[2,512,768]{2,1,0:T(8,128)(2,1)S(1)}, u32[]{:S(2)}, u32[]{:S(2)}) collective-permute-start(bf16[2,512,768]{2,1,0:T(8,128)(2,1)S(1)} %copy-done.31), channel_id=1, source_target_pairs={{0,1},{1,0},{2,3},{3,2},{4,5},{5,4},{6,7},{7,6},{8,9},{9,8},{10,11... | collective-permute-start | bytes 4718600 | tf_op jit(solution)/shard_map/ppermute | solution.py:980
  254.2 8.8 %collective-permute-start.24 = (bf16[2,512,768]{2,1,0:T(8,128)(2,1)}, bf16[2,512,768]{2,1,0:T(8,128)(2,1)S(1)}, u32[]{:S(2)}, u32[]{:S(2)}) collective-permute-start(bf16[2,512,768]{2,1,0:T(8,128)(2,1)} %get-tuple-element.124.u0_ref), channel_id=1, source_target_pairs={{0,1},{1,0},{2,3},{3,2},{4,5},{5,4},{6,7},{7,6},{8,9},{9,8},{10,11... | collective-permute-start | bytes 4718600 | tf_op jit(solution)/shard_map/ppermute | solution.py:980
  255.5 5.4 %collective-permute-start.22 = (bf16[576,512]{1,0:T(8,128)(2,1)S(1)}, bf16[576,512]{1,0:T(8,128)(2,1)S(1)}, u32[]{:S(2)}, u32[]{:S(2)}) collective-permute-start(bf16[576,512]{1,0:T(8,128)(2,1)S(1)} %get-tuple-element.202), channel_id=1, source_target_pairs={{0,1},{1,0},{2,3},{3,2},{4,5},{5,4},{6,7},{7,6},{8,9},{9,8},{10,11... | collective-permute-start | bytes 1769480 | tf_op jit(solution)/shard_map/ppermute | solution.py:980
  255.6 19.5 %collective-permute-start.25 = (bf16[2,512,768]{2,1,0:T(8,128)(2,1)}, bf16[2,512,768]{2,1,0:T(8,128)(2,1)}, u32[]{:S(2)}, u32[]{:S(2)}) collective-permute-start(bf16[2,512,768]{2,1,0:T(8,128)(2,1)} %get-tuple-element.126.g0_ref), channel_id=1, source_target_pairs={{0,1},{1,0},{2,3},{3,2},{4,5},{5,4},{6,7},{7,6},{8,9},{9,8},{10,11... | collective-permute-start | bytes 4718600 | tf_op jit(solution)/shard_map/ppermute | solution.py:980
  256.0 19.1 %collective-permute-start.26 = (bf16[2,512,768]{2,1,0:T(8,128)(2,1)}, bf16[2,512,768]{2,1,0:T(8,128)(2,1)}, u32[]{:S(2)}, u32[]{:S(2)}) collective-permute-start(bf16[2,512,768]{2,1,0:T(8,128)(2,1)} %get-tuple-element.128.u0_ref), channel_id=1, source_target_pairs={{0,1},{1,0},{2,3},{3,2},{4,5},{5,4},{6,7},{7,6},{8,9},{9,8},{10,11... | collective-permute-start | bytes 4718600 | tf_op jit(solution)/shard_map/ppermute | solution.py:980
  272.7 41.2 %collective-permute-start.28 = (bf16[2,576,768]{2,1,0:T(8,128)(2,1)}, bf16[2,576,768]{2,1,0:T(8,128)(2,1)}, u32[]{:S(2)}, u32[]{:S(2)}) collective-permute-start(bf16[2,576,768]{2,1,0:T(8,128)(2,1)} %get-tuple-element.125), channel_id=1, source_target_pairs={{0,8},{8,0},{16,24},{24,16},{1,9},{9,1},{17,25},{25,17},{2,10},{10... | collective-permute-start | bytes 5308424 | tf_op jit(solution)/shard_map/ppermute | solution.py:972
  274.2 40.8 %collective-permute-start.27 = (bf16[2,576,768]{2,1,0:T(8,128)(2,1)}, bf16[2,576,768]{2,1,0:T(8,128)(2,1)S(1)}, u32[]{:S(2)}, u32[]{:S(2)}) collective-permute-start(bf16[2,576,768]{2,1,0:T(8,128)(2,1)} %get-tuple-element.130), channel_id=1, source_target_pairs={{0,16},{8,24},{16,0},{24,8},{1,17},{9,25},{17,1},{25,9},{2,18},{10... | collective-permute-start | bytes 5308424 | tf_op jit(solution)/shard_map/ppermute | solution.py:972
  318.2 21.2 %collective-permute-start.29 = (bf16[576,768]{1,0:T(8,128)(2,1)}, bf16[576,768]{1,0:T(8,128)(2,1)}, u32[]{:S(2)}, u32[]{:S(2)}) collective-permute-start(bf16[576,768]{1,0:T(8,128)(2,1)} %fusion.2), channel_id=1, source_target_pairs={{0,16},{8,24},{16,0},{24,8},{1,17},{9,25},{17,1},{25,9},{2,18},{10... | collective-permute-start | bytes 2654216 | tf_op jit(solution)/shard_map/ppermute | solution.py:972
  320.3 20.8 %collective-permute-start.30 = (bf16[576,768]{1,0:T(8,128)(2,1)}, bf16[576,768]{1,0:T(8,128)(2,1)S(1)}, u32[]{:S(2)}, u32[]{:S(2)}) collective-permute-start(bf16[576,768]{1,0:T(8,128)(2,1)} %fusion.1), channel_id=1, source_target_pairs={{0,8},{8,0},{16,24},{24,16},{1,9},{9,1},{17,25},{25,17},{2,10},{10... | collective-permute-start | bytes 2654216 | tf_op jit(solution)/shard_map/ppermute | solution.py:972
  342.6 17.8 %collective-permute-start.32 = (bf16[2,512,384]{2,1,0:T(8,128)(2,1)S(1)}, bf16[2,512,384]{2,1,0:T(8,128)(2,1)S(1)}, u32[]{:S(2)}, u32[]{:S(2)}) collective-permute-start(bf16[2,512,384]{2,1,0:T(8,128)(2,1)S(1)} %get-tuple-element.193), channel_id=1, source_target_pairs={{0,16},{8,24},{16,0},{24,8},{1,17},{9,25},{17,1},{25,9},{2,18},{10... | collective-permute-start | bytes 2359304 | tf_op jit(solution)/shard_map/ppermute | solution.py:972
  343.8 17.4 %collective-permute-start.31 = (bf16[2,512,384]{2,1,0:T(8,128)(2,1)S(1)}, bf16[2,512,384]{2,1,0:T(8,128)(2,1)S(1)}, u32[]{:S(2)}, u32[]{:S(2)}) collective-permute-start(bf16[2,512,384]{2,1,0:T(8,128)(2,1)S(1)} %get-tuple-element.194), channel_id=1, source_target_pairs={{0,8},{8,0},{16,24},{24,16},{1,9},{9,1},{17,25},{25,17},{2,10},{10... | collective-permute-start | bytes 2359304 | tf_op jit(solution)/shard_map/ppermute | solution.py:972
  360.4 10.4 %copy-start.5 = (bf16[2,512,384]{2,1,0:T(8,128)(2,1)}, bf16[2,512,384]{2,1,0:T(8,128)(2,1)S(1)}, u32[]{:S(2)}) copy-start(bf16[2,512,384]{2,1,0:T(8,128)(2,1)S(1)} %collective-permute-done.32.gy_ref) | copy-start | bytes 2359300
  361.2 9.5 %copy-start.6 = (bf16[2,512,384]{2,1,0:T(8,128)(2,1)}, bf16[2,512,384]{2,1,0:T(8,128)(2,1)S(1)}, u32[]{:S(2)}) copy-start(bf16[2,512,384]{2,1,0:T(8,128)(2,1)S(1)} %collective-permute-done.31.gx_ref) | copy-start | bytes 2359300
  363.7 8.9 %collective-permute-start.34 = (bf16[512,384]{1,0:T(8,128)(2,1)}, bf16[512,384]{1,0:T(8,128)(2,1)S(1)}, u32[]{:S(2)}, u32[]{:S(2)}) collective-permute-start(bf16[512,384]{1,0:T(8,128)(2,1)} %get-tuple-element.191), channel_id=1, source_target_pairs={{0,8},{8,0},{16,24},{24,16},{1,9},{9,1},{17,25},{25,17},{2,10},{10... | collective-permute-start | bytes 1179656 | tf_op jit(solution)/shard_map/ppermute | solution.py:972
  364.3 8.3 %collective-permute-start.33 = (bf16[512,384]{1,0:T(8,128)(2,1)}, bf16[512,384]{1,0:T(8,128)(2,1)S(1)}, u32[]{:S(2)}, u32[]{:S(2)}) collective-permute-start(bf16[512,384]{1,0:T(8,128)(2,1)} %get-tuple-element.192), channel_id=1, source_target_pairs={{0,16},{8,24},{16,0},{24,8},{1,17},{9,25},{17,1},{25,9},{2,18},{10... | collective-permute-start | bytes 1179656 | tf_op jit(solution)/shard_map/ppermute | solution.py:972
  379.3 7.9 %collective-permute-start.35 = (bf16[512,2048]{1,0:T(8,128)(2,1)}, bf16[512,2048]{1,0:T(8,128)(2,1)}, u32[]{:S(2)}, u32[]{:S(2)}) collective-permute-start(bf16[512,2048]{1,0:T(8,128)(2,1)} %make_act.1.r0_ref.act_ref), channel_id=1, source_target_pairs={{0,1},{1,0},{2,3},{3,2},{4,5},{5,4},{6,7},{7,6},{8,9},{9,8},{10,11... | collective-permute-start | bytes 6291464 | tf_op jit(solution)/shard_map/ppermute | solution.py:980
  379.3 45.7 %all-to-all-start.2 = ((bf16[4,2,144,768]{3,2,1,0:T(8,128)(2,1)}), bf16[4,2,144,768]{3,2,1,0:T(8,128)(2,1)S(1)}, u32[]{:S(2)}, u32[]{:S(2)}) async-start(bf16[4,2,144,768]{3,2,1,0:T(8,128)(2,1)} %maximum_maximum_fusion), calls=%async_computation.4 | async-start | bytes 3538944 | tf_op jit(solution)/shard_map/all_to_all | solution.py:999
  385.1 2.1 collective-permute-start.21
  385.6 22.7 %collective-permute-start.40 = (bf16[272,1152]{1,0:T(8,128)(2,1)S(1)}, bf16[272,1152]{1,0:T(8,128)(2,1)S(1)}, u32[]{:S(2)}, u32[]{:S(2)}) collective-permute-start(bf16[272,1152]{1,0:T(8,128)(2,1)S(1)} %pad_maximum_fusion.5), channel_id=1, source_target_pairs={{0,16},{8,24},{16,0},{24,8},{1,17},{9,25},{17,1},{25,9},{2,18},{10... | collective-permute-start | bytes 1880072 | tf_op jit(solution)/shard_map/ppermute | solution.py:972
  395.6 30.5 %collective-permute-start.36 = (bf16[576,512]{1,0:T(8,128)(2,1)}, bf16[576,512]{1,0:T(8,128)(2,1)}, u32[]{:S(2)}, u32[]{:S(2)}) collective-permute-start(bf16[576,512]{1,0:T(8,128)(2,1)} %get-tuple-element.157), channel_id=1, source_target_pairs={{0,8},{8,0},{16,24},{24,16},{1,9},{9,1},{17,25},{25,17},{2,10},{10... | collective-permute-start | bytes 1769480 | tf_op jit(solution)/shard_map/ppermute | solution.py:972
  397.0 30.0 %collective-permute-start.37 = (bf16[576,512]{1,0:T(8,128)(2,1)}, bf16[576,512]{1,0:T(8,128)(2,1)}, u32[]{:S(2)}, u32[]{:S(2)}) collective-permute-start(bf16[576,512]{1,0:T(8,128)(2,1)} %get-tuple-element.159), channel_id=1, source_target_pairs={{0,16},{8,24},{16,0},{24,8},{1,17},{9,25},{17,1},{25,9},{2,18},{10... | collective-permute-start | bytes 1769480 | tf_op jit(solution)/shard_map/ppermute | solution.py:972
  398.5 28.5 %collective-permute-start.38 = (bf16[576,512]{1,0:T(8,128)(2,1)}, bf16[576,512]{1,0:T(8,128)(2,1)}, u32[]{:S(2)}, u32[]{:S(2)}) collective-permute-start(bf16[576,512]{1,0:T(8,128)(2,1)} %get-tuple-element.161), channel_id=1, source_target_pairs={{0,24},{8,16},{16,8},{24,0},{1,25},{9,17},{17,9},{25,1},{2,26},{10... | collective-permute-start | bytes 1769480 | tf_op jit(solution)/shard_map/ppermute | solution.py:972
  399.1 8.5 %copy-start.25 = (f32[1,1152]{1,0:T(1,128)S(1)}, f32[1,1152]{1,0:T(1,128)}, u32[]{:S(2)}) copy-start(f32[1,1152]{1,0:T(1,128)} %get-tuple-element.163) | copy-start | bytes 13828
  399.1 28.0 %copy-start.22 = (bf16[576,512]{1,0:T(8,128)(2,1)S(1)}, bf16[576,512]{1,0:T(8,128)(2,1)}, u32[]{:S(2)}) copy-start(bf16[576,512]{1,0:T(8,128)(2,1)} %get-tuple-element.156) | copy-start | bytes 1769476
  408.2 16.8 %collective-permute-start.39 = (f32[2,1152]{1,0:T(2,128)S(1)}, f32[2,1152]{1,0:T(2,128)S(1)}, u32[]{:S(2)}, u32[]{:S(2)}) collective-permute-start(f32[2,1152]{1,0:T(2,128)S(1)} %pad_maximum_fusion.8), channel_id=1, source_target_pairs={{0,1},{1,0},{2,3},{3,2},{4,5},{5,4},{6,7},{7,6},{8,9},{9,8},{10,11... | collective-permute-start | bytes 27656 | tf_op jit(solution)/shard_map/ppermute | solution.py:980
  409.2 27.7 %collective-permute-start.45 = (bf16[256,1152]{1,0:T(8,128)(2,1)}, bf16[256,1152]{1,0:T(8,128)(2,1)}, u32[]{:S(2)}, u32[]{:S(2)}) collective-permute-start(bf16[256,1152]{1,0:T(8,128)(2,1)} %slice.340), channel_id=1, source_target_pairs={{0,8},{8,0},{16,24},{24,16},{1,9},{9,1},{17,25},{25,17},{2,10},{10... | collective-permute-start | bytes 1769480 | tf_op jit(solution)/shard_map/ppermute | solution.py:972
  429.8 23.7 %all-to-all-start.3 = ((bf16[4,144,640]{2,1,0:T(8,128)(2,1)}), bf16[4,144,640]{2,1,0:T(8,128)(2,1)S(1)}, u32[]{:S(2)}, u32[]{:S(2)}) async-start(bf16[4,144,640]{2,1,0:T(8,128)(2,1)} %fusion.5), calls=%async_computation.5 | async-start | bytes 1474560 | tf_op jit(solution)/shard_map/all_to_all | solution.py:999
  436.9 28.8 %collective-permute-start.41 = (bf16[272,1152]{1,0:T(8,128)(2,1)}, bf16[272,1152]{1,0:T(8,128)(2,1)}, u32[]{:S(2)}, u32[]{:S(2)}) collective-permute-start(bf16[272,1152]{1,0:T(8,128)(2,1)} %add_convert_fusion.2), channel_id=1, source_target_pairs={{0,8},{8,0},{16,24},{24,16},{1,9},{9,1},{17,25},{25,17},{2,10},{10... | collective-permute-start | bytes 1880072 | tf_op jit(solution)/shard_map/ppermute | solution.py:972
  439.7 25.9 %copy-start.4 = (bf16[256,1152]{1,0:T(8,128)(2,1)}, bf16[256,1152]{1,0:T(8,128)(2,1)S(1)}, u32[]{:S(2)}) copy-start(bf16[256,1152]{1,0:T(8,128)(2,1)S(1)} %add_convert_fusion.3) | copy-start | bytes 1769476
  439.7 25.9 %collective-permute-start.46 = (bf16[256,1152]{1,0:T(8,128)(2,1)S(1)}, bf16[256,1152]{1,0:T(8,128)(2,1)}, u32[]{:S(2)}, u32[]{:S(2)}) collective-permute-start(bf16[256,1152]{1,0:T(8,128)(2,1)S(1)} %add_convert_fusion.3), channel_id=1, source_target_pairs={{0,16},{8,24},{16,0},{24,8},{1,17},{9,25},{17,1},{25,9},{2,18},{10... | collective-permute-start | bytes 1769480 | tf_op jit(solution)/shard_map/ppermute | solution.py:972
  442.2 30.6 %collective-permute-start.44 = (bf16[2,144,768]{2,1,0:T(8,128)(2,1)}, bf16[2,144,768]{2,1,0:T(8,128)(2,1)}, u32[]{:S(2)}, u32[]{:S(2)}) collective-permute-start(bf16[2,144,768]{2,1,0:T(8,128)(2,1)} %fusion.6.p0_ref), channel_id=1, source_target_pairs={{0,24},{8,16},{16,8},{24,0},{1,25},{9,17},{17,9},{25,1},{2,26},{10... | collective-permute-start | bytes 1327112 | tf_op jit(solution)/shard_map/ppermute | solution.py:972
  442.8 36.3 %collective-permute-start.43 = (bf16[2,144,768]{2,1,0:T(8,128)(2,1)}, bf16[2,144,768]{2,1,0:T(8,128)(2,1)}, u32[]{:S(2)}, u32[]{:S(2)}) collective-permute-start(bf16[2,144,768]{2,1,0:T(8,128)(2,1)} %fusion.6.p0_ref), channel_id=1, source_target_pairs={{0,16},{8,24},{16,0},{24,8},{1,17},{9,25},{17,1},{25,9},{2,18},{10... | collective-permute-start | bytes 1327112 | tf_op jit(solution)/shard_map/ppermute | solution.py:972
  444.3 34.8 %collective-permute-start.42 = (bf16[2,144,768]{2,1,0:T(8,128)(2,1)}, bf16[2,144,768]{2,1,0:T(8,128)(2,1)}, u32[]{:S(2)}, u32[]{:S(2)}) collective-permute-start(bf16[2,144,768]{2,1,0:T(8,128)(2,1)} %fusion.6.p0_ref), channel_id=1, source_target_pairs={{0,8},{8,0},{16,24},{24,16},{1,9},{9,1},{17,25},{25,17},{2,10},{10... | collective-permute-start | bytes 1327112 | tf_op jit(solution)/shard_map/ppermute | solution.py:972
  468.0 17.7 %all-to-all-start.4 = ((bf16[4,144,640]{2,1,0:T(8,128)(2,1)}), bf16[4,144,640]{2,1,0:T(8,128)(2,1)S(1)}, u32[]{:S(2)}, u32[]{:S(2)}) async-start(bf16[4,144,640]{2,1,0:T(8,128)(2,1)} %broadcast_in_dim.17), calls=%async_computation.6 | async-start | bytes 1474560 | tf_op jit(solution)/shard_map/all_to_all | solution.py:1164
  (26 other events, 66.4 us)
Sparse Core Ops, SparseCore 0:
  252.8 37.4 reduce-scatter.4
  292.6 76.8 reduce-scatter.2

commit v5 on v4

--- a/solution.py
+++ b/solution.py
@@ -999,10 +999,6 @@
     return lax.all_to_all(v, "fsdp", 0, 0, axis_index_groups=LINES, tiled=True)
 
 
-def line_spread(v):
-    return line_all(jnp.broadcast_to(v[None], (4, *v.shape)))
-
-
 def far_pieces(got, z):
     return [lax.dynamic_index_in_dim(got, z ^ k, 0, keepdims=False) for k in (1, 2, 3)]
 
@@ -1073,8 +1069,11 @@
     qkv_slice = slice_of(qkv_own)
     qkv_line = [line(qkv_slice, k) for k in (1, 2, 3)]
     own_all = swap(jnp.concatenate([qkv_own, w_gate, w_up, w_out], 1))
-    qkv_rows = jnp.concatenate(hold(qkv_line, cosine, sine, slots, guo_part))
-    guo_line = line_spread(after(guo_part, *qkv_line))
+    spread = lambda v: jnp.broadcast_to(v[None], (4, *v.shape))
+    d_spread, guo_spread = hold([spread(w_down), spread(guo_part)])
+    qkv_line = hold(qkv_line, cosine, sine, slots, d_spread, guo_spread)
+    qkv_rows = jnp.concatenate(qkv_line)
+    guo_line = line_all(after(guo_spread, *qkv_line))
     qkv_parts = [qkv_rows] + [square(qkv_rows, r) for r in (1, 2, 3)]
     qkv_all = after(jnp.stack(qkv_parts).reshape(4, 3, cut, -1), own_all[1])
     qkv_both = swap(qkv_all)
@@ -1082,7 +1081,7 @@
     a, a_t, q, kv_own, gains, w_qkv = qkv_project(where, x, cosine, sine, qkv_both, own_all)
     kv_near = square_near(kv_own)
     guo_line = after(guo_line, kv_own)
-    d_line = line_all(after(jnp.broadcast_to(w_down[None], (4, *w_down.shape)), guo_line))
+    d_line = line_all(after(d_spread, guo_line))
     kv_far = square_far(*kv_near)
     guo_rows = after(jnp.concatenate(far_pieces(after(guo_line, *kv_near), z)), *kv_far)
     guo_near = square_near(guo_rows)
@@ -1137,12 +1136,12 @@
     half = grad_do.shape[0] // 32 * 16
     do_upper, do_lower = hold([grad_do[:half], grad_do[half:]], kv_x, kv_y)
     do_got = [square(do_upper, 1), square(do_lower, 2)]
-    act = make_act(after(cosine, do_upper, do_lower), sine, [dkv, kv_x, kv_last_y, kv_y, kv_last_x], [dq_0, dq_1], (1, 2), filled)
+    a_mine, a_other = lanes(a_t, core)
+    a_both = (a_mine, other_core(a_other))
+    act = make_act(after(cosine, do_upper, do_lower, *a_both), sine, [dkv, kv_x, kv_last_y, kv_y, kv_last_x], [dq_0, dq_1], (1, 2), filled)
     acts = swap(act)
 
-    a_mine, a_other = lanes(a_t, core)
-    left = (a_mine, other_core(a_other))
-    qkv_keep, *qkv_sends = qkv_products(where, left, acts)
+    qkv_keep, *qkv_sends = qkv_products(where, a_both, acts)
     shares = [qkv_keep] + [square(v, r) for r, v in zip((1, 2, 3), qkv_sends)]
     grad_x, gg1 = last(after(x, qkv_keep), gains, dr, w_qkv, act)
     shares = hold(shares, gg1)

time: 504 us -> 503 us (level)
    ppermute x3, waiting for transfers between devices: 9.25 us -> 0.3 us  [line(): return lax.ppermute(v, 'fsdp', [(f, f ^ 2 * k) for f in range(8)])]
    all_to_all x4, waiting for transfers between devices: 30 us -> 38.8 us  [line_all(): return lax.all_to_all(v, 'fsdp', 0, 0, axis_index_groups=LINES, tiled=True)]
    unnamed x81 -> x85, local copies, waits for them, and re-layouts: 18.7 us -> 16.6 us
  transfers between devices with their start and end apart: 54 -> 54, of which waited for: 31 -> 29; matrix products, arithmetic and copies ran while one was open for 12% -> 13% of each run, Pallas kernels for 25% -> 25%
where the time goes in v5:
time: 503 us; the launch traced here: 496 us
  Pallas kernels  182 us (36%)
  waiting for transfers between devices  157 us (31%)
  starting transfers between devices  59.4 us (12%)
  local copies, waits for them, and re-layouts  45 us (9%)
  other arithmetic  32.8 us (7%)
  between operations  14.8 us (3%)
    ppermute x29, waiting for transfers between devices, square(): return lax.ppermute(v, 'ctx', [(t, t ^ r) for t in range(4)])  93.4 us
    pallas_call x1, Pallas kernels, middle(): pl.pallas_call(middle_kernel, grid_spec=pltpu.PrefetchScalarGridSpec(num_...  53.1 us
    pallas_call x2, Pallas kernels, attend_back(): pl.pallas_call(attend_back_kernel, grid_spec=pltpu.PrefetchScalarGridSpec...  46.6 us
    all_to_all x4, waiting for transfers between devices, line_all(): return lax.all_to_all(v, 'fsdp', 0, 0, axis_index_groups=LINES, tiled=True)  38.8 us
    ppermute x29, starting transfers between devices, square(): return lax.ppermute(v, 'ctx', [(t, t ^ r) for t in range(4)])  31 us
    pallas_call x1, Pallas kernels, attend(): pl.pallas_call(attend_kernel, grid_spec=pltpu.PrefetchScalarGridSpec(num_...  30 us
    ppermute x15, waiting for transfers between devices, other_core(): return lax.ppermute(v, 'fsdp', [(f, f ^ 1) for f in range(8)])  21.7 us
    pallas_call x2, Pallas kernels, gu_products(): pl.pallas_call(gu_products_kernel, grid=(2, 2, cuts), in_specs=[spec, spe...  17.1 us
  transfers between devices with their start and end apart: 54, of which 29 were waited for; matrix products, arithmetic and copies ran while one was open for 13% of the time, Pallas kernels for 25%

profile of v5, /device:TPU:0, one launch (start us, length us, event | category | flops | bytes accessed | tf_op | source)
XLA Modules:
  0.0 495.8 jit_solution(5864774499735361157)
XLA Ops:
  10.6 5.0 %collective-permute-start.2 = (bf16[144,512]{1,0:T(8,128)(2,1)}, bf16[144,512]{1,0:T(8,128)(2,1)}, u32[]{:S(2)}, u32[]{:S(2)}) collective-permute-start(bf16[144,512]{1,0:T(8,128)(2,1)} %constant_dynamic-slice_fusion.5), channel_id=1, source_target_pairs={{0,6},{1,7},{2,4},{3,5},{4,2},{5,3},{6,0},{7,1},{8,14},{9,15},{10,... | collective-permute-start | bytes 442376 | tf_op jit(solution)/shard_map/ppermute | solution.py:976
  19.0 1.8 fusion.28
  20.9 1.7 copy.41
  22.6 1.5 broadcast_in_dim.13
  24.0 2.0 broadcast_in_dim.12
  28.5 4.8 all-to-all-start
  36.1 2.5 collective-permute-start.5
  39.7 10.5 %collective-permute-done.5 = bf16[432,512]{1,0:T(8,128)(2,1)S(1)} collective-permute-done((bf16[432,512]{1,0:T(8,128)(2,1)S(1)}, bf16[432,512]{1,0:T(8,128)(2,1)S(1)}, u32[]{:S(2)}, u32[]{:S(2)}) %collective-permute-start.5) | collective-permute-done | bytes 442400 | tf_op jit(solution)/shard_map/ppermute | solution.py:972
  50.2 8.3 %collective-permute-done.4 = bf16[432,512]{1,0:T(8,128)(2,1)S(1)} collective-permute-done((bf16[432,512]{1,0:T(8,128)(2,1)S(1)}, bf16[432,512]{1,0:T(8,128)(2,1)S(1)}, u32[]{:S(2)}, u32[]{:S(2)}) %collective-permute-start.4) | collective-permute-done | bytes 442400 | tf_op jit(solution)/shard_map/ppermute | solution.py:972
  58.6 1.4 pad_maximum_fusion.1.w0_ref
  61.6 2.4 collective-permute-done.7.w1_ref
  65.1 7.9 %qkv_project.1 = (bf16[512,1152]{1,0:T(8,128)(2,1)}, bf16[1152,512]{1,0:T(8,128)(2,1)}, bf16[512,1152]{1,0:T(8,128)(2,1)}, bf16[512,768]{1,0:T(8,128)(2,1)}, f32...) custom-call(s32[3]{0:T(128)} %pad_add_fusion.at_ref.where_ref, bf16[512,1152]{1,0:T(8,128)(2,1)} %bitcast.152, ...), custom_call_target="tpu_custom_call" | custom-call | flops 2415919104 | bytes 14155776 | tf_op jit(solution)/shard_map/qkv_project/pallas_call | solution.py:341
  73.1 11.3 %all-to-all-done = bf16[4,144,1920]{2,1,0:T(8,128)(2,1)} async-done(((bf16[4,144,1920]{2,1,0:T(8,128)(2,1)}), bf16[4,144,1920]{2,1,0:T(8,128)(2,1)}, u32[]{:S(2)}, u32[]{:S(2)}) %all-to-all-start) | async-done | bytes 2211872 | tf_op jit(solution)/shard_map/all_to_all | solution.py:999
  84.4 4.7 all-to-all-start.1
  89.4 1.6 collective-permute-start.9
  91.0 1.5 collective-permute-start.8
  94.1 14.2 %collective-permute-done.9 = bf16[512,768]{1,0:T(8,128)(2,1)} collective-permute-done((bf16[512,768]{1,0:T(8,128)(2,1)}, bf16[512,768]{1,0:T(8,128)(2,1)}, u32[]{:S(2)}, u32[]{:S(2)}) %collective-permute-start.9) | collective-permute-done | bytes 786464 | tf_op jit(solution)/shard_map/ppermute | solution.py:972
  109.3 1.6 collective-permute-start.10
  111.9 1.6 collective-permute-start.11
  114.7 1.5 dynamic-slice_bitcast_fusion.2
  118.7 2.3 collective-permute-done.11
  120.9 1.5 collective-permute-start.15
  123.1 1.7 copy-done
  124.7 30.0 %attend.1 = (bf16[512,1152]{1,0:T(8,128)(2,1)}, f32[6,2,1,768]{3,2,1,0:T(1,128)}) custom-call(s32[2]{0:T(128)} %slice_bitcast_fusion.4.own_ref, s32[8]{0:T(128)} %scatter_custom_fusion.slot_ref, bf16[512,1152]{1,0:T(8,128)(2,1)} %get-tuple-element.138.q_ref, bf16[2048,768]{1,0:T(8,128)(2,1)} %copy-done, bf16[2048,768]{1,0:T(8,128)(2,1)} %copy-done), custom_call_target="tpu_custom_call" | custom-call | flops 21743271936 | bytes 5505024 | tf_op jit(solution)/shard_map/attend/pallas_call | solution.py:438
  154.8 1.8 collective-permute-done.15
  161.2 15.2 %collective-permute-done.17 = bf16[216,1920]{1,0:T(8,128)(2,1)S(1)} collective-permute-done((bf16[216,1920]{1,0:T(8,128)(2,1)S(1)}, bf16[216,1920]{1,0:T(8,128)(2,1)S(1)}, u32[]{:S(2)}, u32[]{:S(2)}) %collective-permute-start.17) | collective-permute-done | bytes 829472 | tf_op jit(solution)/shard_map/ppermute | solution.py:972
  178.8 6.6 %collective-permute-done.14.refs_3_ = bf16[3,144,1920]{2,1,0:T(8,128)(2,1)S(1)} collective-permute-done((bf16[3,144,1920]{2,1,0:T(8,128)(2,1)}, bf16[3,144,1920]{2,1,0:T(8,128)(2,1)S(1)}, u32[]{:S(2)}, u32[]{:S(2)}) %collective-permute-start.14) | collective-permute-done | bytes 1658912 | tf_op jit(solution)/shard_map/ppermute | solution.py:980
  185.5 2.4 collective-permute-done.16.refs_5_
  188.0 3.4 collective-permute-done.19.refs_7_
  193.6 53.1 %middle.1 = (bf16[512,1152]{1,0:T(8,128)(2,1)}, bf16[512,1152]{1,0:T(8,128)(2,1)}, bf16[2,576,512]{2,1,0:T(8,128)(2,1)}, bf16[4,768,1152]{2,1,0:T(8,128)(2,1)}, ...) custom-call(s32[3]{0:T(128)} %pad_add_fusion.at_ref.where_ref, ...), custom_call_target="tpu_custom_call" | custom-call | flops 24461180928 | bytes 40108032 | tf_op jit(solution)/shard_map/middle/pallas_call | solution.py:734
  246.7 4.5 convolution_convert_fusion
  254.8 4.7 collective-permute-done.22.l1_ref
  259.5 2.2 collective-permute-done.24.u1_ref
  262.9 8.6 %gu_products.2 = (bf16[2,576,768]{2,1,0:T(8,128)(2,1)}, bf16[2,576,768]{2,1,0:T(8,128)(2,1)}) custom-call(bf16[576,512]{1,0:T(8,128)(2,1)} %get-tuple-element.203.l0_ref, bf16[576,512]{1,0:T(8,128)(2,1)} %copy-done.37, bf16[2,512,768]{2,1,0:T(8,128)(2,1)} %get-tuple-element.123.g0_ref, bf16[2,512,768]{2,1,0:T(8,128)(2,1)} %copy-done.35, ...), custom_call_target="tpu_custom_call" | custom-call | flops 3623878656 | bytes 11010048 | tf_op jit(solution)/shard_map/gu_products/pallas_call | solution.py:874
  271.5 1.5 collective-permute-start.28
  274.9 8.5 %gu_products.3 = (bf16[2,576,768]{2,1,0:T(8,128)(2,1)}, bf16[2,576,768]{2,1,0:T(8,128)(2,1)}) custom-call(bf16[576,512]{1,0:T(8,128)(2,1)} %get-tuple-element.203.l0_ref, bf16[576,512]{1,0:T(8,128)(2,1)} %copy-done.37, bf16[2,512,768]{2,1,0:T(8,128)(2,1)} %get-tuple-element.126.g0_ref, bf16[2,512,768]{2,1,0:T(8,128)(2,1)} %collective-permute-done.25.g1_ref, ...), custom_call_target="tpu_custom_call" | custom-call | flops 3623878656 | bytes 11010048 | tf_op jit(solution)/shard_map/gu_products/pallas_call | solution.py:874
  283.4 29.9 %attend_back.2 = (bf16[512,768]{1,0:T(8,128)(2,1)}, bf16[2,4,512,384]{3,2,1,0:T(8,128)(2,1)}) custom-call(s32[2]{0:T(128)} %slice_bitcast_fusion.4.own_ref, s32[8]{0:T(128)} %scatter_custom_fusion.slot_ref, s32[3]{0:T(128)} %pad_add_fusion.at_ref.where_ref, bf16[512,1152]{1,0:T(8,128)(2,1)} %get-tuple-element.138.q_ref, bf16[2048,768]{1,0:T(8,128)(2,1)} %copy-done, ...), custom_call_target="tpu_custom_call" | custom-call | flops 1000 | bytes 1000 | tf_op jit(solution)/shard_map/attend_back/pallas_call | solution.py:528
  313.8 3.3 fusion.2
  319.6 16.8 %attend_back.3 = (bf16[512,384]{1,0:T(8,128)(2,1)}, bf16[2,4,512,384]{3,2,1,0:T(8,128)(2,1)}) custom-call(s32[2]{0:T(128)} %slice_bitcast_fusion.4.own_ref, s32[8]{0:T(128)} %scatter_custom_fusion.slot_ref, s32[3]{0:T(128)} %pad_add_fusion.at_ref.where_ref, bf16[512,1152]{1,0:T(8,128)(2,1)} %get-tuple-element.138.q_ref, ...), custom_call_target="tpu_custom_call", output_to_operand_aliasing={{1}: (11, {})} | custom-call | flops 18119393280 | bytes 3670016 | tf_op jit(solution)/shard_map/attend_back/pallas_call | solution.py:528
  336.3 2.6 collective-permute-done.29
  338.9 2.1 collective-permute-done.30
  341.0 1.5 slice_bitcast_fusion
  343.9 2.2 fusion.15
  347.8 13.7 %collective-permute-done.32.gy_ref = bf16[2,512,384]{2,1,0:T(8,128)(2,1)S(1)} collective-permute-done((bf16[2,512,384]{2,1,0:T(8,128)(2,1)S(1)}, bf16[2,512,384]{2,1,0:T(8,128)(2,1)S(1)}, u32[]{:S(2)}, u32[]{:S(2)}) %collective-permute-start.32) | collective-permute-done | bytes 786464 | tf_op jit(solution)/shard_map/ppermute | solution.py:972
  361.6 2.7 fusion.3
  364.8 1.4 collective-permute-start.33
  366.2 2.0 reduce-scatter.3.cloned.1.call-done
  371.3 2.9 collective-permute-done.34.lastx_ref
  375.7 5.2 %make_act.1.r0_ref.act_ref = bf16[512,2048]{1,0:T(8,128)(2,1)} custom-call(f32[512,128]{1,0:T(8,128)} %copy.49.cos_ref, f32[512,128]{1,0:T(8,128)} %pad_maximum_fusion.7.sin_ref, bf16[2,4,512,384]{3,2,1,0:T(8,128)(2,1)} %get-tuple-element.144.dkv_ref, bf16[2,512,384]{2,1,0:T(8,128)(2,1)} %copy-done.6, bf16[512,384]{1,0:T(8,128)(2,1)} %copy-done.26, ...), custom_call_target="tpu_custom_call" | custom-call | flops 10485760 | bytes 6291456 | tf_op jit(solution)/shard_map/make_act/pallas_call | solution.py:797
  380.9 3.9 all-to-all-start.2
  385.7 7.5 %qkv_products.1 = (bf16[576,512]{1,0:T(8,128)(2,1)}, bf16[576,512]{1,0:T(8,128)(2,1)}, bf16[576,512]{1,0:T(8,128)(2,1)}, bf16[576,512]{1,0:T(8,128)(2,1)}) custom-call(s32[3]{0:T(128)} %pad_add_fusion.at_ref.where_ref, bf16[576,512]{1,0:T(8,128)(2,1)} %bitcast.162, bf16[576,512]{1,0:T(8,128)(2,1)} %collective-permute-done.21.l1_ref, ...), custom_call_target="tpu_custom_call" | custom-call | flops 2415919104 | bytes 7733248 | tf_op jit(solution)/shard_map/qkv_products/pallas_call | solution.py:901
  395.3 1.4 collective-permute-start.38
  396.7 8.5 %last.1 = (bf16[512,1152]{1,0:T(8,128)(2,1)}, f32[1,1152]{1,0:T(1,128)}) custom-call(bf16[512,1152]{1,0:T(8,128)(2,1)} %bitcast.154, f32[8,1152]{1,0:T(8,128)} %get-tuple-element.109.gain_ref, f32[512,1152]{1,0:T(8,128)} %get-tuple-element.152.dr_ref, bf16[1152,2048]{1,0:T(8,128)(2,1)} %get-tuple-element.153.w_ref, bf16[512,2048]{1,0:T(8,128)(2,1)} %make_act.1.r0_ref.act_ref), custom_call_target="tpu_custom_call" | custom-call | flops 2264924160 | bytes 10321920 | tf_op jit(solution)/shard_map/last/pallas_call | solution.py:821
  407.8 18.8 %all-to-all-done.2 = bf16[4,2,144,768]{3,2,1,0:T(8,128)(2,1)S(1)} async-done(((bf16[4,2,144,768]{3,2,1,0:T(8,128)(2,1)}), bf16[4,2,144,768]{3,2,1,0:T(8,128)(2,1)S(1)}, u32[]{:S(2)}, u32[]{:S(2)}) %all-to-all-start.2) | async-done | bytes 1769504 | tf_op jit(solution)/shard_map/all_to_all | solution.py:999
  427.7 1.8 fusion.24
  430.4 3.6 all-to-all-start.3
  434.0 2.0 add_convert_fusion.2
  444.1 8.7 %all-to-all-done.3 = bf16[4,144,640]{2,1,0:T(8,128)(2,1)S(1)} async-done(((bf16[4,144,640]{2,1,0:T(8,128)(2,1)}), bf16[4,144,640]{2,1,0:T(8,128)(2,1)S(1)}, u32[]{:S(2)}, u32[]{:S(2)}) %all-to-all-start.3) | async-done | bytes 737312 | tf_op jit(solution)/shard_map/all_to_all | solution.py:999
  452.9 11.5 %collective-permute-done.46 = bf16[256,1152]{1,0:T(8,128)(2,1)} collective-permute-done((bf16[256,1152]{1,0:T(8,128)(2,1)S(1)}, bf16[256,1152]{1,0:T(8,128)(2,1)}, u32[]{:S(2)}, u32[]{:S(2)}) %collective-permute-start.46) | collective-permute-done | bytes 589856 | tf_op jit(solution)/shard_map/ppermute | solution.py:972
  464.4 1.4 convert_add_fusion
  466.7 3.5 all-to-all-start.4
  471.6 6.2 %collective-permute-done.43.p2_ref = bf16[2,144,768]{2,1,0:T(8,128)(2,1)} collective-permute-done((bf16[2,144,768]{2,1,0:T(8,128)(2,1)}, bf16[2,144,768]{2,1,0:T(8,128)(2,1)}, u32[]{:S(2)}, u32[]{:S(2)}) %collective-permute-start.43) | collective-permute-done | bytes 442400 | tf_op jit(solution)/shard_map/ppermute | solution.py:972
  477.8 4.4 place_gu.1
  485.3 2.1 place_qkv.1
  (211 shorter events, 73.7 us)
Async XLA Ops:
  7.2 9.1 %copy-start.16 = (bf16[144,1152]{1,0:T(8,128)(2,1)S(1)}, bf16[144,1152]{1,0:T(8,128)(2,1)}, u32[]{:S(2)}) copy-start(bf16[144,1152]{1,0:T(8,128)(2,1)} %param.18) | copy-start | bytes 995332
  10.6 17.5 %collective-permute-start.2 = (bf16[144,512]{1,0:T(8,128)(2,1)}, bf16[144,512]{1,0:T(8,128)(2,1)}, u32[]{:S(2)}, u32[]{:S(2)}) collective-permute-start(bf16[144,512]{1,0:T(8,128)(2,1)} %constant_dynamic-slice_fusion.5), channel_id=1, source_target_pairs={{0,6},{1,7},{2,4},{3,5},{4,2},{5,3},{6,0},{7,1},{8,14},{9,15},{10,... | collective-permute-start | bytes 442376 | tf_op jit(solution)/shard_map/ppermute | solution.py:976
  15.7 12.8 %collective-permute-start.1 = (bf16[144,512]{1,0:T(8,128)(2,1)}, bf16[144,512]{1,0:T(8,128)(2,1)}, u32[]{:S(2)}, u32[]{:S(2)}) collective-permute-start(bf16[144,512]{1,0:T(8,128)(2,1)} %constant_dynamic-slice_fusion.5), channel_id=1, source_target_pairs={{0,4},{1,5},{2,6},{3,7},{4,0},{5,1},{6,2},{7,3},{8,12},{9,13},{10,... | collective-permute-start | bytes 442376 | tf_op jit(solution)/shard_map/ppermute | solution.py:976
  15.7 12.8 %collective-permute-start = (bf16[144,512]{1,0:T(8,128)(2,1)}, bf16[144,512]{1,0:T(8,128)(2,1)}, u32[]{:S(2)}, u32[]{:S(2)}) collective-permute-start(bf16[144,512]{1,0:T(8,128)(2,1)} %constant_dynamic-slice_fusion.5), channel_id=1, source_target_pairs={{0,2},{1,3},{2,0},{3,1},{4,6},{5,7},{6,4},{7,5},{8,10},{9,11},{10,... | collective-permute-start | bytes 442376 | tf_op jit(solution)/shard_map/ppermute | solution.py:976
  16.6 43.4 %collective-permute-start.6 = (bf16[144,9344]{1,0:T(8,128)(2,1)S(1)}, bf16[144,9344]{1,0:T(8,128)(2,1)}, u32[]{:S(2)}, u32[]{:S(2)}) collective-permute-start(bf16[144,9344]{1,0:T(8,128)(2,1)S(1)} %pad_maximum_fusion.own0_ref.refs_10_), channel_id=1, source_target_pairs={{0,1},{1,0},{2,3},{3,2},{4,5},{5,4},{6,7},{7,6},{8,9},{9,8},{10,11... | collective-permute-start | bytes 8073224 | tf_op jit(solution)/shard_map/ppermute | solution.py:980
  28.5 55.9 %all-to-all-start = ((bf16[4,144,1920]{2,1,0:T(8,128)(2,1)}), bf16[4,144,1920]{2,1,0:T(8,128)(2,1)}, u32[]{:S(2)}, u32[]{:S(2)}) async-start(bf16[4,144,1920]{2,1,0:T(8,128)(2,1)} %broadcast_in_dim.13), calls=%async_computation | async-start | bytes 4423680 | tf_op jit(solution)/shard_map/all_to_all | solution.py:999
  36.1 14.1 %collective-permute-start.5 = (bf16[432,512]{1,0:T(8,128)(2,1)S(1)}, bf16[432,512]{1,0:T(8,128)(2,1)S(1)}, u32[]{:S(2)}, u32[]{:S(2)}) collective-permute-start(bf16[432,512]{1,0:T(8,128)(2,1)S(1)} %constant_dynamic-update-slice_fusion), channel_id=1, source_target_pairs={{0,24},{8,16},{16,8},{24,0},{1,25},{9,17},{17,9},{25,1},{2,26},{10... | collective-permute-start | bytes 1327112 | tf_op jit(solution)/shard_map/ppermute | solution.py:972
  38.6 19.9 %collective-permute-start.4 = (bf16[432,512]{1,0:T(8,128)(2,1)S(1)}, bf16[432,512]{1,0:T(8,128)(2,1)S(1)}, u32[]{:S(2)}, u32[]{:S(2)}) collective-permute-start(bf16[432,512]{1,0:T(8,128)(2,1)S(1)} %constant_dynamic-update-slice_fusion), channel_id=1, source_target_pairs={{0,16},{8,24},{16,0},{24,8},{1,17},{9,25},{17,1},{25,9},{2,18},{10... | collective-permute-start | bytes 1327112 | tf_op jit(solution)/shard_map/ppermute | solution.py:972
  39.1 19.5 %collective-permute-start.3 = (bf16[432,512]{1,0:T(8,128)(2,1)S(1)}, bf16[432,512]{1,0:T(8,128)(2,1)S(1)}, u32[]{:S(2)}, u32[]{:S(2)}) collective-permute-start(bf16[432,512]{1,0:T(8,128)(2,1)S(1)} %constant_dynamic-update-slice_fusion), channel_id=1, source_target_pairs={{0,8},{8,0},{16,24},{24,16},{1,9},{9,1},{17,25},{25,17},{2,10},{10... | collective-permute-start | bytes 1327112 | tf_op jit(solution)/shard_map/ppermute | solution.py:972
  60.0 3.9 collective-permute-start.7
  84.4 92.2 %all-to-all-start.1 = ((bf16[4,384,1152]{2,1,0:T(8,128)(2,1)}), bf16[4,384,1152]{2,1,0:T(8,128)(2,1)}, u32[]{:S(2)}, u32[]{:S(2)}) async-start(bf16[4,384,1152]{2,1,0:T(8,128)(2,1)} %broadcast_in_dim.12), calls=%async_computation.1 | async-start | bytes 7077888 | tf_op jit(solution)/shard_map/all_to_all | solution.py:999
  89.1 277.1 %reduce-scatter.5.cloned.1.call-start = ((), (), s32[]{:S(2)}) async-start(), calls=%async_computation.8 | async-start | bytes 2985984 | tf_op jit(solution)/shard_map/reduce_scatter | solution.py:1107
  89.4 18.9 %collective-permute-start.9 = (bf16[512,768]{1,0:T(8,128)(2,1)}, bf16[512,768]{1,0:T(8,128)(2,1)}, u32[]{:S(2)}, u32[]{:S(2)}) collective-permute-start(bf16[512,768]{1,0:T(8,128)(2,1)} %get-tuple-element.103), channel_id=1, source_target_pairs={{0,16},{8,24},{16,0},{24,8},{1,17},{9,25},{17,1},{25,9},{2,18},{10... | collective-permute-start | bytes 2359304 | tf_op jit(solution)/shard_map/ppermute | solution.py:972
  91.0 19.9 %collective-permute-start.8 = (bf16[512,768]{1,0:T(8,128)(2,1)}, bf16[512,768]{1,0:T(8,128)(2,1)}, u32[]{:S(2)}, u32[]{:S(2)}) collective-permute-start(bf16[512,768]{1,0:T(8,128)(2,1)} %get-tuple-element.103), channel_id=1, source_target_pairs={{0,8},{8,0},{16,24},{24,16},{1,9},{9,1},{17,25},{25,17},{2,10},{10... | collective-permute-start | bytes 2359304 | tf_op jit(solution)/shard_map/ppermute | solution.py:972
  109.3 9.4 %collective-permute-start.10 = (bf16[256,768]{1,0:T(8,128)(2,1)S(1)}, bf16[256,768]{1,0:T(8,128)(2,1)S(1)}, u32[]{:S(2)}, u32[]{:S(2)}) collective-permute-start(bf16[256,768]{1,0:T(8,128)(2,1)S(1)} %slice.338), channel_id=1, source_target_pairs={{0,8},{8,0},{16,24},{24,16},{1,9},{9,1},{17,25},{25,17},{2,10},{10... | collective-permute-start | bytes 1179656 | tf_op jit(solution)/shard_map/ppermute | solution.py:972
  111.9 9.0 %collective-permute-start.11 = (bf16[256,768]{1,0:T(8,128)(2,1)S(1)}, bf16[256,768]{1,0:T(8,128)(2,1)S(1)}, u32[]{:S(2)}, u32[]{:S(2)}) collective-permute-start(bf16[256,768]{1,0:T(8,128)(2,1)S(1)} %slice.339), channel_id=1, source_target_pairs={{0,16},{8,24},{16,0},{24,8},{1,17},{9,25},{17,1},{25,9},{2,18},{10... | collective-permute-start | bytes 1179656 | tf_op jit(solution)/shard_map/ppermute | solution.py:972
  120.9 35.6 %collective-permute-start.15 = (bf16[432,1920]{1,0:T(8,128)(2,1)}, bf16[432,1920]{1,0:T(8,128)(2,1)}, u32[]{:S(2)}, u32[]{:S(2)}) collective-permute-start(bf16[432,1920]{1,0:T(8,128)(2,1)} %pad_maximum_fusion.3), channel_id=1, source_target_pairs={{0,16},{8,24},{16,0},{24,8},{1,17},{9,25},{17,1},{25,9},{2,18},{10... | collective-permute-start | bytes 4976648 | tf_op jit(solution)/shard_map/ppermute | solution.py:972
  122.5 35.2 %collective-permute-start.13 = (bf16[432,1920]{1,0:T(8,128)(2,1)}, bf16[432,1920]{1,0:T(8,128)(2,1)}, u32[]{:S(2)}, u32[]{:S(2)}) collective-permute-start(bf16[432,1920]{1,0:T(8,128)(2,1)} %pad_maximum_fusion.3), channel_id=1, source_target_pairs={{0,8},{8,0},{16,24},{24,16},{1,9},{9,1},{17,25},{25,17},{2,10},{10... | collective-permute-start | bytes 4976648 | tf_op jit(solution)/shard_map/ppermute | solution.py:972
  160.1 16.3 %collective-permute-start.17 = (bf16[216,1920]{1,0:T(8,128)(2,1)S(1)}, bf16[216,1920]{1,0:T(8,128)(2,1)S(1)}, u32[]{:S(2)}, u32[]{:S(2)}) collective-permute-start(bf16[216,1920]{1,0:T(8,128)(2,1)S(1)} %slice.268), channel_id=1, source_target_pairs={{0,8},{8,0},{16,24},{24,16},{1,9},{9,1},{17,25},{25,17},{2,10},{10... | collective-permute-start | bytes 2488328 | tf_op jit(solution)/shard_map/ppermute | solution.py:972
  160.7 15.9 %collective-permute-start.18 = (bf16[216,1920]{1,0:T(8,128)(2,1)S(1)}, bf16[216,1920]{1,0:T(8,128)(2,1)S(1)}, u32[]{:S(2)}, u32[]{:S(2)}) collective-permute-start(bf16[216,1920]{1,0:T(8,128)(2,1)S(1)} %slice.269), channel_id=1, source_target_pairs={{0,16},{8,24},{16,0},{24,8},{1,17},{9,25},{17,1},{25,9},{2,18},{10... | collective-permute-start | bytes 2488328 | tf_op jit(solution)/shard_map/ppermute | solution.py:972
  161.2 16.3 %collective-permute-start.12 = (bf16[3,144,1920]{2,1,0:T(8,128)(2,1)}, bf16[3,144,1920]{2,1,0:T(8,128)(2,1)}, u32[]{:S(2)}, u32[]{:S(2)}) collective-permute-start(bf16[3,144,1920]{2,1,0:T(8,128)(2,1)} %bitcast.16.refs_0_), channel_id=1, source_target_pairs={{0,1},{1,0},{2,3},{3,2},{4,5},{5,4},{6,7},{7,6},{8,9},{9,8},{10,11... | collective-permute-start | bytes 4976648 | tf_op jit(solution)/shard_map/ppermute | solution.py:980
  176.7 14.7 %collective-permute-start.20 = (bf16[4,384,1152]{2,1,0:T(8,128)(2,1)}, bf16[4,384,1152]{2,1,0:T(8,128)(2,1)S(1)}, u32[]{:S(2)}, u32[]{:S(2)}) collective-permute-start(bf16[4,384,1152]{2,1,0:T(8,128)(2,1)} %all-to-all-done.1.refs_8_), channel_id=1, source_target_pairs={{0,1},{1,0},{2,3},{3,2},{4,5},{5,4},{6,7},{7,6},{8,9},{9,8},{10,11... | collective-permute-start | bytes 10616840 | tf_op jit(solution)/shard_map/ppermute | solution.py:980
  176.7 8.8 %collective-permute-start.14 = (bf16[3,144,1920]{2,1,0:T(8,128)(2,1)}, bf16[3,144,1920]{2,1,0:T(8,128)(2,1)S(1)}, u32[]{:S(2)}, u32[]{:S(2)}) collective-permute-start(bf16[3,144,1920]{2,1,0:T(8,128)(2,1)} %bitcast.17.refs_2_), channel_id=1, source_target_pairs={{0,1},{1,0},{2,3},{3,2},{4,5},{5,4},{6,7},{7,6},{8,9},{9,8},{10,11... | collective-permute-start | bytes 4976648 | tf_op jit(solution)/shard_map/ppermute | solution.py:980
  177.2 10.7 %collective-permute-start.16 = (bf16[3,144,1920]{2,1,0:T(8,128)(2,1)}, bf16[3,144,1920]{2,1,0:T(8,128)(2,1)S(1)}, u32[]{:S(2)}, u32[]{:S(2)}) collective-permute-start(bf16[3,144,1920]{2,1,0:T(8,128)(2,1)} %bitcast.18.refs_4_), channel_id=1, source_target_pairs={{0,1},{1,0},{2,3},{3,2},{4,5},{5,4},{6,7},{7,6},{8,9},{9,8},{10,11... | collective-permute-start | bytes 4976648 | tf_op jit(solution)/shard_map/ppermute | solution.py:980
  178.8 14.8 %copy-start.13 = (bf16[432,1920]{1,0:T(8,128)(2,1)}, bf16[432,1920]{1,0:T(8,128)(2,1)S(1)}, u32[]{:S(2)}) copy-start(bf16[432,1920]{1,0:T(8,128)(2,1)S(1)} %pad_maximum_fusion.4) | copy-start | bytes 4976644
  187.8 3.5 collective-permute-start.19
  193.6 53.1 %copy-start.17 = (bf16[512,1152]{1,0:T(8,128)(2,1)S(1)}, bf16[512,1152]{1,0:T(8,128)(2,1)}, u32[]{:S(2)}) copy-start(bf16[512,1152]{1,0:T(8,128)(2,1)} %get-tuple-element.108.ho_ref.o_ref) | copy-start | bytes 3538948
  251.3 116.9 %reduce-scatter.3.cloned.1.call-start = ((), (), s32[]{:S(2)}) async-start(), calls=%async_computation.7 | async-start | bytes 7962624 | tf_op jit(solution)/shard_map/reduce_scatter | solution.py:1107
  252.8 6.8 %collective-permute-start.23 = (bf16[2,512,768]{2,1,0:T(8,128)(2,1)S(1)}, bf16[2,512,768]{2,1,0:T(8,128)(2,1)S(1)}, u32[]{:S(2)}, u32[]{:S(2)}) collective-permute-start(bf16[2,512,768]{2,1,0:T(8,128)(2,1)S(1)} %copy-done.34), channel_id=1, source_target_pairs={{0,1},{1,0},{2,3},{3,2},{4,5},{5,4},{6,7},{7,6},{8,9},{9,8},{10,11... | collective-permute-start | bytes 4718600 | tf_op jit(solution)/shard_map/ppermute | solution.py:980
  252.9 8.8 %collective-permute-start.24 = (bf16[2,512,768]{2,1,0:T(8,128)(2,1)}, bf16[2,512,768]{2,1,0:T(8,128)(2,1)S(1)}, u32[]{:S(2)}, u32[]{:S(2)}) collective-permute-start(bf16[2,512,768]{2,1,0:T(8,128)(2,1)} %get-tuple-element.124.u0_ref), channel_id=1, source_target_pairs={{0,1},{1,0},{2,3},{3,2},{4,5},{5,4},{6,7},{7,6},{8,9},{9,8},{10,11... | collective-permute-start | bytes 4718600 | tf_op jit(solution)/shard_map/ppermute | solution.py:980
  254.2 5.4 %collective-permute-start.22 = (bf16[576,512]{1,0:T(8,128)(2,1)S(1)}, bf16[576,512]{1,0:T(8,128)(2,1)S(1)}, u32[]{:S(2)}, u32[]{:S(2)}) collective-permute-start(bf16[576,512]{1,0:T(8,128)(2,1)S(1)} %get-tuple-element.202), channel_id=1, source_target_pairs={{0,1},{1,0},{2,3},{3,2},{4,5},{5,4},{6,7},{7,6},{8,9},{9,8},{10,11... | collective-permute-start | bytes 1769480 | tf_op jit(solution)/shard_map/ppermute | solution.py:980
  254.3 20.5 %collective-permute-start.25 = (bf16[2,512,768]{2,1,0:T(8,128)(2,1)}, bf16[2,512,768]{2,1,0:T(8,128)(2,1)}, u32[]{:S(2)}, u32[]{:S(2)}) collective-permute-start(bf16[2,512,768]{2,1,0:T(8,128)(2,1)} %get-tuple-element.126.g0_ref), channel_id=1, source_target_pairs={{0,1},{1,0},{2,3},{3,2},{4,5},{5,4},{6,7},{7,6},{8,9},{9,8},{10,11... | collective-permute-start | bytes 4718600 | tf_op jit(solution)/shard_map/ppermute | solution.py:980
  254.7 20.2 %collective-permute-start.26 = (bf16[2,512,768]{2,1,0:T(8,128)(2,1)}, bf16[2,512,768]{2,1,0:T(8,128)(2,1)}, u32[]{:S(2)}, u32[]{:S(2)}) collective-permute-start(bf16[2,512,768]{2,1,0:T(8,128)(2,1)} %get-tuple-element.128.u0_ref), channel_id=1, source_target_pairs={{0,1},{1,0},{2,3},{3,2},{4,5},{5,4},{6,7},{7,6},{8,9},{9,8},{10,11... | collective-permute-start | bytes 4718600 | tf_op jit(solution)/shard_map/ppermute | solution.py:980
  262.9 10.9 %copy-start.18 = (bf16[1152,512]{1,0:T(8,128)(2,1)S(1)}, bf16[1152,512]{1,0:T(8,128)(2,1)}, u32[]{:S(2)}) copy-start(bf16[1152,512]{1,0:T(8,128)(2,1)} %get-tuple-element.117) | copy-start | bytes 3538948
  271.5 41.8 %collective-permute-start.28 = (bf16[2,576,768]{2,1,0:T(8,128)(2,1)}, bf16[2,576,768]{2,1,0:T(8,128)(2,1)}, u32[]{:S(2)}, u32[]{:S(2)}) collective-permute-start(bf16[2,576,768]{2,1,0:T(8,128)(2,1)} %get-tuple-element.125), channel_id=1, source_target_pairs={{0,8},{8,0},{16,24},{24,16},{1,9},{9,1},{17,25},{25,17},{2,10},{10... | collective-permute-start | bytes 5308424 | tf_op jit(solution)/shard_map/ppermute | solution.py:972
  273.0 40.8 %collective-permute-start.27 = (bf16[2,576,768]{2,1,0:T(8,128)(2,1)}, bf16[2,576,768]{2,1,0:T(8,128)(2,1)S(1)}, u32[]{:S(2)}, u32[]{:S(2)}) collective-permute-start(bf16[2,576,768]{2,1,0:T(8,128)(2,1)} %get-tuple-element.130), channel_id=1, source_target_pairs={{0,16},{8,24},{16,0},{24,8},{1,17},{9,25},{17,1},{25,9},{2,18},{10... | collective-permute-start | bytes 5308424 | tf_op jit(solution)/shard_map/ppermute | solution.py:972
  274.8 95.6 %collective-permute-start.21 = (bf16[576,512]{1,0:T(8,128)(2,1)}, bf16[576,512]{1,0:T(8,128)(2,1)}, u32[]{:S(2)}, u32[]{:S(2)}) collective-permute-start(bf16[576,512]{1,0:T(8,128)(2,1)} %bitcast.23), channel_id=1, source_target_pairs={{0,1},{1,0},{2,3},{3,2},{4,5},{5,4},{6,7},{7,6},{8,9},{9,8},{10,11... | collective-permute-start | bytes 1769480 | tf_op jit(solution)/shard_map/ppermute | solution.py:980
  317.0 21.9 %collective-permute-start.29 = (bf16[576,768]{1,0:T(8,128)(2,1)}, bf16[576,768]{1,0:T(8,128)(2,1)}, u32[]{:S(2)}, u32[]{:S(2)}) collective-permute-start(bf16[576,768]{1,0:T(8,128)(2,1)} %fusion.2), channel_id=1, source_target_pairs={{0,16},{8,24},{16,0},{24,8},{1,17},{9,25},{17,1},{25,9},{2,18},{10... | collective-permute-start | bytes 2654216 | tf_op jit(solution)/shard_map/ppermute | solution.py:972
  319.0 22.0 %collective-permute-start.30 = (bf16[576,768]{1,0:T(8,128)(2,1)}, bf16[576,768]{1,0:T(8,128)(2,1)S(1)}, u32[]{:S(2)}, u32[]{:S(2)}) collective-permute-start(bf16[576,768]{1,0:T(8,128)(2,1)} %fusion.1), channel_id=1, source_target_pairs={{0,8},{8,0},{16,24},{24,16},{1,9},{9,1},{17,25},{25,17},{2,10},{10... | collective-permute-start | bytes 2654216 | tf_op jit(solution)/shard_map/ppermute | solution.py:972
  336.3 7.6 %copy-start.11 = (bf16[2,576,768]{2,1,0:T(8,128)(2,1)S(1)}, bf16[2,576,768]{2,1,0:T(8,128)(2,1)}, u32[]{:S(2)}) copy-start(bf16[2,576,768]{2,1,0:T(8,128)(2,1)} %get-tuple-element.131) | copy-start | bytes 5308420
  342.5 19.0 %collective-permute-start.32 = (bf16[2,512,384]{2,1,0:T(8,128)(2,1)S(1)}, bf16[2,512,384]{2,1,0:T(8,128)(2,1)S(1)}, u32[]{:S(2)}, u32[]{:S(2)}) collective-permute-start(bf16[2,512,384]{2,1,0:T(8,128)(2,1)S(1)} %get-tuple-element.193), channel_id=1, source_target_pairs={{0,16},{8,24},{16,0},{24,8},{1,17},{9,25},{17,1},{25,9},{2,18},{10... | collective-permute-start | bytes 2359304 | tf_op jit(solution)/shard_map/ppermute | solution.py:972
  343.3 18.3 %collective-permute-start.31 = (bf16[2,512,384]{2,1,0:T(8,128)(2,1)S(1)}, bf16[2,512,384]{2,1,0:T(8,128)(2,1)S(1)}, u32[]{:S(2)}, u32[]{:S(2)}) collective-permute-start(bf16[2,512,384]{2,1,0:T(8,128)(2,1)S(1)} %get-tuple-element.194), channel_id=1, source_target_pairs={{0,8},{8,0},{16,24},{24,16},{1,9},{9,1},{17,25},{25,17},{2,10},{10... | collective-permute-start | bytes 2359304 | tf_op jit(solution)/shard_map/ppermute | solution.py:972
  361.5 7.9 %copy-start.5 = (bf16[2,512,384]{2,1,0:T(8,128)(2,1)}, bf16[2,512,384]{2,1,0:T(8,128)(2,1)S(1)}, u32[]{:S(2)}) copy-start(bf16[2,512,384]{2,1,0:T(8,128)(2,1)S(1)} %collective-permute-done.32.gy_ref) | copy-start | bytes 2359300
  361.6 7.8 %copy-start.6 = (bf16[2,512,384]{2,1,0:T(8,128)(2,1)}, bf16[2,512,384]{2,1,0:T(8,128)(2,1)S(1)}, u32[]{:S(2)}) copy-start(bf16[2,512,384]{2,1,0:T(8,128)(2,1)S(1)} %collective-permute-done.31.gx_ref) | copy-start | bytes 2359300
  364.3 9.9 %collective-permute-start.34 = (bf16[512,384]{1,0:T(8,128)(2,1)}, bf16[512,384]{1,0:T(8,128)(2,1)S(1)}, u32[]{:S(2)}, u32[]{:S(2)}) collective-permute-start(bf16[512,384]{1,0:T(8,128)(2,1)} %get-tuple-element.191), channel_id=1, source_target_pairs={{0,8},{8,0},{16,24},{24,16},{1,9},{9,1},{17,25},{25,17},{2,10},{10... | collective-permute-start | bytes 1179656 | tf_op jit(solution)/shard_map/ppermute | solution.py:972
  364.8 9.6 %collective-permute-start.33 = (bf16[512,384]{1,0:T(8,128)(2,1)}, bf16[512,384]{1,0:T(8,128)(2,1)S(1)}, u32[]{:S(2)}, u32[]{:S(2)}) collective-permute-start(bf16[512,384]{1,0:T(8,128)(2,1)} %get-tuple-element.192), channel_id=1, source_target_pairs={{0,16},{8,24},{16,0},{24,8},{1,17},{9,25},{17,1},{25,9},{2,18},{10... | collective-permute-start | bytes 1179656 | tf_op jit(solution)/shard_map/ppermute | solution.py:972
  380.9 4.8 collective-permute-start.35
  380.9 45.7 %all-to-all-start.2 = ((bf16[4,2,144,768]{3,2,1,0:T(8,128)(2,1)}), bf16[4,2,144,768]{3,2,1,0:T(8,128)(2,1)S(1)}, u32[]{:S(2)}, u32[]{:S(2)}) async-start(bf16[4,2,144,768]{3,2,1,0:T(8,128)(2,1)} %maximum_maximum_fusion), calls=%async_computation.4 | async-start | bytes 3538944 | tf_op jit(solution)/shard_map/all_to_all | solution.py:999
  384.8 21.2 %collective-permute-start.40 = (bf16[272,1152]{1,0:T(8,128)(2,1)S(1)}, bf16[272,1152]{1,0:T(8,128)(2,1)S(1)}, u32[]{:S(2)}, u32[]{:S(2)}) collective-permute-start(bf16[272,1152]{1,0:T(8,128)(2,1)S(1)} %pad_maximum_fusion.5), channel_id=1, source_target_pairs={{0,16},{8,24},{16,0},{24,8},{1,17},{9,25},{17,1},{25,9},{2,18},{10... | collective-permute-start | bytes 1880072 | tf_op jit(solution)/shard_map/ppermute | solution.py:972
  393.2 34.4 %collective-permute-start.36 = (bf16[576,512]{1,0:T(8,128)(2,1)}, bf16[576,512]{1,0:T(8,128)(2,1)}, u32[]{:S(2)}, u32[]{:S(2)}) collective-permute-start(bf16[576,512]{1,0:T(8,128)(2,1)} %get-tuple-element.157), channel_id=1, source_target_pairs={{0,8},{8,0},{16,24},{24,16},{1,9},{9,1},{17,25},{25,17},{2,10},{10... | collective-permute-start | bytes 1769480 | tf_op jit(solution)/shard_map/ppermute | solution.py:972
  394.2 33.4 %collective-permute-start.37 = (bf16[576,512]{1,0:T(8,128)(2,1)}, bf16[576,512]{1,0:T(8,128)(2,1)}, u32[]{:S(2)}, u32[]{:S(2)}) collective-permute-start(bf16[576,512]{1,0:T(8,128)(2,1)} %get-tuple-element.159), channel_id=1, source_target_pairs={{0,16},{8,24},{16,0},{24,8},{1,17},{9,25},{17,1},{25,9},{2,18},{10... | collective-permute-start | bytes 1769480 | tf_op jit(solution)/shard_map/ppermute | solution.py:972
  395.3 32.3 %collective-permute-start.38 = (bf16[576,512]{1,0:T(8,128)(2,1)}, bf16[576,512]{1,0:T(8,128)(2,1)}, u32[]{:S(2)}, u32[]{:S(2)}) collective-permute-start(bf16[576,512]{1,0:T(8,128)(2,1)} %get-tuple-element.161), channel_id=1, source_target_pairs={{0,24},{8,16},{16,8},{24,0},{1,25},{9,17},{17,9},{25,1},{2,26},{10... | collective-permute-start | bytes 1769480 | tf_op jit(solution)/shard_map/ppermute | solution.py:972
  396.7 8.5 %copy-start.28 = (f32[1,1152]{1,0:T(1,128)S(1)}, f32[1,1152]{1,0:T(1,128)}, u32[]{:S(2)}) copy-start(f32[1,1152]{1,0:T(1,128)} %get-tuple-element.163) | copy-start | bytes 13828
  396.7 30.9 %copy-start.24 = (bf16[576,512]{1,0:T(8,128)(2,1)S(1)}, bf16[576,512]{1,0:T(8,128)(2,1)}, u32[]{:S(2)}) copy-start(bf16[576,512]{1,0:T(8,128)(2,1)} %get-tuple-element.156) | copy-start | bytes 1769476
  405.9 20.7 %collective-permute-start.39 = (f32[2,1152]{1,0:T(2,128)S(1)}, f32[2,1152]{1,0:T(2,128)S(1)}, u32[]{:S(2)}, u32[]{:S(2)}) collective-permute-start(f32[2,1152]{1,0:T(2,128)S(1)} %pad_maximum_fusion.8), channel_id=1, source_target_pairs={{0,1},{1,0},{2,3},{3,2},{4,5},{5,4},{6,7},{7,6},{8,9},{9,8},{10,11... | collective-permute-start | bytes 27656 | tf_op jit(solution)/shard_map/ppermute | solution.py:980
  406.8 29.2 %collective-permute-start.45 = (bf16[256,1152]{1,0:T(8,128)(2,1)}, bf16[256,1152]{1,0:T(8,128)(2,1)}, u32[]{:S(2)}, u32[]{:S(2)}) collective-permute-start(bf16[256,1152]{1,0:T(8,128)(2,1)} %slice.340), channel_id=1, source_target_pairs={{0,8},{8,0},{16,24},{24,16},{1,9},{9,1},{17,25},{25,17},{2,10},{10... | collective-permute-start | bytes 1769480 | tf_op jit(solution)/shard_map/ppermute | solution.py:972
  430.4 22.4 %all-to-all-start.3 = ((bf16[4,144,640]{2,1,0:T(8,128)(2,1)}), bf16[4,144,640]{2,1,0:T(8,128)(2,1)S(1)}, u32[]{:S(2)}, u32[]{:S(2)}) async-start(bf16[4,144,640]{2,1,0:T(8,128)(2,1)} %fusion.5), calls=%async_computation.5 | async-start | bytes 1474560 | tf_op jit(solution)/shard_map/all_to_all | solution.py:999
  436.0 28.3 %collective-permute-start.41 = (bf16[272,1152]{1,0:T(8,128)(2,1)}, bf16[272,1152]{1,0:T(8,128)(2,1)}, u32[]{:S(2)}, u32[]{:S(2)}) collective-permute-start(bf16[272,1152]{1,0:T(8,128)(2,1)} %add_convert_fusion.2), channel_id=1, source_target_pairs={{0,8},{8,0},{16,24},{24,16},{1,9},{9,1},{17,25},{25,17},{2,10},{10... | collective-permute-start | bytes 1880072 | tf_op jit(solution)/shard_map/ppermute | solution.py:972
  438.4 25.9 %copy-start.4 = (bf16[256,1152]{1,0:T(8,128)(2,1)}, bf16[256,1152]{1,0:T(8,128)(2,1)S(1)}, u32[]{:S(2)}) copy-start(bf16[256,1152]{1,0:T(8,128)(2,1)S(1)} %add_convert_fusion.3) | copy-start | bytes 1769476
  438.4 25.9 %collective-permute-start.46 = (bf16[256,1152]{1,0:T(8,128)(2,1)S(1)}, bf16[256,1152]{1,0:T(8,128)(2,1)}, u32[]{:S(2)}, u32[]{:S(2)}) collective-permute-start(bf16[256,1152]{1,0:T(8,128)(2,1)S(1)} %add_convert_fusion.3), channel_id=1, source_target_pairs={{0,16},{8,24},{16,0},{24,8},{1,17},{9,25},{17,1},{25,9},{2,18},{10... | collective-permute-start | bytes 1769480 | tf_op jit(solution)/shard_map/ppermute | solution.py:972
  440.6 30.9 %collective-permute-start.44 = (bf16[2,144,768]{2,1,0:T(8,128)(2,1)}, bf16[2,144,768]{2,1,0:T(8,128)(2,1)}, u32[]{:S(2)}, u32[]{:S(2)}) collective-permute-start(bf16[2,144,768]{2,1,0:T(8,128)(2,1)} %fusion.6.p0_ref), channel_id=1, source_target_pairs={{0,24},{8,16},{16,8},{24,0},{1,25},{9,17},{17,9},{25,1},{2,26},{10... | collective-permute-start | bytes 1327112 | tf_op jit(solution)/shard_map/ppermute | solution.py:972
  442.0 35.8 %collective-permute-start.43 = (bf16[2,144,768]{2,1,0:T(8,128)(2,1)}, bf16[2,144,768]{2,1,0:T(8,128)(2,1)}, u32[]{:S(2)}, u32[]{:S(2)}) collective-permute-start(bf16[2,144,768]{2,1,0:T(8,128)(2,1)} %fusion.6.p0_ref), channel_id=1, source_target_pairs={{0,16},{8,24},{16,0},{24,8},{1,17},{9,25},{17,1},{25,9},{2,18},{10... | collective-permute-start | bytes 1327112 | tf_op jit(solution)/shard_map/ppermute | solution.py:972
  443.1 34.7 %collective-permute-start.42 = (bf16[2,144,768]{2,1,0:T(8,128)(2,1)}, bf16[2,144,768]{2,1,0:T(8,128)(2,1)}, u32[]{:S(2)}, u32[]{:S(2)}) collective-permute-start(bf16[2,144,768]{2,1,0:T(8,128)(2,1)} %fusion.6.p0_ref), channel_id=1, source_target_pairs={{0,8},{8,0},{16,24},{24,16},{1,9},{9,1},{17,25},{25,17},{2,10},{10... | collective-permute-start | bytes 1327112 | tf_op jit(solution)/shard_map/ppermute | solution.py:972
  466.7 17.7 %all-to-all-start.4 = ((bf16[4,144,640]{2,1,0:T(8,128)(2,1)}), bf16[4,144,640]{2,1,0:T(8,128)(2,1)S(1)}, u32[]{:S(2)}, u32[]{:S(2)}) async-start(bf16[4,144,640]{2,1,0:T(8,128)(2,1)} %broadcast_in_dim.17), calls=%async_computation.6 | async-start | bytes 1474560 | tf_op jit(solution)/shard_map/all_to_all | solution.py:1163
  (28 other events, 74.9 us)
Sparse Core Ops, SparseCore 0:
  251.4 37.5 reduce-scatter.4
  291.4 76.7 reduce-scatter.2
